TPU v7x, 32 devices: a whole 2x2x4 slice. The times are simulated.
32 devices in a mesh: groups: 2 (over y), dp: 8 (over z, x), tensor: 2 (over core).
Axes of the slice: x: 2, y: 2, z: 4, core: 2. Of those that a mesh axis runs over, the one named last changes fastest.
Arguments:
- inputs: bfloat16 [2048, 14336], P(('groups', 'dp'), 'tensor'), parts along dimension 0, may hold values from -6 to 6
- out_grads: bfloat16 [2048, 4096], P(('groups', 'dp'), 'tensor'), parts along dimension 0, may hold values from -6 to 6
- proj_in: bfloat16 [14336, 64], replicated, may hold values from -0.046875 to 0.046875
- proj_out: bfloat16 [4096, 64], replicated, may hold values from -0.09375 to 0.09375
- doc_ids: int32 [16, 128], P(('groups', 'dp')), parts along dimension 0, may hold values from 0 to 7, never falling along the last dimension, each value on 1 to 64 neighbouring positions
- queries: float32 [16, 4096], replicated, may hold values from -6 to 6
Outputs:
- gram: float32 [128, 64], P(('groups', 'dp'), 'tensor'), parts along dimension 0
- scores: float32 [128, 16], P(('groups', 'dp')), parts along dimension 0
There are 2 independent parts, one for each index of `groups`. A program takes and returns all parts, laid end to end along the dimension named above; an argument that names none is the same for every part. Nothing has to cross between parts.
Inputs may be any that keep to these rules, and one draw needn't show every extreme that they name: `doc_ids`: within each block of 128 tokens ids never fall, every id 0 to 7 occurs, and one document has exactly 64 tokens.
All inputs are finite; a program needn't handle non-finite values.
Results may differ from a plain program's by a relative error of at most 0.0003.
Values may be sent and summed in bfloat16 or wider, within the bound.
No kernel may reach another device: no remote copies, remote signals or barrier semaphores. Data moves between devices by JAX's collectives and lax.ppermute only.
A program may use at most 64 MiB of HBM per device.

v0:
```python
import jax
import jax.numpy as jnp
from jax import lax
from jax.sharding import PartitionSpec as P

DOCS_DEV = 8


def local(inputs, out_grads, proj_in, proj_out, doc_ids, queries):
    position = lax.axis_index("tensor")
    pair_size = lax.axis_size("tensor")
    rank = proj_in.shape[1]
    full_in, full_grad = (
        lax.all_gather(inputs, "tensor", axis=1, tiled=True),
        lax.all_gather(out_grads, "tensor", axis=1, tiled=True),
    )
    in_code = jnp.dot(full_in, proj_in, preferred_element_type=jnp.float32)
    grad_code = jnp.dot(full_grad, proj_out, preferred_element_type=jnp.float32)
    tok_count = inputs.shape[0]
    onehot = (doc_ids[0][:, None] == jnp.arange(DOCS_DEV, dtype=jnp.int32)[None, :]).astype(
        jnp.float32
    )
    weighted = (onehot[:, :, None] * grad_code[:, None, :]).reshape(tok_count, DOCS_DEV * rank)
    raw = lax.dot_general(
        weighted,
        in_code,
        (((0,), (0,)), ((), ())),
        precision=lax.Precision.HIGHEST,
        preferred_element_type=jnp.float32,
    )
    count = jnp.sum(onehot, axis=0)
    features = raw.reshape(DOCS_DEV, rank, rank) / jnp.sqrt(count)[:, None, None]
    flat = features.reshape(DOCS_DEV, rank * rank)
    gathered = lax.all_gather(flat, "dp", axis=0, tiled=True)
    half = gathered.shape[0] // pair_size
    columns = lax.dynamic_slice_in_dim(gathered, position * half, half, 0)
    gram = lax.dot_general(
        flat,
        columns,
        (((1,), (1,)), ((), ())),
        precision=lax.Precision.HIGHEST,
        preferred_element_type=jnp.float32,
    ) / (rank * rank)
    scores = (
        lax.dot_general(
            flat,
            queries,
            (((1,), (1,)), ((), ())),
            precision=lax.Precision.HIGHEST,
            preferred_element_type=jnp.float32,
        )
        / rank
    )
    return (gram, scores)


def solution(mesh):
    return jax.shard_map(
        local,
        mesh=mesh,
        in_specs=(
            P(("groups", "dp"), "tensor"),
            P(("groups", "dp"), "tensor"),
            P(),
            P(),
            P(("groups", "dp"), None),
            P(),
        ),
        out_specs=(P(("groups", "dp"), "tensor"), P(("groups", "dp"), None)),
        check_vma=False,
    )
```

profile of v0, /device:TPU:0, one launch (start us, length us, event | category | flops | bytes accessed | tf_op | source)
XLA Modules:
  0.0 91.8 jit_solution(3958615541139983874)
XLA Ops:
  7.2 0.0 copy-start
  7.2 0.0 copy-start.3
  7.2 0.0 copy-start.1
  7.2 0.0 all-gather.4.cloned.1.call-start
  7.2 0.7 all-gather.4.cloned.1.call-update
  7.9 0.0 all-gather.6.cloned.1.call-start
  8.0 0.7 all-gather.6.cloned.1.call-update
  8.7 0.0 all-gather.8.cloned.1.call-start
  8.7 0.0 copy-done.3
  8.7 0.1 fusion.6
  8.9 12.5 %all-gather.4.cloned.1.call-done = bf16[128,4096]{1,0:T(8,128)(2,1)} async-done(((bf16[128,2048]{1,0:T(8,128)(2,1)}), bf16[128,4096]{1,0:T(8,128)(2,1)}) %all-gather.4.cloned.1.call-update) | async-done | bytes 1048592 | tf_op jit(solution)/shard_map/all_gather | solution.py:15
  21.3 0.0 copy-done.1
  21.4 1.7 %fusion.8 = f32[128,64]{0,1:T(8,128)S(1)} fusion(bf16[128,4096]{1,0:T(8,128)(2,1)} %all-gather.4.cloned.1.call-done, bf16[4096,64]{0,1:T(8,128)(2,1)S(1)} %copy-done.1), kind=kOutput, calls=%fused_computation.13 | convolution fusion | flops 67108864 | bytes 1605632 | tf_op jit(solution)/shard_map/dot_general | solution.py:18
  23.1 0.0 copy-start.2
  23.1 13.9 %all-gather.6.cloned.1.call-done = bf16[128,14336]{1,0:T(8,128)(2,1)} async-done(((bf16[128,7168]{1,0:T(8,128)(2,1)}), bf16[128,14336]{1,0:T(8,128)(2,1)}) %all-gather.6.cloned.1.call-update) | async-done | bytes 3670032 | tf_op jit(solution)/shard_map/all_gather | solution.py:14
  37.0 0.0 copy-done
  37.0 3.4 %convolution_bitcast_fusion = f32[128,64,1]{0,1,2:T(8,128)S(1)} fusion(bf16[128,14336]{1,0:T(8,128)(2,1)} %all-gather.6.cloned.1.call-done, bf16[14336,64]{0,1:T(8,128)(2,1)S(1)} %copy-done), kind=kOutput, calls=%fused_computation.1 | convolution fusion | flops 234881024 | bytes 5537792 | tf_op jit(solution)/shard_map/dot_general | solution.py:17
  40.4 0.4 convolution_divide_fusion
  40.8 0.8 reshape.42
  41.6 0.0 all-gather.8.cloned.1.call-update
  41.6 0.0 copy-done.2
  41.6 1.9 %convolution_multiply_fusion.1 = f32[8,16]{1,0:T(8,128)} fusion(f32[8,4096]{1,0:T(8,128)} %reshape.42, f32[16,4096]{1,0:T(8,128)S(1)} %copy-done.2), kind=kOutput, calls=%fused_computation.3 | convolution fusion | flops 6291584 | bytes 393728 | tf_op jit(solution)/shard_map/dot_general | solution.py:45
  43.5 39.5 %all-gather.8.cloned.1.call-done = f32[64,4096]{1,0:T(8,128)} async-done(((f32[8,4096]{1,0:T(8,128)}), f32[64,4096]{1,0:T(8,128)}) %all-gather.8.cloned.1.call-update) | async-done | bytes 1048592 | tf_op jit(solution)/shard_map/all_gather | solution.py:34
  83.1 2.2 %convolution_multiply_fusion = f32[8,32]{1,0:T(8,128)} fusion(f32[8,4096]{1,0:T(8,128)} %reshape.42, f32[64,4096]{1,0:T(8,128)} %all-gather.8.cloned.1.call-done, s32[]{:T(128)S(6)} %select_n.3), kind=kOutput, calls=%fused_computation.2 | convolution fusion | flops 12583168 | bytes 656388 | tf_op jit(solution)/shard_map/dot_general | solution.py:37
  (2 shorter events, 0.0 us)
Async XLA Ops:
  7.2 29.8 %copy-start = (bf16[14336,64]{0,1:T(8,128)(2,1)S(1)}, bf16[14336,64]{0,1:T(8,128)(2,1)}, u32[]{:S(2)}) copy-start(bf16[14336,64]{0,1:T(8,128)(2,1)} %param.8) | copy-start | bytes 5505028
  7.2 1.6 %copy-start.3 = (s32[1,128]{1,0:T(1,128)S(1)}, s32[1,128]{1,0:T(1,128)}, u32[]{:S(2)}) copy-start(s32[1,128]{1,0:T(1,128)} %param.10) | copy-start | bytes 1540
  7.2 14.2 %copy-start.1 = (bf16[4096,64]{0,1:T(8,128)(2,1)S(1)}, bf16[4096,64]{0,1:T(8,128)(2,1)}, u32[]{:S(2)}) copy-start(bf16[4096,64]{0,1:T(8,128)(2,1)} %param.9) | copy-start | bytes 1572868
  7.2 14.1 %all-gather.4.cloned.1.call-start = ((), (), s32[]{:S(2)}) async-start(), calls=%async_computation | async-start | bytes 1572864 | tf_op jit(solution)/shard_map/all_gather | solution.py:15
  7.9 29.1 %all-gather.6.cloned.1.call-start = ((), (), s32[]{:S(2)}) async-start(), calls=%async_computation.1 | async-start | bytes 5505024 | tf_op jit(solution)/shard_map/all_gather | solution.py:14
  8.7 74.4 %all-gather.8.cloned.1.call-start = ((), (), s32[]{:S(2)}) async-start(), calls=%async_computation.2 | async-start | bytes 1179648 | tf_op jit(solution)/shard_map/all_gather | solution.py:34
  23.1 18.5 %copy-start.2 = (f32[16,4096]{1,0:T(8,128)S(1)}, f32[16,4096]{1,0:T(8,128)}, u32[]{:S(2)}) copy-start(f32[16,4096]{1,0:T(8,128)} %param.11) | copy-start | bytes 786436
Sparse Core Ops, SparseCore 0:
  9.6 11.7 all-gather.3
  22.9 14.0 all-gather.5
  41.7 41.3 all-gather.7
where the time goes:
time: 92 us; the launch traced here: 91.8 us
  waiting for transfers between devices  67.3 us (73%)
  between operations  13.8 us (15%)
  matrix products  9.63 us (10%)
    all_gather x1, waiting for transfers between devices, local(): gathered = lax.all_gather(flat, 'dp', axis=0, tiled=True)  39.5 us
    all_gather x1, waiting for transfers between devices, local(): lax.all_gather(inputs, 'tensor', axis=1, tiled=True)  13.9 us
    all_gather x1, waiting for transfers between devices, local(): lax.all_gather(out_grads, 'tensor', axis=1, tiled=True)  12.5 us
    dot_general x1, matrix products, local(): in_code = jnp.dot(full_in, proj_in, preferred_element_type=jnp.float32)  3.42 us
    dot_general x1, matrix products, local(): lax.dot_general(flat, columns, (((1,), (1,)), ((), ())), precision=lax.Pr...  2.23 us
    dot_general x1, matrix products, local(): lax.dot_general(flat, queries, (((1,), (1,)), ((), ())), precision=lax.Pr...  1.91 us
  transfers between devices with their start and end apart: 3, of which 3 were waited for; matrix products, arithmetic and copies ran while one was open for 4% of the time, Pallas kernels for 0%

commit v1 on v0

v1 whole, which is shorter than its diff:
```python
import functools

import jax
import jax.numpy as jnp
from jax import lax
from jax.experimental import pallas as pl
from jax.experimental.pallas import tpu as pltpu
from jax.sharding import PartitionSpec as P

DOCS_DEV = 8
HIGHEST = lax.Precision.HIGHEST
NT = (((1,), (1,)), ((), ()))
TN = (((0,), (0,)), ((), ()))


def chunks_of(depth):
    for size in (1024, 512, 256, 128):
        if depth % size == 0:
            return [(at, size) for at in range(0, depth, size)]
    return [(0, depth)]


def codes_kernel(x_hbm, y_hbm, wx_hbm, wy_hbm, out_ref, x, y, wx, wy, sems):
    at_core = lax.axis_index("tensor")
    rank = wx.shape[0]
    jobs = []
    for src, w_src, dst, w_dst, row in ((y_hbm, wy_hbm, y, wy, 0), (x_hbm, wx_hbm, x, wx, rank)):
        depth = dst.shape[1]
        for at, size in chunks_of(depth):
            jobs.append((src, w_src, dst, w_dst, row, depth, at, size))
    copies = []
    for n, (src, w_src, dst, w_dst, row, depth, at, size) in enumerate(jobs):
        w_at = pl.multiple_of(at_core * depth + at, 128)
        pair = (
            pltpu.make_async_copy(w_src.at[:, pl.ds(w_at, size)], w_dst.at[:, pl.ds(at, size)], sems.at[2 * n]),
            pltpu.make_async_copy(src.at[:, pl.ds(at, size)], dst.at[:, pl.ds(at, size)], sems.at[2 * n + 1]),
        )
        for copy in pair:
            copy.start()
        copies.append(pair)
    totals = {}
    for (src, w_src, dst, w_dst, row, depth, at, size), pair in zip(jobs, copies):
        for copy in pair:
            copy.wait()
        part = lax.dot_general(
            w_dst[:, at : at + size], dst[:, at : at + size], NT, preferred_element_type=jnp.float32
        )
        totals[row] = part if row not in totals else totals[row] + part
    for row, total in totals.items():
        out_ref[row : row + rank, :] = total


def partial_codes(inputs, out_grads, proj_in_t, proj_out_t):
    tokens, depth_in = inputs.shape
    depth_out = out_grads.shape[1]
    rank = proj_in_t.shape[0]
    jobs = len(chunks_of(depth_in)) + len(chunks_of(depth_out))
    return pl.pallas_call(
        codes_kernel,
        out_shape=jax.ShapeDtypeStruct((2 * rank, tokens), jnp.float32),
        in_specs=[pl.BlockSpec(memory_space=pl.ANY)] * 4,
        out_specs=pl.BlockSpec(memory_space=pltpu.VMEM),
        scratch_shapes=[
            pltpu.VMEM((tokens, depth_in), inputs.dtype),
            pltpu.VMEM((tokens, depth_out), out_grads.dtype),
            pltpu.VMEM((rank, depth_in), proj_in_t.dtype),
            pltpu.VMEM((rank, depth_out), proj_out_t.dtype),
            pltpu.SemaphoreType.DMA((2 * jobs,)),
        ],
        compiler_params=pltpu.CompilerParams(vmem_limit_bytes=24 << 20),
        name="partial_codes",
    )(inputs, out_grads, proj_in_t, proj_out_t)


def add_kernel(mine_ref, other_ref, ids_ref, out_ref):
    rows, tokens = mine_ref.shape
    out_ref[:rows, :] = mine_ref[...] + other_ref[...]
    out_ref[rows:, :] = jnp.broadcast_to(ids_ref[...].astype(jnp.float32), (8, tokens))


def add_pair(mine, other, ids):
    rows, tokens = mine.shape
    return pl.pallas_call(
        add_kernel,
        out_shape=jax.ShapeDtypeStruct((rows + 8, tokens), jnp.float32),
        name="add_pair",
    )(mine, other, ids)


def doc_weights(ids, first, docs):
    tokens = ids.shape[1]
    rows = lax.broadcasted_iota(jnp.int32, (docs, tokens), 0)
    onehot = (rows == ids.astype(jnp.int32) + first).astype(jnp.float32)
    count = jnp.sum(onehot, axis=1, keepdims=True)
    return onehot / jnp.sqrt(jnp.maximum(count, 1.0))


def scores_kernel(codes_ref, queries_ref, out_ref):
    rows, tokens = codes_ref.shape
    rank = (rows - 8) // 2
    weights = doc_weights(codes_ref[2 * rank : 2 * rank + 1, :], 0, DOCS_DEV)
    grads = codes_ref[:rank, :]
    ins = codes_ref[rank : 2 * rank, :]
    weighted = (grads[:, None, :] * weights[None, :, :]).reshape(rank * DOCS_DEV, tokens)
    twice = jnp.concatenate([ins, ins], axis=0)
    feats = lax.dot_general(weighted, twice, NT, precision=HIGHEST, preferred_element_type=jnp.float32)
    feats = feats.reshape(rank, DOCS_DEV, 2 * rank)
    low = lax.broadcasted_iota(jnp.int32, (DOCS_DEV, 2 * rank), 1) < rank
    flat = jnp.concatenate(
        [jnp.where(low, feats[i], feats[i + 1]) for i in range(0, rank, 2)], axis=1
    )
    out_ref[...] = lax.dot_general(
        flat, queries_ref[...], NT, precision=HIGHEST, preferred_element_type=jnp.float32
    ) * (1.0 / rank)


def score_docs(codes, queries):
    return pl.pallas_call(
        scores_kernel,
        out_shape=jax.ShapeDtypeStruct((DOCS_DEV, queries.shape[0]), jnp.float32),
        cost_estimate=pl.CostEstimate(flops=1 << 26, bytes_accessed=1 << 19, transcendentals=0),
        name="score_docs",
    )(codes, queries)


def gram_kernel(place_ref, own_ref, *refs):
    blocks, out_ref = refs[:-1], refs[-1]
    rank = (own_ref.shape[0] - 8) // 2
    half = len(blocks)
    own_grads, own_ins = own_ref[:rank, :], own_ref[rank : 2 * rank, :]
    weights = doc_weights(own_ref[2 * rank : 2 * rank + 1, :], 0, DOCS_DEV)
    total = jnp.zeros(out_ref.shape, jnp.float32)
    for n, block_ref in enumerate(blocks):
        block = block_ref[...]
        if n == 0:
            block = jnp.where(place_ref[half] == 1, own_ref[...], block)
        dots = functools.partial(
            lax.dot_general, precision=HIGHEST, preferred_element_type=jnp.float32
        )
        product = dots(own_grads, block[:rank, :], TN) * dots(own_ins, block[rank : 2 * rank, :], TN)
        theirs = doc_weights(
            block[2 * rank : 2 * rank + 1, :], place_ref[n] * DOCS_DEV, half * DOCS_DEV
        )
        rows = lax.dot_general(
            weights, product, (((1,), (0,)), ((), ())), precision=HIGHEST, preferred_element_type=jnp.float32
        )
        total = total + dots(rows, theirs, NT)
    out_ref[...] = total * (1.0 / (rank * rank))


def gram_of(place, own, blocks):
    half = len(blocks)
    return pl.pallas_call(
        gram_kernel,
        out_shape=jax.ShapeDtypeStruct((DOCS_DEV, half * DOCS_DEV), jnp.float32),
        in_specs=[pl.BlockSpec(memory_space=pltpu.SMEM)]
        + [pl.BlockSpec(memory_space=pltpu.VMEM)] * (1 + half),
        compiler_params=pltpu.CompilerParams(vmem_limit_bytes=24 << 20),
        name="gram_rows",
    )(place, own, *blocks)


def local(inputs, out_grads, proj_in, proj_out, doc_ids, queries):
    shards = lax.axis_size("dp")
    half = shards // 2
    shard, core = lax.axis_index("dp"), lax.axis_index("tensor")
    mine = partial_codes(inputs, out_grads, proj_in.T, proj_out.T)
    other = lax.ppermute(mine, "tensor", [(0, 1), (1, 0)])
    own = add_pair(mine, other, doc_ids)
    blocks, places = [], []
    for step in range(half):
        moves = []
        for s in range(shards):
            side = s // half
            if step:
                moves.append((s * 2 + side, (s + step) % shards * 2 + side))
            moves.append((s * 2 + 1 - side, (s + step + half) % shards * 2 + side))
        blocks.append(lax.ppermute(own, ("dp", "tensor"), moves))
        near = lax.rem(shard - step + shards, shards)
        places.append(lax.rem(near, half))
    is_own = (shard // half == core).astype(jnp.int32)
    place = jnp.stack(places + [is_own]).astype(jnp.int32)
    scores = score_docs(own, queries)
    return gram_of(place, own, blocks), scores


def solution(mesh):
    return jax.shard_map(
        local,
        mesh=mesh,
        in_specs=(
            P(("groups", "dp"), "tensor"),
            P(("groups", "dp"), "tensor"),
            P(),
            P(),
            P(("groups", "dp"), None),
            P(),
        ),
        out_specs=(P(("groups", "dp"), "tensor"), P(("groups", "dp"), None)),
        check_vma=False,
    )
```

time: 92 us -> 31.2 us (0.34)
  the two profiles are of different devices: /device:TPU:0 before, /device:TPU:1 now
where the time goes in v1:
time: 31.2 us; the launch traced here: 30.8 us
  starting transfers between devices  10.4 us (33%)
  Pallas kernels  9.58 us (31%)
  local copies, waits for them, and re-layouts  6.66 us (21%)
  waiting for transfers between devices  3.55 us (11%)
  between operations  0.68 us (2%)
    ppermute x4, starting transfers between devices, local(): blocks.append(lax.ppermute(own, ('dp', 'tensor'), moves))  10.2 us
    unnamed x14, local copies, waits for them, and re-layouts  6.57 us
    pallas_call x1, Pallas kernels, gram_of(): pl.pallas_call(gram_kernel, out_shape=jax.ShapeDtypeStruct((DOCS_DEV, hal...  3.12 us
    pallas_call x1, Pallas kernels, score_docs(): pl.pallas_call(scores_kernel, out_shape=jax.ShapeDtypeStruct((DOCS_DEV, q...  2.72 us
    ppermute x4, waiting for transfers between devices, local(): blocks.append(lax.ppermute(own, ('dp', 'tensor'), moves))  2.36 us
    pallas_call x1, Pallas kernels, partial_codes(): pl.pallas_call(codes_kernel, out_shape=jax.ShapeDtypeStruct((2 * rank, to...  2.24 us
    pallas_call x1, Pallas kernels, add_pair(): pl.pallas_call(add_kernel, out_shape=jax.ShapeDtypeStruct((rows + 8, toke...  1.51 us
    ppermute x1, waiting for transfers between devices, local(): other = lax.ppermute(mine, 'tensor', [(0, 1), (1, 0)])  1.2 us
  transfers between devices with their start and end apart: 5, of which 2 were waited for; matrix products, arithmetic and copies ran while one was open for 0% of the time, Pallas kernels for 9%

profile of v1, /device:TPU:1, one launch (start us, length us, event | category | flops | bytes accessed | tf_op | source)
XLA Modules:
  0.0 30.8 jit_solution(1032255610644925986)
XLA Ops:
  0.6 0.0 copy-start
  0.6 1.5 %copy-done = bf16[128,7168]{1,0:T(8,128)(2,1)S(1)} copy-done((bf16[128,7168]{1,0:T(8,128)(2,1)S(1)}, bf16[128,7168]{1,0:T(8,128)(2,1)}, u32[]{:S(2)}) %copy-start) | copy-done | bytes 1835032
  2.1 1.5 %copy-done.1 = bf16[14336,64]{0,1:T(8,128)(2,1)S(1)} copy-done((bf16[14336,64]{0,1:T(8,128)(2,1)S(1)}, bf16[14336,64]{0,1:T(8,128)(2,1)}, u32[]{:S(2)}) %copy-start.1) | copy-done | bytes 1835032
  3.6 1.0 %copy-done.3 = bf16[128,2048]{1,0:T(8,128)(2,1)S(1)} copy-done((bf16[128,2048]{1,0:T(8,128)(2,1)S(1)}, bf16[128,2048]{1,0:T(8,128)(2,1)}, u32[]{:S(2)}) %copy-start.3) | copy-done | bytes 524312
  4.7 1.0 %copy-done.4 = bf16[4096,64]{0,1:T(8,128)(2,1)S(1)} copy-done((bf16[4096,64]{0,1:T(8,128)(2,1)S(1)}, bf16[4096,64]{0,1:T(8,128)(2,1)}, u32[]{:S(2)}) %copy-start.4) | copy-done | bytes 524312
  5.7 2.2 %partial_codes.1.mine_ref = f32[128,128]{1,0:T(8,128)S(1)} custom-call(bf16[128,7168]{1,0:T(8,128)(2,1)S(1)} %copy-done, bf16[128,2048]{1,0:T(8,128)(2,1)S(1)} %copy-done.3, bf16[64,14336]{1,0:T(8,128)(2,1)S(1)} %bitcast.7, bf16[64,4096]{1,0:T(8,128)(2,1)S(1)} %bitcast.8), custom_call_target="tpu_custom_call" | custom-call | tf_op jit(solution)/shard_map/partial_codes/pallas_call | solution.py:58
  8.0 0.0 copy-start.5
  8.0 0.1 collective-permute-start
  8.1 1.2 %collective-permute-done.other_ref = f32[128,128]{1,0:T(8,128)S(1)} collective-permute-done((f32[128,128]{1,0:T(8,128)S(1)}, f32[128,128]{1,0:T(8,128)S(1)}, u32[]{:S(2)}, u32[]{:S(2)}) %collective-permute-start) | collective-permute-done | bytes 65568 | tf_op jit(solution)/shard_map/ppermute | solution.py:168
  9.3 0.0 copy-done.5
  9.3 0.6 %copy-done.6 = f32[128,128]{1,0:T(8,128)} copy-done((f32[128,128]{1,0:T(8,128)}, f32[128,128]{1,0:T(8,128)S(1)}, u32[]{:S(2)}) %copy-start.6) | copy-done | bytes 65560
  9.9 1.5 %add_pair.1.own_ref.codes_ref = f32[136,128]{1,0:T(8,128)} custom-call(f32[128,128]{1,0:T(8,128)} %copy-done.5, f32[128,128]{1,0:T(8,128)} %copy-done.6, s32[1,128]{1,0:T(1,128)} %ids_ref.1), custom_call_target="tpu_custom_call" | custom-call | tf_op jit(solution)/shard_map/add_pair/pallas_call | solution.py:83
  11.4 5.6 %collective-permute-start.1 = (f32[136,128]{1,0:T(8,128)}, f32[136,128]{1,0:T(8,128)S(1)}, u32[]{:S(2)}, u32[]{:S(2)}) collective-permute-start(f32[136,128]{1,0:T(8,128)} %add_pair.1.own_ref.codes_ref), channel_id=1, source_target_pairs={{1,8},{3,10},{5,12},{7,14},{8,1},{10,3},{12,5},{14,7},{17,24},{19,... | collective-permute-start | bytes 208904 | tf_op jit(solution)/shard_map/ppermute | solution.py:178
  17.0 1.1 %collective-permute-start.2 = (f32[136,128]{1,0:T(8,128)}, f32[136,128]{1,0:T(8,128)S(1)}, u32[]{:S(2)}, u32[]{:S(2)}) collective-permute-start(f32[136,128]{1,0:T(8,128)} %add_pair.1.own_ref.codes_ref), channel_id=1, source_target_pairs={{0,2},{1,10},{2,4},{3,12},{4,6},{5,14},{6,8},{7,0},{9,11},{8,3},{1... | collective-permute-start | bytes 208904 | tf_op jit(solution)/shard_map/ppermute | solution.py:178
  18.1 3.6 %collective-permute-start.3 = (f32[136,128]{1,0:T(8,128)}, f32[136,128]{1,0:T(8,128)S(1)}, u32[]{:S(2)}, u32[]{:S(2)}) collective-permute-start(f32[136,128]{1,0:T(8,128)} %add_pair.1.own_ref.codes_ref), channel_id=1, source_target_pairs={{0,4},{1,12},{2,6},{3,14},{4,8},{5,0},{6,10},{7,2},{9,13},{8,5},{1... | collective-permute-start | bytes 208904 | tf_op jit(solution)/shard_map/ppermute | solution.py:178
  21.7 0.0 collective-permute-start.4
  21.7 0.1 stack.27.place_ref
  21.8 2.7 %score_docs.1 = f32[8,16]{1,0:T(8,128)} custom-call(f32[136,128]{1,0:T(8,128)} %add_pair.1.own_ref.codes_ref, f32[16,4096]{1,0:T(8,128)} %queries_ref.1), custom_call_target="tpu_custom_call" | custom-call | flops 67108864 | bytes 524288 | tf_op jit(solution)/shard_map/score_docs/pallas_call | solution.py:118
  24.5 0.0 collective-permute-done.1.refs_0_
  24.5 0.0 collective-permute-done.2.refs_1_
  24.5 0.0 collective-permute-done.3.refs_2_
  24.5 2.4 %collective-permute-done.4.refs_3_ = f32[136,128]{1,0:T(8,128)S(1)} collective-permute-done((f32[136,128]{1,0:T(8,128)}, f32[136,128]{1,0:T(8,128)S(1)}, u32[]{:S(2)}, u32[]{:S(2)}) %collective-permute-start.4) | collective-permute-done | bytes 69664 | tf_op jit(solution)/shard_map/ppermute | solution.py:178
  26.8 0.9 %copy-done.2 = f32[136,128]{1,0:T(8,128)S(1)} copy-done((f32[136,128]{1,0:T(8,128)S(1)}, f32[136,128]{1,0:T(8,128)}, u32[]{:S(2)}) %copy-start.2) | copy-done | bytes 69656
  27.7 3.1 %gram_rows.1 = f32[8,32]{1,0:T(8,128)} custom-call(s32[5]{0:T(128)S(1)} %stack.27.place_ref, f32[136,128]{1,0:T(8,128)S(1)} %copy-done.2, f32[136,128]{1,0:T(8,128)S(1)} %collective-permute-done.1.refs_0_, f32[136,128]{1,0:T(8,128)S(1)} %collective-permute-done.2.refs_1_, f32[136,128]{1,0:T(8,128)S(1)} %collective-permute-done.3.refs_2_, ...), custom_call_target="tpu_custom_call" | custom-call | tf_op jit(solution)/shard_map/gram_rows/pallas_call | solution.py:153
  (5 shorter events, 0.0 us)
Async XLA Ops:
  0.6 1.5 %copy-start = (bf16[128,7168]{1,0:T(8,128)(2,1)S(1)}, bf16[128,7168]{1,0:T(8,128)(2,1)}, u32[]{:S(2)}) copy-start(bf16[128,7168]{1,0:T(8,128)(2,1)} %x_hbm.1) | copy-start | bytes 5505028
  2.1 1.5 %copy-start.1 = (bf16[14336,64]{0,1:T(8,128)(2,1)S(1)}, bf16[14336,64]{0,1:T(8,128)(2,1)}, u32[]{:S(2)}) copy-start(bf16[14336,64]{0,1:T(8,128)(2,1)} %param.8) | copy-start | bytes 5505028
  3.6 1.0 %copy-start.3 = (bf16[128,2048]{1,0:T(8,128)(2,1)S(1)}, bf16[128,2048]{1,0:T(8,128)(2,1)}, u32[]{:S(2)}) copy-start(bf16[128,2048]{1,0:T(8,128)(2,1)} %y_hbm.1) | copy-start | bytes 1572868
  4.7 1.0 %copy-start.4 = (bf16[4096,64]{0,1:T(8,128)(2,1)S(1)}, bf16[4096,64]{0,1:T(8,128)(2,1)}, u32[]{:S(2)}) copy-start(bf16[4096,64]{0,1:T(8,128)(2,1)} %param.9) | copy-start | bytes 1572868
  8.0 1.3 %copy-start.5 = (f32[128,128]{1,0:T(8,128)}, f32[128,128]{1,0:T(8,128)S(1)}, u32[]{:S(2)}) copy-start(f32[128,128]{1,0:T(8,128)S(1)} %partial_codes.1.mine_ref) | copy-start | bytes 196612
  8.0 1.3 %collective-permute-start = (f32[128,128]{1,0:T(8,128)S(1)}, f32[128,128]{1,0:T(8,128)S(1)}, u32[]{:S(2)}, u32[]{:S(2)}) collective-permute-start(f32[128,128]{1,0:T(8,128)S(1)} %partial_codes.1.mine_ref), channel_id=1, source_target_pairs={{0,1},{1,0},{2,3},{3,2},{4,5},{5,4},{6,7},{7,6},{8,9},{9,8},{10,11... | collective-permute-start | bytes 196616 | tf_op jit(solution)/shard_map/ppermute | solution.py:168
  9.3 0.6 %copy-start.6 = (f32[128,128]{1,0:T(8,128)}, f32[128,128]{1,0:T(8,128)S(1)}, u32[]{:S(2)}) copy-start(f32[128,128]{1,0:T(8,128)S(1)} %collective-permute-done.other_ref) | copy-start | bytes 196612
  11.4 13.1 %collective-permute-start.1 = (f32[136,128]{1,0:T(8,128)}, f32[136,128]{1,0:T(8,128)S(1)}, u32[]{:S(2)}, u32[]{:S(2)}) collective-permute-start(f32[136,128]{1,0:T(8,128)} %add_pair.1.own_ref.codes_ref), channel_id=1, source_target_pairs={{1,8},{3,10},{5,12},{7,14},{8,1},{10,3},{12,5},{14,7},{17,24},{19,... | collective-permute-start | bytes 208904 | tf_op jit(solution)/shard_map/ppermute | solution.py:178
  17.0 7.5 %collective-permute-start.2 = (f32[136,128]{1,0:T(8,128)}, f32[136,128]{1,0:T(8,128)S(1)}, u32[]{:S(2)}, u32[]{:S(2)}) collective-permute-start(f32[136,128]{1,0:T(8,128)} %add_pair.1.own_ref.codes_ref), channel_id=1, source_target_pairs={{0,2},{1,10},{2,4},{3,12},{4,6},{5,14},{6,8},{7,0},{9,11},{8,3},{1... | collective-permute-start | bytes 208904 | tf_op jit(solution)/shard_map/ppermute | solution.py:178
  18.1 6.4 %collective-permute-start.3 = (f32[136,128]{1,0:T(8,128)}, f32[136,128]{1,0:T(8,128)S(1)}, u32[]{:S(2)}, u32[]{:S(2)}) collective-permute-start(f32[136,128]{1,0:T(8,128)} %add_pair.1.own_ref.codes_ref), channel_id=1, source_target_pairs={{0,4},{1,12},{2,6},{3,14},{4,8},{5,0},{6,10},{7,2},{9,13},{8,5},{1... | collective-permute-start | bytes 208904 | tf_op jit(solution)/shard_map/ppermute | solution.py:178
  21.7 5.2 %collective-permute-start.4 = (f32[136,128]{1,0:T(8,128)}, f32[136,128]{1,0:T(8,128)S(1)}, u32[]{:S(2)}, u32[]{:S(2)}) collective-permute-start(f32[136,128]{1,0:T(8,128)} %add_pair.1.own_ref.codes_ref), channel_id=1, source_target_pairs={{0,6},{1,14},{2,8},{3,0},{4,10},{5,2},{6,12},{7,4},{9,15},{8,7},{1... | collective-permute-start | bytes 208904 | tf_op jit(solution)/shard_map/ppermute | solution.py:178
  26.8 0.9 %copy-start.2 = (f32[136,128]{1,0:T(8,128)S(1)}, f32[136,128]{1,0:T(8,128)}, u32[]{:S(2)}) copy-start(f32[136,128]{1,0:T(8,128)} %add_pair.1.own_ref.codes_ref) | copy-start | bytes 208900

commit v2 on v1

v2 whole, which is shorter than its diff:
```python
import functools

import jax
import jax.numpy as jnp
from jax import lax
from jax.experimental import pallas as pl
from jax.experimental.pallas import tpu as pltpu
from jax.sharding import PartitionSpec as P

DOCS_DEV = 8
EXTRA = 8
STEPS = 8.0
TOP = 32767.0
NT = (((1,), (1,)), ((), ()))
NN = (((1,), (0,)), ((), ()))
VMEM = pl.BlockSpec(memory_space=pltpu.VMEM)
HBM = pl.BlockSpec(memory_space=pltpu.HBM)

dot = functools.partial(lax.dot_general, preferred_element_type=jnp.float32)


def chunks_of(depth):
    for size in (1024, 512, 256, 128):
        if depth % size == 0:
            return [(at, size) for at in range(0, depth, size)]
    return [(0, depth)]


def halves(values):
    high = values.astype(jnp.bfloat16)
    return high, (values - high.astype(jnp.float32)).astype(jnp.bfloat16)


def members(ids, docs):
    rows = lax.broadcasted_iota(jnp.int32, (docs, ids.shape[1]), 0)
    return (rows == ids).astype(jnp.float32)


def codes_kernel(x_hbm, y_hbm, wx_hbm, wy_hbm, out_ref, x, y, wx, wy, sems):
    at_core = lax.axis_index("tensor")
    rank = wx.shape[0]
    copies = []
    for src, w_src, dst, w_dst, row in ((y_hbm, wy_hbm, y, wy, 0), (x_hbm, wx_hbm, x, wx, rank)):
        depth = dst.shape[1]
        for at, size in chunks_of(depth):
            w_at = pl.multiple_of(at_core * depth + at, 128)
            here = pl.ds(at, size)
            sem = 2 * len(copies)
            pair = (
                pltpu.make_async_copy(w_src.at[:, pl.ds(w_at, size)], w_dst.at[:, here], sems.at[sem]),
                pltpu.make_async_copy(src.at[:, here], dst.at[:, here], sems.at[sem + 1]),
            )
            for copy in pair:
                copy.start()
            copies.append((pair, dst, w_dst, row, at, size))
    totals = {}
    for pair, dst, w_dst, row, at, size in copies:
        for copy in pair:
            copy.wait()
        part = dot(w_dst[:, at : at + size], dst[:, at : at + size], NT)
        totals[row] = totals[row] + part if row in totals else part
    out_ref[:rank, :] = totals[0]
    out_ref[rank:, :] = totals[rank]


def partial_codes(inputs, out_grads, proj_in_t, proj_out_t):
    tokens, depth_in = inputs.shape
    depth_out = out_grads.shape[1]
    rank = proj_in_t.shape[0]
    jobs = len(chunks_of(depth_in)) + len(chunks_of(depth_out))
    return pl.pallas_call(
        codes_kernel,
        out_shape=jax.ShapeDtypeStruct((2 * rank, tokens), jnp.float32),
        in_specs=[HBM] * 4,
        out_specs=VMEM,
        scratch_shapes=[
            pltpu.VMEM((tokens, depth_in), inputs.dtype),
            pltpu.VMEM((tokens, depth_out), out_grads.dtype),
            pltpu.VMEM((rank, depth_in), proj_in_t.dtype),
            pltpu.VMEM((rank, depth_out), proj_out_t.dtype),
            pltpu.SemaphoreType.DMA((2 * jobs,)),
        ],
        compiler_params=pltpu.CompilerParams(vmem_limit_bytes=56_000_000),
        name="partial_codes",
    )(inputs, out_grads, proj_in_t, proj_out_t)


def fixed_point(values):
    largest = jnp.max(jnp.abs(values), axis=0, keepdims=True)
    grade = jnp.ceil(jnp.log(jnp.maximum(largest, 1e-30)) * (STEPS / 0.6931471805599453) + 0.01)
    units = values * (TOP * jnp.exp2(grade * (-1.0 / STEPS)))
    units = jnp.clip(jnp.floor(units + 0.5), -TOP, TOP)
    return units.astype(jnp.int32), grade.astype(jnp.int32)


def pack_kernel(mine_ref, other_ref, ids_ref, own_ref, message_ref):
    rows, tokens = mine_ref.shape
    rank = rows // 2
    ids = ids_ref[...]
    onehot = members(ids, DOCS_DEV)
    count = jnp.maximum(jnp.sum(onehot, axis=1, keepdims=True), 1.0)
    weight = jnp.sum(onehot / jnp.sqrt(count), axis=0, keepdims=True)
    grads = mine_ref[:rank, :] + other_ref[:rank, :]
    ins = (mine_ref[rank:, :] + other_ref[rank:, :]) * weight
    own_ref[:rank, :] = grads
    own_ref[rank:, :] = ins
    grad_units, grad_grade = fixed_point(grads)
    in_units, in_grade = fixed_point(ins)
    message_ref[:rank, :] = lax.shift_left(grad_units, 16) | (in_units & 0xFFFF)
    line = lax.broadcasted_iota(jnp.int32, (EXTRA, tokens), 0)
    message_ref[rank:, :] = jnp.where(
        line == 0, ids, jnp.where(line == 1, grad_grade, in_grade)
    )


def pack(mine, other, doc_ids):
    rows, tokens = mine.shape
    rank = rows // 2
    return pl.pallas_call(
        pack_kernel,
        out_shape=(
            jax.ShapeDtypeStruct((rows, tokens), jnp.float32),
            jax.ShapeDtypeStruct((rank + EXTRA, tokens), jnp.int32),
        ),
        in_specs=[VMEM] * 3,
        out_specs=(VMEM, VMEM),
        name="pack_codes",
    )(mine, other, doc_ids)


def scores_kernel(own_ref, message_ref, queries, scores_ref, grads_ref, ins_ref):
    rows, tokens = own_ref.shape
    rank = rows // 2
    grads = own_ref[:rank, :]
    ins = own_ref[rank:, :]
    onehot = members(message_ref[rank : rank + 1, :], DOCS_DEV)
    for values, ref in ((grads, grads_ref), (ins, ins_ref)):
        high, low = halves(values)
        stacked = jnp.concatenate([high, high, low, low], axis=0)
        ref[...] = stacked.T
    weighted = (grads[:, None, :] * onehot[None, :, :]).reshape(rank * DOCS_DEV, tokens)
    w_high, w_low = halves(weighted)
    i_high, i_low = halves(jnp.concatenate([ins, ins], axis=0))
    feats = dot(
        jnp.concatenate([w_high, w_high, w_low], axis=1),
        jnp.concatenate([i_high, i_low, i_high], axis=1),
        NT,
    )
    left = lax.broadcasted_iota(jnp.int32, (DOCS_DEV, 2 * rank), 1) < rank
    pairs = [
        jnp.where(
            left,
            feats[i * DOCS_DEV : (i + 1) * DOCS_DEV],
            feats[(i + 1) * DOCS_DEV : (i + 2) * DOCS_DEV],
        )
        for i in range(0, rank, 2)
    ]
    count = queries.shape[0]
    sums = [None] * count
    for n, pair in enumerate(pairs):
        block = queries[:, n * 2 * rank : (n + 1) * 2 * rank]
        for q in range(count):
            term = pair * block[q : q + 1, :]
            sums[q] = term if n == 0 else sums[q] + term
    columns = [jnp.sum(total, axis=1, keepdims=True) for total in sums]
    scores_ref[...] = jnp.concatenate(columns, axis=1) * (1.0 / rank)


def score_docs(own, message, queries):
    rows, tokens = own.shape
    rank = rows // 2
    operand = jax.ShapeDtypeStruct((tokens, 4 * rank), jnp.bfloat16)
    return pl.pallas_call(
        scores_kernel,
        out_shape=(
            jax.ShapeDtypeStruct((DOCS_DEV, queries.shape[0]), jnp.float32),
            operand,
            operand,
        ),
        in_specs=[VMEM] * 3,
        out_specs=(VMEM, VMEM, VMEM),
        compiler_params=pltpu.CompilerParams(vmem_limit_bytes=24 << 20),
        cost_estimate=pl.CostEstimate(flops=1 << 26, bytes_accessed=1 << 19, transcendentals=0),
        name="score_docs",
    )(own, message, queries)


def gram_kernel(message_ref, grads_ref, ins_ref, *refs):
    blocks, out_ref = refs[:-1], refs[-1]
    half = len(blocks)
    shards = 2 * half
    rank = message_ref.shape[0] - EXTRA
    shard, core = lax.axis_index("dp"), lax.axis_index("tensor")
    onehot = members(message_ref[rank : rank + 1, :], DOCS_DEV).astype(jnp.bfloat16)
    doubled = jnp.concatenate([onehot, onehot], axis=1)
    total = None
    width = min(4, half)
    for first in range(0, half, width):
        codes, ids, scales = [], [], []
        for n in range(first, min(first + width, half)):
            block = blocks[n][...]
            if n == 0:
                block = jnp.where(lax.div(shard, half) == core, message_ref[...], block)
            place = lax.rem(lax.rem(shard - n + shards, shards), half)
            codes.append(block[:rank, :])
            ids.append(block[rank : rank + 1, :] + place * DOCS_DEV)
            scales.append((block[rank + 1 : rank + 2, :] + block[rank + 2 : rank + 3, :]).astype(jnp.float32))
        codes, ids, scales = (jnp.concatenate(part, axis=1) for part in (codes, ids, scales))
        product = None
        for units, left in (
            (lax.shift_right_arithmetic(codes, 16), grads_ref),
            (lax.shift_right_arithmetic(lax.shift_left(codes, 16), 16), ins_ref),
        ):
            high, low = halves(units.astype(jnp.float32))
            part = dot(left[...], jnp.concatenate([high, low, high, low], axis=0), NN)
            product = part if product is None else product * part
        high, low = halves(product)
        by_doc = dot(doubled, jnp.concatenate([high, low], axis=0), NN)
        by_doc = by_doc * (jnp.exp2(scales * (1.0 / STEPS)) * (1.0 / (TOP * TOP)))
        high, low = halves(by_doc)
        theirs = members(ids, half * DOCS_DEV).astype(jnp.bfloat16)
        part = dot(jnp.concatenate([high, low], axis=0), theirs, NT)
        total = part if total is None else total + part
    out_ref[...] = (total[:DOCS_DEV, :] + total[DOCS_DEV:, :]) * (1.0 / (rank * rank))


def gram_of(message, grads, ins, blocks):
    half = len(blocks)
    return pl.pallas_call(
        gram_kernel,
        out_shape=jax.ShapeDtypeStruct((DOCS_DEV, half * DOCS_DEV), jnp.float32),
        in_specs=[VMEM] * (3 + half),
        out_specs=VMEM,
        compiler_params=pltpu.CompilerParams(vmem_limit_bytes=24 << 20),
        name="gram_rows",
    )(message, grads, ins, *blocks)


def local(inputs, out_grads, proj_in, proj_out, doc_ids, queries):
    shards = lax.axis_size("dp")
    half = shards // 2
    mine = partial_codes(inputs, out_grads, proj_in.T, proj_out.T)
    other = lax.ppermute(mine, "tensor", [(0, 1), (1, 0)])
    own, message = pack(mine, other, doc_ids)
    blocks = []
    for step in range(half):
        moves = []
        for s in range(shards):
            side = s // half
            if step:
                moves.append((s * 2 + side, (s + step) % shards * 2 + side))
            moves.append((s * 2 + 1 - side, (s + step + half) % shards * 2 + side))
        blocks.append(lax.ppermute(message, ("dp", "tensor"), moves))
    scores, grads, ins = score_docs(own, message, queries)
    return gram_of(message, grads, ins, blocks), scores


def solution(mesh):
    return jax.shard_map(
        local,
        mesh=mesh,
        in_specs=(
            P(("groups", "dp"), "tensor"),
            P(("groups", "dp"), "tensor"),
            P(),
            P(),
            P(("groups", "dp"), None),
            P(),
        ),
        out_specs=(P(("groups", "dp"), "tensor"), P(("groups", "dp"), None)),
        check_vma=False,
    )
```

time: 31.2 us -> 24.6 us (0.79)
  local copies, waits for them, and re-layouts: 6.66 us -> 3.07 us
  Pallas kernels: 9.58 us -> 6.83 us
    unnamed x14 -> x12, local copies, waits for them, and re-layouts: 6.57 us -> 3.07 us
    pallas_call x1, Pallas kernels: 3.12 us -> 1.1 us  [gram_of(): pl.pallas_call(gram_kernel, out_shape=jax.ShapeDtypeStruct((DOCS_DEV, hal...]
    pallas_call x2, Pallas kernels: 4.23 us -> 2.69 us  [the longest x1 1.63 us: pack(): pl.pallas_call(pack_kernel, out_shape=(jax.ShapeDtypeStruct((rows, tokens...]
    pallas_call x1, Pallas kernels: 2.24 us -> 3.05 us  [partial_codes(): pl.pallas_call(codes_kernel, out_shape=jax.ShapeDtypeStruct((2 * rank, to...]
  transfers between devices with their start and end apart: 5 -> 5, of which waited for: 2 -> 2; matrix products, arithmetic and copies ran while one was open for 0% -> 0% of each run, Pallas kernels for 9% -> 4%
where the time goes in v2:
time: 24.6 us; the launch traced here: 24.2 us
  starting transfers between devices  10.4 us (42%)
  Pallas kernels  6.83 us (28%)
  waiting for transfers between devices  3.28 us (13%)
  local copies, waits for them, and re-layouts  3.07 us (12%)
  between operations  0.68 us (3%)
    ppermute x4, starting transfers between devices, local(): blocks.append(lax.ppermute(message, ('dp', 'tensor'), moves))  10.2 us
    unnamed x12, local copies, waits for them, and re-layouts  3.07 us
    pallas_call x1, Pallas kernels, partial_codes(): pl.pallas_call(codes_kernel, out_shape=jax.ShapeDtypeStruct((2 * rank, to...  3.05 us
    ppermute x4, waiting for transfers between devices, local(): blocks.append(lax.ppermute(message, ('dp', 'tensor'), moves))  2.08 us
    pallas_call x1, Pallas kernels, pack(): pl.pallas_call(pack_kernel, out_shape=(jax.ShapeDtypeStruct((rows, tokens...  1.63 us
    ppermute x1, waiting for transfers between devices, local(): other = lax.ppermute(mine, 'tensor', [(0, 1), (1, 0)])  1.2 us
    pallas_call x1, Pallas kernels, gram_of(): pl.pallas_call(gram_kernel, out_shape=jax.ShapeDtypeStruct((DOCS_DEV, hal...  1.1 us
    pallas_call x1, Pallas kernels, score_docs(): pl.pallas_call(scores_kernel, out_shape=(jax.ShapeDtypeStruct((DOCS_DEV,...  1.05 us
  transfers between devices with their start and end apart: 5, of which 2 were waited for; matrix products, arithmetic and copies ran while one was open for 0% of the time, Pallas kernels for 4%

profile of v2, /device:TPU:1, one launch (start us, length us, event | category | flops | bytes accessed | tf_op | source)
XLA Modules:
  0.0 24.2 jit_solution(2948280606655863311)
XLA Ops:
  0.6 0.0 copy-start.1
  0.6 3.0 %partial_codes.1.mine_ref = f32[128,128]{1,0:T(8,128)S(1)} custom-call(bf16[128,7168]{1,0:T(8,128)(2,1)} %x_hbm.1, bf16[128,2048]{1,0:T(8,128)(2,1)} %y_hbm.1, bf16[64,14336]{1,0:T(8,128)(2,1)} %bitcast.2, bf16[64,4096]{1,0:T(8,128)(2,1)} %bitcast.3), custom_call_target="tpu_custom_call" | custom-call | tf_op jit(solution)/shard_map/partial_codes/pallas_call | solution.py:71
  3.7 0.0 copy-start
  3.7 0.1 collective-permute-start
  3.8 1.2 %collective-permute-done.other_ref = f32[128,128]{1,0:T(8,128)S(1)} collective-permute-done((f32[128,128]{1,0:T(8,128)S(1)}, f32[128,128]{1,0:T(8,128)S(1)}, u32[]{:S(2)}, u32[]{:S(2)}) %collective-permute-start) | collective-permute-done | bytes 65568 | tf_op jit(solution)/shard_map/ppermute | solution.py:243
  5.0 0.0 copy-done
  5.0 0.0 copy-start.5
  5.0 0.6 %copy-done.5 = f32[128,128]{1,0:T(8,128)} copy-done((f32[128,128]{1,0:T(8,128)}, f32[128,128]{1,0:T(8,128)S(1)}, u32[]{:S(2)}) %copy-start.5) | copy-done | bytes 65560
  5.7 1.6 %pack_codes.1 = (f32[128,128]{1,0:T(8,128)}, s32[72,128]{1,0:T(8,128)}) custom-call(f32[128,128]{1,0:T(8,128)} %copy-done, f32[128,128]{1,0:T(8,128)} %copy-done.5, s32[1,128]{1,0:T(1,128)} %ids_ref.1), custom_call_target="tpu_custom_call" | custom-call | tf_op jit(solution)/shard_map/pack_codes/pallas_call | solution.py:119
  7.3 5.6 %collective-permute-start.1 = (s32[72,128]{1,0:T(8,128)}, s32[72,128]{1,0:T(8,128)S(1)}, u32[]{:S(2)}, u32[]{:S(2)}) collective-permute-start(s32[72,128]{1,0:T(8,128)} %get-tuple-element.7.message_ref), channel_id=1, source_target_pairs={{1,8},{3,10},{5,12},{7,14},{8,1},{10,3},{12,5},{14,7},{17,24},{19,... | collective-permute-start | bytes 110600 | tf_op jit(solution)/shard_map/ppermute | solution.py:253
  12.9 1.1 %collective-permute-start.2 = (s32[72,128]{1,0:T(8,128)}, s32[72,128]{1,0:T(8,128)S(1)}, u32[]{:S(2)}, u32[]{:S(2)}) collective-permute-start(s32[72,128]{1,0:T(8,128)} %get-tuple-element.7.message_ref), channel_id=1, source_target_pairs={{0,2},{1,10},{2,4},{3,12},{4,6},{5,14},{6,8},{7,0},{9,11},{8,3},{1... | collective-permute-start | bytes 110600 | tf_op jit(solution)/shard_map/ppermute | solution.py:253
  14.0 3.6 %collective-permute-start.3 = (s32[72,128]{1,0:T(8,128)}, s32[72,128]{1,0:T(8,128)S(1)}, u32[]{:S(2)}, u32[]{:S(2)}) collective-permute-start(s32[72,128]{1,0:T(8,128)} %get-tuple-element.7.message_ref), channel_id=1, source_target_pairs={{0,4},{1,12},{2,6},{3,14},{4,8},{5,0},{6,10},{7,2},{9,13},{8,5},{1... | collective-permute-start | bytes 110600 | tf_op jit(solution)/shard_map/ppermute | solution.py:253
  17.5 0.0 collective-permute-start.4
  17.5 0.0 copy-done.1
  17.5 0.0 copy-start.2
  17.5 0.8 %copy-done.2 = s32[72,128]{1,0:T(8,128)S(1)} copy-done((s32[72,128]{1,0:T(8,128)S(1)}, s32[72,128]{1,0:T(8,128)}, u32[]{:S(2)}) %copy-start.2) | copy-done | bytes 36888
  18.4 0.8 %copy-done.4 = f32[128,128]{1,0:T(8,128)S(1)} copy-done((f32[128,128]{1,0:T(8,128)S(1)}, f32[128,128]{1,0:T(8,128)}, u32[]{:S(2)}) %copy-start.4) | copy-done | bytes 65560
  19.2 1.1 %score_docs.1 = (f32[8,16]{1,0:T(8,128)}, bf16[128,256]{1,0:T(8,128)(2,1)S(1)}, bf16[128,256]{1,0:T(8,128)(2,1)S(1)}) custom-call(f32[128,128]{1,0:T(8,128)S(1)} %copy-done.4, s32[72,128]{1,0:T(8,128)S(1)} %copy-done.2, f32[16,4096]{1,0:T(8,128)S(1)} %copy-done.1), custom_call_target="tpu_custom_call" | custom-call | flops 67108864 | bytes 524288 | tf_op jit(solution)/shard_map/score_docs/pallas_call | solution.py:173
  20.3 0.0 collective-permute-done.1.refs_0_
  20.3 0.0 collective-permute-done.2.refs_1_
  20.3 0.0 collective-permute-done.3.refs_2_
  20.3 2.1 %collective-permute-done.4.refs_3_ = s32[72,128]{1,0:T(8,128)S(1)} collective-permute-done((s32[72,128]{1,0:T(8,128)}, s32[72,128]{1,0:T(8,128)S(1)}, u32[]{:S(2)}, u32[]{:S(2)}) %collective-permute-start.4) | collective-permute-done | bytes 36896 | tf_op jit(solution)/shard_map/ppermute | solution.py:253
  22.4 0.8 %copy-done.3 = s32[72,128]{1,0:T(8,128)S(1)} copy-done((s32[72,128]{1,0:T(8,128)S(1)}, s32[72,128]{1,0:T(8,128)}, u32[]{:S(2)}) %copy-start.3) | copy-done | bytes 36888
  23.1 1.1 %gram_rows.1 = f32[8,32]{1,0:T(8,128)} custom-call(s32[72,128]{1,0:T(8,128)S(1)} %copy-done.3, bf16[128,256]{1,0:T(8,128)(2,1)S(1)} %get-tuple-element.9.grads_ref, bf16[128,256]{1,0:T(8,128)(2,1)S(1)} %get-tuple-element.10.ins_ref, s32[72,128]{1,0:T(8,128)S(1)} %collective-permute-done.1.refs_0_, s32[72,128]{1,0:T(8,128)S(1)} %collective-permute-done.2.refs_1_, ...), custom_call_target="tpu_custom_call" | custom-call | tf_op jit(solution)/shard_map/gram_rows/pallas_call | solution.py:229
  (2 shorter events, 0.0 us)
Async XLA Ops:
  0.6 16.9 %copy-start.1 = (f32[16,4096]{1,0:T(8,128)S(1)}, f32[16,4096]{1,0:T(8,128)}, u32[]{:S(2)}) copy-start(f32[16,4096]{1,0:T(8,128)} %queries.1) | copy-start | bytes 786436
  3.7 1.3 %copy-start = (f32[128,128]{1,0:T(8,128)}, f32[128,128]{1,0:T(8,128)S(1)}, u32[]{:S(2)}) copy-start(f32[128,128]{1,0:T(8,128)S(1)} %partial_codes.1.mine_ref) | copy-start | bytes 196612
  3.7 1.3 %collective-permute-start = (f32[128,128]{1,0:T(8,128)S(1)}, f32[128,128]{1,0:T(8,128)S(1)}, u32[]{:S(2)}, u32[]{:S(2)}) collective-permute-start(f32[128,128]{1,0:T(8,128)S(1)} %partial_codes.1.mine_ref), channel_id=1, source_target_pairs={{0,1},{1,0},{2,3},{3,2},{4,5},{5,4},{6,7},{7,6},{8,9},{9,8},{10,11... | collective-permute-start | bytes 196616 | tf_op jit(solution)/shard_map/ppermute | solution.py:243
  5.0 0.6 %copy-start.5 = (f32[128,128]{1,0:T(8,128)}, f32[128,128]{1,0:T(8,128)S(1)}, u32[]{:S(2)}) copy-start(f32[128,128]{1,0:T(8,128)S(1)} %collective-permute-done.other_ref) | copy-start | bytes 196612
  7.3 13.0 %collective-permute-start.1 = (s32[72,128]{1,0:T(8,128)}, s32[72,128]{1,0:T(8,128)S(1)}, u32[]{:S(2)}, u32[]{:S(2)}) collective-permute-start(s32[72,128]{1,0:T(8,128)} %get-tuple-element.7.message_ref), channel_id=1, source_target_pairs={{1,8},{3,10},{5,12},{7,14},{8,1},{10,3},{12,5},{14,7},{17,24},{19,... | collective-permute-start | bytes 110600 | tf_op jit(solution)/shard_map/ppermute | solution.py:253
  12.9 7.4 %collective-permute-start.2 = (s32[72,128]{1,0:T(8,128)}, s32[72,128]{1,0:T(8,128)S(1)}, u32[]{:S(2)}, u32[]{:S(2)}) collective-permute-start(s32[72,128]{1,0:T(8,128)} %get-tuple-element.7.message_ref), channel_id=1, source_target_pairs={{0,2},{1,10},{2,4},{3,12},{4,6},{5,14},{6,8},{7,0},{9,11},{8,3},{1... | collective-permute-start | bytes 110600 | tf_op jit(solution)/shard_map/ppermute | solution.py:253
  14.0 6.3 %collective-permute-start.3 = (s32[72,128]{1,0:T(8,128)}, s32[72,128]{1,0:T(8,128)S(1)}, u32[]{:S(2)}, u32[]{:S(2)}) collective-permute-start(s32[72,128]{1,0:T(8,128)} %get-tuple-element.7.message_ref), channel_id=1, source_target_pairs={{0,4},{1,12},{2,6},{3,14},{4,8},{5,0},{6,10},{7,2},{9,13},{8,5},{1... | collective-permute-start | bytes 110600 | tf_op jit(solution)/shard_map/ppermute | solution.py:253
  17.5 4.8 %collective-permute-start.4 = (s32[72,128]{1,0:T(8,128)}, s32[72,128]{1,0:T(8,128)S(1)}, u32[]{:S(2)}, u32[]{:S(2)}) collective-permute-start(s32[72,128]{1,0:T(8,128)} %get-tuple-element.7.message_ref), channel_id=1, source_target_pairs={{0,6},{1,14},{2,8},{3,0},{4,10},{5,2},{6,12},{7,4},{9,15},{8,7},{1... | collective-permute-start | bytes 110600 | tf_op jit(solution)/shard_map/ppermute | solution.py:253
  17.5 0.8 %copy-start.2 = (s32[72,128]{1,0:T(8,128)S(1)}, s32[72,128]{1,0:T(8,128)}, u32[]{:S(2)}) copy-start(s32[72,128]{1,0:T(8,128)} %get-tuple-element.7.message_ref) | copy-start | bytes 110596
  18.4 0.8 %copy-start.4 = (f32[128,128]{1,0:T(8,128)S(1)}, f32[128,128]{1,0:T(8,128)}, u32[]{:S(2)}) copy-start(f32[128,128]{1,0:T(8,128)} %get-tuple-element.8.own_ref) | copy-start | bytes 196612
  22.4 0.8 %copy-start.3 = (s32[72,128]{1,0:T(8,128)S(1)}, s32[72,128]{1,0:T(8,128)}, u32[]{:S(2)}) copy-start(s32[72,128]{1,0:T(8,128)} %get-tuple-element.7.message_ref) | copy-start | bytes 110596

commit v3 on v2

--- a/solution.py
+++ b/solution.py
@@ -15,6 +15,7 @@
 NN = (((1,), (0,)), ((), ()))
 VMEM = pl.BlockSpec(memory_space=pltpu.VMEM)
 HBM = pl.BlockSpec(memory_space=pltpu.HBM)
+SMALL = pltpu.CompilerParams(vmem_limit_bytes=16 << 20)
 
 dot = functools.partial(lax.dot_general, preferred_element_type=jnp.float32)
 
@@ -57,10 +58,9 @@
     for pair, dst, w_dst, row, at, size in copies:
         for copy in pair:
             copy.wait()
-        part = dot(w_dst[:, at : at + size], dst[:, at : at + size], NT)
+        part = dot(dst[:, at : at + size], w_dst[:, at : at + size], NT)
         totals[row] = totals[row] + part if row in totals else part
-    out_ref[:rank, :] = totals[0]
-    out_ref[rank:, :] = totals[rank]
+    out_ref[...] = jnp.concatenate([totals[0], totals[rank]], axis=1).T
 
 
 def partial_codes(inputs, out_grads, proj_in_t, proj_out_t):
@@ -93,7 +93,11 @@
     return units.astype(jnp.int32), grade.astype(jnp.int32)
 
 
-def pack_kernel(mine_ref, other_ref, ids_ref, own_ref, message_ref):
+def swap(values):
+    return pltpu.roll(values, values.shape[1] // 2, 1)
+
+
+def pack_kernel(mine_ref, other_ref, ids_ref, own_ref, notes_ref, message_ref):
     rows, tokens = mine_ref.shape
     rank = rows // 2
     ids = ids_ref[...]
@@ -106,34 +110,44 @@
     own_ref[rank:, :] = ins
     grad_units, grad_grade = fixed_point(grads)
     in_units, in_grade = fixed_point(ins)
-    message_ref[:rank, :] = lax.shift_left(grad_units, 16) | (in_units & 0xFFFF)
+    units = lax.shift_left(grad_units, 16) | (in_units & 0xFFFF)
     line = lax.broadcasted_iota(jnp.int32, (EXTRA, tokens), 0)
-    message_ref[rank:, :] = jnp.where(
-        line == 0, ids, jnp.where(line == 1, grad_grade, in_grade)
-    )
-
-
-def pack(mine, other, doc_ids):
+    notes = jnp.where(line == 0, ids, jnp.where(line == 1, grad_grade, in_grade))
+    notes_ref[...] = notes
+    left = lax.broadcasted_iota(jnp.int32, (rank // 2, tokens), 1) < tokens // 2
+    first = lax.axis_index("tensor") == 0
+    top, bottom = units[: rank // 2, :], units[rank // 2 :, :]
+    top_away, bottom_away = swap(top), swap(bottom)
+    message = jnp.where(left, jnp.where(first, top, top_away), jnp.where(first, bottom_away, bottom))
+    notes = jnp.where(first, notes, swap(notes))
+    for s in range(message_ref.shape[0]):
+        message_ref[s, : rank // 2, :] = message
+        message_ref[s, rank // 2 :, :] = notes
+
+
+def pack(mine, other, doc_ids, shards):
     rows, tokens = mine.shape
     rank = rows // 2
     return pl.pallas_call(
         pack_kernel,
         out_shape=(
             jax.ShapeDtypeStruct((rows, tokens), jnp.float32),
-            jax.ShapeDtypeStruct((rank + EXTRA, tokens), jnp.int32),
+            jax.ShapeDtypeStruct((EXTRA, tokens), jnp.int32),
+            jax.ShapeDtypeStruct((shards, rank // 2 + EXTRA, tokens), jnp.int32),
         ),
         in_specs=[VMEM] * 3,
-        out_specs=(VMEM, VMEM),
+        out_specs=(VMEM,) * 3,
+        compiler_params=SMALL,
         name="pack_codes",
     )(mine, other, doc_ids)
 
 
-def scores_kernel(own_ref, message_ref, queries, scores_ref, grads_ref, ins_ref):
+def scores_kernel(own_ref, notes_ref, queries, scores_ref, grads_ref, ins_ref):
     rows, tokens = own_ref.shape
     rank = rows // 2
     grads = own_ref[:rank, :]
     ins = own_ref[rank:, :]
-    onehot = members(message_ref[rank : rank + 1, :], DOCS_DEV)
+    onehot = members(notes_ref[:1, :], DOCS_DEV)
     for values, ref in ((grads, grads_ref), (ins, ins_ref)):
         high, low = halves(values)
         stacked = jnp.concatenate([high, high, low, low], axis=0)
@@ -166,7 +180,7 @@
     scores_ref[...] = jnp.concatenate(columns, axis=1) * (1.0 / rank)
 
 
-def score_docs(own, message, queries):
+def score_docs(own, notes, queries):
     rows, tokens = own.shape
     rank = rows // 2
     operand = jax.ShapeDtypeStruct((tokens, 4 * rank), jnp.bfloat16)
@@ -179,80 +193,77 @@
         ),
         in_specs=[VMEM] * 3,
         out_specs=(VMEM, VMEM, VMEM),
-        compiler_params=pltpu.CompilerParams(vmem_limit_bytes=24 << 20),
+        compiler_params=SMALL,
         cost_estimate=pl.CostEstimate(flops=1 << 26, bytes_accessed=1 << 19, transcendentals=0),
         name="score_docs",
-    )(own, message, queries)
-
-
-def gram_kernel(message_ref, grads_ref, ins_ref, *refs):
-    blocks, out_ref = refs[:-1], refs[-1]
-    half = len(blocks)
-    shards = 2 * half
-    rank = message_ref.shape[0] - EXTRA
-    shard, core = lax.axis_index("dp"), lax.axis_index("tensor")
-    onehot = members(message_ref[rank : rank + 1, :], DOCS_DEV).astype(jnp.bfloat16)
+    )(own, notes, queries)
+
+
+def gram_kernel(notes_ref, grads_ref, ins_ref, blocks_ref, keep_ref, give_ref):
+    shards = blocks_ref.shape[0]
+    half = shards // 2
+    tokens = notes_ref.shape[1]
+    rank = 2 * (blocks_ref.shape[1] - EXTRA)
+    core = lax.axis_index("tensor")
+    onehot = members(notes_ref[:1, :], DOCS_DEV).astype(jnp.bfloat16)
     doubled = jnp.concatenate([onehot, onehot], axis=1)
+    left = lax.broadcasted_iota(jnp.int32, (blocks_ref.shape[1], tokens), 1) < tokens // 2
+    left_line = left[:1, :]
     total = None
-    width = min(4, half)
-    for first in range(0, half, width):
+    width = min(8, shards)
+    for start in range(0, shards, width):
         codes, ids, scales = [], [], []
-        for n in range(first, min(first + width, half)):
-            block = blocks[n][...]
-            if n == 0:
-                block = jnp.where(lax.div(shard, half) == core, message_ref[...], block)
-            place = lax.rem(lax.rem(shard - n + shards, shards), half)
-            codes.append(block[:rank, :])
-            ids.append(block[rank : rank + 1, :] + place * DOCS_DEV)
-            scales.append((block[rank + 1 : rank + 2, :] + block[rank + 2 : rank + 3, :]).astype(jnp.float32))
+        for s in range(start, start + width, 2):
+            one, two = blocks_ref[s], blocks_ref[s + 1]
+            top = jnp.where(left, one, swap(two))
+            bottom = jnp.where(left[: rank // 2], swap(one[: rank // 2, :]), two[: rank // 2, :])
+            codes.append(jnp.concatenate([top[: rank // 2, :], bottom], axis=0))
+            notes = top[rank // 2 :, :]
+            first, second = (lax.rem(at + core * half, shards) * DOCS_DEV for at in (s, s + 1))
+            ids.append(notes[:1, :] + jnp.where(left_line, first, second))
+            scales.append((notes[1:2, :] + notes[2:3, :]).astype(jnp.float32))
         codes, ids, scales = (jnp.concatenate(part, axis=1) for part in (codes, ids, scales))
         product = None
-        for units, left in (
+        for units, side in (
             (lax.shift_right_arithmetic(codes, 16), grads_ref),
             (lax.shift_right_arithmetic(lax.shift_left(codes, 16), 16), ins_ref),
         ):
             high, low = halves(units.astype(jnp.float32))
-            part = dot(left[...], jnp.concatenate([high, low, high, low], axis=0), NN)
+            part = dot(side[...], jnp.concatenate([high, low, high, low], axis=0), NN)
             product = part if product is None else product * part
         high, low = halves(product)
         by_doc = dot(doubled, jnp.concatenate([high, low], axis=0), NN)
         by_doc = by_doc * (jnp.exp2(scales * (1.0 / STEPS)) * (1.0 / (TOP * TOP)))
         high, low = halves(by_doc)
-        theirs = members(ids, half * DOCS_DEV).astype(jnp.bfloat16)
+        theirs = members(ids, shards * DOCS_DEV).astype(jnp.bfloat16)
         part = dot(jnp.concatenate([high, low], axis=0), theirs, NT)
         total = part if total is None else total + part
-    out_ref[...] = (total[:DOCS_DEV, :] + total[DOCS_DEV:, :]) * (1.0 / (rank * rank))
-
-
-def gram_of(message, grads, ins, blocks):
-    half = len(blocks)
+    total = (total[:DOCS_DEV, :] + total[DOCS_DEV:, :]) * (1.0 / (rank * rank))
+    keep_ref[...] = total[:, : half * DOCS_DEV]
+    give_ref[...] = total[:, half * DOCS_DEV :]
+
+
+def gram_parts(notes, grads, ins, blocks):
+    part = jax.ShapeDtypeStruct((DOCS_DEV, blocks.shape[0] // 2 * DOCS_DEV), jnp.float32)
     return pl.pallas_call(
         gram_kernel,
-        out_shape=jax.ShapeDtypeStruct((DOCS_DEV, half * DOCS_DEV), jnp.float32),
-        in_specs=[VMEM] * (3 + half),
-        out_specs=VMEM,
-        compiler_params=pltpu.CompilerParams(vmem_limit_bytes=24 << 20),
-        name="gram_rows",
-    )(message, grads, ins, *blocks)
+        out_shape=(part, part),
+        in_specs=[VMEM] * 4,
+        out_specs=(VMEM,) * 2,
+        compiler_params=SMALL,
+        name="gram_parts",
+    )(notes, grads, ins, blocks)
 
 
 def local(inputs, out_grads, proj_in, proj_out, doc_ids, queries):
-    shards = lax.axis_size("dp")
-    half = shards // 2
+    pairs = [(0, 1), (1, 0)]
     mine = partial_codes(inputs, out_grads, proj_in.T, proj_out.T)
-    other = lax.ppermute(mine, "tensor", [(0, 1), (1, 0)])
-    own, message = pack(mine, other, doc_ids)
-    blocks = []
-    for step in range(half):
-        moves = []
-        for s in range(shards):
-            side = s // half
-            if step:
-                moves.append((s * 2 + side, (s + step) % shards * 2 + side))
-            moves.append((s * 2 + 1 - side, (s + step + half) % shards * 2 + side))
-        blocks.append(lax.ppermute(message, ("dp", "tensor"), moves))
-    scores, grads, ins = score_docs(own, message, queries)
-    return gram_of(message, grads, ins, blocks), scores
+    other = lax.ppermute(mine, "tensor", pairs)
+    own, notes, messages = pack(mine, other, doc_ids, lax.axis_size("dp"))
+    blocks = lax.all_to_all(messages, "dp", 0, 0, tiled=True)
+    scores, grads, ins = score_docs(own, notes, queries)
+    keep, give = gram_parts(notes, grads, ins, blocks)
+    return keep + lax.ppermute(give, "tensor", pairs), scores
 
 
 def solution(mesh):

time: 24.6 us -> 23.7 us (0.963)
  the two profiles are of different devices: /device:TPU:1 before, /device:TPU:0 now
where the time goes in v3:
time: 23.7 us; the launch traced here: 23.5 us
  waiting for transfers between devices  8.81 us (37%)
  starting transfers between devices  7.68 us (32%)
  Pallas kernels  5.74 us (24%)
  between operations  0.66 us (3%)
  other arithmetic  0.6 us (3%)
    all_to_all x1, starting transfers between devices, local(): blocks = lax.all_to_all(messages, 'dp', 0, 0, tiled=True)  7.16 us
    all_to_all x1, waiting for transfers between devices, local(): blocks = lax.all_to_all(messages, 'dp', 0, 0, tiled=True)  6.74 us
    pallas_call x1, Pallas kernels, partial_codes(): pl.pallas_call(codes_kernel, out_shape=jax.ShapeDtypeStruct((2 * rank, to...  3.17 us
    ppermute x1, waiting for transfers between devices, local(): return (keep + lax.ppermute(give, 'tensor', pairs), scores)  1.17 us
    pallas_call x1, Pallas kernels, score_docs(): pl.pallas_call(scores_kernel, out_shape=(jax.ShapeDtypeStruct((DOCS_DEV,...  1.05 us
    ppermute x1, waiting for transfers between devices, local(): other = lax.ppermute(mine, 'tensor', pairs)  0.9 us
    pallas_call x1, Pallas kernels, pack(): pl.pallas_call(pack_kernel, out_shape=(jax.ShapeDtypeStruct((rows, tokens...  0.87 us
    pallas_call x1, Pallas kernels, gram_parts(): pl.pallas_call(gram_kernel, out_shape=(part, part), in_specs=[VMEM] * 4,...  0.66 us
  transfers between devices with their start and end apart: 3, of which 3 were waited for; matrix products, arithmetic and copies ran while one was open for 0% of the time, Pallas kernels for 4%

profile of v3, /device:TPU:0, one launch (start us, length us, event | category | flops | bytes accessed | tf_op | source)
XLA Modules:
  0.0 23.5 jit_solution(10144370960934101025)
XLA Ops:
  0.6 0.0 copy-start.1
  0.6 0.0 copy-start
  0.7 3.2 %partial_codes.1.mine_ref = f32[128,128]{1,0:T(8,128)S(1)} custom-call(bf16[128,7168]{1,0:T(8,128)(2,1)} %x_hbm.1, bf16[128,2048]{1,0:T(8,128)(2,1)} %y_hbm.1, bf16[64,14336]{1,0:T(8,128)(2,1)} %bitcast.2, bf16[64,4096]{1,0:T(8,128)(2,1)} %bitcast.3), custom_call_target="tpu_custom_call" | custom-call | tf_op jit(solution)/shard_map/partial_codes/pallas_call | solution.py:71
  3.8 0.5 %collective-permute-start = (f32[128,128]{1,0:T(8,128)S(1)}, f32[128,128]{1,0:T(8,128)S(1)}, u32[]{:S(2)}, u32[]{:S(2)}) collective-permute-start(f32[128,128]{1,0:T(8,128)S(1)} %partial_codes.1.mine_ref), channel_id=1, source_target_pairs={{0,1},{1,0},{2,3},{3,2},{4,5},{5,4},{6,7},{7,6},{8,9},{9,8},{10,11... | collective-permute-start | bytes 196616 | tf_op jit(solution)/shard_map/ppermute | solution.py:261
  4.3 0.9 %collective-permute-done.other_ref = f32[128,128]{1,0:T(8,128)S(1)} collective-permute-done((f32[128,128]{1,0:T(8,128)S(1)}, f32[128,128]{1,0:T(8,128)S(1)}, u32[]{:S(2)}, u32[]{:S(2)}) %collective-permute-start) | collective-permute-done | bytes 65568 | tf_op jit(solution)/shard_map/ppermute | solution.py:261
  5.2 0.0 copy-done.1
  5.2 0.9 %pack_codes.1 = (f32[128,128]{1,0:T(8,128)S(1)}, s32[8,128]{1,0:T(8,128)S(1)}, s32[8,40,128]{2,1,0:T(8,128)}) custom-call(f32[128,128]{1,0:T(8,128)S(1)} %partial_codes.1.mine_ref, f32[128,128]{1,0:T(8,128)S(1)} %collective-permute-done.other_ref, s32[1,128]{1,0:T(1,128)S(1)} %copy-done.1), custom_call_target="tpu_custom_call" | custom-call | tf_op jit(solution)/shard_map/pack_codes/pallas_call | solution.py:131
  6.1 7.2 %all-to-all-start = ((s32[8,40,128]{2,1,0:T(8,128)}), s32[8,40,128]{2,1,0:T(8,128)S(1)}, u32[]{:S(2)}, u32[]{:S(2)}) async-start(s32[8,40,128]{2,1,0:T(8,128)} %get-tuple-element.14), calls=%async_computation | async-start | bytes 327680 | tf_op jit(solution)/shard_map/all_to_all | solution.py:263
  13.3 0.0 copy-done
  13.3 1.0 %score_docs.1 = (f32[8,16]{1,0:T(8,128)}, bf16[128,256]{1,0:T(8,128)(2,1)S(1)}, bf16[128,256]{1,0:T(8,128)(2,1)S(1)}) custom-call(f32[128,128]{1,0:T(8,128)S(1)} %get-tuple-element.11.own_ref, s32[8,128]{1,0:T(8,128)S(1)} %get-tuple-element.10.notes_ref, f32[16,4096]{1,0:T(8,128)S(1)} %copy-done), custom_call_target="tpu_custom_call" | custom-call | flops 67108864 | bytes 524288 | tf_op jit(solution)/shard_map/score_docs/pallas_call | solution.py:187
  14.3 6.7 %all-to-all-done.blocks_ref = s32[8,40,128]{2,1,0:T(8,128)S(1)} async-done(((s32[8,40,128]{2,1,0:T(8,128)}), s32[8,40,128]{2,1,0:T(8,128)S(1)}, u32[]{:S(2)}, u32[]{:S(2)}) %all-to-all-start) | async-done | bytes 163872 | tf_op jit(solution)/shard_map/all_to_all | solution.py:263
  21.1 0.7 %gram_parts.1 = (f32[8,32]{1,0:T(8,128)S(1)}, f32[8,32]{1,0:T(8,128)S(1)}) custom-call(s32[8,128]{1,0:T(8,128)S(1)} %get-tuple-element.10.notes_ref, bf16[128,256]{1,0:T(8,128)(2,1)S(1)} %get-tuple-element.12.grads_ref, bf16[128,256]{1,0:T(8,128)(2,1)S(1)} %get-tuple-element.13.ins_ref, s32[8,40,128]{2,1,0:T(8,128)S(1)} %all-to-all-done.blocks_ref), custom_call_target="tpu_custom_call" | custom-call | tf_op jit(solution)/shard_map/gram_parts/pallas_call | solution.py:248
  21.7 0.0 collective-permute-start.1
  21.7 1.2 %collective-permute-done.1 = f32[8,32]{1,0:T(8,128)S(1)} collective-permute-done((f32[8,32]{1,0:T(8,128)S(1)}, f32[8,32]{1,0:T(8,128)S(1)}, u32[]{:S(2)}, u32[]{:S(2)}) %collective-permute-start.1) | collective-permute-done | bytes 1056 | tf_op jit(solution)/shard_map/ppermute | solution.py:266
  22.9 0.6 %add.3 = f32[8,32]{1,0:T(8,128)} add(f32[8,32]{1,0:T(8,128)S(1)} %get-tuple-element.15, f32[8,32]{1,0:T(8,128)S(1)} %collective-permute-done.1) | non-fusion elementwise | flops 256 | bytes 3072 | tf_op jit(solution)/shard_map/add | solution.py:266
Async XLA Ops:
  0.6 4.6 %copy-start.1 = (s32[1,128]{1,0:T(1,128)S(1)}, s32[1,128]{1,0:T(1,128)}, u32[]{:S(2)}) copy-start(s32[1,128]{1,0:T(1,128)} %ids_ref.1) | copy-start | bytes 1540
  0.6 12.6 %copy-start = (f32[16,4096]{1,0:T(8,128)S(1)}, f32[16,4096]{1,0:T(8,128)}, u32[]{:S(2)}) copy-start(f32[16,4096]{1,0:T(8,128)} %queries.1) | copy-start | bytes 786436
  3.8 1.4 %collective-permute-start = (f32[128,128]{1,0:T(8,128)S(1)}, f32[128,128]{1,0:T(8,128)S(1)}, u32[]{:S(2)}, u32[]{:S(2)}) collective-permute-start(f32[128,128]{1,0:T(8,128)S(1)} %partial_codes.1.mine_ref), channel_id=1, source_target_pairs={{0,1},{1,0},{2,3},{3,2},{4,5},{5,4},{6,7},{7,6},{8,9},{9,8},{10,11... | collective-permute-start | bytes 196616 | tf_op jit(solution)/shard_map/ppermute | solution.py:261
  6.1 14.9 %all-to-all-start = ((s32[8,40,128]{2,1,0:T(8,128)}), s32[8,40,128]{2,1,0:T(8,128)S(1)}, u32[]{:S(2)}, u32[]{:S(2)}) async-start(s32[8,40,128]{2,1,0:T(8,128)} %get-tuple-element.14), calls=%async_computation | async-start | bytes 327680 | tf_op jit(solution)/shard_map/all_to_all | solution.py:263
  21.7 1.2 %collective-permute-start.1 = (f32[8,32]{1,0:T(8,128)S(1)}, f32[8,32]{1,0:T(8,128)S(1)}, u32[]{:S(2)}, u32[]{:S(2)}) collective-permute-start(f32[8,32]{1,0:T(8,128)S(1)} %get-tuple-element.16), channel_id=1, source_target_pairs={{0,1},{1,0},{2,3},{3,2},{4,5},{5,4},{6,7},{7,6},{8,9},{9,8},{10,11... | collective-permute-start | bytes 3080 | tf_op jit(solution)/shard_map/ppermute | solution.py:266

commit v4 on v2

--- a/solution.py
+++ b/solution.py
@@ -15,15 +15,14 @@
 NN = (((1,), (0,)), ((), ()))
 VMEM = pl.BlockSpec(memory_space=pltpu.VMEM)
 HBM = pl.BlockSpec(memory_space=pltpu.HBM)
+SMALL = pltpu.CompilerParams(vmem_limit_bytes=16 << 20)
 
 dot = functools.partial(lax.dot_general, preferred_element_type=jnp.float32)
 
 
 def chunks_of(depth):
-    for size in (1024, 512, 256, 128):
-        if depth % size == 0:
-            return [(at, size) for at in range(0, depth, size)]
-    return [(0, depth)]
+    size = next(size for size in (2048, 1792, 1024, 512, 256, 128, depth) if depth % size == 0)
+    return [(at, size) for at in range(0, depth, size)]
 
 
 def halves(values):
@@ -124,6 +123,7 @@
         ),
         in_specs=[VMEM] * 3,
         out_specs=(VMEM, VMEM),
+        compiler_params=SMALL,
         name="pack_codes",
     )(mine, other, doc_ids)
 
@@ -179,32 +179,51 @@
         ),
         in_specs=[VMEM] * 3,
         out_specs=(VMEM, VMEM, VMEM),
-        compiler_params=pltpu.CompilerParams(vmem_limit_bytes=24 << 20),
+        compiler_params=SMALL,
         cost_estimate=pl.CostEstimate(flops=1 << 26, bytes_accessed=1 << 19, transcendentals=0),
         name="score_docs",
     )(own, message, queries)
 
 
-def gram_kernel(message_ref, grads_ref, ins_ref, *refs):
+def join_kernel(mine_ref, other_ref, out_ref):
+    out_ref[0] = mine_ref[...]
+    out_ref[1] = other_ref[...]
+
+
+def join(mine, other):
+    return pl.pallas_call(
+        join_kernel,
+        out_shape=jax.ShapeDtypeStruct((2,) + mine.shape, mine.dtype),
+        in_specs=[VMEM] * 2,
+        out_specs=VMEM,
+        compiler_params=SMALL,
+        name="join_plane",
+    )(mine, other)
+
+
+def gram_kernel(plane_ref, grads_ref, ins_ref, *refs):
     blocks, out_ref = refs[:-1], refs[-1]
     half = len(blocks)
-    shards = 2 * half
-    rank = message_ref.shape[0] - EXTRA
+    rank = plane_ref.shape[1] - EXTRA
     shard, core = lax.axis_index("dp"), lax.axis_index("tensor")
-    onehot = members(message_ref[rank : rank + 1, :], DOCS_DEV).astype(jnp.bfloat16)
+    plane, side = lax.div(shard, 2), lax.rem(shard, 2)
+    own_half = lax.div(plane, half) == core
+    onehot = members(plane_ref[0, rank : rank + 1, :], DOCS_DEV).astype(jnp.bfloat16)
     doubled = jnp.concatenate([onehot, onehot], axis=1)
     total = None
-    width = min(4, half)
+    width = min(2, half)
     for first in range(0, half, width):
         codes, ids, scales = [], [], []
-        for n in range(first, min(first + width, half)):
-            block = blocks[n][...]
-            if n == 0:
-                block = jnp.where(lax.div(shard, half) == core, message_ref[...], block)
-            place = lax.rem(lax.rem(shard - n + shards, shards), half)
-            codes.append(block[:rank, :])
-            ids.append(block[rank : rank + 1, :] + place * DOCS_DEV)
-            scales.append((block[rank + 1 : rank + 2, :] + block[rank + 2 : rank + 3, :]).astype(jnp.float32))
+        for n in range(first, first + width):
+            block, near, far = blocks[n][...], n + 1, 2 * half - 1 - n
+            if n == half - 1:
+                block, near = jnp.where(own_half, plane_ref[...], block), 0
+            source = lax.rem(lax.bitwise_xor(plane, jnp.where(own_half, near, far)), half)
+            for slot, at in ((0, side), (1, 1 - side)):
+                codes.append(block[slot, :rank, :])
+                ids.append(block[slot, rank : rank + 1, :] + (2 * source + at) * DOCS_DEV)
+                grades = block[slot, rank + 1 : rank + 2, :] + block[slot, rank + 2 : rank + 3, :]
+                scales.append(grades.astype(jnp.float32))
         codes, ids, scales = (jnp.concatenate(part, axis=1) for part in (codes, ids, scales))
         product = None
         for units, left in (
@@ -218,41 +237,44 @@
         by_doc = dot(doubled, jnp.concatenate([high, low], axis=0), NN)
         by_doc = by_doc * (jnp.exp2(scales * (1.0 / STEPS)) * (1.0 / (TOP * TOP)))
         high, low = halves(by_doc)
-        theirs = members(ids, half * DOCS_DEV).astype(jnp.bfloat16)
+        theirs = members(ids, 2 * half * DOCS_DEV).astype(jnp.bfloat16)
         part = dot(jnp.concatenate([high, low], axis=0), theirs, NT)
         total = part if total is None else total + part
     out_ref[...] = (total[:DOCS_DEV, :] + total[DOCS_DEV:, :]) * (1.0 / (rank * rank))
 
 
-def gram_of(message, grads, ins, blocks):
-    half = len(blocks)
+def gram_of(plane, grads, ins, blocks):
     return pl.pallas_call(
         gram_kernel,
-        out_shape=jax.ShapeDtypeStruct((DOCS_DEV, half * DOCS_DEV), jnp.float32),
-        in_specs=[VMEM] * (3 + half),
+        out_shape=jax.ShapeDtypeStruct((DOCS_DEV, 2 * len(blocks) * DOCS_DEV), jnp.float32),
+        in_specs=[VMEM] * (3 + len(blocks)),
         out_specs=VMEM,
-        compiler_params=pltpu.CompilerParams(vmem_limit_bytes=24 << 20),
+        compiler_params=SMALL,
         name="gram_rows",
-    )(message, grads, ins, *blocks)
+    )(plane, grads, ins, *blocks)
 
 
 def local(inputs, out_grads, proj_in, proj_out, doc_ids, queries):
     shards = lax.axis_size("dp")
-    half = shards // 2
+    planes = shards // 2
+    half = planes // 2
     mine = partial_codes(inputs, out_grads, proj_in.T, proj_out.T)
     other = lax.ppermute(mine, "tensor", [(0, 1), (1, 0)])
     own, message = pack(mine, other, doc_ids)
+    plane = join(message, lax.ppermute(message, "dp", [(s, s ^ 1) for s in range(shards)]))
     blocks = []
-    for step in range(half):
+    for n in range(half):
         moves = []
-        for s in range(shards):
-            side = s // half
-            if step:
-                moves.append((s * 2 + side, (s + step) % shards * 2 + side))
-            moves.append((s * 2 + 1 - side, (s + step + half) % shards * 2 + side))
-        blocks.append(lax.ppermute(message, ("dp", "tensor"), moves))
+        for p in range(planes):
+            for x in range(2):
+                core = p // half
+                if n < half - 1:
+                    moves.append((4 * p + 2 * x + core, 4 * (p ^ (n + 1)) + 2 * x + core))
+                far = p ^ (planes - 1 - n)
+                moves.append((4 * p + 2 * x + 1 - core, 4 * far + 2 * x + 1 - far // half))
+        blocks.append(lax.ppermute(plane, ("dp", "tensor"), moves))
     scores, grads, ins = score_docs(own, message, queries)
-    return gram_of(message, grads, ins, blocks), scores
+    return gram_of(plane, grads, ins, blocks), scores
 
 
 def solution(mesh):

time: 24.6 us -> 21.5 us (0.87)
  local copies, waits for them, and re-layouts: 3.07 us -> 0.01 us
  waiting for transfers between devices: 3.28 us -> 6.06 us
  Pallas kernels: 6.83 us -> 5.11 us
  starting transfers between devices: 10.4 us -> 9.49 us
    unnamed x12 -> x4, local copies, waits for them, and re-layouts: 3.07 us -> 0.01 us
    ppermute x4 -> x3, waiting for transfers between devices: 2.08 us -> 4.86 us  [the longest x2 3.51 us: local(): blocks.append(lax.ppermute(plane, ('dp', 'tensor'), moves))]
    pallas_call x1, Pallas kernels: 1.63 us -> 0.14 us  [pack(): pl.pallas_call(pack_kernel, out_shape=(jax.ShapeDtypeStruct((rows, tokens...]
    ppermute x4 -> x3, starting transfers between devices: 10.2 us -> 9.37 us  [the longest x2 6.94 us: local(): blocks.append(lax.ppermute(plane, ('dp', 'tensor'), moves))]
    pallas_call x1 -> x2, Pallas kernels: 1.1 us -> 1.11 us  [the longest x1 1.1 us: gram_of(): pl.pallas_call(gram_kernel, out_shape=jax.ShapeDtypeStruct((DOCS_DEV, 2 *...]
  transfers between devices with their start and end apart: 5 -> 4, of which waited for: 2 -> 3; matrix products, arithmetic and copies ran while one was open for 0% -> 0% of each run, Pallas kernels for 4% -> 5%
where the time goes in v4:
time: 21.5 us; the launch traced here: 21.3 us
  starting transfers between devices  9.49 us (44%)
  waiting for transfers between devices  6.06 us (28%)
  Pallas kernels  5.11 us (24%)
  between operations  0.68 us (3%)
    ppermute x2, starting transfers between devices, local(): blocks.append(lax.ppermute(plane, ('dp', 'tensor'), moves))  6.94 us
    ppermute x2, waiting for transfers between devices, local(): blocks.append(lax.ppermute(plane, ('dp', 'tensor'), moves))  3.51 us
    pallas_call x1, Pallas kernels, partial_codes(): pl.pallas_call(codes_kernel, out_shape=jax.ShapeDtypeStruct((2 * rank, to...  2.83 us
    ppermute x1, starting transfers between devices, local(): lax.ppermute(message, 'dp', [(s, s ^ 1) for s in range(shards)])  2.43 us
    ppermute x1, waiting for transfers between devices, local(): lax.ppermute(message, 'dp', [(s, s ^ 1) for s in range(shards)])  1.35 us
    ppermute x1, waiting for transfers between devices, local(): other = lax.ppermute(mine, 'tensor', [(0, 1), (1, 0)])  1.2 us
    pallas_call x1, Pallas kernels, gram_of(): pl.pallas_call(gram_kernel, out_shape=jax.ShapeDtypeStruct((DOCS_DEV, 2 *...  1.1 us
    pallas_call x1, Pallas kernels, score_docs(): pl.pallas_call(scores_kernel, out_shape=(jax.ShapeDtypeStruct((DOCS_DEV,...  1.04 us
  transfers between devices with their start and end apart: 4, of which 3 were waited for; matrix products, arithmetic and copies ran while one was open for 0% of the time, Pallas kernels for 5%

profile of v4, /device:TPU:1, one launch (start us, length us, event | category | flops | bytes accessed | tf_op | source)
XLA Modules:
  0.0 21.3 jit_solution(2045666645358956008)
XLA Ops:
  0.6 0.0 copy-start.1
  0.6 0.0 copy-start
  0.7 2.8 %partial_codes.1.mine_ref = f32[128,128]{1,0:T(8,128)S(1)} custom-call(bf16[128,7168]{1,0:T(8,128)(2,1)} %x_hbm.1, bf16[128,2048]{1,0:T(8,128)(2,1)} %y_hbm.1, bf16[64,14336]{1,0:T(8,128)(2,1)} %bitcast.2, bf16[64,4096]{1,0:T(8,128)(2,1)} %bitcast.3), custom_call_target="tpu_custom_call" | custom-call | tf_op jit(solution)/shard_map/partial_codes/pallas_call | solution.py:70
  3.5 0.1 collective-permute-start
  3.6 1.2 %collective-permute-done.other_ref = f32[128,128]{1,0:T(8,128)S(1)} collective-permute-done((f32[128,128]{1,0:T(8,128)S(1)}, f32[128,128]{1,0:T(8,128)S(1)}, u32[]{:S(2)}, u32[]{:S(2)}) %collective-permute-start) | collective-permute-done | bytes 65568 | tf_op jit(solution)/shard_map/ppermute | solution.py:262
  4.8 0.0 copy-done.1
  4.8 0.1 pack_codes.1
  5.0 2.4 %collective-permute-start.1 = (s32[72,128]{1,0:T(8,128)S(1)}, s32[72,128]{1,0:T(8,128)S(1)}, u32[]{:S(2)}, u32[]{:S(2)}) collective-permute-start(s32[72,128]{1,0:T(8,128)S(1)} %get-tuple-element.7.mine_ref.message_ref), channel_id=1, source_target_pairs={{0,2},{2,0},{4,6},{6,4},{8,10},{10,8},{12,14},{14,12},{1,3},{3,1},... | collective-permute-start | bytes 110600 | tf_op jit(solution)/shard_map/ppermute | solution.py:264
  7.4 1.3 %collective-permute-done.1.other_ref = s32[72,128]{1,0:T(8,128)S(1)} collective-permute-done((s32[72,128]{1,0:T(8,128)S(1)}, s32[72,128]{1,0:T(8,128)S(1)}, u32[]{:S(2)}, u32[]{:S(2)}) %collective-permute-start.1) | collective-permute-done | bytes 36896 | tf_op jit(solution)/shard_map/ppermute | solution.py:264
  8.7 5.8 %collective-permute-start.3 = (s32[2,72,128]{2,1,0:T(8,128)S(1)}, s32[2,72,128]{2,1,0:T(8,128)S(1)}, u32[]{:S(2)}, u32[]{:S(2)}) collective-permute-start(s32[2,72,128]{2,1,0:T(8,128)S(1)} %join_plane.1.plane_ref), channel_id=1, source_target_pairs={{1,8},{3,10},{5,12},{7,14},{8,1},{10,3},{12,5},{14,7},{17,24},{19,... | collective-permute-start | bytes 221192 | tf_op jit(solution)/shard_map/ppermute | solution.py:275
  14.6 1.1 %collective-permute-start.2 = (s32[2,72,128]{2,1,0:T(8,128)S(1)}, s32[2,72,128]{2,1,0:T(8,128)S(1)}, u32[]{:S(2)}, u32[]{:S(2)}) collective-permute-start(s32[2,72,128]{2,1,0:T(8,128)S(1)} %join_plane.1.plane_ref), channel_id=1, source_target_pairs={{0,4},{1,12},{2,6},{3,14},{4,0},{5,8},{6,2},{7,10},{9,13},{8,5},{1... | collective-permute-start | bytes 221192 | tf_op jit(solution)/shard_map/ppermute | solution.py:275
  15.7 0.0 copy-done
  15.7 1.0 %score_docs.1 = (f32[8,16]{1,0:T(8,128)}, bf16[128,256]{1,0:T(8,128)(2,1)S(1)}, bf16[128,256]{1,0:T(8,128)(2,1)S(1)}) custom-call(f32[128,128]{1,0:T(8,128)S(1)} %get-tuple-element.8.own_ref, s32[72,128]{1,0:T(8,128)S(1)} %get-tuple-element.7.mine_ref.message_ref, f32[16,4096]{1,0:T(8,128)S(1)} %copy-done), custom_call_target="tpu_custom_call" | custom-call | flops 67108864 | bytes 524288 | tf_op jit(solution)/shard_map/score_docs/pallas_call | solution.py:173
  16.7 0.0 collective-permute-done.3.refs_1_
  16.7 3.5 %collective-permute-done.2.refs_0_ = s32[2,72,128]{2,1,0:T(8,128)S(1)} collective-permute-done((s32[2,72,128]{2,1,0:T(8,128)S(1)}, s32[2,72,128]{2,1,0:T(8,128)S(1)}, u32[]{:S(2)}, u32[]{:S(2)}) %collective-permute-start.2) | collective-permute-done | bytes 73760 | tf_op jit(solution)/shard_map/ppermute | solution.py:275
  20.2 1.1 %gram_rows.1 = f32[8,32]{1,0:T(8,128)} custom-call(s32[2,72,128]{2,1,0:T(8,128)S(1)} %join_plane.1.plane_ref, bf16[128,256]{1,0:T(8,128)(2,1)S(1)} %get-tuple-element.9.grads_ref, bf16[128,256]{1,0:T(8,128)(2,1)S(1)} %get-tuple-element.10.ins_ref, s32[2,72,128]{2,1,0:T(8,128)S(1)} %collective-permute-done.2.refs_0_, ...), custom_call_target="tpu_custom_call" | custom-call | tf_op jit(solution)/shard_map/gram_rows/pallas_call | solution.py:247
  (1 shorter events, 0.0 us)
Async XLA Ops:
  0.6 4.2 %copy-start.1 = (s32[1,128]{1,0:T(1,128)S(1)}, s32[1,128]{1,0:T(1,128)}, u32[]{:S(2)}) copy-start(s32[1,128]{1,0:T(1,128)} %ids_ref.1) | copy-start | bytes 1540
  0.6 15.0 %copy-start = (f32[16,4096]{1,0:T(8,128)S(1)}, f32[16,4096]{1,0:T(8,128)}, u32[]{:S(2)}) copy-start(f32[16,4096]{1,0:T(8,128)} %queries.1) | copy-start | bytes 786436
  3.5 1.3 %collective-permute-start = (f32[128,128]{1,0:T(8,128)S(1)}, f32[128,128]{1,0:T(8,128)S(1)}, u32[]{:S(2)}, u32[]{:S(2)}) collective-permute-start(f32[128,128]{1,0:T(8,128)S(1)} %partial_codes.1.mine_ref), channel_id=1, source_target_pairs={{0,1},{1,0},{2,3},{3,2},{4,5},{5,4},{6,7},{7,6},{8,9},{9,8},{10,11... | collective-permute-start | bytes 196616 | tf_op jit(solution)/shard_map/ppermute | solution.py:262
  5.0 3.8 %collective-permute-start.1 = (s32[72,128]{1,0:T(8,128)S(1)}, s32[72,128]{1,0:T(8,128)S(1)}, u32[]{:S(2)}, u32[]{:S(2)}) collective-permute-start(s32[72,128]{1,0:T(8,128)S(1)} %get-tuple-element.7.mine_ref.message_ref), channel_id=1, source_target_pairs={{0,2},{2,0},{4,6},{6,4},{8,10},{10,8},{12,14},{14,12},{1,3},{3,1},... | collective-permute-start | bytes 110600 | tf_op jit(solution)/shard_map/ppermute | solution.py:264
  8.7 8.0 %collective-permute-start.3 = (s32[2,72,128]{2,1,0:T(8,128)S(1)}, s32[2,72,128]{2,1,0:T(8,128)S(1)}, u32[]{:S(2)}, u32[]{:S(2)}) collective-permute-start(s32[2,72,128]{2,1,0:T(8,128)S(1)} %join_plane.1.plane_ref), channel_id=1, source_target_pairs={{1,8},{3,10},{5,12},{7,14},{8,1},{10,3},{12,5},{14,7},{17,24},{19,... | collective-permute-start | bytes 221192 | tf_op jit(solution)/shard_map/ppermute | solution.py:275
  14.6 5.6 %collective-permute-start.2 = (s32[2,72,128]{2,1,0:T(8,128)S(1)}, s32[2,72,128]{2,1,0:T(8,128)S(1)}, u32[]{:S(2)}, u32[]{:S(2)}) collective-permute-start(s32[2,72,128]{2,1,0:T(8,128)S(1)} %join_plane.1.plane_ref), channel_id=1, source_target_pairs={{0,4},{1,12},{2,6},{3,14},{4,0},{5,8},{6,2},{7,10},{9,13},{8,5},{1... | collective-permute-start | bytes 221192 | tf_op jit(solution)/shard_map/ppermute | solution.py:275

commit v5 on v2

--- a/solution.py
+++ b/solution.py
@@ -15,15 +15,14 @@
 NN = (((1,), (0,)), ((), ()))
 VMEM = pl.BlockSpec(memory_space=pltpu.VMEM)
 HBM = pl.BlockSpec(memory_space=pltpu.HBM)
+SMALL = pltpu.CompilerParams(vmem_limit_bytes=16 << 20)
 
 dot = functools.partial(lax.dot_general, preferred_element_type=jnp.float32)
 
 
 def chunks_of(depth):
-    for size in (1024, 512, 256, 128):
-        if depth % size == 0:
-            return [(at, size) for at in range(0, depth, size)]
-    return [(0, depth)]
+    size = next(size for size in (2048, 1792, 1024, 512, 256, 128, depth) if depth % size == 0)
+    return [(at, size) for at in range(0, depth, size)]
 
 
 def halves(values):
@@ -124,6 +123,7 @@
         ),
         in_specs=[VMEM] * 3,
         out_specs=(VMEM, VMEM),
+        compiler_params=SMALL,
         name="pack_codes",
     )(mine, other, doc_ids)
 
@@ -179,29 +179,36 @@
         ),
         in_specs=[VMEM] * 3,
         out_specs=(VMEM, VMEM, VMEM),
-        compiler_params=pltpu.CompilerParams(vmem_limit_bytes=24 << 20),
+        compiler_params=SMALL,
         cost_estimate=pl.CostEstimate(flops=1 << 26, bytes_accessed=1 << 19, transcendentals=0),
         name="score_docs",
     )(own, message, queries)
 
 
+def partners(shards):
+    half = shards // 2
+    order = [*range(half // 2, 0, -1), *range(half - 1, half // 2, -1), 0]
+    return [half ^ n for n in order], [1] + [n ^ (n >> 1) for n in range(1, half)]
+
+
 def gram_kernel(message_ref, grads_ref, ins_ref, *refs):
     blocks, out_ref = refs[:-1], refs[-1]
     half = len(blocks)
-    shards = 2 * half
     rank = message_ref.shape[0] - EXTRA
     shard, core = lax.axis_index("dp"), lax.axis_index("tensor")
+    own_half = lax.div(shard, half) == core
     onehot = members(message_ref[rank : rank + 1, :], DOCS_DEV).astype(jnp.bfloat16)
     doubled = jnp.concatenate([onehot, onehot], axis=1)
+    far, near = partners(2 * half)
     total = None
     width = min(4, half)
     for first in range(0, half, width):
         codes, ids, scales = [], [], []
-        for n in range(first, min(first + width, half)):
-            block = blocks[n][...]
+        for n in range(first, first + width):
+            block, change = blocks[n][...], near[n]
             if n == 0:
-                block = jnp.where(lax.div(shard, half) == core, message_ref[...], block)
-            place = lax.rem(lax.rem(shard - n + shards, shards), half)
+                block, change = jnp.where(own_half, message_ref[...], block), 0
+            place = lax.rem(lax.bitwise_xor(shard, jnp.where(own_half, change, far[n])), half)
             codes.append(block[:rank, :])
             ids.append(block[rank : rank + 1, :] + place * DOCS_DEV)
             scales.append((block[rank + 1 : rank + 2, :] + block[rank + 2 : rank + 3, :]).astype(jnp.float32))
@@ -225,13 +232,12 @@
 
 
 def gram_of(message, grads, ins, blocks):
-    half = len(blocks)
     return pl.pallas_call(
         gram_kernel,
-        out_shape=jax.ShapeDtypeStruct((DOCS_DEV, half * DOCS_DEV), jnp.float32),
-        in_specs=[VMEM] * (3 + half),
+        out_shape=jax.ShapeDtypeStruct((DOCS_DEV, len(blocks) * DOCS_DEV), jnp.float32),
+        in_specs=[VMEM] * (3 + len(blocks)),
         out_specs=VMEM,
-        compiler_params=pltpu.CompilerParams(vmem_limit_bytes=24 << 20),
+        compiler_params=SMALL,
         name="gram_rows",
     )(message, grads, ins, *blocks)
 
@@ -243,13 +249,12 @@
     other = lax.ppermute(mine, "tensor", [(0, 1), (1, 0)])
     own, message = pack(mine, other, doc_ids)
     blocks = []
-    for step in range(half):
+    for far, near in zip(*partners(shards)):
         moves = []
         for s in range(shards):
-            side = s // half
-            if step:
-                moves.append((s * 2 + side, (s + step) % shards * 2 + side))
-            moves.append((s * 2 + 1 - side, (s + step + half) % shards * 2 + side))
+            core = s // half
+            moves.append((2 * s + core, 2 * (s ^ near) + core))
+            moves.append((2 * s + 1 - core, 2 * (s ^ far) + core))
         blocks.append(lax.ppermute(message, ("dp", "tensor"), moves))
     scores, grads, ins = score_docs(own, message, queries)
     return gram_of(message, grads, ins, blocks), scores

time: 24.6 us -> 17.8 us (0.72)
  local copies, waits for them, and re-layouts: 3.07 us -> 0.01 us
  starting transfers between devices: 10.4 us -> 8.48 us
  Pallas kernels: 6.83 us -> 5.1 us
    unnamed x12 -> x4, local copies, waits for them, and re-layouts: 3.07 us -> 0.01 us
    ppermute x4, starting transfers between devices: 10.2 us -> 8.35 us  [local(): blocks.append(lax.ppermute(message, ('dp', 'tensor'), moves))]
    pallas_call x1, Pallas kernels: 1.63 us -> 0.14 us  [pack(): pl.pallas_call(pack_kernel, out_shape=(jax.ShapeDtypeStruct((rows, tokens...]
  transfers between devices with their start and end apart: 5 -> 5, of which waited for: 2 -> 4; matrix products, arithmetic and copies ran while one was open for 0% -> 0% of each run, Pallas kernels for 4% -> 6%
where the time goes in v5:
time: 17.8 us; the launch traced here: 17.6 us
  starting transfers between devices  8.48 us (48%)
  Pallas kernels  5.1 us (29%)
  waiting for transfers between devices  3.39 us (19%)
  between operations  0.67 us (4%)
    ppermute x4, starting transfers between devices, local(): blocks.append(lax.ppermute(message, ('dp', 'tensor'), moves))  8.35 us
    pallas_call x1, Pallas kernels, partial_codes(): pl.pallas_call(codes_kernel, out_shape=jax.ShapeDtypeStruct((2 * rank, to...  2.83 us
    ppermute x4, waiting for transfers between devices, local(): blocks.append(lax.ppermute(message, ('dp', 'tensor'), moves))  2.2 us
    ppermute x1, waiting for transfers between devices, local(): other = lax.ppermute(mine, 'tensor', [(0, 1), (1, 0)])  1.2 us
    pallas_call x1, Pallas kernels, gram_of(): pl.pallas_call(gram_kernel, out_shape=jax.ShapeDtypeStruct((DOCS_DEV, len...  1.1 us
    pallas_call x1, Pallas kernels, score_docs(): pl.pallas_call(scores_kernel, out_shape=(jax.ShapeDtypeStruct((DOCS_DEV,...  1.04 us
  transfers between devices with their start and end apart: 5, of which 4 were waited for; matrix products, arithmetic and copies ran while one was open for 0% of the time, Pallas kernels for 6%

profile of v5, /device:TPU:1, one launch (start us, length us, event | category | flops | bytes accessed | tf_op | source)
XLA Modules:
  0.0 17.6 jit_solution(12107425233169977180)
XLA Ops:
  0.6 0.0 copy-start.1
  0.6 0.0 copy-start
  0.7 2.8 %partial_codes.1.mine_ref = f32[128,128]{1,0:T(8,128)S(1)} custom-call(bf16[128,7168]{1,0:T(8,128)(2,1)} %x_hbm.1, bf16[128,2048]{1,0:T(8,128)(2,1)} %y_hbm.1, bf16[64,14336]{1,0:T(8,128)(2,1)} %bitcast.2, bf16[64,4096]{1,0:T(8,128)(2,1)} %bitcast.3), custom_call_target="tpu_custom_call" | custom-call | tf_op jit(solution)/shard_map/partial_codes/pallas_call | solution.py:70
  3.5 0.1 collective-permute-start
  3.6 1.2 %collective-permute-done.other_ref = f32[128,128]{1,0:T(8,128)S(1)} collective-permute-done((f32[128,128]{1,0:T(8,128)S(1)}, f32[128,128]{1,0:T(8,128)S(1)}, u32[]{:S(2)}, u32[]{:S(2)}) %collective-permute-start) | collective-permute-done | bytes 65568 | tf_op jit(solution)/shard_map/ppermute | solution.py:249
  4.8 0.0 copy-done.1
  4.8 0.1 pack_codes.1
  5.0 4.8 %collective-permute-start.1 = (s32[72,128]{1,0:T(8,128)S(1)}, s32[72,128]{1,0:T(8,128)S(1)}, u32[]{:S(2)}, u32[]{:S(2)}) collective-permute-start(s32[72,128]{1,0:T(8,128)S(1)} %get-tuple-element.7.message_ref), channel_id=1, source_target_pairs={{0,2},{1,12},{2,0},{3,14},{4,6},{5,8},{6,4},{7,10},{9,11},{8,5},{1... | collective-permute-start | bytes 110600 | tf_op jit(solution)/shard_map/ppermute | solution.py:258
  9.7 0.1 collective-permute-start.2
  9.9 2.4 %collective-permute-start.3 = (s32[72,128]{1,0:T(8,128)S(1)}, s32[72,128]{1,0:T(8,128)S(1)}, u32[]{:S(2)}, u32[]{:S(2)}) collective-permute-start(s32[72,128]{1,0:T(8,128)S(1)} %get-tuple-element.7.message_ref), channel_id=1, source_target_pairs={{0,6},{1,14},{2,4},{3,12},{4,2},{5,10},{6,0},{7,8},{9,15},{8,7},{1... | collective-permute-start | bytes 110600 | tf_op jit(solution)/shard_map/ppermute | solution.py:258
  12.3 1.0 %collective-permute-start.4 = (s32[72,128]{1,0:T(8,128)S(1)}, s32[72,128]{1,0:T(8,128)S(1)}, u32[]{:S(2)}, u32[]{:S(2)}) collective-permute-start(s32[72,128]{1,0:T(8,128)S(1)} %get-tuple-element.7.message_ref), channel_id=1, source_target_pairs={{0,4},{1,8},{2,6},{3,10},{4,0},{5,12},{6,2},{7,14},{9,13},{8,1},{1... | collective-permute-start | bytes 110600 | tf_op jit(solution)/shard_map/ppermute | solution.py:258
  13.3 0.0 copy-done
  13.3 1.0 %score_docs.1 = (f32[8,16]{1,0:T(8,128)}, bf16[128,256]{1,0:T(8,128)(2,1)S(1)}, bf16[128,256]{1,0:T(8,128)(2,1)S(1)}) custom-call(f32[128,128]{1,0:T(8,128)S(1)} %get-tuple-element.8.own_ref, s32[72,128]{1,0:T(8,128)S(1)} %get-tuple-element.7.message_ref, f32[16,4096]{1,0:T(8,128)S(1)} %copy-done), custom_call_target="tpu_custom_call" | custom-call | flops 67108864 | bytes 524288 | tf_op jit(solution)/shard_map/score_docs/pallas_call | solution.py:173
  14.4 0.0 collective-permute-done.1.refs_0_
  14.4 0.6 %collective-permute-done.2.refs_1_ = s32[72,128]{1,0:T(8,128)S(1)} collective-permute-done((s32[72,128]{1,0:T(8,128)S(1)}, s32[72,128]{1,0:T(8,128)S(1)}, u32[]{:S(2)}, u32[]{:S(2)}) %collective-permute-start.2) | collective-permute-done | bytes 36896 | tf_op jit(solution)/shard_map/ppermute | solution.py:258
  14.9 1.0 %collective-permute-done.3.refs_2_ = s32[72,128]{1,0:T(8,128)S(1)} collective-permute-done((s32[72,128]{1,0:T(8,128)S(1)}, s32[72,128]{1,0:T(8,128)S(1)}, u32[]{:S(2)}, u32[]{:S(2)}) %collective-permute-start.3) | collective-permute-done | bytes 36896 | tf_op jit(solution)/shard_map/ppermute | solution.py:258
  15.9 0.6 %collective-permute-done.4.refs_3_ = s32[72,128]{1,0:T(8,128)S(1)} collective-permute-done((s32[72,128]{1,0:T(8,128)S(1)}, s32[72,128]{1,0:T(8,128)S(1)}, u32[]{:S(2)}, u32[]{:S(2)}) %collective-permute-start.4) | collective-permute-done | bytes 36896 | tf_op jit(solution)/shard_map/ppermute | solution.py:258
  16.6 1.1 %gram_rows.1 = f32[8,32]{1,0:T(8,128)} custom-call(s32[72,128]{1,0:T(8,128)S(1)} %get-tuple-element.7.message_ref, bf16[128,256]{1,0:T(8,128)(2,1)S(1)} %get-tuple-element.9.grads_ref, bf16[128,256]{1,0:T(8,128)(2,1)S(1)} %get-tuple-element.10.ins_ref, s32[72,128]{1,0:T(8,128)S(1)} %collective-permute-done.1.refs_0_, ...), custom_call_target="tpu_custom_call" | custom-call | tf_op jit(solution)/shard_map/gram_rows/pallas_call | solution.py:235
Async XLA Ops:
  0.6 4.2 %copy-start.1 = (s32[1,128]{1,0:T(1,128)S(1)}, s32[1,128]{1,0:T(1,128)}, u32[]{:S(2)}) copy-start(s32[1,128]{1,0:T(1,128)} %ids_ref.1) | copy-start | bytes 1540
  0.6 12.7 %copy-start = (f32[16,4096]{1,0:T(8,128)S(1)}, f32[16,4096]{1,0:T(8,128)}, u32[]{:S(2)}) copy-start(f32[16,4096]{1,0:T(8,128)} %queries.1) | copy-start | bytes 786436
  3.5 1.3 %collective-permute-start = (f32[128,128]{1,0:T(8,128)S(1)}, f32[128,128]{1,0:T(8,128)S(1)}, u32[]{:S(2)}, u32[]{:S(2)}) collective-permute-start(f32[128,128]{1,0:T(8,128)S(1)} %partial_codes.1.mine_ref), channel_id=1, source_target_pairs={{0,1},{1,0},{2,3},{3,2},{4,5},{5,4},{6,7},{7,6},{8,9},{9,8},{10,11... | collective-permute-start | bytes 196616 | tf_op jit(solution)/shard_map/ppermute | solution.py:249
  5.0 9.4 %collective-permute-start.1 = (s32[72,128]{1,0:T(8,128)S(1)}, s32[72,128]{1,0:T(8,128)S(1)}, u32[]{:S(2)}, u32[]{:S(2)}) collective-permute-start(s32[72,128]{1,0:T(8,128)S(1)} %get-tuple-element.7.message_ref), channel_id=1, source_target_pairs={{0,2},{1,12},{2,0},{3,14},{4,6},{5,8},{6,4},{7,10},{9,11},{8,5},{1... | collective-permute-start | bytes 110600 | tf_op jit(solution)/shard_map/ppermute | solution.py:258
  9.7 5.2 %collective-permute-start.2 = (s32[72,128]{1,0:T(8,128)S(1)}, s32[72,128]{1,0:T(8,128)S(1)}, u32[]{:S(2)}, u32[]{:S(2)}) collective-permute-start(s32[72,128]{1,0:T(8,128)S(1)} %get-tuple-element.7.message_ref), channel_id=1, source_target_pairs={{0,2},{1,10},{2,0},{3,8},{4,6},{5,14},{6,4},{7,12},{9,11},{8,3},{1... | collective-permute-start | bytes 110600 | tf_op jit(solution)/shard_map/ppermute | solution.py:258
  9.9 6.1 %collective-permute-start.3 = (s32[72,128]{1,0:T(8,128)S(1)}, s32[72,128]{1,0:T(8,128)S(1)}, u32[]{:S(2)}, u32[]{:S(2)}) collective-permute-start(s32[72,128]{1,0:T(8,128)S(1)} %get-tuple-element.7.message_ref), channel_id=1, source_target_pairs={{0,6},{1,14},{2,4},{3,12},{4,2},{5,10},{6,0},{7,8},{9,15},{8,7},{1... | collective-permute-start | bytes 110600 | tf_op jit(solution)/shard_map/ppermute | solution.py:258
  12.3 4.3 %collective-permute-start.4 = (s32[72,128]{1,0:T(8,128)S(1)}, s32[72,128]{1,0:T(8,128)S(1)}, u32[]{:S(2)}, u32[]{:S(2)}) collective-permute-start(s32[72,128]{1,0:T(8,128)S(1)} %get-tuple-element.7.message_ref), channel_id=1, source_target_pairs={{0,4},{1,8},{2,6},{3,10},{4,0},{5,12},{6,2},{7,14},{9,13},{8,1},{1... | collective-permute-start | bytes 110600 | tf_op jit(solution)/shard_map/ppermute | solution.py:258

commit v6 on v5

--- a/solution.py
+++ b/solution.py
@@ -21,8 +21,12 @@
 
 
 def chunks_of(depth):
-    size = next(size for size in (2048, 1792, 1024, 512, 256, 128, depth) if depth % size == 0)
-    return [(at, size) for at in range(0, depth, size)]
+    pieces, at = [], 0
+    while at < depth:
+        size = min(1024 if at == 0 and depth > 2048 else 2048, depth - at)
+        pieces.append((at, size))
+        at += size
+    return pieces
 
 
 def halves(values):
@@ -39,7 +43,7 @@
     at_core = lax.axis_index("tensor")
     rank = wx.shape[0]
     copies = []
-    for src, w_src, dst, w_dst, row in ((y_hbm, wy_hbm, y, wy, 0), (x_hbm, wx_hbm, x, wx, rank)):
+    for src, w_src, dst, w_dst, row in ((x_hbm, wx_hbm, x, wx, rank), (y_hbm, wy_hbm, y, wy, 0)):
         depth = dst.shape[1]
         for at, size in chunks_of(depth):
             w_at = pl.multiple_of(at_core * depth + at, 128)
@@ -56,10 +60,11 @@
     for pair, dst, w_dst, row, at, size in copies:
         for copy in pair:
             copy.wait()
-        part = dot(w_dst[:, at : at + size], dst[:, at : at + size], NT)
-        totals[row] = totals[row] + part if row in totals else part
-    out_ref[:rank, :] = totals[0]
-    out_ref[rank:, :] = totals[rank]
+        cut = size // 2 if size % 256 == 0 else size
+        for first in range(at, at + size, cut):
+            part = dot(dst[:, first : first + cut], w_dst[:, first : first + cut], NT)
+            totals[row] = totals[row] + part if row in totals else part
+    out_ref[...] = jnp.concatenate([totals[0], totals[rank]], axis=1).T
 
 
 def partial_codes(inputs, out_grads, proj_in_t, proj_out_t):
@@ -191,55 +196,52 @@
     return [half ^ n for n in order], [1] + [n ^ (n >> 1) for n in range(1, half)]
 
 
-def gram_kernel(message_ref, grads_ref, ins_ref, *refs):
-    blocks, out_ref = refs[:-1], refs[-1]
-    half = len(blocks)
+def gram_kernel(round_, half, message_ref, grads_ref, ins_ref, block_ref, *refs):
+    sum_ref, out_ref = refs if round_ else (None, *refs)
     rank = message_ref.shape[0] - EXTRA
     shard, core = lax.axis_index("dp"), lax.axis_index("tensor")
     own_half = lax.div(shard, half) == core
     onehot = members(message_ref[rank : rank + 1, :], DOCS_DEV).astype(jnp.bfloat16)
-    doubled = jnp.concatenate([onehot, onehot], axis=1)
-    far, near = partners(2 * half)
-    total = None
-    width = min(4, half)
-    for first in range(0, half, width):
-        codes, ids, scales = [], [], []
-        for n in range(first, first + width):
-            block, change = blocks[n][...], near[n]
-            if n == 0:
-                block, change = jnp.where(own_half, message_ref[...], block), 0
-            place = lax.rem(lax.bitwise_xor(shard, jnp.where(own_half, change, far[n])), half)
-            codes.append(block[:rank, :])
-            ids.append(block[rank : rank + 1, :] + place * DOCS_DEV)
-            scales.append((block[rank + 1 : rank + 2, :] + block[rank + 2 : rank + 3, :]).astype(jnp.float32))
-        codes, ids, scales = (jnp.concatenate(part, axis=1) for part in (codes, ids, scales))
-        product = None
-        for units, left in (
-            (lax.shift_right_arithmetic(codes, 16), grads_ref),
-            (lax.shift_right_arithmetic(lax.shift_left(codes, 16), 16), ins_ref),
-        ):
-            high, low = halves(units.astype(jnp.float32))
-            part = dot(left[...], jnp.concatenate([high, low, high, low], axis=0), NN)
-            product = part if product is None else product * part
-        high, low = halves(product)
-        by_doc = dot(doubled, jnp.concatenate([high, low], axis=0), NN)
-        by_doc = by_doc * (jnp.exp2(scales * (1.0 / STEPS)) * (1.0 / (TOP * TOP)))
-        high, low = halves(by_doc)
-        theirs = members(ids, half * DOCS_DEV).astype(jnp.bfloat16)
-        part = dot(jnp.concatenate([high, low], axis=0), theirs, NT)
-        total = part if total is None else total + part
-    out_ref[...] = (total[:DOCS_DEV, :] + total[DOCS_DEV:, :]) * (1.0 / (rank * rank))
+    far, near = (changes[round_] for changes in partners(2 * half))
+    block = block_ref[...]
+    if round_ == 0:
+        block, near = jnp.where(own_half, message_ref[...], block), 0
+    place = lax.rem(lax.bitwise_xor(shard, jnp.where(own_half, near, far)), half)
+    codes = block[:rank, :]
+    grades = block[rank + 1 : rank + 2, :] + block[rank + 2 : rank + 3, :]
+    scales = jnp.exp2(grades.astype(jnp.float32) * (1.0 / STEPS))
+    theirs = members(block[rank : rank + 1, :] + place * DOCS_DEV, half * DOCS_DEV).astype(jnp.bfloat16)
+    product = None
+    for units, left in (
+        (lax.shift_right_arithmetic(codes, 16), grads_ref),
+        (lax.shift_right_arithmetic(lax.shift_left(codes, 16), 16), ins_ref),
+    ):
+        high, low = halves(units.astype(jnp.float32))
+        part = dot(left[...], jnp.concatenate([high, low, high, low], axis=0), NN)
+        product = part if product is None else product * part
+    high, low = halves(product)
+    by_doc = dot(jnp.concatenate([onehot, onehot], axis=1), jnp.concatenate([high, low], axis=0), NN)
+    high, low = halves(by_doc * (scales * (1.0 / (TOP * TOP * rank * rank))))
+    part = dot(jnp.concatenate([high, low], axis=0), theirs, NT)
+    total = part[:DOCS_DEV, :] + part[DOCS_DEV:, :]
+    out_ref[...] = total if sum_ref is None else sum_ref[...] + total
 
 
 def gram_of(message, grads, ins, blocks):
-    return pl.pallas_call(
-        gram_kernel,
-        out_shape=jax.ShapeDtypeStruct((DOCS_DEV, len(blocks) * DOCS_DEV), jnp.float32),
-        in_specs=[VMEM] * (3 + len(blocks)),
-        out_specs=VMEM,
-        compiler_params=SMALL,
-        name="gram_rows",
-    )(message, grads, ins, *blocks)
+    half = len(blocks)
+    total = ()
+    for round_, block in enumerate(blocks):
+        total = (
+            pl.pallas_call(
+                functools.partial(gram_kernel, round_, half),
+                out_shape=jax.ShapeDtypeStruct((DOCS_DEV, half * DOCS_DEV), jnp.float32),
+                in_specs=[VMEM] * (4 + len(total)),
+                out_specs=VMEM,
+                compiler_params=SMALL,
+                name="gram_block",
+            )(message, grads, ins, block, *total),
+        )
+    return total[0]
 
 
 def local(inputs, out_grads, proj_in, proj_out, doc_ids, queries):

time: 17.8 us -> 17.8 us (level)
  waiting for transfers between devices: 3.39 us -> 2.14 us
  Pallas kernels: 5.1 us -> 6.34 us
    ppermute x4, waiting for transfers between devices: 2.2 us -> 0.94 us  [local(): blocks.append(lax.ppermute(message, ('dp', 'tensor'), moves))]
    pallas_call x1 -> x4, Pallas kernels: 1.1 us -> 2.27 us  [gram_of(): pl.pallas_call(functools.partial(gram_kernel, round_, half), out_shape=ja...]
  transfers between devices with their start and end apart: 5 -> 5, of which waited for: 4 -> 4; matrix products, arithmetic and copies ran while one was open for 0% -> 0% of each run, Pallas kernels for 6% -> 13%
where the time goes in v6:
time: 17.8 us; the launch traced here: 17.6 us
  starting transfers between devices  8.48 us (48%)
  Pallas kernels  6.34 us (36%)
  waiting for transfers between devices  2.14 us (12%)
  between operations  0.67 us (4%)
    ppermute x4, starting transfers between devices, local(): blocks.append(lax.ppermute(message, ('dp', 'tensor'), moves))  8.35 us
    pallas_call x1, Pallas kernels, partial_codes(): pl.pallas_call(codes_kernel, out_shape=jax.ShapeDtypeStruct((2 * rank, to...  2.9 us
    pallas_call x4, Pallas kernels, gram_of(): pl.pallas_call(functools.partial(gram_kernel, round_, half), out_shape=ja...  2.27 us
    ppermute x1, waiting for transfers between devices, local(): other = lax.ppermute(mine, 'tensor', [(0, 1), (1, 0)])  1.2 us
    pallas_call x1, Pallas kernels, score_docs(): pl.pallas_call(scores_kernel, out_shape=(jax.ShapeDtypeStruct((DOCS_DEV,...  1.04 us
    ppermute x4, waiting for transfers between devices, local(): blocks.append(lax.ppermute(message, ('dp', 'tensor'), moves))  0.94 us
  transfers between devices with their start and end apart: 5, of which 4 were waited for; matrix products, arithmetic and copies ran while one was open for 0% of the time, Pallas kernels for 13%

profile of v6, /device:TPU:1, one launch (start us, length us, event | category | flops | bytes accessed | tf_op | source)
XLA Modules:
  0.0 17.6 jit_solution(14496373025880432704)
XLA Ops:
  0.6 0.0 copy-start.1
  0.6 0.0 copy-start
  0.7 2.9 %partial_codes.1.mine_ref = f32[128,128]{1,0:T(8,128)S(1)} custom-call(bf16[128,7168]{1,0:T(8,128)(2,1)} %x_hbm.1, bf16[128,2048]{1,0:T(8,128)(2,1)} %y_hbm.1, bf16[64,14336]{1,0:T(8,128)(2,1)} %bitcast.2, bf16[64,4096]{1,0:T(8,128)(2,1)} %bitcast.3), custom_call_target="tpu_custom_call" | custom-call | tf_op jit(solution)/shard_map/partial_codes/pallas_call | solution.py:75
  3.6 0.1 collective-permute-start
  3.7 1.2 %collective-permute-done.other_ref = f32[128,128]{1,0:T(8,128)S(1)} collective-permute-done((f32[128,128]{1,0:T(8,128)S(1)}, f32[128,128]{1,0:T(8,128)S(1)}, u32[]{:S(2)}, u32[]{:S(2)}) %collective-permute-start) | collective-permute-done | bytes 65568 | tf_op jit(solution)/shard_map/ppermute | solution.py:251
  4.9 0.0 copy-done.1
  4.9 0.1 pack_codes.1
  5.0 4.8 %collective-permute-start.4 = (s32[72,128]{1,0:T(8,128)S(1)}, s32[72,128]{1,0:T(8,128)S(1)}, u32[]{:S(2)}, u32[]{:S(2)}) collective-permute-start(s32[72,128]{1,0:T(8,128)S(1)} %get-tuple-element.7.message_ref), channel_id=1, source_target_pairs={{0,2},{1,12},{2,0},{3,14},{4,6},{5,8},{6,4},{7,10},{9,11},{8,5},{1... | collective-permute-start | bytes 110600 | tf_op jit(solution)/shard_map/ppermute | solution.py:260
  9.8 0.1 collective-permute-start.3
  9.9 2.4 %collective-permute-start.2 = (s32[72,128]{1,0:T(8,128)S(1)}, s32[72,128]{1,0:T(8,128)S(1)}, u32[]{:S(2)}, u32[]{:S(2)}) collective-permute-start(s32[72,128]{1,0:T(8,128)S(1)} %get-tuple-element.7.message_ref), channel_id=1, source_target_pairs={{0,6},{1,14},{2,4},{3,12},{4,2},{5,10},{6,0},{7,8},{9,15},{8,7},{1... | collective-permute-start | bytes 110600 | tf_op jit(solution)/shard_map/ppermute | solution.py:260
  12.3 1.0 %collective-permute-start.1 = (s32[72,128]{1,0:T(8,128)S(1)}, s32[72,128]{1,0:T(8,128)S(1)}, u32[]{:S(2)}, u32[]{:S(2)}) collective-permute-start(s32[72,128]{1,0:T(8,128)S(1)} %get-tuple-element.7.message_ref), channel_id=1, source_target_pairs={{0,4},{1,8},{2,6},{3,10},{4,0},{5,12},{6,2},{7,14},{9,13},{8,1},{1... | collective-permute-start | bytes 110600 | tf_op jit(solution)/shard_map/ppermute | solution.py:260
  13.4 0.0 copy-done
  13.4 1.0 %score_docs.1 = (f32[8,16]{1,0:T(8,128)}, bf16[128,256]{1,0:T(8,128)(2,1)S(1)}, bf16[128,256]{1,0:T(8,128)(2,1)S(1)}) custom-call(f32[128,128]{1,0:T(8,128)S(1)} %get-tuple-element.8.own_ref, s32[72,128]{1,0:T(8,128)S(1)} %get-tuple-element.7.message_ref, f32[16,4096]{1,0:T(8,128)S(1)} %copy-done), custom_call_target="tpu_custom_call" | custom-call | flops 67108864 | bytes 524288 | tf_op jit(solution)/shard_map/score_docs/pallas_call | solution.py:178
  14.4 0.0 collective-permute-done.4.block_ref
  14.4 0.4 %gram_block.4.refs_0_ = f32[8,32]{1,0:T(8,128)S(1)} custom-call(s32[72,128]{1,0:T(8,128)S(1)} %get-tuple-element.7.message_ref, bf16[128,256]{1,0:T(8,128)(2,1)S(1)} %get-tuple-element.9.grads_ref, bf16[128,256]{1,0:T(8,128)(2,1)S(1)} %get-tuple-element.10.ins_ref, s32[72,128]{1,0:T(8,128)S(1)} %collective-permute-done.4.block_ref), custom_call_target="tpu_custom_call" | custom-call | tf_op jit(solution)/shard_map/gram_block/pallas_call | solution.py:235
  14.8 0.1 collective-permute-done.3.block_ref
  15.0 0.4 %gram_block.5.refs_0_ = f32[8,32]{1,0:T(8,128)S(1)} custom-call(s32[72,128]{1,0:T(8,128)S(1)} %get-tuple-element.7.message_ref, bf16[128,256]{1,0:T(8,128)(2,1)S(1)} %get-tuple-element.9.grads_ref, bf16[128,256]{1,0:T(8,128)(2,1)S(1)} %get-tuple-element.10.ins_ref, s32[72,128]{1,0:T(8,128)S(1)} %collective-permute-done.3.block_ref, ...), custom_call_target="tpu_custom_call" | custom-call | tf_op jit(solution)/shard_map/gram_block/pallas_call | solution.py:235
  15.4 0.6 %collective-permute-done.2.block_ref = s32[72,128]{1,0:T(8,128)S(1)} collective-permute-done((s32[72,128]{1,0:T(8,128)S(1)}, s32[72,128]{1,0:T(8,128)S(1)}, u32[]{:S(2)}, u32[]{:S(2)}) %collective-permute-start.2) | collective-permute-done | bytes 36896 | tf_op jit(solution)/shard_map/ppermute | solution.py:260
  16.0 0.4 %gram_block.6.refs_0_ = f32[8,32]{1,0:T(8,128)S(1)} custom-call(s32[72,128]{1,0:T(8,128)S(1)} %get-tuple-element.7.message_ref, bf16[128,256]{1,0:T(8,128)(2,1)S(1)} %get-tuple-element.9.grads_ref, bf16[128,256]{1,0:T(8,128)(2,1)S(1)} %get-tuple-element.10.ins_ref, s32[72,128]{1,0:T(8,128)S(1)} %collective-permute-done.2.block_ref, ...), custom_call_target="tpu_custom_call" | custom-call | tf_op jit(solution)/shard_map/gram_block/pallas_call | solution.py:235
  16.4 0.2 %collective-permute-done.1.block_ref = s32[72,128]{1,0:T(8,128)S(1)} collective-permute-done((s32[72,128]{1,0:T(8,128)S(1)}, s32[72,128]{1,0:T(8,128)S(1)}, u32[]{:S(2)}, u32[]{:S(2)}) %collective-permute-start.1) | collective-permute-done | bytes 36896 | tf_op jit(solution)/shard_map/ppermute | solution.py:260
  16.6 1.0 %gram_block.7 = f32[8,32]{1,0:T(8,128)} custom-call(s32[72,128]{1,0:T(8,128)S(1)} %get-tuple-element.7.message_ref, bf16[128,256]{1,0:T(8,128)(2,1)S(1)} %get-tuple-element.9.grads_ref, bf16[128,256]{1,0:T(8,128)(2,1)S(1)} %get-tuple-element.10.ins_ref, s32[72,128]{1,0:T(8,128)S(1)} %collective-permute-done.1.block_ref, f32[8,32]{1,0:T(8,128)S(1)} %gram_block.6.refs_0_), custom_call_target="tpu_custom_call" | custom-call | tf_op jit(solution)/shard_map/gram_block/pallas_call | solution.py:235
Async XLA Ops:
  0.6 4.3 %copy-start.1 = (s32[1,128]{1,0:T(1,128)S(1)}, s32[1,128]{1,0:T(1,128)}, u32[]{:S(2)}) copy-start(s32[1,128]{1,0:T(1,128)} %ids_ref.1) | copy-start | bytes 1540
  0.6 12.7 %copy-start = (f32[16,4096]{1,0:T(8,128)S(1)}, f32[16,4096]{1,0:T(8,128)}, u32[]{:S(2)}) copy-start(f32[16,4096]{1,0:T(8,128)} %queries.1) | copy-start | bytes 786436
  3.6 1.3 %collective-permute-start = (f32[128,128]{1,0:T(8,128)S(1)}, f32[128,128]{1,0:T(8,128)S(1)}, u32[]{:S(2)}, u32[]{:S(2)}) collective-permute-start(f32[128,128]{1,0:T(8,128)S(1)} %partial_codes.1.mine_ref), channel_id=1, source_target_pairs={{0,1},{1,0},{2,3},{3,2},{4,5},{5,4},{6,7},{7,6},{8,9},{9,8},{10,11... | collective-permute-start | bytes 196616 | tf_op jit(solution)/shard_map/ppermute | solution.py:251
  5.0 9.4 %collective-permute-start.4 = (s32[72,128]{1,0:T(8,128)S(1)}, s32[72,128]{1,0:T(8,128)S(1)}, u32[]{:S(2)}, u32[]{:S(2)}) collective-permute-start(s32[72,128]{1,0:T(8,128)S(1)} %get-tuple-element.7.message_ref), channel_id=1, source_target_pairs={{0,2},{1,12},{2,0},{3,14},{4,6},{5,8},{6,4},{7,10},{9,11},{8,5},{1... | collective-permute-start | bytes 110600 | tf_op jit(solution)/shard_map/ppermute | solution.py:260
  9.8 5.2 %collective-permute-start.3 = (s32[72,128]{1,0:T(8,128)S(1)}, s32[72,128]{1,0:T(8,128)S(1)}, u32[]{:S(2)}, u32[]{:S(2)}) collective-permute-start(s32[72,128]{1,0:T(8,128)S(1)} %get-tuple-element.7.message_ref), channel_id=1, source_target_pairs={{0,2},{1,10},{2,0},{3,8},{4,6},{5,14},{6,4},{7,12},{9,11},{8,3},{1... | collective-permute-start | bytes 110600 | tf_op jit(solution)/shard_map/ppermute | solution.py:260
  9.9 6.1 %collective-permute-start.2 = (s32[72,128]{1,0:T(8,128)S(1)}, s32[72,128]{1,0:T(8,128)S(1)}, u32[]{:S(2)}, u32[]{:S(2)}) collective-permute-start(s32[72,128]{1,0:T(8,128)S(1)} %get-tuple-element.7.message_ref), channel_id=1, source_target_pairs={{0,6},{1,14},{2,4},{3,12},{4,2},{5,10},{6,0},{7,8},{9,15},{8,7},{1... | collective-permute-start | bytes 110600 | tf_op jit(solution)/shard_map/ppermute | solution.py:260
  12.3 4.3 %collective-permute-start.1 = (s32[72,128]{1,0:T(8,128)S(1)}, s32[72,128]{1,0:T(8,128)S(1)}, u32[]{:S(2)}, u32[]{:S(2)}) collective-permute-start(s32[72,128]{1,0:T(8,128)S(1)} %get-tuple-element.7.message_ref), channel_id=1, source_target_pairs={{0,4},{1,8},{2,6},{3,10},{4,0},{5,12},{6,2},{7,14},{9,13},{8,1},{1... | collective-permute-start | bytes 110600 | tf_op jit(solution)/shard_map/ppermute | solution.py:260

commit v7 on v6

--- a/solution.py
+++ b/solution.py
@@ -27,6 +27,12 @@
         pieces.append((at, size))
         at += size
     return pieces
+
+
+def sum_of(parts):
+    while len(parts) > 1:
+        parts = [sum(parts[n : n + 2]) for n in range(0, len(parts), 2)]
+    return parts[0]
 
 
 def halves(values):
@@ -60,11 +66,10 @@
     for pair, dst, w_dst, row, at, size in copies:
         for copy in pair:
             copy.wait()
-        cut = size // 2 if size % 256 == 0 else size
-        for first in range(at, at + size, cut):
-            part = dot(dst[:, first : first + cut], w_dst[:, first : first + cut], NT)
-            totals[row] = totals[row] + part if row in totals else part
-    out_ref[...] = jnp.concatenate([totals[0], totals[rank]], axis=1).T
+        for first in range(at, at + size, 256):
+            here = slice(first, min(first + 256, at + size))
+            totals.setdefault(row, []).append(dot(dst[:, here], w_dst[:, here], NT))
+    out_ref[...] = jnp.concatenate([sum_of(totals[0]), sum_of(totals[rank])], axis=1).T
 
 
 def partial_codes(inputs, out_grads, proj_in_t, proj_out_t):
@@ -133,7 +138,7 @@
     )(mine, other, doc_ids)
 
 
-def scores_kernel(own_ref, message_ref, queries, scores_ref, grads_ref, ins_ref):
+def scores_kernel(own_ref, message_ref, queries, _, scores_ref, grads_ref, ins_ref):
     rows, tokens = own_ref.shape
     rank = rows // 2
     grads = own_ref[:rank, :]
@@ -171,7 +176,7 @@
     scores_ref[...] = jnp.concatenate(columns, axis=1) * (1.0 / rank)
 
 
-def score_docs(own, message, queries):
+def score_docs(own, message, queries, after):
     rows, tokens = own.shape
     rank = rows // 2
     operand = jax.ShapeDtypeStruct((tokens, 4 * rank), jnp.bfloat16)
@@ -182,18 +187,28 @@
             operand,
             operand,
         ),
-        in_specs=[VMEM] * 3,
+        in_specs=[VMEM] * 4,
         out_specs=(VMEM, VMEM, VMEM),
         compiler_params=SMALL,
         cost_estimate=pl.CostEstimate(flops=1 << 26, bytes_accessed=1 << 19, transcendentals=0),
         name="score_docs",
-    )(own, message, queries)
-
-
-def partners(shards):
+    )(own, message, queries, after)
+
+
+def plan(shards):
     half = shards // 2
-    order = [*range(half // 2, 0, -1), *range(half - 1, half // 2, -1), 0]
-    return [half ^ n for n in order], [1] + [n ^ (n >> 1) for n in range(1, half)]
+    if half == 4:
+        return [(-1, 4, 2), (-1, 7, 1), (0, 2, 2), (0, 1, 1)]
+    direct = [(-1, half + n, n) for n in range(0, half, 2)]
+    return direct + [(n, 1, 1) for n in range(half // 2)]
+
+
+def origins(shards):
+    found = []
+    for what, other, own in plan(shards):
+        before = found[what] if what >= 0 else (0, 0)
+        found.append((before[0] ^ other, before[1] ^ own))
+    return found
 
 
 def gram_kernel(round_, half, message_ref, grads_ref, ins_ref, block_ref, *refs):
@@ -202,10 +217,8 @@
     shard, core = lax.axis_index("dp"), lax.axis_index("tensor")
     own_half = lax.div(shard, half) == core
     onehot = members(message_ref[rank : rank + 1, :], DOCS_DEV).astype(jnp.bfloat16)
-    far, near = (changes[round_] for changes in partners(2 * half))
+    far, near = origins(2 * half)[round_]
     block = block_ref[...]
-    if round_ == 0:
-        block, near = jnp.where(own_half, message_ref[...], block), 0
     place = lax.rem(lax.bitwise_xor(shard, jnp.where(own_half, near, far)), half)
     codes = block[:rank, :]
     grades = block[rank + 1 : rank + 2, :] + block[rank + 2 : rank + 3, :]
@@ -251,14 +264,14 @@
     other = lax.ppermute(mine, "tensor", [(0, 1), (1, 0)])
     own, message = pack(mine, other, doc_ids)
     blocks = []
-    for far, near in zip(*partners(shards)):
+    for what, far, near in plan(shards):
         moves = []
         for s in range(shards):
-            core = s // half
-            moves.append((2 * s + core, 2 * (s ^ near) + core))
-            moves.append((2 * s + 1 - core, 2 * (s ^ far) + core))
-        blocks.append(lax.ppermute(message, ("dp", "tensor"), moves))
-    scores, grads, ins = score_docs(own, message, queries)
+            for core in range(2):
+                to = s ^ (near if core == s // half else far)
+                moves.append((2 * s + core, 2 * to + (core if s // half == to // half else 1 - core)))
+        blocks.append(lax.ppermute(blocks[what] if what >= 0 else message, ("dp", "tensor"), moves))
+    scores, grads, ins = score_docs(own, message, queries, blocks[0])
     return gram_of(message, grads, ins, blocks), scores
 
 

time: 17.8 us -> 17.3 us (0.972)
  the two profiles are of different devices: /device:TPU:1 before, /device:TPU:0 now
where the time goes in v7:
time: 17.3 us; the launch traced here: 17.2 us
  starting transfers between devices  8.5 us (49%)
  Pallas kernels  6.33 us (37%)
  waiting for transfers between devices  1.64 us (9%)
  between operations  0.67 us (4%)
    ppermute x4, starting transfers between devices, local(): lax.ppermute(blocks[what] if what >= 0 else message, ('dp', 'tensor'), mo...  7.99 us
    pallas_call x1, Pallas kernels, partial_codes(): pl.pallas_call(codes_kernel, out_shape=jax.ShapeDtypeStruct((2 * rank, to...  2.87 us
    pallas_call x4, Pallas kernels, gram_of(): pl.pallas_call(functools.partial(gram_kernel, round_, half), out_shape=ja...  2.29 us
    pallas_call x1, Pallas kernels, score_docs(): pl.pallas_call(scores_kernel, out_shape=(jax.ShapeDtypeStruct((DOCS_DEV,...  1.04 us
    ppermute x1, waiting for transfers between devices, local(): other = lax.ppermute(mine, 'tensor', [(0, 1), (1, 0)])  0.9 us
    ppermute x4, waiting for transfers between devices, local(): lax.ppermute(blocks[what] if what >= 0 else message, ('dp', 'tensor'), mo...  0.74 us
    ppermute x1, starting transfers between devices, local(): other = lax.ppermute(mine, 'tensor', [(0, 1), (1, 0)])  0.52 us
  transfers between devices with their start and end apart: 5, of which 3 were waited for; matrix products, arithmetic and copies ran while one was open for 0% of the time, Pallas kernels for 13%

profile of v7, /device:TPU:0, one launch (start us, length us, event | category | flops | bytes accessed | tf_op | source)
XLA Modules:
  0.0 17.2 jit_solution(347243400836337268)
XLA Ops:
  0.6 0.0 copy-start.1
  0.6 0.0 copy-start
  0.7 2.9 %partial_codes.1.mine_ref = f32[128,128]{1,0:T(8,128)S(1)} custom-call(bf16[128,7168]{1,0:T(8,128)(2,1)} %x_hbm.1, bf16[128,2048]{1,0:T(8,128)(2,1)} %y_hbm.1, bf16[64,14336]{1,0:T(8,128)(2,1)} %bitcast.2, bf16[64,4096]{1,0:T(8,128)(2,1)} %bitcast.3), custom_call_target="tpu_custom_call" | custom-call | tf_op jit(solution)/shard_map/partial_codes/pallas_call | solution.py:80
  3.5 0.5 %collective-permute-start = (f32[128,128]{1,0:T(8,128)S(1)}, f32[128,128]{1,0:T(8,128)S(1)}, u32[]{:S(2)}, u32[]{:S(2)}) collective-permute-start(f32[128,128]{1,0:T(8,128)S(1)} %partial_codes.1.mine_ref), channel_id=1, source_target_pairs={{0,1},{1,0},{2,3},{3,2},{4,5},{5,4},{6,7},{7,6},{8,9},{9,8},{10,11... | collective-permute-start | bytes 196616 | tf_op jit(solution)/shard_map/ppermute | solution.py:264
  4.0 0.9 %collective-permute-done.other_ref = f32[128,128]{1,0:T(8,128)S(1)} collective-permute-done((f32[128,128]{1,0:T(8,128)S(1)}, f32[128,128]{1,0:T(8,128)S(1)}, u32[]{:S(2)}, u32[]{:S(2)}) %collective-permute-start) | collective-permute-done | bytes 65568 | tf_op jit(solution)/shard_map/ppermute | solution.py:264
  5.0 0.0 copy-done.1
  5.0 0.1 pack_codes.1
  5.1 3.0 %collective-permute-start.1 = (s32[72,128]{1,0:T(8,128)S(1)}, s32[72,128]{1,0:T(8,128)S(1)}, u32[]{:S(2)}, u32[]{:S(2)}) collective-permute-start(s32[72,128]{1,0:T(8,128)S(1)} %get-tuple-element.7.message_ref), channel_id=1, source_target_pairs={{0,4},{1,8},{2,6},{3,10},{4,0},{5,12},{6,2},{7,14},{8,1},{9,13},{1... | collective-permute-start | bytes 110600 | tf_op jit(solution)/shard_map/ppermute | solution.py:273
  8.1 1.5 %collective-permute-start.4 = (s32[72,128]{1,0:T(8,128)S(1)}, s32[72,128]{1,0:T(8,128)S(1)}, u32[]{:S(2)}, u32[]{:S(2)}) collective-permute-start(s32[72,128]{1,0:T(8,128)S(1)} %get-tuple-element.7.message_ref), channel_id=1, source_target_pairs={{0,2},{1,14},{2,0},{3,12},{4,6},{5,10},{6,4},{7,8},{8,7},{9,11},{1... | collective-permute-start | bytes 110600 | tf_op jit(solution)/shard_map/ppermute | solution.py:273
  9.6 0.5 %collective-permute-done.1._.block_ref = s32[72,128]{1,0:T(8,128)S(1)} collective-permute-done((s32[72,128]{1,0:T(8,128)S(1)}, s32[72,128]{1,0:T(8,128)S(1)}, u32[]{:S(2)}, u32[]{:S(2)}) %collective-permute-start.1) | collective-permute-done | bytes 36896 | tf_op jit(solution)/shard_map/ppermute | solution.py:273
  10.0 2.0 %collective-permute-start.3 = (s32[72,128]{1,0:T(8,128)S(1)}, s32[72,128]{1,0:T(8,128)S(1)}, u32[]{:S(2)}, u32[]{:S(2)}) collective-permute-start(s32[72,128]{1,0:T(8,128)S(1)} %collective-permute-done.1._.block_ref), channel_id=1, source_target_pairs={{0,4},{1,5},{2,6},{3,7},{4,0},{5,1},{6,2},{7,3},{8,12},{9,13},{10,... | collective-permute-start | bytes 110600 | tf_op jit(solution)/shard_map/ppermute | solution.py:273
  12.1 1.5 %collective-permute-start.2 = (s32[72,128]{1,0:T(8,128)S(1)}, s32[72,128]{1,0:T(8,128)S(1)}, u32[]{:S(2)}, u32[]{:S(2)}) collective-permute-start(s32[72,128]{1,0:T(8,128)S(1)} %collective-permute-done.1._.block_ref), channel_id=1, source_target_pairs={{0,2},{1,3},{2,0},{3,1},{4,6},{5,7},{6,4},{7,5},{8,10},{9,11},{10,... | collective-permute-start | bytes 110600 | tf_op jit(solution)/shard_map/ppermute | solution.py:273
  13.5 0.0 copy-done
  13.5 1.0 %score_docs.1 = (f32[8,16]{1,0:T(8,128)}, bf16[128,256]{1,0:T(8,128)(2,1)S(1)}, bf16[128,256]{1,0:T(8,128)(2,1)S(1)}) custom-call(f32[128,128]{1,0:T(8,128)S(1)} %get-tuple-element.8.own_ref, s32[72,128]{1,0:T(8,128)S(1)} %get-tuple-element.7.message_ref, f32[16,4096]{1,0:T(8,128)S(1)} %copy-done, s32[72,128]{1,0:T(8,128)S(1)} %collective-permute-done.1._.block_ref), custom_call_target="tpu_custom_call" | custom-call | flops 67108864 | bytes 524288 | tf_op jit(solution)/shard_map/score_docs/pallas_call | solution.py:183
  14.6 0.4 %gram_block.4.refs_0_ = f32[8,32]{1,0:T(8,128)S(1)} custom-call(s32[72,128]{1,0:T(8,128)S(1)} %get-tuple-element.7.message_ref, bf16[128,256]{1,0:T(8,128)(2,1)S(1)} %get-tuple-element.9.grads_ref, bf16[128,256]{1,0:T(8,128)(2,1)S(1)} %get-tuple-element.10.ins_ref, s32[72,128]{1,0:T(8,128)S(1)} %collective-permute-done.1._.block_ref), custom_call_target="tpu_custom_call" | custom-call | tf_op jit(solution)/shard_map/gram_block/pallas_call | solution.py:248
  15.0 0.0 collective-permute-done.4.block_ref
  15.0 0.4 %gram_block.5.refs_0_ = f32[8,32]{1,0:T(8,128)S(1)} custom-call(s32[72,128]{1,0:T(8,128)S(1)} %get-tuple-element.7.message_ref, bf16[128,256]{1,0:T(8,128)(2,1)S(1)} %get-tuple-element.9.grads_ref, bf16[128,256]{1,0:T(8,128)(2,1)S(1)} %get-tuple-element.10.ins_ref, s32[72,128]{1,0:T(8,128)S(1)} %collective-permute-done.4.block_ref, ...), custom_call_target="tpu_custom_call" | custom-call | tf_op jit(solution)/shard_map/gram_block/pallas_call | solution.py:248
  15.4 0.0 collective-permute-done.3.block_ref
  15.4 0.4 %gram_block.6.refs_0_ = f32[8,32]{1,0:T(8,128)S(1)} custom-call(s32[72,128]{1,0:T(8,128)S(1)} %get-tuple-element.7.message_ref, bf16[128,256]{1,0:T(8,128)(2,1)S(1)} %get-tuple-element.9.grads_ref, bf16[128,256]{1,0:T(8,128)(2,1)S(1)} %get-tuple-element.10.ins_ref, s32[72,128]{1,0:T(8,128)S(1)} %collective-permute-done.3.block_ref, ...), custom_call_target="tpu_custom_call" | custom-call | tf_op jit(solution)/shard_map/gram_block/pallas_call | solution.py:248
  15.9 0.3 %collective-permute-done.2.block_ref = s32[72,128]{1,0:T(8,128)S(1)} collective-permute-done((s32[72,128]{1,0:T(8,128)S(1)}, s32[72,128]{1,0:T(8,128)S(1)}, u32[]{:S(2)}, u32[]{:S(2)}) %collective-permute-start.2) | collective-permute-done | bytes 36896 | tf_op jit(solution)/shard_map/ppermute | solution.py:273
  16.1 1.0 %gram_block.7 = f32[8,32]{1,0:T(8,128)} custom-call(s32[72,128]{1,0:T(8,128)S(1)} %get-tuple-element.7.message_ref, bf16[128,256]{1,0:T(8,128)(2,1)S(1)} %get-tuple-element.9.grads_ref, bf16[128,256]{1,0:T(8,128)(2,1)S(1)} %get-tuple-element.10.ins_ref, s32[72,128]{1,0:T(8,128)S(1)} %collective-permute-done.2.block_ref, f32[8,32]{1,0:T(8,128)S(1)} %gram_block.6.refs_0_), custom_call_target="tpu_custom_call" | custom-call | tf_op jit(solution)/shard_map/gram_block/pallas_call | solution.py:248
Async XLA Ops:
  0.6 4.3 %copy-start.1 = (s32[1,128]{1,0:T(1,128)S(1)}, s32[1,128]{1,0:T(1,128)}, u32[]{:S(2)}) copy-start(s32[1,128]{1,0:T(1,128)} %ids_ref.1) | copy-start | bytes 1540
  0.6 12.9 %copy-start = (f32[16,4096]{1,0:T(8,128)S(1)}, f32[16,4096]{1,0:T(8,128)}, u32[]{:S(2)}) copy-start(f32[16,4096]{1,0:T(8,128)} %queries.1) | copy-start | bytes 786436
  3.5 1.4 %collective-permute-start = (f32[128,128]{1,0:T(8,128)S(1)}, f32[128,128]{1,0:T(8,128)S(1)}, u32[]{:S(2)}, u32[]{:S(2)}) collective-permute-start(f32[128,128]{1,0:T(8,128)S(1)} %partial_codes.1.mine_ref), channel_id=1, source_target_pairs={{0,1},{1,0},{2,3},{3,2},{4,5},{5,4},{6,7},{7,6},{8,9},{9,8},{10,11... | collective-permute-start | bytes 196616 | tf_op jit(solution)/shard_map/ppermute | solution.py:264
  5.1 4.9 %collective-permute-start.1 = (s32[72,128]{1,0:T(8,128)S(1)}, s32[72,128]{1,0:T(8,128)S(1)}, u32[]{:S(2)}, u32[]{:S(2)}) collective-permute-start(s32[72,128]{1,0:T(8,128)S(1)} %get-tuple-element.7.message_ref), channel_id=1, source_target_pairs={{0,4},{1,8},{2,6},{3,10},{4,0},{5,12},{6,2},{7,14},{8,1},{9,13},{1... | collective-permute-start | bytes 110600 | tf_op jit(solution)/shard_map/ppermute | solution.py:273
  8.1 6.9 %collective-permute-start.4 = (s32[72,128]{1,0:T(8,128)S(1)}, s32[72,128]{1,0:T(8,128)S(1)}, u32[]{:S(2)}, u32[]{:S(2)}) collective-permute-start(s32[72,128]{1,0:T(8,128)S(1)} %get-tuple-element.7.message_ref), channel_id=1, source_target_pairs={{0,2},{1,14},{2,0},{3,12},{4,6},{5,10},{6,4},{7,8},{8,7},{9,11},{1... | collective-permute-start | bytes 110600 | tf_op jit(solution)/shard_map/ppermute | solution.py:273
  10.0 5.4 %collective-permute-start.3 = (s32[72,128]{1,0:T(8,128)S(1)}, s32[72,128]{1,0:T(8,128)S(1)}, u32[]{:S(2)}, u32[]{:S(2)}) collective-permute-start(s32[72,128]{1,0:T(8,128)S(1)} %collective-permute-done.1._.block_ref), channel_id=1, source_target_pairs={{0,4},{1,5},{2,6},{3,7},{4,0},{5,1},{6,2},{7,3},{8,12},{9,13},{10,... | collective-permute-start | bytes 110600 | tf_op jit(solution)/shard_map/ppermute | solution.py:273
  12.1 4.1 %collective-permute-start.2 = (s32[72,128]{1,0:T(8,128)S(1)}, s32[72,128]{1,0:T(8,128)S(1)}, u32[]{:S(2)}, u32[]{:S(2)}) collective-permute-start(s32[72,128]{1,0:T(8,128)S(1)} %collective-permute-done.1._.block_ref), channel_id=1, source_target_pairs={{0,2},{1,3},{2,0},{3,1},{4,6},{5,7},{6,4},{7,5},{8,10},{9,11},{10,... | collective-permute-start | bytes 110600 | tf_op jit(solution)/shard_map/ppermute | solution.py:273

commit v8 on v5

--- a/solution.py
+++ b/solution.py
@@ -20,9 +20,28 @@
 dot = functools.partial(lax.dot_general, preferred_element_type=jnp.float32)
 
 
-def chunks_of(depth):
-    size = next(size for size in (2048, 1792, 1024, 512, 256, 128, depth) if depth % size == 0)
-    return [(at, size) for at in range(0, depth, size)]
+def pieces_of(depth):
+    pieces, at = [], 0
+    while at < depth:
+        size = min(2048 if at else 1024, depth - at)
+        pieces.append((at, size))
+        at += size
+    return pieces
+
+
+def last_pieces_of(depth):
+    pieces, at = [], 0
+    while at < depth:
+        size = min(max((depth - at) // 1024 * 512, 512), depth - at)
+        pieces.append((at, size))
+        at += size
+    return pieces
+
+
+def sum_of(parts):
+    while len(parts) > 1:
+        parts = [sum(parts[n : n + 2]) for n in range(0, len(parts), 2)]
+    return parts[0]
 
 
 def halves(values):
@@ -38,35 +57,44 @@
 def codes_kernel(x_hbm, y_hbm, wx_hbm, wy_hbm, out_ref, x, y, wx, wy, sems):
     at_core = lax.axis_index("tensor")
     rank = wx.shape[0]
-    copies = []
-    for src, w_src, dst, w_dst, row in ((y_hbm, wy_hbm, y, wy, 0), (x_hbm, wx_hbm, x, wx, rank)):
-        depth = dst.shape[1]
-        for at, size in chunks_of(depth):
-            w_at = pl.multiple_of(at_core * depth + at, 128)
-            here = pl.ds(at, size)
-            sem = 2 * len(copies)
-            pair = (
-                pltpu.make_async_copy(w_src.at[:, pl.ds(w_at, size)], w_dst.at[:, here], sems.at[sem]),
-                pltpu.make_async_copy(src.at[:, here], dst.at[:, here], sems.at[sem + 1]),
-            )
-            for copy in pair:
-                copy.start()
-            copies.append((pair, dst, w_dst, row, at, size))
+    sent = []
+
+    def fetch(src, dst):
+        sent.append(pltpu.make_async_copy(src, dst, sems.at[len(sent)]))
+        sent[-1].start()
+        return sent[-1]
+
+    def fetch_weights(src, dst, at, size):
+        there = pl.multiple_of(at_core * dst.shape[1] + at, 128)
+        return fetch(src.at[:, pl.ds(there, size)], dst.at[:, pl.ds(at, size)])
+
+    jobs = []
+    for src, w_src, dst, w_dst, row, pieces in (
+        (x_hbm, wx_hbm, x, wx, rank, pieces_of(x.shape[1])),
+        (y_hbm, wy_hbm, y, wy, 0, last_pieces_of(y.shape[1])),
+    ):
+        for n, (at, size) in enumerate(pieces):
+            needed = []
+            if n == 0 or (n == 1 and row):
+                upto = dst.shape[1] if n or not row else size
+                needed.append(fetch_weights(w_src, w_dst, at, upto - at))
+            needed.append(fetch(src.at[:, pl.ds(at, size)], dst.at[:, pl.ds(at, size)]))
+            jobs.append((needed, dst, w_dst, row, at, size))
     totals = {}
-    for pair, dst, w_dst, row, at, size in copies:
-        for copy in pair:
+    for needed, dst, w_dst, row, at, size in jobs:
+        for copy in needed:
             copy.wait()
-        part = dot(w_dst[:, at : at + size], dst[:, at : at + size], NT)
-        totals[row] = totals[row] + part if row in totals else part
-    out_ref[:rank, :] = totals[0]
-    out_ref[rank:, :] = totals[rank]
+        for first in range(at, at + size, 512):
+            here = slice(first, min(first + 512, at + size))
+            totals.setdefault(row, []).append(dot(dst[:, here], w_dst[:, here], NT))
+    out_ref[...] = jnp.concatenate([sum_of(totals[0]), sum_of(totals[rank])], axis=1).T
 
 
 def partial_codes(inputs, out_grads, proj_in_t, proj_out_t):
     tokens, depth_in = inputs.shape
     depth_out = out_grads.shape[1]
     rank = proj_in_t.shape[0]
-    jobs = len(chunks_of(depth_in)) + len(chunks_of(depth_out))
+    copies = len(pieces_of(depth_in)) + len(last_pieces_of(depth_out)) + 3
     return pl.pallas_call(
         codes_kernel,
         out_shape=jax.ShapeDtypeStruct((2 * rank, tokens), jnp.float32),
@@ -77,7 +105,7 @@
             pltpu.VMEM((tokens, depth_out), out_grads.dtype),
             pltpu.VMEM((rank, depth_in), proj_in_t.dtype),
             pltpu.VMEM((rank, depth_out), proj_out_t.dtype),
-            pltpu.SemaphoreType.DMA((2 * jobs,)),
+            pltpu.SemaphoreType.DMA((copies,)),
         ],
         compiler_params=pltpu.CompilerParams(vmem_limit_bytes=56_000_000),
         name="partial_codes",
@@ -185,33 +213,43 @@
     )(own, message, queries)
 
 
-def partners(shards):
+def plan(shards):
     half = shards // 2
-    order = [*range(half // 2, 0, -1), *range(half - 1, half // 2, -1), 0]
-    return [half ^ n for n in order], [1] + [n ^ (n >> 1) for n in range(1, half)]
-
-
-def gram_kernel(message_ref, grads_ref, ins_ref, *refs):
-    blocks, out_ref = refs[:-1], refs[-1]
+    if half == 4:
+        return [(-1, 4, 1), (-1, 7, 2), (0, 2, 2), (0, 1, 1)]
+    direct = [(-1, half + n, n) for n in range(0, half, 2)]
+    return direct + [(n, 1, 1) for n in range(half // 2)]
+
+
+def origins(shards):
+    found = []
+    for what, other, own in plan(shards):
+        before = found[what] if what >= 0 else (0, 0)
+        found.append((before[0] ^ other, before[1] ^ own))
+    return found
+
+
+def gram_kernel(message_ref, grads_ref, ins_ref, scores_ref, *refs):
+    blocks, (out_ref, scores_out_ref) = refs[:-2], refs[-2:]
+    scores_out_ref[...] = scores_ref[...]
     half = len(blocks)
     rank = message_ref.shape[0] - EXTRA
     shard, core = lax.axis_index("dp"), lax.axis_index("tensor")
     own_half = lax.div(shard, half) == core
     onehot = members(message_ref[rank : rank + 1, :], DOCS_DEV).astype(jnp.bfloat16)
     doubled = jnp.concatenate([onehot, onehot], axis=1)
-    far, near = partners(2 * half)
+    found = origins(2 * half)
     total = None
     width = min(4, half)
     for first in range(0, half, width):
         codes, ids, scales = [], [], []
         for n in range(first, first + width):
-            block, change = blocks[n][...], near[n]
-            if n == 0:
-                block, change = jnp.where(own_half, message_ref[...], block), 0
-            place = lax.rem(lax.bitwise_xor(shard, jnp.where(own_half, change, far[n])), half)
+            block, (far, near) = blocks[n][...], found[n]
+            place = lax.rem(lax.bitwise_xor(shard, jnp.where(own_half, near, far)), half)
             codes.append(block[:rank, :])
             ids.append(block[rank : rank + 1, :] + place * DOCS_DEV)
-            scales.append((block[rank + 1 : rank + 2, :] + block[rank + 2 : rank + 3, :]).astype(jnp.float32))
+            grades = block[rank + 1 : rank + 2, :] + block[rank + 2 : rank + 3, :]
+            scales.append(grades.astype(jnp.float32))
         codes, ids, scales = (jnp.concatenate(part, axis=1) for part in (codes, ids, scales))
         product = None
         for units, left in (
@@ -223,23 +261,27 @@
             product = part if product is None else product * part
         high, low = halves(product)
         by_doc = dot(doubled, jnp.concatenate([high, low], axis=0), NN)
-        by_doc = by_doc * (jnp.exp2(scales * (1.0 / STEPS)) * (1.0 / (TOP * TOP)))
+        by_doc = by_doc * (jnp.exp2(scales * (1.0 / STEPS)) * (1.0 / (TOP * TOP * rank * rank)))
         high, low = halves(by_doc)
         theirs = members(ids, half * DOCS_DEV).astype(jnp.bfloat16)
         part = dot(jnp.concatenate([high, low], axis=0), theirs, NT)
         total = part if total is None else total + part
-    out_ref[...] = (total[:DOCS_DEV, :] + total[DOCS_DEV:, :]) * (1.0 / (rank * rank))
-
-
-def gram_of(message, grads, ins, blocks):
+    out_ref[...] = total[:DOCS_DEV, :] + total[DOCS_DEV:, :]
+
+
+def gram_of(message, grads, ins, scores, blocks):
+    half = len(blocks)
     return pl.pallas_call(
         gram_kernel,
-        out_shape=jax.ShapeDtypeStruct((DOCS_DEV, len(blocks) * DOCS_DEV), jnp.float32),
-        in_specs=[VMEM] * (3 + len(blocks)),
-        out_specs=VMEM,
+        out_shape=(
+            jax.ShapeDtypeStruct((DOCS_DEV, half * DOCS_DEV), jnp.float32),
+            jax.ShapeDtypeStruct(scores.shape, scores.dtype),
+        ),
+        in_specs=[VMEM] * (4 + half),
+        out_specs=(VMEM, VMEM),
         compiler_params=SMALL,
         name="gram_rows",
-    )(message, grads, ins, *blocks)
+    )(message, grads, ins, scores, *blocks)
 
 
 def local(inputs, out_grads, proj_in, proj_out, doc_ids, queries):
@@ -249,15 +291,15 @@
     other = lax.ppermute(mine, "tensor", [(0, 1), (1, 0)])
     own, message = pack(mine, other, doc_ids)
     blocks = []
-    for far, near in zip(*partners(shards)):
+    for what, far, near in plan(shards):
         moves = []
         for s in range(shards):
-            core = s // half
-            moves.append((2 * s + core, 2 * (s ^ near) + core))
-            moves.append((2 * s + 1 - core, 2 * (s ^ far) + core))
-        blocks.append(lax.ppermute(message, ("dp", "tensor"), moves))
+            for core in range(2):
+                to = s ^ (near if core == s // half else far)
+                moves.append((2 * s + core, 2 * to + (core if s // half == to // half else 1 - core)))
+        blocks.append(lax.ppermute(blocks[what] if what >= 0 else message, ("dp", "tensor"), moves))
     scores, grads, ins = score_docs(own, message, queries)
-    return gram_of(message, grads, ins, blocks), scores
+    return gram_of(message, grads, ins, scores, blocks)
 
 
 def solution(mesh):

time: 17.8 us -> 17.6 us (0.989)
  the two profiles are of different devices: /device:TPU:1 before, /device:TPU:0 now
where the time goes in v8:
time: 17.6 us; the launch traced here: 17.4 us
  starting transfers between devices  8.62 us (49%)
  Pallas kernels  4.77 us (27%)
  waiting for transfers between devices  3.35 us (19%)
  between operations  0.68 us (4%)
    ppermute x4, starting transfers between devices, local(): lax.ppermute(blocks[what] if what >= 0 else message, ('dp', 'tensor'), mo...  8.1 us
    pallas_call x1, Pallas kernels, partial_codes(): pl.pallas_call(codes_kernel, out_shape=jax.ShapeDtypeStruct((2 * rank, to...  3.06 us
    ppermute x4, waiting for transfers between devices, local(): lax.ppermute(blocks[what] if what >= 0 else message, ('dp', 'tensor'), mo...  2.44 us
    pallas_call x1, Pallas kernels, gram_of(): pl.pallas_call(gram_kernel, out_shape=(jax.ShapeDtypeStruct((DOCS_DEV, ha...  1.1 us
    ppermute x1, waiting for transfers between devices, local(): other = lax.ppermute(mine, 'tensor', [(0, 1), (1, 0)])  0.9 us
    ppermute x1, starting transfers between devices, local(): other = lax.ppermute(mine, 'tensor', [(0, 1), (1, 0)])  0.52 us
    pallas_call x1, Pallas kernels, score_docs(): pl.pallas_call(scores_kernel, out_shape=(jax.ShapeDtypeStruct((DOCS_DEV,...  0.47 us
  transfers between devices with their start and end apart: 5, of which 4 were waited for; matrix products, arithmetic and copies ran while one was open for 0% of the time, Pallas kernels for 3%

profile of v8, /device:TPU:0, one launch (start us, length us, event | category | flops | bytes accessed | tf_op | source)
XLA Modules:
  0.0 17.4 jit_solution(16019458715591421915)
XLA Ops:
  0.6 0.0 copy-start.1
  0.6 0.0 copy-start
  0.7 3.1 %partial_codes.1.mine_ref = f32[128,128]{1,0:T(8,128)S(1)} custom-call(bf16[128,7168]{1,0:T(8,128)(2,1)} %x_hbm.1, bf16[128,2048]{1,0:T(8,128)(2,1)} %y_hbm.1, bf16[64,14336]{1,0:T(8,128)(2,1)} %bitcast.2, bf16[64,4096]{1,0:T(8,128)(2,1)} %bitcast.3), custom_call_target="tpu_custom_call" | custom-call | tf_op jit(solution)/shard_map/partial_codes/pallas_call | solution.py:98
  3.7 0.5 %collective-permute-start = (f32[128,128]{1,0:T(8,128)S(1)}, f32[128,128]{1,0:T(8,128)S(1)}, u32[]{:S(2)}, u32[]{:S(2)}) collective-permute-start(f32[128,128]{1,0:T(8,128)S(1)} %partial_codes.1.mine_ref), channel_id=1, source_target_pairs={{0,1},{1,0},{2,3},{3,2},{4,5},{5,4},{6,7},{7,6},{8,9},{9,8},{10,11... | collective-permute-start | bytes 196616 | tf_op jit(solution)/shard_map/ppermute | solution.py:291
  4.2 0.9 %collective-permute-done.other_ref = f32[128,128]{1,0:T(8,128)S(1)} collective-permute-done((f32[128,128]{1,0:T(8,128)S(1)}, f32[128,128]{1,0:T(8,128)S(1)}, u32[]{:S(2)}, u32[]{:S(2)}) %collective-permute-start) | collective-permute-done | bytes 65568 | tf_op jit(solution)/shard_map/ppermute | solution.py:291
  5.1 0.0 copy-done.1
  5.1 0.1 pack_codes.1
  5.3 2.9 %collective-permute-start.1 = (s32[72,128]{1,0:T(8,128)S(1)}, s32[72,128]{1,0:T(8,128)S(1)}, u32[]{:S(2)}, u32[]{:S(2)}) collective-permute-start(s32[72,128]{1,0:T(8,128)S(1)} %get-tuple-element.7.message_ref), channel_id=1, source_target_pairs={{0,2},{1,8},{2,0},{3,10},{4,6},{5,12},{6,4},{7,14},{8,1},{9,11},{1... | collective-permute-start | bytes 110600 | tf_op jit(solution)/shard_map/ppermute | solution.py:300
  8.2 1.6 %collective-permute-start.2 = (s32[72,128]{1,0:T(8,128)S(1)}, s32[72,128]{1,0:T(8,128)S(1)}, u32[]{:S(2)}, u32[]{:S(2)}) collective-permute-start(s32[72,128]{1,0:T(8,128)S(1)} %get-tuple-element.7.message_ref), channel_id=1, source_target_pairs={{0,4},{1,14},{2,6},{3,12},{4,0},{5,10},{6,2},{7,8},{8,7},{9,13},{1... | collective-permute-start | bytes 110600 | tf_op jit(solution)/shard_map/ppermute | solution.py:300
  9.8 0.4 %collective-permute-done.1.refs_0_ = s32[72,128]{1,0:T(8,128)S(1)} collective-permute-done((s32[72,128]{1,0:T(8,128)S(1)}, s32[72,128]{1,0:T(8,128)S(1)}, u32[]{:S(2)}, u32[]{:S(2)}) %collective-permute-start.1) | collective-permute-done | bytes 36896 | tf_op jit(solution)/shard_map/ppermute | solution.py:300
  10.1 2.1 %collective-permute-start.3 = (s32[72,128]{1,0:T(8,128)S(1)}, s32[72,128]{1,0:T(8,128)S(1)}, u32[]{:S(2)}, u32[]{:S(2)}) collective-permute-start(s32[72,128]{1,0:T(8,128)S(1)} %collective-permute-done.1.refs_0_), channel_id=1, source_target_pairs={{0,4},{1,5},{2,6},{3,7},{4,0},{5,1},{6,2},{7,3},{8,12},{9,13},{10,... | collective-permute-start | bytes 110600 | tf_op jit(solution)/shard_map/ppermute | solution.py:300
  12.2 1.5 %collective-permute-start.4 = (s32[72,128]{1,0:T(8,128)S(1)}, s32[72,128]{1,0:T(8,128)S(1)}, u32[]{:S(2)}, u32[]{:S(2)}) collective-permute-start(s32[72,128]{1,0:T(8,128)S(1)} %collective-permute-done.1.refs_0_), channel_id=1, source_target_pairs={{0,2},{1,3},{2,0},{3,1},{4,6},{5,7},{6,4},{7,5},{8,10},{9,11},{10,... | collective-permute-start | bytes 110600 | tf_op jit(solution)/shard_map/ppermute | solution.py:300
  13.8 0.0 copy-done
  13.8 0.5 %score_docs.1 = (f32[8,16]{1,0:T(8,128)S(1)}, bf16[128,256]{1,0:T(8,128)(2,1)S(1)}, bf16[128,256]{1,0:T(8,128)(2,1)S(1)}) custom-call(f32[128,128]{1,0:T(8,128)S(1)} %get-tuple-element.8.own_ref, s32[72,128]{1,0:T(8,128)S(1)} %get-tuple-element.7.message_ref, f32[16,4096]{1,0:T(8,128)S(1)} %copy-done), custom_call_target="tpu_custom_call" | custom-call | flops 67108864 | bytes 524288 | tf_op jit(solution)/shard_map/score_docs/pallas_call | solution.py:201
  14.2 0.0 collective-permute-done.2.refs_1_
  14.2 0.1 collective-permute-done.3.refs_2_
  14.3 2.0 %collective-permute-done.4.refs_3_ = s32[72,128]{1,0:T(8,128)S(1)} collective-permute-done((s32[72,128]{1,0:T(8,128)S(1)}, s32[72,128]{1,0:T(8,128)S(1)}, u32[]{:S(2)}, u32[]{:S(2)}) %collective-permute-start.4) | collective-permute-done | bytes 36896 | tf_op jit(solution)/shard_map/ppermute | solution.py:300
  16.3 1.1 %gram_rows.1 = (f32[8,32]{1,0:T(8,128)}, f32[8,16]{1,0:T(8,128)}) custom-call(s32[72,128]{1,0:T(8,128)S(1)} %get-tuple-element.7.message_ref, bf16[128,256]{1,0:T(8,128)(2,1)S(1)} %get-tuple-element.9.grads_ref, bf16[128,256]{1,0:T(8,128)(2,1)S(1)} %get-tuple-element.10.ins_ref, f32[8,16]{1,0:T(8,128)S(1)} %get-tuple-element.11.scores_ref, ...), custom_call_target="tpu_custom_call" | custom-call | tf_op jit(solution)/shard_map/gram_rows/pallas_call | solution.py:274
Async XLA Ops:
  0.6 4.5 %copy-start.1 = (s32[1,128]{1,0:T(1,128)S(1)}, s32[1,128]{1,0:T(1,128)}, u32[]{:S(2)}) copy-start(s32[1,128]{1,0:T(1,128)} %ids_ref.1) | copy-start | bytes 1540
  0.6 13.1 %copy-start = (f32[16,4096]{1,0:T(8,128)S(1)}, f32[16,4096]{1,0:T(8,128)}, u32[]{:S(2)}) copy-start(f32[16,4096]{1,0:T(8,128)} %queries.1) | copy-start | bytes 786436
  3.7 1.4 %collective-permute-start = (f32[128,128]{1,0:T(8,128)S(1)}, f32[128,128]{1,0:T(8,128)S(1)}, u32[]{:S(2)}, u32[]{:S(2)}) collective-permute-start(f32[128,128]{1,0:T(8,128)S(1)} %partial_codes.1.mine_ref), channel_id=1, source_target_pairs={{0,1},{1,0},{2,3},{3,2},{4,5},{5,4},{6,7},{7,6},{8,9},{9,8},{10,11... | collective-permute-start | bytes 196616 | tf_op jit(solution)/shard_map/ppermute | solution.py:291
  5.3 4.8 %collective-permute-start.1 = (s32[72,128]{1,0:T(8,128)S(1)}, s32[72,128]{1,0:T(8,128)S(1)}, u32[]{:S(2)}, u32[]{:S(2)}) collective-permute-start(s32[72,128]{1,0:T(8,128)S(1)} %get-tuple-element.7.message_ref), channel_id=1, source_target_pairs={{0,2},{1,8},{2,0},{3,10},{4,6},{5,12},{6,4},{7,14},{8,1},{9,11},{1... | collective-permute-start | bytes 110600 | tf_op jit(solution)/shard_map/ppermute | solution.py:300
  8.2 6.0 %collective-permute-start.2 = (s32[72,128]{1,0:T(8,128)S(1)}, s32[72,128]{1,0:T(8,128)S(1)}, u32[]{:S(2)}, u32[]{:S(2)}) collective-permute-start(s32[72,128]{1,0:T(8,128)S(1)} %get-tuple-element.7.message_ref), channel_id=1, source_target_pairs={{0,4},{1,14},{2,6},{3,12},{4,0},{5,10},{6,2},{7,8},{8,7},{9,13},{1... | collective-permute-start | bytes 110600 | tf_op jit(solution)/shard_map/ppermute | solution.py:300
  10.1 4.2 %collective-permute-start.3 = (s32[72,128]{1,0:T(8,128)S(1)}, s32[72,128]{1,0:T(8,128)S(1)}, u32[]{:S(2)}, u32[]{:S(2)}) collective-permute-start(s32[72,128]{1,0:T(8,128)S(1)} %collective-permute-done.1.refs_0_), channel_id=1, source_target_pairs={{0,4},{1,5},{2,6},{3,7},{4,0},{5,1},{6,2},{7,3},{8,12},{9,13},{10,... | collective-permute-start | bytes 110600 | tf_op jit(solution)/shard_map/ppermute | solution.py:300
  12.2 4.1 %collective-permute-start.4 = (s32[72,128]{1,0:T(8,128)S(1)}, s32[72,128]{1,0:T(8,128)S(1)}, u32[]{:S(2)}, u32[]{:S(2)}) collective-permute-start(s32[72,128]{1,0:T(8,128)S(1)} %collective-permute-done.1.refs_0_), channel_id=1, source_target_pairs={{0,2},{1,3},{2,0},{3,1},{4,6},{5,7},{6,4},{7,5},{8,10},{9,11},{10,... | collective-permute-start | bytes 110600 | tf_op jit(solution)/shard_map/ppermute | solution.py:300

commit v9 on v8

--- a/solution.py
+++ b/solution.py
@@ -21,21 +21,8 @@
 
 
 def pieces_of(depth):
-    pieces, at = [], 0
-    while at < depth:
-        size = min(2048 if at else 1024, depth - at)
-        pieces.append((at, size))
-        at += size
-    return pieces
-
-
-def last_pieces_of(depth):
-    pieces, at = [], 0
-    while at < depth:
-        size = min(max((depth - at) // 1024 * 512, 512), depth - at)
-        pieces.append((at, size))
-        at += size
-    return pieces
+    size = next(size for size in (2048, 1792, 1024, 512, 256, 128, depth) if depth % size == 0)
+    return [(at, size) for at in range(0, depth, size)]
 
 
 def sum_of(parts):
@@ -57,44 +44,36 @@
 def codes_kernel(x_hbm, y_hbm, wx_hbm, wy_hbm, out_ref, x, y, wx, wy, sems):
     at_core = lax.axis_index("tensor")
     rank = wx.shape[0]
-    sent = []
-
-    def fetch(src, dst):
-        sent.append(pltpu.make_async_copy(src, dst, sems.at[len(sent)]))
-        sent[-1].start()
-        return sent[-1]
-
-    def fetch_weights(src, dst, at, size):
-        there = pl.multiple_of(at_core * dst.shape[1] + at, 128)
-        return fetch(src.at[:, pl.ds(there, size)], dst.at[:, pl.ds(at, size)])
-
     jobs = []
-    for src, w_src, dst, w_dst, row, pieces in (
-        (x_hbm, wx_hbm, x, wx, rank, pieces_of(x.shape[1])),
-        (y_hbm, wy_hbm, y, wy, 0, last_pieces_of(y.shape[1])),
-    ):
-        for n, (at, size) in enumerate(pieces):
-            needed = []
-            if n == 0 or (n == 1 and row):
-                upto = dst.shape[1] if n or not row else size
-                needed.append(fetch_weights(w_src, w_dst, at, upto - at))
-            needed.append(fetch(src.at[:, pl.ds(at, size)], dst.at[:, pl.ds(at, size)]))
-            jobs.append((needed, dst, w_dst, row, at, size))
+    for src, w_src, dst, w_dst, row in ((y_hbm, wy_hbm, y, wy, 0), (x_hbm, wx_hbm, x, wx, rank)):
+        depth = dst.shape[1]
+        for at, size in pieces_of(depth):
+            there = pl.multiple_of(at_core * depth + at, 128)
+            here = pl.ds(at, size)
+            sem = 2 * len(jobs)
+            copies = (
+                pltpu.make_async_copy(w_src.at[:, pl.ds(there, size)], w_dst.at[:, here], sems.at[sem]),
+                pltpu.make_async_copy(src.at[:, here], dst.at[:, here], sems.at[sem + 1]),
+            )
+            for copy in copies:
+                copy.start()
+            jobs.append((copies, dst, w_dst, row, at, size))
     totals = {}
-    for needed, dst, w_dst, row, at, size in jobs:
-        for copy in needed:
+    for copies, dst, w_dst, row, at, size in jobs:
+        for copy in copies:
             copy.wait()
-        for first in range(at, at + size, 512):
-            here = slice(first, min(first + 512, at + size))
-            totals.setdefault(row, []).append(dot(dst[:, here], w_dst[:, here], NT))
-    out_ref[...] = jnp.concatenate([sum_of(totals[0]), sum_of(totals[rank])], axis=1).T
+        for first in range(at, at + size, 256):
+            here = slice(first, min(first + 256, at + size))
+            totals.setdefault(row, []).append(dot(w_dst[:, here], dst[:, here], NT))
+    for row, parts in totals.items():
+        out_ref[row : row + rank, :] = sum_of(parts)
 
 
 def partial_codes(inputs, out_grads, proj_in_t, proj_out_t):
     tokens, depth_in = inputs.shape
     depth_out = out_grads.shape[1]
     rank = proj_in_t.shape[0]
-    copies = len(pieces_of(depth_in)) + len(last_pieces_of(depth_out)) + 3
+    copies = 2 * (len(pieces_of(depth_in)) + len(pieces_of(depth_out)))
     return pl.pallas_call(
         codes_kernel,
         out_shape=jax.ShapeDtypeStruct((2 * rank, tokens), jnp.float32),
@@ -216,7 +195,7 @@
 def plan(shards):
     half = shards // 2
     if half == 4:
-        return [(-1, 4, 1), (-1, 7, 2), (0, 2, 2), (0, 1, 1)]
+        return [(-1, 4, 1), (-1, 7, 2), (0, 2, 2), (0, 1, 0)]
     direct = [(-1, half + n, n) for n in range(0, half, 2)]
     return direct + [(n, 1, 1) for n in range(half // 2)]
 
@@ -245,6 +224,8 @@
         codes, ids, scales = [], [], []
         for n in range(first, first + width):
             block, (far, near) = blocks[n][...], found[n]
+            if near in [own for _, own in found[:n]]:
+                block, near = jnp.where(own_half, message_ref[...], block), 0
             place = lax.rem(lax.bitwise_xor(shard, jnp.where(own_half, near, far)), half)
             codes.append(block[:rank, :])
             ids.append(block[rank : rank + 1, :] + place * DOCS_DEV)

time: 17.6 us -> 18.5 us (1.051)
  the two profiles are of different devices: /device:TPU:0 before, /device:TPU:16 now
where the time goes in v9:
time: 18.5 us; the launch traced here: 18.3 us
  starting transfers between devices  9.04 us (49%)
  Pallas kernels  4.62 us (25%)
  waiting for transfers between devices  3.92 us (21%)
  between operations  0.72 us (4%)
    ppermute x4, starting transfers between devices, local(): lax.ppermute(blocks[what] if what >= 0 else message, ('dp', 'tensor'), mo...  8.97 us
    pallas_call x1, Pallas kernels, partial_codes(): pl.pallas_call(codes_kernel, out_shape=jax.ShapeDtypeStruct((2 * rank, to...  2.93 us
    ppermute x4, waiting for transfers between devices, local(): lax.ppermute(blocks[what] if what >= 0 else message, ('dp', 'tensor'), mo...  2.67 us
    ppermute x1, waiting for transfers between devices, local(): other = lax.ppermute(mine, 'tensor', [(0, 1), (1, 0)])  1.24 us
    pallas_call x1, Pallas kernels, gram_of(): pl.pallas_call(gram_kernel, out_shape=(jax.ShapeDtypeStruct((DOCS_DEV, ha...  1.1 us
    pallas_call x1, Pallas kernels, score_docs(): pl.pallas_call(scores_kernel, out_shape=(jax.ShapeDtypeStruct((DOCS_DEV,...  0.46 us
  transfers between devices with their start and end apart: 5, of which 3 were waited for; matrix products, arithmetic and copies ran while one was open for 0% of the time, Pallas kernels for 3%

profile of v9, /device:TPU:16, one launch (start us, length us, event | category | flops | bytes accessed | tf_op | source)
XLA Modules:
  0.0 18.3 jit_solution(4592165552282095511)
XLA Ops:
  0.6 0.0 copy-start.1
  0.6 0.0 copy-start
  0.7 2.9 %partial_codes.1.mine_ref = f32[128,128]{1,0:T(8,128)S(1)} custom-call(bf16[128,7168]{1,0:T(8,128)(2,1)} %x_hbm.1, bf16[128,2048]{1,0:T(8,128)(2,1)} %y_hbm.1, bf16[64,14336]{1,0:T(8,128)(2,1)} %bitcast.2, bf16[64,4096]{1,0:T(8,128)(2,1)} %bitcast.3), custom_call_target="tpu_custom_call" | custom-call | tf_op jit(solution)/shard_map/partial_codes/pallas_call | solution.py:77
  3.6 0.1 collective-permute-start
  3.7 1.2 %collective-permute-done.other_ref = f32[128,128]{1,0:T(8,128)S(1)} collective-permute-done((f32[128,128]{1,0:T(8,128)S(1)}, f32[128,128]{1,0:T(8,128)S(1)}, u32[]{:S(2)}, u32[]{:S(2)}) %collective-permute-start) | collective-permute-done | bytes 65568 | tf_op jit(solution)/shard_map/ppermute | solution.py:272
  4.9 0.0 copy-done.1
  4.9 0.1 pack_codes.1
  5.1 0.1 collective-permute-start.1
  5.1 3.7 %collective-permute-start.2 = (s32[72,128]{1,0:T(8,128)S(1)}, s32[72,128]{1,0:T(8,128)S(1)}, u32[]{:S(2)}, u32[]{:S(2)}) collective-permute-start(s32[72,128]{1,0:T(8,128)S(1)} %get-tuple-element.7.message_ref), channel_id=1, source_target_pairs={{0,4},{1,14},{2,6},{3,12},{4,0},{5,10},{6,2},{7,8},{8,7},{9,13},{1... | collective-permute-start | bytes 110600 | tf_op jit(solution)/shard_map/ppermute | solution.py:281
  8.8 0.6 %collective-permute-done.1.refs_0_ = s32[72,128]{1,0:T(8,128)S(1)} collective-permute-done((s32[72,128]{1,0:T(8,128)S(1)}, s32[72,128]{1,0:T(8,128)S(1)}, u32[]{:S(2)}, u32[]{:S(2)}) %collective-permute-start.1) | collective-permute-done | bytes 36896 | tf_op jit(solution)/shard_map/ppermute | solution.py:281
  9.4 1.9 %collective-permute-start.3 = (s32[72,128]{1,0:T(8,128)S(1)}, s32[72,128]{1,0:T(8,128)S(1)}, u32[]{:S(2)}, u32[]{:S(2)}) collective-permute-start(s32[72,128]{1,0:T(8,128)S(1)} %collective-permute-done.1.refs_0_), channel_id=1, source_target_pairs={{0,4},{1,5},{2,6},{3,7},{4,0},{5,1},{6,2},{7,3},{8,12},{9,13},{10,... | collective-permute-start | bytes 110600 | tf_op jit(solution)/shard_map/ppermute | solution.py:281
  11.4 3.3 %collective-permute-start.4 = (s32[72,128]{1,0:T(8,128)S(1)}, s32[72,128]{1,0:T(8,128)S(1)}, u32[]{:S(2)}, u32[]{:S(2)}) collective-permute-start(s32[72,128]{1,0:T(8,128)S(1)} %collective-permute-done.1.refs_0_), channel_id=1, source_target_pairs={{0,0},{1,3},{2,2},{3,1},{4,4},{5,7},{6,6},{7,5},{8,10},{9,9},{10,8... | collective-permute-start | bytes 110600 | tf_op jit(solution)/shard_map/ppermute | solution.py:281
  14.7 0.0 copy-done
  14.7 0.5 %score_docs.1 = (f32[8,16]{1,0:T(8,128)S(1)}, bf16[128,256]{1,0:T(8,128)(2,1)S(1)}, bf16[128,256]{1,0:T(8,128)(2,1)S(1)}) custom-call(f32[128,128]{1,0:T(8,128)S(1)} %get-tuple-element.8.own_ref, s32[72,128]{1,0:T(8,128)S(1)} %get-tuple-element.7.message_ref, f32[16,4096]{1,0:T(8,128)S(1)} %copy-done), custom_call_target="tpu_custom_call" | custom-call | flops 67108864 | bytes 524288 | tf_op jit(solution)/shard_map/score_docs/pallas_call | solution.py:180
  15.1 0.0 collective-permute-done.2.refs_1_
  15.1 0.0 collective-permute-done.3.refs_2_
  15.2 2.0 %collective-permute-done.4.refs_3_ = s32[72,128]{1,0:T(8,128)S(1)} collective-permute-done((s32[72,128]{1,0:T(8,128)S(1)}, s32[72,128]{1,0:T(8,128)S(1)}, u32[]{:S(2)}, u32[]{:S(2)}) %collective-permute-start.4) | collective-permute-done | bytes 36896 | tf_op jit(solution)/shard_map/ppermute | solution.py:281
  17.2 1.1 %gram_rows.1 = (f32[8,32]{1,0:T(8,128)}, f32[8,16]{1,0:T(8,128)}) custom-call(s32[72,128]{1,0:T(8,128)S(1)} %get-tuple-element.7.message_ref, bf16[128,256]{1,0:T(8,128)(2,1)S(1)} %get-tuple-element.9.grads_ref, bf16[128,256]{1,0:T(8,128)(2,1)S(1)} %get-tuple-element.10.ins_ref, f32[8,16]{1,0:T(8,128)S(1)} %get-tuple-element.11.scores_ref, ...), custom_call_target="tpu_custom_call" | custom-call | tf_op jit(solution)/shard_map/gram_rows/pallas_call | solution.py:255
Async XLA Ops:
  0.6 4.3 %copy-start.1 = (s32[1,128]{1,0:T(1,128)S(1)}, s32[1,128]{1,0:T(1,128)}, u32[]{:S(2)}) copy-start(s32[1,128]{1,0:T(1,128)} %ids_ref.1) | copy-start | bytes 1540
  0.6 14.0 %copy-start = (f32[16,4096]{1,0:T(8,128)S(1)}, f32[16,4096]{1,0:T(8,128)}, u32[]{:S(2)}) copy-start(f32[16,4096]{1,0:T(8,128)} %queries.1) | copy-start | bytes 786436
  3.6 1.3 %collective-permute-start = (f32[128,128]{1,0:T(8,128)S(1)}, f32[128,128]{1,0:T(8,128)S(1)}, u32[]{:S(2)}, u32[]{:S(2)}) collective-permute-start(f32[128,128]{1,0:T(8,128)S(1)} %partial_codes.1.mine_ref), channel_id=1, source_target_pairs={{0,1},{1,0},{2,3},{3,2},{4,5},{5,4},{6,7},{7,6},{8,9},{9,8},{10,11... | collective-permute-start | bytes 196616 | tf_op jit(solution)/shard_map/ppermute | solution.py:272
  5.1 4.4 %collective-permute-start.1 = (s32[72,128]{1,0:T(8,128)S(1)}, s32[72,128]{1,0:T(8,128)S(1)}, u32[]{:S(2)}, u32[]{:S(2)}) collective-permute-start(s32[72,128]{1,0:T(8,128)S(1)} %get-tuple-element.7.message_ref), channel_id=1, source_target_pairs={{0,2},{1,8},{2,0},{3,10},{4,6},{5,12},{6,4},{7,14},{8,1},{9,11},{1... | collective-permute-start | bytes 110600 | tf_op jit(solution)/shard_map/ppermute | solution.py:281
  5.1 10.0 %collective-permute-start.2 = (s32[72,128]{1,0:T(8,128)S(1)}, s32[72,128]{1,0:T(8,128)S(1)}, u32[]{:S(2)}, u32[]{:S(2)}) collective-permute-start(s32[72,128]{1,0:T(8,128)S(1)} %get-tuple-element.7.message_ref), channel_id=1, source_target_pairs={{0,4},{1,14},{2,6},{3,12},{4,0},{5,10},{6,2},{7,8},{8,7},{9,13},{1... | collective-permute-start | bytes 110600 | tf_op jit(solution)/shard_map/ppermute | solution.py:281
  9.4 5.7 %collective-permute-start.3 = (s32[72,128]{1,0:T(8,128)S(1)}, s32[72,128]{1,0:T(8,128)S(1)}, u32[]{:S(2)}, u32[]{:S(2)}) collective-permute-start(s32[72,128]{1,0:T(8,128)S(1)} %collective-permute-done.1.refs_0_), channel_id=1, source_target_pairs={{0,4},{1,5},{2,6},{3,7},{4,0},{5,1},{6,2},{7,3},{8,12},{9,13},{10,... | collective-permute-start | bytes 110600 | tf_op jit(solution)/shard_map/ppermute | solution.py:281
  11.4 5.8 %collective-permute-start.4 = (s32[72,128]{1,0:T(8,128)S(1)}, s32[72,128]{1,0:T(8,128)S(1)}, u32[]{:S(2)}, u32[]{:S(2)}) collective-permute-start(s32[72,128]{1,0:T(8,128)S(1)} %collective-permute-done.1.refs_0_), channel_id=1, source_target_pairs={{0,0},{1,3},{2,2},{3,1},{4,4},{5,7},{6,6},{7,5},{8,10},{9,9},{10,8... | collective-permute-start | bytes 110600 | tf_op jit(solution)/shard_map/ppermute | solution.py:281

commit v10 on v9

--- a/solution.py
+++ b/solution.py
@@ -62,11 +62,9 @@
     for copies, dst, w_dst, row, at, size in jobs:
         for copy in copies:
             copy.wait()
-        for first in range(at, at + size, 256):
-            here = slice(first, min(first + 256, at + size))
-            totals.setdefault(row, []).append(dot(w_dst[:, here], dst[:, here], NT))
-    for row, parts in totals.items():
-        out_ref[row : row + rank, :] = sum_of(parts)
+        here = slice(at, at + size)
+        totals.setdefault(row, []).append(dot(dst[:, here], w_dst[:, here], NT))
+    out_ref[...] = jnp.concatenate([sum_of(totals[0]), sum_of(totals[rank])], axis=1).T
 
 
 def partial_codes(inputs, out_grads, proj_in_t, proj_out_t):
@@ -196,7 +194,7 @@
     half = shards // 2
     if half == 4:
         return [(-1, 4, 1), (-1, 7, 2), (0, 2, 2), (0, 1, 0)]
-    direct = [(-1, half + n, n) for n in range(0, half, 2)]
+    direct = [(-1, half + n, n + 1) for n in range(0, half, 2)]
     return direct + [(n, 1, 1) for n in range(half // 2)]
 
 
@@ -204,7 +202,7 @@
     found = []
     for what, other, own in plan(shards):
         before = found[what] if what >= 0 else (0, 0)
-        found.append((before[0] ^ other, before[1] ^ own))
+        found.append((before[0] ^ other, before[1] ^ own if own else 0))
     return found
 
 
@@ -224,8 +222,8 @@
         codes, ids, scales = [], [], []
         for n in range(first, first + width):
             block, (far, near) = blocks[n][...], found[n]
-            if near in [own for _, own in found[:n]]:
-                block, near = jnp.where(own_half, message_ref[...], block), 0
+            if near == 0:
+                block = jnp.where(own_half, message_ref[...], block)
             place = lax.rem(lax.bitwise_xor(shard, jnp.where(own_half, near, far)), half)
             codes.append(block[:rank, :])
             ids.append(block[rank : rank + 1, :] + place * DOCS_DEV)
@@ -272,13 +270,17 @@
     other = lax.ppermute(mine, "tensor", [(0, 1), (1, 0)])
     own, message = pack(mine, other, doc_ids)
     blocks = []
+    groups = lax.axis_size("groups")
     for what, far, near in plan(shards):
         moves = []
-        for s in range(shards):
-            for core in range(2):
-                to = s ^ (near if core == s // half else far)
-                moves.append((2 * s + core, 2 * to + (core if s // half == to // half else 1 - core)))
-        blocks.append(lax.ppermute(blocks[what] if what >= 0 else message, ("dp", "tensor"), moves))
+        for group in range(groups):
+            for s in range(shards):
+                for core in range(2):
+                    to = s ^ (near if core == s // half else far)
+                    to_group = (group + 1) % groups if to == s else group
+                    to_core = core if s // half == to // half else 1 - core
+                    moves.append((2 * (shards * group + s) + core, 2 * (shards * to_group + to) + to_core))
+        blocks.append(lax.ppermute(blocks[what] if what >= 0 else message, ("groups", "dp", "tensor"), moves))
     scores, grads, ins = score_docs(own, message, queries)
     return gram_of(message, grads, ins, scores, blocks)
 

time: 18.5 us -> 17.3 us (0.935)
  the two profiles are of different devices: /device:TPU:16 before, /device:TPU:0 now
where the time goes in v10:
time: 17.3 us; the launch traced here: 17.2 us
  starting transfers between devices  8.62 us (50%)
  Pallas kernels  4.67 us (27%)
  waiting for transfers between devices  3.21 us (19%)
  between operations  0.68 us (4%)
    ppermute x4, starting transfers between devices, local(): lax.ppermute(blocks[what] if what >= 0 else message, ('groups', 'dp', 'te...  8.1 us
    pallas_call x1, Pallas kernels, partial_codes(): pl.pallas_call(codes_kernel, out_shape=jax.ShapeDtypeStruct((2 * rank, to...  2.96 us
    ppermute x4, waiting for transfers between devices, local(): lax.ppermute(blocks[what] if what >= 0 else message, ('groups', 'dp', 'te...  2.31 us
    pallas_call x1, Pallas kernels, gram_of(): pl.pallas_call(gram_kernel, out_shape=(jax.ShapeDtypeStruct((DOCS_DEV, ha...  1.1 us
    ppermute x1, waiting for transfers between devices, local(): other = lax.ppermute(mine, 'tensor', [(0, 1), (1, 0)])  0.9 us
    ppermute x1, starting transfers between devices, local(): other = lax.ppermute(mine, 'tensor', [(0, 1), (1, 0)])  0.52 us
    pallas_call x1, Pallas kernels, score_docs(): pl.pallas_call(scores_kernel, out_shape=(jax.ShapeDtypeStruct((DOCS_DEV,...  0.47 us
  transfers between devices with their start and end apart: 5, of which 3 were waited for; matrix products, arithmetic and copies ran while one was open for 0% of the time, Pallas kernels for 3%

profile of v10, /device:TPU:0, one launch (start us, length us, event | category | flops | bytes accessed | tf_op | source)
XLA Modules:
  0.0 17.2 jit_solution(15191886660972573213)
XLA Ops:
  0.6 0.0 copy-start.1
  0.6 0.0 copy-start
  0.7 3.0 %partial_codes.1.mine_ref = f32[128,128]{1,0:T(8,128)S(1)} custom-call(bf16[128,7168]{1,0:T(8,128)(2,1)} %x_hbm.1, bf16[128,2048]{1,0:T(8,128)(2,1)} %y_hbm.1, bf16[64,14336]{1,0:T(8,128)(2,1)} %bitcast.2, bf16[64,4096]{1,0:T(8,128)(2,1)} %bitcast.3), custom_call_target="tpu_custom_call" | custom-call | tf_op jit(solution)/shard_map/partial_codes/pallas_call | solution.py:75
  3.6 0.5 %collective-permute-start = (f32[128,128]{1,0:T(8,128)S(1)}, f32[128,128]{1,0:T(8,128)S(1)}, u32[]{:S(2)}, u32[]{:S(2)}) collective-permute-start(f32[128,128]{1,0:T(8,128)S(1)} %partial_codes.1.mine_ref), channel_id=1, source_target_pairs={{0,1},{1,0},{2,3},{3,2},{4,5},{5,4},{6,7},{7,6},{8,9},{9,8},{10,11... | collective-permute-start | bytes 196616 | tf_op jit(solution)/shard_map/ppermute | solution.py:270
  4.1 0.9 %collective-permute-done.other_ref = f32[128,128]{1,0:T(8,128)S(1)} collective-permute-done((f32[128,128]{1,0:T(8,128)S(1)}, f32[128,128]{1,0:T(8,128)S(1)}, u32[]{:S(2)}, u32[]{:S(2)}) %collective-permute-start) | collective-permute-done | bytes 65568 | tf_op jit(solution)/shard_map/ppermute | solution.py:270
  5.0 0.0 copy-done.1
  5.0 0.1 pack_codes.1
  5.2 2.9 %collective-permute-start.1 = (s32[72,128]{1,0:T(8,128)S(1)}, s32[72,128]{1,0:T(8,128)S(1)}, u32[]{:S(2)}, u32[]{:S(2)}) collective-permute-start(s32[72,128]{1,0:T(8,128)S(1)} %get-tuple-element.7.message_ref), channel_id=1, source_target_pairs={{0,2},{1,8},{2,0},{3,10},{4,6},{5,12},{6,4},{7,14},{8,1},{9,11},{1... | collective-permute-start | bytes 110600 | tf_op jit(solution)/shard_map/ppermute | solution.py:283
  8.1 1.6 %collective-permute-start.2 = (s32[72,128]{1,0:T(8,128)S(1)}, s32[72,128]{1,0:T(8,128)S(1)}, u32[]{:S(2)}, u32[]{:S(2)}) collective-permute-start(s32[72,128]{1,0:T(8,128)S(1)} %get-tuple-element.7.message_ref), channel_id=1, source_target_pairs={{0,4},{1,14},{2,6},{3,12},{4,0},{5,10},{6,2},{7,8},{8,7},{9,13},{1... | collective-permute-start | bytes 110600 | tf_op jit(solution)/shard_map/ppermute | solution.py:283
  9.7 0.4 %collective-permute-done.1.refs_0_ = s32[72,128]{1,0:T(8,128)S(1)} collective-permute-done((s32[72,128]{1,0:T(8,128)S(1)}, s32[72,128]{1,0:T(8,128)S(1)}, u32[]{:S(2)}, u32[]{:S(2)}) %collective-permute-start.1) | collective-permute-done | bytes 36896 | tf_op jit(solution)/shard_map/ppermute | solution.py:283
  10.0 2.1 %collective-permute-start.3 = (s32[72,128]{1,0:T(8,128)S(1)}, s32[72,128]{1,0:T(8,128)S(1)}, u32[]{:S(2)}, u32[]{:S(2)}) collective-permute-start(s32[72,128]{1,0:T(8,128)S(1)} %collective-permute-done.1.refs_0_), channel_id=1, source_target_pairs={{0,4},{1,5},{2,6},{3,7},{4,0},{5,1},{6,2},{7,3},{8,12},{9,13},{10,... | collective-permute-start | bytes 110600 | tf_op jit(solution)/shard_map/ppermute | solution.py:283
  12.1 1.5 %collective-permute-start.4 = (s32[72,128]{1,0:T(8,128)S(1)}, s32[72,128]{1,0:T(8,128)S(1)}, u32[]{:S(2)}, u32[]{:S(2)}) collective-permute-start(s32[72,128]{1,0:T(8,128)S(1)} %collective-permute-done.1.refs_0_), channel_id=1, source_target_pairs={{0,16},{1,3},{2,18},{3,1},{4,20},{5,7},{6,22},{7,5},{8,10},{9,25},... | collective-permute-start | bytes 110600 | tf_op jit(solution)/shard_map/ppermute | solution.py:283
  13.7 0.0 copy-done
  13.7 0.5 %score_docs.1 = (f32[8,16]{1,0:T(8,128)S(1)}, bf16[128,256]{1,0:T(8,128)(2,1)S(1)}, bf16[128,256]{1,0:T(8,128)(2,1)S(1)}) custom-call(f32[128,128]{1,0:T(8,128)S(1)} %get-tuple-element.8.own_ref, s32[72,128]{1,0:T(8,128)S(1)} %get-tuple-element.7.message_ref, f32[16,4096]{1,0:T(8,128)S(1)} %copy-done), custom_call_target="tpu_custom_call" | custom-call | flops 67108864 | bytes 524288 | tf_op jit(solution)/shard_map/score_docs/pallas_call | solution.py:178
  14.1 0.0 collective-permute-done.2.refs_1_
  14.1 0.0 collective-permute-done.3.refs_2_
  14.2 1.9 %collective-permute-done.4.refs_3_ = s32[72,128]{1,0:T(8,128)S(1)} collective-permute-done((s32[72,128]{1,0:T(8,128)S(1)}, s32[72,128]{1,0:T(8,128)S(1)}, u32[]{:S(2)}, u32[]{:S(2)}) %collective-permute-start.4) | collective-permute-done | bytes 36896 | tf_op jit(solution)/shard_map/ppermute | solution.py:283
  16.1 1.1 %gram_rows.1 = (f32[8,32]{1,0:T(8,128)}, f32[8,16]{1,0:T(8,128)}) custom-call(s32[72,128]{1,0:T(8,128)S(1)} %get-tuple-element.7.message_ref, bf16[128,256]{1,0:T(8,128)(2,1)S(1)} %get-tuple-element.9.grads_ref, bf16[128,256]{1,0:T(8,128)(2,1)S(1)} %get-tuple-element.10.ins_ref, f32[8,16]{1,0:T(8,128)S(1)} %get-tuple-element.11.scores_ref, ...), custom_call_target="tpu_custom_call" | custom-call | tf_op jit(solution)/shard_map/gram_rows/pallas_call | solution.py:253
Async XLA Ops:
  0.6 4.4 %copy-start.1 = (s32[1,128]{1,0:T(1,128)S(1)}, s32[1,128]{1,0:T(1,128)}, u32[]{:S(2)}) copy-start(s32[1,128]{1,0:T(1,128)} %ids_ref.1) | copy-start | bytes 1540
  0.6 13.0 %copy-start = (f32[16,4096]{1,0:T(8,128)S(1)}, f32[16,4096]{1,0:T(8,128)}, u32[]{:S(2)}) copy-start(f32[16,4096]{1,0:T(8,128)} %queries.1) | copy-start | bytes 786436
  3.6 1.4 %collective-permute-start = (f32[128,128]{1,0:T(8,128)S(1)}, f32[128,128]{1,0:T(8,128)S(1)}, u32[]{:S(2)}, u32[]{:S(2)}) collective-permute-start(f32[128,128]{1,0:T(8,128)S(1)} %partial_codes.1.mine_ref), channel_id=1, source_target_pairs={{0,1},{1,0},{2,3},{3,2},{4,5},{5,4},{6,7},{7,6},{8,9},{9,8},{10,11... | collective-permute-start | bytes 196616 | tf_op jit(solution)/shard_map/ppermute | solution.py:270
  5.2 4.8 %collective-permute-start.1 = (s32[72,128]{1,0:T(8,128)S(1)}, s32[72,128]{1,0:T(8,128)S(1)}, u32[]{:S(2)}, u32[]{:S(2)}) collective-permute-start(s32[72,128]{1,0:T(8,128)S(1)} %get-tuple-element.7.message_ref), channel_id=1, source_target_pairs={{0,2},{1,8},{2,0},{3,10},{4,6},{5,12},{6,4},{7,14},{8,1},{9,11},{1... | collective-permute-start | bytes 110600 | tf_op jit(solution)/shard_map/ppermute | solution.py:283
  8.1 6.0 %collective-permute-start.2 = (s32[72,128]{1,0:T(8,128)S(1)}, s32[72,128]{1,0:T(8,128)S(1)}, u32[]{:S(2)}, u32[]{:S(2)}) collective-permute-start(s32[72,128]{1,0:T(8,128)S(1)} %get-tuple-element.7.message_ref), channel_id=1, source_target_pairs={{0,4},{1,14},{2,6},{3,12},{4,0},{5,10},{6,2},{7,8},{8,7},{9,13},{1... | collective-permute-start | bytes 110600 | tf_op jit(solution)/shard_map/ppermute | solution.py:283
  10.0 4.2 %collective-permute-start.3 = (s32[72,128]{1,0:T(8,128)S(1)}, s32[72,128]{1,0:T(8,128)S(1)}, u32[]{:S(2)}, u32[]{:S(2)}) collective-permute-start(s32[72,128]{1,0:T(8,128)S(1)} %collective-permute-done.1.refs_0_), channel_id=1, source_target_pairs={{0,4},{1,5},{2,6},{3,7},{4,0},{5,1},{6,2},{7,3},{8,12},{9,13},{10,... | collective-permute-start | bytes 110600 | tf_op jit(solution)/shard_map/ppermute | solution.py:283
  12.1 4.0 %collective-permute-start.4 = (s32[72,128]{1,0:T(8,128)S(1)}, s32[72,128]{1,0:T(8,128)S(1)}, u32[]{:S(2)}, u32[]{:S(2)}) collective-permute-start(s32[72,128]{1,0:T(8,128)S(1)} %collective-permute-done.1.refs_0_), channel_id=1, source_target_pairs={{0,16},{1,3},{2,18},{3,1},{4,20},{5,7},{6,22},{7,5},{8,10},{9,25},... | collective-permute-start | bytes 110600 | tf_op jit(solution)/shard_map/ppermute | solution.py:283

commit v11 on v10

--- a/solution.py
+++ b/solution.py
@@ -21,7 +21,7 @@
 
 
 def pieces_of(depth):
-    size = next(size for size in (2048, 1792, 1024, 512, 256, 128, depth) if depth % size == 0)
+    size = next(size for size in (1792, 1024, 512, 256, 128, depth) if depth % size == 0)
     return [(at, size) for at in range(0, depth, size)]
 
 
@@ -63,8 +63,9 @@
         for copy in copies:
             copy.wait()
         here = slice(at, at + size)
-        totals.setdefault(row, []).append(dot(dst[:, here], w_dst[:, here], NT))
-    out_ref[...] = jnp.concatenate([sum_of(totals[0]), sum_of(totals[rank])], axis=1).T
+        totals.setdefault(row, []).append(dot(w_dst[:, here], dst[:, here], NT))
+    for row, parts in totals.items():
+        out_ref[row : row + rank, :] = sum_of(parts)
 
 
 def partial_codes(inputs, out_grads, proj_in_t, proj_out_t):
@@ -193,7 +194,7 @@
 def plan(shards):
     half = shards // 2
     if half == 4:
-        return [(-1, 4, 1), (-1, 7, 2), (0, 2, 2), (0, 1, 0)]
+        return [(-1, 4, 2), (-1, 7, 1), (0, 1, 0), (0, 2, 1)]
     direct = [(-1, half + n, n + 1) for n in range(0, half, 2)]
     return direct + [(n, 1, 1) for n in range(half // 2)]
 
@@ -275,11 +276,13 @@
         moves = []
         for group in range(groups):
             for s in range(shards):
+                side = s // half
                 for core in range(2):
-                    to = s ^ (near if core == s // half else far)
+                    to = s ^ (near if core == side else far)
                     to_group = (group + 1) % groups if to == s else group
-                    to_core = core if s // half == to // half else 1 - core
-                    moves.append((2 * (shards * group + s) + core, 2 * (shards * to_group + to) + to_core))
+                    to_core = core if to // half == side else 1 - core
+                    by = 1 - core if what < 0 and side == 1 else core
+                    moves.append((2 * (shards * group + s) + by, 2 * (shards * to_group + to) + to_core))
         blocks.append(lax.ppermute(blocks[what] if what >= 0 else message, ("groups", "dp", "tensor"), moves))
     scores, grads, ins = score_docs(own, message, queries)
     return gram_of(message, grads, ins, scores, blocks)

time: 17.3 us -> 17.7 us (1.023)
  starting transfers between devices: 8.62 us -> 8.84 us
    ppermute x4, starting transfers between devices: 8.1 us -> 8.32 us  [local(): lax.ppermute(blocks[what] if what >= 0 else message, ('groups', 'dp', 'te...]
where the time goes in v11:
time: 17.7 us; the launch traced here: 17.5 us
  starting transfers between devices  8.84 us (50%)
  Pallas kernels  4.67 us (26%)
  waiting for transfers between devices  3.33 us (19%)
  between operations  0.69 us (4%)
    ppermute x4, starting transfers between devices, local(): lax.ppermute(blocks[what] if what >= 0 else message, ('groups', 'dp', 'te...  8.32 us
    pallas_call x1, Pallas kernels, partial_codes(): pl.pallas_call(codes_kernel, out_shape=jax.ShapeDtypeStruct((2 * rank, to...  2.98 us
    ppermute x4, waiting for transfers between devices, local(): lax.ppermute(blocks[what] if what >= 0 else message, ('groups', 'dp', 'te...  2.43 us
    pallas_call x1, Pallas kernels, gram_of(): pl.pallas_call(gram_kernel, out_shape=(jax.ShapeDtypeStruct((DOCS_DEV, ha...  1.1 us
    ppermute x1, waiting for transfers between devices, local(): other = lax.ppermute(mine, 'tensor', [(0, 1), (1, 0)])  0.9 us
    ppermute x1, starting transfers between devices, local(): other = lax.ppermute(mine, 'tensor', [(0, 1), (1, 0)])  0.52 us
    pallas_call x1, Pallas kernels, score_docs(): pl.pallas_call(scores_kernel, out_shape=(jax.ShapeDtypeStruct((DOCS_DEV,...  0.46 us
  transfers between devices with their start and end apart: 5, of which 3 were waited for; matrix products, arithmetic and copies ran while one was open for 0% of the time, Pallas kernels for 3%

profile of v11, /device:TPU:0, one launch (start us, length us, event | category | flops | bytes accessed | tf_op | source)
XLA Modules:
  0.0 17.5 jit_solution(3443216884687070581)
XLA Ops:
  0.6 0.0 copy-start.1
  0.6 0.0 copy-start
  0.7 3.0 %partial_codes.1.mine_ref = f32[128,128]{1,0:T(8,128)S(1)} custom-call(bf16[128,7168]{1,0:T(8,128)(2,1)} %x_hbm.1, bf16[128,2048]{1,0:T(8,128)(2,1)} %y_hbm.1, bf16[64,14336]{1,0:T(8,128)(2,1)} %bitcast.2, bf16[64,4096]{1,0:T(8,128)(2,1)} %bitcast.3), custom_call_target="tpu_custom_call" | custom-call | tf_op jit(solution)/shard_map/partial_codes/pallas_call | solution.py:76
  3.6 0.5 %collective-permute-start = (f32[128,128]{1,0:T(8,128)S(1)}, f32[128,128]{1,0:T(8,128)S(1)}, u32[]{:S(2)}, u32[]{:S(2)}) collective-permute-start(f32[128,128]{1,0:T(8,128)S(1)} %partial_codes.1.mine_ref), channel_id=1, source_target_pairs={{0,1},{1,0},{2,3},{3,2},{4,5},{5,4},{6,7},{7,6},{8,9},{9,8},{10,11... | collective-permute-start | bytes 196616 | tf_op jit(solution)/shard_map/ppermute | solution.py:271
  4.2 0.9 %collective-permute-done.other_ref = f32[128,128]{1,0:T(8,128)S(1)} collective-permute-done((f32[128,128]{1,0:T(8,128)S(1)}, f32[128,128]{1,0:T(8,128)S(1)}, u32[]{:S(2)}, u32[]{:S(2)}) %collective-permute-start) | collective-permute-done | bytes 65568 | tf_op jit(solution)/shard_map/ppermute | solution.py:271
  5.1 0.0 copy-done.1
  5.1 0.1 pack_codes.1
  5.2 3.0 %collective-permute-start.1 = (s32[72,128]{1,0:T(8,128)S(1)}, s32[72,128]{1,0:T(8,128)S(1)}, u32[]{:S(2)}, u32[]{:S(2)}) collective-permute-start(s32[72,128]{1,0:T(8,128)S(1)} %get-tuple-element.7.message_ref), channel_id=1, source_target_pairs={{0,4},{1,8},{2,6},{3,10},{4,0},{5,12},{6,2},{7,14},{9,1},{8,13},{1... | collective-permute-start | bytes 110600 | tf_op jit(solution)/shard_map/ppermute | solution.py:286
  8.2 1.5 %collective-permute-start.2 = (s32[72,128]{1,0:T(8,128)S(1)}, s32[72,128]{1,0:T(8,128)S(1)}, u32[]{:S(2)}, u32[]{:S(2)}) collective-permute-start(s32[72,128]{1,0:T(8,128)S(1)} %get-tuple-element.7.message_ref), channel_id=1, source_target_pairs={{0,2},{1,14},{2,0},{3,12},{4,6},{5,10},{6,4},{7,8},{9,7},{8,11},{1... | collective-permute-start | bytes 110600 | tf_op jit(solution)/shard_map/ppermute | solution.py:286
  9.7 0.4 %collective-permute-done.1.refs_0_ = s32[72,128]{1,0:T(8,128)S(1)} collective-permute-done((s32[72,128]{1,0:T(8,128)S(1)}, s32[72,128]{1,0:T(8,128)S(1)}, u32[]{:S(2)}, u32[]{:S(2)}) %collective-permute-start.1) | collective-permute-done | bytes 36896 | tf_op jit(solution)/shard_map/ppermute | solution.py:286
  10.1 2.4 %collective-permute-start.3 = (s32[72,128]{1,0:T(8,128)S(1)}, s32[72,128]{1,0:T(8,128)S(1)}, u32[]{:S(2)}, u32[]{:S(2)}) collective-permute-start(s32[72,128]{1,0:T(8,128)S(1)} %collective-permute-done.1.refs_0_), channel_id=1, source_target_pairs={{0,16},{1,3},{2,18},{3,1},{4,20},{5,7},{6,22},{7,5},{8,10},{9,25},... | collective-permute-start | bytes 110600 | tf_op jit(solution)/shard_map/ppermute | solution.py:286
  12.5 1.5 %collective-permute-start.4 = (s32[72,128]{1,0:T(8,128)S(1)}, s32[72,128]{1,0:T(8,128)S(1)}, u32[]{:S(2)}, u32[]{:S(2)}) collective-permute-start(s32[72,128]{1,0:T(8,128)S(1)} %collective-permute-done.1.refs_0_), channel_id=1, source_target_pairs={{0,2},{1,5},{2,0},{3,7},{4,6},{5,1},{6,4},{7,3},{8,12},{9,11},{10,... | collective-permute-start | bytes 110600 | tf_op jit(solution)/shard_map/ppermute | solution.py:286
  14.0 0.0 copy-done
  14.0 0.5 %score_docs.1 = (f32[8,16]{1,0:T(8,128)S(1)}, bf16[128,256]{1,0:T(8,128)(2,1)S(1)}, bf16[128,256]{1,0:T(8,128)(2,1)S(1)}) custom-call(f32[128,128]{1,0:T(8,128)S(1)} %get-tuple-element.8.own_ref, s32[72,128]{1,0:T(8,128)S(1)} %get-tuple-element.7.message_ref, f32[16,4096]{1,0:T(8,128)S(1)} %copy-done), custom_call_target="tpu_custom_call" | custom-call | flops 67108864 | bytes 524288 | tf_op jit(solution)/shard_map/score_docs/pallas_call | solution.py:179
  14.4 0.0 collective-permute-done.2.refs_1_
  14.4 0.0 collective-permute-done.3.refs_2_
  14.4 2.0 %collective-permute-done.4.refs_3_ = s32[72,128]{1,0:T(8,128)S(1)} collective-permute-done((s32[72,128]{1,0:T(8,128)S(1)}, s32[72,128]{1,0:T(8,128)S(1)}, u32[]{:S(2)}, u32[]{:S(2)}) %collective-permute-start.4) | collective-permute-done | bytes 36896 | tf_op jit(solution)/shard_map/ppermute | solution.py:286
  16.4 1.1 %gram_rows.1 = (f32[8,32]{1,0:T(8,128)}, f32[8,16]{1,0:T(8,128)}) custom-call(s32[72,128]{1,0:T(8,128)S(1)} %get-tuple-element.7.message_ref, bf16[128,256]{1,0:T(8,128)(2,1)S(1)} %get-tuple-element.9.grads_ref, bf16[128,256]{1,0:T(8,128)(2,1)S(1)} %get-tuple-element.10.ins_ref, f32[8,16]{1,0:T(8,128)S(1)} %get-tuple-element.11.scores_ref, ...), custom_call_target="tpu_custom_call" | custom-call | tf_op jit(solution)/shard_map/gram_rows/pallas_call | solution.py:254
Async XLA Ops:
  0.6 4.4 %copy-start.1 = (s32[1,128]{1,0:T(1,128)S(1)}, s32[1,128]{1,0:T(1,128)}, u32[]{:S(2)}) copy-start(s32[1,128]{1,0:T(1,128)} %ids_ref.1) | copy-start | bytes 1540
  0.6 13.3 %copy-start = (f32[16,4096]{1,0:T(8,128)S(1)}, f32[16,4096]{1,0:T(8,128)}, u32[]{:S(2)}) copy-start(f32[16,4096]{1,0:T(8,128)} %queries.1) | copy-start | bytes 786436
  3.6 1.4 %collective-permute-start = (f32[128,128]{1,0:T(8,128)S(1)}, f32[128,128]{1,0:T(8,128)S(1)}, u32[]{:S(2)}, u32[]{:S(2)}) collective-permute-start(f32[128,128]{1,0:T(8,128)S(1)} %partial_codes.1.mine_ref), channel_id=1, source_target_pairs={{0,1},{1,0},{2,3},{3,2},{4,5},{5,4},{6,7},{7,6},{8,9},{9,8},{10,11... | collective-permute-start | bytes 196616 | tf_op jit(solution)/shard_map/ppermute | solution.py:271
  5.2 4.9 %collective-permute-start.1 = (s32[72,128]{1,0:T(8,128)S(1)}, s32[72,128]{1,0:T(8,128)S(1)}, u32[]{:S(2)}, u32[]{:S(2)}) collective-permute-start(s32[72,128]{1,0:T(8,128)S(1)} %get-tuple-element.7.message_ref), channel_id=1, source_target_pairs={{0,4},{1,8},{2,6},{3,10},{4,0},{5,12},{6,2},{7,14},{9,1},{8,13},{1... | collective-permute-start | bytes 110600 | tf_op jit(solution)/shard_map/ppermute | solution.py:286
  8.2 6.3 %collective-permute-start.2 = (s32[72,128]{1,0:T(8,128)S(1)}, s32[72,128]{1,0:T(8,128)S(1)}, u32[]{:S(2)}, u32[]{:S(2)}) collective-permute-start(s32[72,128]{1,0:T(8,128)S(1)} %get-tuple-element.7.message_ref), channel_id=1, source_target_pairs={{0,2},{1,14},{2,0},{3,12},{4,6},{5,10},{6,4},{7,8},{9,7},{8,11},{1... | collective-permute-start | bytes 110600 | tf_op jit(solution)/shard_map/ppermute | solution.py:286
  10.1 4.3 %collective-permute-start.3 = (s32[72,128]{1,0:T(8,128)S(1)}, s32[72,128]{1,0:T(8,128)S(1)}, u32[]{:S(2)}, u32[]{:S(2)}) collective-permute-start(s32[72,128]{1,0:T(8,128)S(1)} %collective-permute-done.1.refs_0_), channel_id=1, source_target_pairs={{0,16},{1,3},{2,18},{3,1},{4,20},{5,7},{6,22},{7,5},{8,10},{9,25},... | collective-permute-start | bytes 110600 | tf_op jit(solution)/shard_map/ppermute | solution.py:286
  12.5 4.0 %collective-permute-start.4 = (s32[72,128]{1,0:T(8,128)S(1)}, s32[72,128]{1,0:T(8,128)S(1)}, u32[]{:S(2)}, u32[]{:S(2)}) collective-permute-start(s32[72,128]{1,0:T(8,128)S(1)} %collective-permute-done.1.refs_0_), channel_id=1, source_target_pairs={{0,2},{1,5},{2,0},{3,7},{4,6},{5,1},{6,4},{7,3},{8,12},{9,11},{10,... | collective-permute-start | bytes 110600 | tf_op jit(solution)/shard_map/ppermute | solution.py:286

commit v12 on v11

--- a/solution.py
+++ b/solution.py
@@ -21,7 +21,7 @@
 
 
 def pieces_of(depth):
-    size = next(size for size in (1792, 1024, 512, 256, 128, depth) if depth % size == 0)
+    size = next(size for size in (2048, 1792, 1024, 512, 256, 128, depth) if depth % size == 0)
     return [(at, size) for at in range(0, depth, size)]
 
 
@@ -194,14 +194,14 @@
 def plan(shards):
     half = shards // 2
     if half == 4:
-        return [(-1, 4, 2), (-1, 7, 1), (0, 1, 0), (0, 2, 1)]
-    direct = [(-1, half + n, n + 1) for n in range(0, half, 2)]
-    return direct + [(n, 1, 1) for n in range(half // 2)]
+        return [(-1, 4, 2, (0, 1)), (-1, 7, 1, (1,)), (0, 1, 1, ()), (0, 2, 0, ())]
+    direct = [(-1, half + n, n + 1, ()) for n in range(0, half, 2)]
+    return direct + [(n, 1, 1, ()) for n in range(half // 2)]
 
 
 def origins(shards):
     found = []
-    for what, other, own in plan(shards):
+    for what, other, own, _ in plan(shards):
         before = found[what] if what >= 0 else (0, 0)
         found.append((before[0] ^ other, before[1] ^ own if own else 0))
     return found
@@ -272,7 +272,7 @@
     own, message = pack(mine, other, doc_ids)
     blocks = []
     groups = lax.axis_size("groups")
-    for what, far, near in plan(shards):
+    for what, far, near, crossed in plan(shards):
         moves = []
         for group in range(groups):
             for s in range(shards):
@@ -281,7 +281,7 @@
                     to = s ^ (near if core == side else far)
                     to_group = (group + 1) % groups if to == s else group
                     to_core = core if to // half == side else 1 - core
-                    by = 1 - core if what < 0 and side == 1 else core
+                    by = 1 - core if side in crossed else core
                     moves.append((2 * (shards * group + s) + by, 2 * (shards * to_group + to) + to_core))
         blocks.append(lax.ppermute(blocks[what] if what >= 0 else message, ("groups", "dp", "tensor"), moves))
     scores, grads, ins = score_docs(own, message, queries)

time: 17.7 us -> 17.5 us (0.989)
  waiting for transfers between devices: 3.33 us -> 2.99 us
  starting transfers between devices: 8.84 us -> 9.02 us
    ppermute x4, waiting for transfers between devices: 2.43 us -> 2.09 us  [local(): lax.ppermute(blocks[what] if what >= 0 else message, ('groups', 'dp', 'te...]
    ppermute x4, starting transfers between devices: 8.32 us -> 8.51 us  [local(): lax.ppermute(blocks[what] if what >= 0 else message, ('groups', 'dp', 'te...]
  transfers between devices with their start and end apart: 5 -> 5, of which waited for: 3 -> 4; matrix products, arithmetic and copies ran while one was open for 0% -> 0% of each run, Pallas kernels for 3% -> 3%
where the time goes in v12:
time: 17.5 us; the launch traced here: 17.3 us
  starting transfers between devices  9.02 us (52%)
  Pallas kernels  4.57 us (26%)
  waiting for transfers between devices  2.99 us (17%)
  between operations  0.68 us (4%)
    ppermute x4, starting transfers between devices, local(): lax.ppermute(blocks[what] if what >= 0 else message, ('groups', 'dp', 'te...  8.51 us
    pallas_call x1, Pallas kernels, partial_codes(): pl.pallas_call(codes_kernel, out_shape=jax.ShapeDtypeStruct((2 * rank, to...  2.87 us
    ppermute x4, waiting for transfers between devices, local(): lax.ppermute(blocks[what] if what >= 0 else message, ('groups', 'dp', 'te...  2.09 us
    pallas_call x1, Pallas kernels, gram_of(): pl.pallas_call(gram_kernel, out_shape=(jax.ShapeDtypeStruct((DOCS_DEV, ha...  1.1 us
    ppermute x1, waiting for transfers between devices, local(): other = lax.ppermute(mine, 'tensor', [(0, 1), (1, 0)])  0.9 us
    ppermute x1, starting transfers between devices, local(): other = lax.ppermute(mine, 'tensor', [(0, 1), (1, 0)])  0.52 us
    pallas_call x1, Pallas kernels, score_docs(): pl.pallas_call(scores_kernel, out_shape=(jax.ShapeDtypeStruct((DOCS_DEV,...  0.47 us
  transfers between devices with their start and end apart: 5, of which 4 were waited for; matrix products, arithmetic and copies ran while one was open for 0% of the time, Pallas kernels for 3%

profile of v12, /device:TPU:0, one launch (start us, length us, event | category | flops | bytes accessed | tf_op | source)
XLA Modules:
  0.0 17.3 jit_solution(8342595040164597135)
XLA Ops:
  0.6 0.0 copy-start.1
  0.6 0.0 copy-start
  0.7 2.9 %partial_codes.1.mine_ref = f32[128,128]{1,0:T(8,128)S(1)} custom-call(bf16[128,7168]{1,0:T(8,128)(2,1)} %x_hbm.1, bf16[128,2048]{1,0:T(8,128)(2,1)} %y_hbm.1, bf16[64,14336]{1,0:T(8,128)(2,1)} %bitcast.2, bf16[64,4096]{1,0:T(8,128)(2,1)} %bitcast.3), custom_call_target="tpu_custom_call" | custom-call | tf_op jit(solution)/shard_map/partial_codes/pallas_call | solution.py:76
  3.5 0.5 %collective-permute-start = (f32[128,128]{1,0:T(8,128)S(1)}, f32[128,128]{1,0:T(8,128)S(1)}, u32[]{:S(2)}, u32[]{:S(2)}) collective-permute-start(f32[128,128]{1,0:T(8,128)S(1)} %partial_codes.1.mine_ref), channel_id=1, source_target_pairs={{0,1},{1,0},{2,3},{3,2},{4,5},{5,4},{6,7},{7,6},{8,9},{9,8},{10,11... | collective-permute-start | bytes 196616 | tf_op jit(solution)/shard_map/ppermute | solution.py:271
  4.0 0.9 %collective-permute-done.other_ref = f32[128,128]{1,0:T(8,128)S(1)} collective-permute-done((f32[128,128]{1,0:T(8,128)S(1)}, f32[128,128]{1,0:T(8,128)S(1)}, u32[]{:S(2)}, u32[]{:S(2)}) %collective-permute-start) | collective-permute-done | bytes 65568 | tf_op jit(solution)/shard_map/ppermute | solution.py:271
  4.9 0.0 copy-done.1
  4.9 0.1 pack_codes.1
  5.1 4.0 %collective-permute-start.1 = (s32[72,128]{1,0:T(8,128)S(1)}, s32[72,128]{1,0:T(8,128)S(1)}, u32[]{:S(2)}, u32[]{:S(2)}) collective-permute-start(s32[72,128]{1,0:T(8,128)S(1)} %get-tuple-element.7.message_ref), channel_id=1, source_target_pairs={{1,4},{0,8},{3,6},{2,10},{5,0},{4,12},{7,2},{6,14},{9,1},{8,13},{1... | collective-permute-start | bytes 110600 | tf_op jit(solution)/shard_map/ppermute | solution.py:286
  9.1 1.5 %collective-permute-start.2 = (s32[72,128]{1,0:T(8,128)S(1)}, s32[72,128]{1,0:T(8,128)S(1)}, u32[]{:S(2)}, u32[]{:S(2)}) collective-permute-start(s32[72,128]{1,0:T(8,128)S(1)} %get-tuple-element.7.message_ref), channel_id=1, source_target_pairs={{0,2},{1,14},{2,0},{3,12},{4,6},{5,10},{6,4},{7,8},{9,7},{8,11},{1... | collective-permute-start | bytes 110600 | tf_op jit(solution)/shard_map/ppermute | solution.py:286
  10.6 0.1 collective-permute-done.1.refs_0_
  10.7 1.5 %collective-permute-start.3 = (s32[72,128]{1,0:T(8,128)S(1)}, s32[72,128]{1,0:T(8,128)S(1)}, u32[]{:S(2)}, u32[]{:S(2)}) collective-permute-start(s32[72,128]{1,0:T(8,128)S(1)} %collective-permute-done.1.refs_0_), channel_id=1, source_target_pairs={{0,2},{1,3},{2,0},{3,1},{4,6},{5,7},{6,4},{7,5},{8,10},{9,11},{10,... | collective-permute-start | bytes 110600 | tf_op jit(solution)/shard_map/ppermute | solution.py:286
  12.2 1.5 %collective-permute-start.4 = (s32[72,128]{1,0:T(8,128)S(1)}, s32[72,128]{1,0:T(8,128)S(1)}, u32[]{:S(2)}, u32[]{:S(2)}) collective-permute-start(s32[72,128]{1,0:T(8,128)S(1)} %collective-permute-done.1.refs_0_), channel_id=1, source_target_pairs={{0,16},{1,5},{2,18},{3,7},{4,20},{5,1},{6,22},{7,3},{8,12},{9,25},... | collective-permute-start | bytes 110600 | tf_op jit(solution)/shard_map/ppermute | solution.py:286
  13.7 0.0 copy-done
  13.7 0.5 %score_docs.1 = (f32[8,16]{1,0:T(8,128)S(1)}, bf16[128,256]{1,0:T(8,128)(2,1)S(1)}, bf16[128,256]{1,0:T(8,128)(2,1)S(1)}) custom-call(f32[128,128]{1,0:T(8,128)S(1)} %get-tuple-element.8.own_ref, s32[72,128]{1,0:T(8,128)S(1)} %get-tuple-element.7.message_ref, f32[16,4096]{1,0:T(8,128)S(1)} %copy-done), custom_call_target="tpu_custom_call" | custom-call | flops 67108864 | bytes 524288 | tf_op jit(solution)/shard_map/score_docs/pallas_call | solution.py:179
  14.2 0.0 collective-permute-done.2.refs_1_
  14.2 0.5 %collective-permute-done.3.refs_2_ = s32[72,128]{1,0:T(8,128)S(1)} collective-permute-done((s32[72,128]{1,0:T(8,128)S(1)}, s32[72,128]{1,0:T(8,128)S(1)}, u32[]{:S(2)}, u32[]{:S(2)}) %collective-permute-start.3) | collective-permute-done | bytes 36896 | tf_op jit(solution)/shard_map/ppermute | solution.py:286
  14.7 1.4 %collective-permute-done.4.refs_3_ = s32[72,128]{1,0:T(8,128)S(1)} collective-permute-done((s32[72,128]{1,0:T(8,128)S(1)}, s32[72,128]{1,0:T(8,128)S(1)}, u32[]{:S(2)}, u32[]{:S(2)}) %collective-permute-start.4) | collective-permute-done | bytes 36896 | tf_op jit(solution)/shard_map/ppermute | solution.py:286
  16.2 1.1 %gram_rows.1 = (f32[8,32]{1,0:T(8,128)}, f32[8,16]{1,0:T(8,128)}) custom-call(s32[72,128]{1,0:T(8,128)S(1)} %get-tuple-element.7.message_ref, bf16[128,256]{1,0:T(8,128)(2,1)S(1)} %get-tuple-element.9.grads_ref, bf16[128,256]{1,0:T(8,128)(2,1)S(1)} %get-tuple-element.10.ins_ref, f32[8,16]{1,0:T(8,128)S(1)} %get-tuple-element.11.scores_ref, ...), custom_call_target="tpu_custom_call" | custom-call | tf_op jit(solution)/shard_map/gram_rows/pallas_call | solution.py:254
Async XLA Ops:
  0.6 4.3 %copy-start.1 = (s32[1,128]{1,0:T(1,128)S(1)}, s32[1,128]{1,0:T(1,128)}, u32[]{:S(2)}) copy-start(s32[1,128]{1,0:T(1,128)} %ids_ref.1) | copy-start | bytes 1540
  0.6 13.1 %copy-start = (f32[16,4096]{1,0:T(8,128)S(1)}, f32[16,4096]{1,0:T(8,128)}, u32[]{:S(2)}) copy-start(f32[16,4096]{1,0:T(8,128)} %queries.1) | copy-start | bytes 786436
  3.5 1.4 %collective-permute-start = (f32[128,128]{1,0:T(8,128)S(1)}, f32[128,128]{1,0:T(8,128)S(1)}, u32[]{:S(2)}, u32[]{:S(2)}) collective-permute-start(f32[128,128]{1,0:T(8,128)S(1)} %partial_codes.1.mine_ref), channel_id=1, source_target_pairs={{0,1},{1,0},{2,3},{3,2},{4,5},{5,4},{6,7},{7,6},{8,9},{9,8},{10,11... | collective-permute-start | bytes 196616 | tf_op jit(solution)/shard_map/ppermute | solution.py:271
  5.1 5.6 %collective-permute-start.1 = (s32[72,128]{1,0:T(8,128)S(1)}, s32[72,128]{1,0:T(8,128)S(1)}, u32[]{:S(2)}, u32[]{:S(2)}) collective-permute-start(s32[72,128]{1,0:T(8,128)S(1)} %get-tuple-element.7.message_ref), channel_id=1, source_target_pairs={{1,4},{0,8},{3,6},{2,10},{5,0},{4,12},{7,2},{6,14},{9,1},{8,13},{1... | collective-permute-start | bytes 110600 | tf_op jit(solution)/shard_map/ppermute | solution.py:286
  9.1 5.1 %collective-permute-start.2 = (s32[72,128]{1,0:T(8,128)S(1)}, s32[72,128]{1,0:T(8,128)S(1)}, u32[]{:S(2)}, u32[]{:S(2)}) collective-permute-start(s32[72,128]{1,0:T(8,128)S(1)} %get-tuple-element.7.message_ref), channel_id=1, source_target_pairs={{0,2},{1,14},{2,0},{3,12},{4,6},{5,10},{6,4},{7,8},{9,7},{8,11},{1... | collective-permute-start | bytes 110600 | tf_op jit(solution)/shard_map/ppermute | solution.py:286
  10.7 4.0 %collective-permute-start.3 = (s32[72,128]{1,0:T(8,128)S(1)}, s32[72,128]{1,0:T(8,128)S(1)}, u32[]{:S(2)}, u32[]{:S(2)}) collective-permute-start(s32[72,128]{1,0:T(8,128)S(1)} %collective-permute-done.1.refs_0_), channel_id=1, source_target_pairs={{0,2},{1,3},{2,0},{3,1},{4,6},{5,7},{6,4},{7,5},{8,10},{9,11},{10,... | collective-permute-start | bytes 110600 | tf_op jit(solution)/shard_map/ppermute | solution.py:286
  12.2 4.0 %collective-permute-start.4 = (s32[72,128]{1,0:T(8,128)S(1)}, s32[72,128]{1,0:T(8,128)S(1)}, u32[]{:S(2)}, u32[]{:S(2)}) collective-permute-start(s32[72,128]{1,0:T(8,128)S(1)} %collective-permute-done.1.refs_0_), channel_id=1, source_target_pairs={{0,16},{1,5},{2,18},{3,7},{4,20},{5,1},{6,22},{7,3},{8,12},{9,25},... | collective-permute-start | bytes 110600 | tf_op jit(solution)/shard_map/ppermute | solution.py:286

commit v13 on v12

--- a/solution.py
+++ b/solution.py
@@ -194,9 +194,9 @@
 def plan(shards):
     half = shards // 2
     if half == 4:
-        return [(-1, 4, 2, (0, 1)), (-1, 7, 1, (1,)), (0, 1, 1, ()), (0, 2, 0, ())]
+        return [(-1, 4, 2, (1,)), (-1, 7, 1, (1,)), (0, 2, 1, ()), (0, 1, 0, ())]
     direct = [(-1, half + n, n + 1, ()) for n in range(0, half, 2)]
-    return direct + [(n, 1, 1, ()) for n in range(half // 2)]
+    return direct + [(n, 1, 1, ()) for n in reversed(range(half // 2))]
 
 
 def origins(shards):
@@ -207,25 +207,14 @@
     return found
 
 
-def gram_kernel(message_ref, grads_ref, ins_ref, scores_ref, *refs):
-    blocks, (out_ref, scores_out_ref) = refs[:-2], refs[-2:]
-    scores_out_ref[...] = scores_ref[...]
-    half = len(blocks)
+def gram_sum(half, message_ref, grads_ref, ins_ref, parts):
     rank = message_ref.shape[0] - EXTRA
-    shard, core = lax.axis_index("dp"), lax.axis_index("tensor")
-    own_half = lax.div(shard, half) == core
     onehot = members(message_ref[rank : rank + 1, :], DOCS_DEV).astype(jnp.bfloat16)
     doubled = jnp.concatenate([onehot, onehot], axis=1)
-    found = origins(2 * half)
     total = None
-    width = min(4, half)
-    for first in range(0, half, width):
+    for first in range(0, len(parts), 4):
         codes, ids, scales = [], [], []
-        for n in range(first, first + width):
-            block, (far, near) = blocks[n][...], found[n]
-            if near == 0:
-                block = jnp.where(own_half, message_ref[...], block)
-            place = lax.rem(lax.bitwise_xor(shard, jnp.where(own_half, near, far)), half)
+        for block, place in parts[first : first + 4]:
             codes.append(block[:rank, :])
             ids.append(block[rank : rank + 1, :] + place * DOCS_DEV)
             grades = block[rank + 1 : rank + 2, :] + block[rank + 2 : rank + 3, :]
@@ -246,22 +235,74 @@
         theirs = members(ids, half * DOCS_DEV).astype(jnp.bfloat16)
         part = dot(jnp.concatenate([high, low], axis=0), theirs, NT)
         total = part if total is None else total + part
-    out_ref[...] = total[:DOCS_DEV, :] + total[DOCS_DEV:, :]
+    return total[:DOCS_DEV, :] + total[DOCS_DEV:, :]
+
+
+def place_of(shard, half, own_half, origin):
+    far, near = origin
+    return lax.rem(lax.bitwise_xor(shard, jnp.where(own_half, near, far)), half)
+
+
+def gram_kernel(message_ref, grads_ref, ins_ref, scores_ref, *refs):
+    blocks, (sum_ref, out_ref, scores_out_ref, sems) = refs[:-4], refs[-4:]
+    scores_copy = pltpu.make_async_copy(scores_ref, scores_out_ref, sems.at[0])
+    scores_copy.start()
+    half = len(blocks) + 1
+    shard, core = lax.axis_index("dp"), lax.axis_index("tensor")
+    own_half = lax.div(shard, half) == core
+    found = origins(2 * half)
+    parts = [
+        (block[...], place_of(shard, half, own_half, origin)) for block, origin in zip(blocks, found)
+    ]
+    parts.append((message_ref[...], jnp.where(own_half, lax.rem(shard, half), -half)))
+    sum_ref[...] = gram_sum(half, message_ref, grads_ref, ins_ref, parts)
+
+    @pl.when(own_half)
+    def _():
+        copy = pltpu.make_async_copy(sum_ref, out_ref, sems.at[1])
+        copy.start()
+        copy.wait()
+
+    scores_copy.wait()
+
+
+def last_kernel(half, message_ref, grads_ref, ins_ref, block_ref, sum_ref, _, out_ref, total, sem):
+    shard, core = lax.axis_index("dp"), lax.axis_index("tensor")
+    own_half = lax.div(shard, half) == core
+
+    @pl.when(jnp.logical_not(own_half))
+    def _():
+        place = place_of(shard, half, own_half, origins(2 * half)[-1])
+        parts = [(block_ref[...], place)]
+        total[...] = sum_ref[...] + gram_sum(half, message_ref, grads_ref, ins_ref, parts)
+        copy = pltpu.make_async_copy(total, out_ref, sem)
+        copy.start()
+        copy.wait()
 
 
 def gram_of(message, grads, ins, scores, blocks):
     half = len(blocks)
-    return pl.pallas_call(
+    rows = jax.ShapeDtypeStruct((DOCS_DEV, half * DOCS_DEV), jnp.float32)
+    so_far, gram, scores = pl.pallas_call(
         gram_kernel,
-        out_shape=(
-            jax.ShapeDtypeStruct((DOCS_DEV, half * DOCS_DEV), jnp.float32),
-            jax.ShapeDtypeStruct(scores.shape, scores.dtype),
-        ),
-        in_specs=[VMEM] * (4 + half),
-        out_specs=(VMEM, VMEM),
+        out_shape=(rows, rows, jax.ShapeDtypeStruct(scores.shape, scores.dtype)),
+        in_specs=[VMEM] * (3 + half),
+        out_specs=(VMEM, HBM, HBM),
+        scratch_shapes=[pltpu.SemaphoreType.DMA((2,))],
         compiler_params=SMALL,
         name="gram_rows",
-    )(message, grads, ins, scores, *blocks)
+    )(message, grads, ins, scores, *blocks[:-1])
+    gram = pl.pallas_call(
+        functools.partial(last_kernel, half),
+        out_shape=rows,
+        in_specs=[VMEM] * 5 + [HBM],
+        out_specs=HBM,
+        scratch_shapes=[pltpu.VMEM(rows.shape, rows.dtype), pltpu.SemaphoreType.DMA],
+        input_output_aliases={5: 0},
+        compiler_params=SMALL,
+        name="gram_last",
+    )(message, grads, ins, blocks[-1], so_far, gram)
+    return gram, scores
 
 
 def local(inputs, out_grads, proj_in, proj_out, doc_ids, queries):

time: 17.5 us -> 16.4 us (0.937)
  waiting for transfers between devices: 2.99 us -> 2.18 us
  starting transfers between devices: 9.02 us -> 8.84 us
    ppermute x4, waiting for transfers between devices: 2.09 us -> 1.28 us  [local(): lax.ppermute(blocks[what] if what >= 0 else message, ('groups', 'dp', 'te...]
    ppermute x4, starting transfers between devices: 8.51 us -> 8.32 us  [local(): lax.ppermute(blocks[what] if what >= 0 else message, ('groups', 'dp', 'te...]
    pallas_call x1 -> x2, Pallas kernels: 1.1 us -> 1.12 us  [the longest x1 1.11 us: gram_of(): pl.pallas_call(gram_kernel, out_shape=(rows, rows, jax.ShapeDtypeStruct(s...]
  transfers between devices with their start and end apart: 5 -> 5, of which waited for: 4 -> 4; matrix products, arithmetic and copies ran while one was open for 0% -> 0% of each run, Pallas kernels for 3% -> 10%
where the time goes in v13:
time: 16.4 us; the launch traced here: 16.3 us
  starting transfers between devices  8.84 us (54%)
  Pallas kernels  4.58 us (28%)
  waiting for transfers between devices  2.18 us (13%)
  between operations  0.69 us (4%)
    ppermute x4, starting transfers between devices, local(): lax.ppermute(blocks[what] if what >= 0 else message, ('groups', 'dp', 'te...  8.32 us
    pallas_call x1, Pallas kernels, partial_codes(): pl.pallas_call(codes_kernel, out_shape=jax.ShapeDtypeStruct((2 * rank, to...  2.87 us
    ppermute x4, waiting for transfers between devices, local(): lax.ppermute(blocks[what] if what >= 0 else message, ('groups', 'dp', 'te...  1.28 us
    pallas_call x1, Pallas kernels, gram_of(): pl.pallas_call(gram_kernel, out_shape=(rows, rows, jax.ShapeDtypeStruct(s...  1.11 us
    ppermute x1, waiting for transfers between devices, local(): other = lax.ppermute(mine, 'tensor', [(0, 1), (1, 0)])  0.9 us
    ppermute x1, starting transfers between devices, local(): other = lax.ppermute(mine, 'tensor', [(0, 1), (1, 0)])  0.52 us
    pallas_call x1, Pallas kernels, score_docs(): pl.pallas_call(scores_kernel, out_shape=(jax.ShapeDtypeStruct((DOCS_DEV,...  0.46 us
  transfers between devices with their start and end apart: 5, of which 4 were waited for; matrix products, arithmetic and copies ran while one was open for 0% of the time, Pallas kernels for 10%

profile of v13, /device:TPU:0, one launch (start us, length us, event | category | flops | bytes accessed | tf_op | source)
XLA Modules:
  0.0 16.3 jit_solution(12936397450448568458)
XLA Ops:
  0.6 0.0 copy-start.1
  0.6 0.0 copy-start
  0.7 2.9 %partial_codes.1.mine_ref = f32[128,128]{1,0:T(8,128)S(1)} custom-call(bf16[128,7168]{1,0:T(8,128)(2,1)} %x_hbm.1, bf16[128,2048]{1,0:T(8,128)(2,1)} %y_hbm.1, bf16[64,14336]{1,0:T(8,128)(2,1)} %bitcast.2, bf16[64,4096]{1,0:T(8,128)(2,1)} %bitcast.3), custom_call_target="tpu_custom_call" | custom-call | tf_op jit(solution)/shard_map/partial_codes/pallas_call | solution.py:76
  3.5 0.5 %collective-permute-start = (f32[128,128]{1,0:T(8,128)S(1)}, f32[128,128]{1,0:T(8,128)S(1)}, u32[]{:S(2)}, u32[]{:S(2)}) collective-permute-start(f32[128,128]{1,0:T(8,128)S(1)} %partial_codes.1.mine_ref), channel_id=1, source_target_pairs={{0,1},{1,0},{2,3},{3,2},{4,5},{5,4},{6,7},{7,6},{8,9},{9,8},{10,11... | collective-permute-start | bytes 196616 | tf_op jit(solution)/shard_map/ppermute | solution.py:312
  4.0 0.9 %collective-permute-done.other_ref = f32[128,128]{1,0:T(8,128)S(1)} collective-permute-done((f32[128,128]{1,0:T(8,128)S(1)}, f32[128,128]{1,0:T(8,128)S(1)}, u32[]{:S(2)}, u32[]{:S(2)}) %collective-permute-start) | collective-permute-done | bytes 65568 | tf_op jit(solution)/shard_map/ppermute | solution.py:312
  4.9 0.0 copy-done.1
  4.9 0.1 pack_codes.1
  5.1 3.0 %collective-permute-start.1 = (s32[72,128]{1,0:T(8,128)S(1)}, s32[72,128]{1,0:T(8,128)S(1)}, u32[]{:S(2)}, u32[]{:S(2)}) collective-permute-start(s32[72,128]{1,0:T(8,128)S(1)} %get-tuple-element.10.message_ref), channel_id=1, source_target_pairs={{0,4},{1,8},{2,6},{3,10},{4,0},{5,12},{6,2},{7,14},{9,1},{8,13},{1... | collective-permute-start | bytes 110600 | tf_op jit(solution)/shard_map/ppermute | solution.py:327
  8.1 1.5 %collective-permute-start.3 = (s32[72,128]{1,0:T(8,128)S(1)}, s32[72,128]{1,0:T(8,128)S(1)}, u32[]{:S(2)}, u32[]{:S(2)}) collective-permute-start(s32[72,128]{1,0:T(8,128)S(1)} %get-tuple-element.10.message_ref), channel_id=1, source_target_pairs={{0,2},{1,14},{2,0},{3,12},{4,6},{5,10},{6,4},{7,8},{9,7},{8,11},{1... | collective-permute-start | bytes 110600 | tf_op jit(solution)/shard_map/ppermute | solution.py:327
  9.6 0.4 %collective-permute-done.1.refs_0_ = s32[72,128]{1,0:T(8,128)S(1)} collective-permute-done((s32[72,128]{1,0:T(8,128)S(1)}, s32[72,128]{1,0:T(8,128)S(1)}, u32[]{:S(2)}, u32[]{:S(2)}) %collective-permute-start.1) | collective-permute-done | bytes 36896 | tf_op jit(solution)/shard_map/ppermute | solution.py:327
  10.0 2.3 %collective-permute-start.4 = (s32[72,128]{1,0:T(8,128)S(1)}, s32[72,128]{1,0:T(8,128)S(1)}, u32[]{:S(2)}, u32[]{:S(2)}) collective-permute-start(s32[72,128]{1,0:T(8,128)S(1)} %collective-permute-done.1.refs_0_), channel_id=1, source_target_pairs={{0,2},{1,5},{2,0},{3,7},{4,6},{5,1},{6,4},{7,3},{8,12},{9,11},{10,... | collective-permute-start | bytes 110600 | tf_op jit(solution)/shard_map/ppermute | solution.py:327
  12.3 1.5 %collective-permute-start.2 = (s32[72,128]{1,0:T(8,128)S(1)}, s32[72,128]{1,0:T(8,128)S(1)}, u32[]{:S(2)}, u32[]{:S(2)}) collective-permute-start(s32[72,128]{1,0:T(8,128)S(1)} %collective-permute-done.1.refs_0_), channel_id=1, source_target_pairs={{0,16},{1,3},{2,18},{3,1},{4,20},{5,7},{6,22},{7,5},{8,10},{9,25},... | collective-permute-start | bytes 110600 | tf_op jit(solution)/shard_map/ppermute | solution.py:327
  13.9 0.0 copy-done
  13.9 0.5 %score_docs.1 = (f32[8,16]{1,0:T(8,128)S(1)}, bf16[128,256]{1,0:T(8,128)(2,1)S(1)}, bf16[128,256]{1,0:T(8,128)(2,1)S(1)}) custom-call(f32[128,128]{1,0:T(8,128)S(1)} %get-tuple-element.11.own_ref, s32[72,128]{1,0:T(8,128)S(1)} %get-tuple-element.10.message_ref, f32[16,4096]{1,0:T(8,128)S(1)} %copy-done), custom_call_target="tpu_custom_call" | custom-call | flops 67108864 | bytes 524288 | tf_op jit(solution)/shard_map/score_docs/pallas_call | solution.py:179
  14.3 0.0 collective-permute-done.3.refs_1_
  14.3 0.2 %collective-permute-done.4.refs_2_ = s32[72,128]{1,0:T(8,128)S(1)} collective-permute-done((s32[72,128]{1,0:T(8,128)S(1)}, s32[72,128]{1,0:T(8,128)S(1)}, u32[]{:S(2)}, u32[]{:S(2)}) %collective-permute-start.4) | collective-permute-done | bytes 36896 | tf_op jit(solution)/shard_map/ppermute | solution.py:327
  14.5 1.1 %gram_rows.1 = (f32[8,32]{1,0:T(8,128)S(1)}, f32[8,32]{1,0:T(8,128)}, f32[8,16]{1,0:T(8,128)}) custom-call(s32[72,128]{1,0:T(8,128)S(1)} %get-tuple-element.10.message_ref, bf16[128,256]{1,0:T(8,128)(2,1)S(1)} %get-tuple-element.12.grads_ref, bf16[128,256]{1,0:T(8,128)(2,1)S(1)} %get-tuple-element.13.ins_ref, f32[8,16]{1,0:T(8,128)S(1)} %get-tuple-element.14.scores_ref, ...), custom_call_target="tpu_custom_call" | custom-call | tf_op jit(solution)/shard_map/gram_rows/pallas_call | solution.py:286
  15.6 0.7 %collective-permute-done.2.block_ref = s32[72,128]{1,0:T(8,128)S(1)} collective-permute-done((s32[72,128]{1,0:T(8,128)S(1)}, s32[72,128]{1,0:T(8,128)S(1)}, u32[]{:S(2)}, u32[]{:S(2)}) %collective-permute-start.2) | collective-permute-done | bytes 36896 | tf_op jit(solution)/shard_map/ppermute | solution.py:327
  (1 shorter events, 0.0 us)
Async XLA Ops:
  0.6 4.3 %copy-start.1 = (s32[1,128]{1,0:T(1,128)S(1)}, s32[1,128]{1,0:T(1,128)}, u32[]{:S(2)}) copy-start(s32[1,128]{1,0:T(1,128)} %ids_ref.1) | copy-start | bytes 1540
  0.6 13.2 %copy-start = (f32[16,4096]{1,0:T(8,128)S(1)}, f32[16,4096]{1,0:T(8,128)}, u32[]{:S(2)}) copy-start(f32[16,4096]{1,0:T(8,128)} %queries.1) | copy-start | bytes 786436
  3.5 1.4 %collective-permute-start = (f32[128,128]{1,0:T(8,128)S(1)}, f32[128,128]{1,0:T(8,128)S(1)}, u32[]{:S(2)}, u32[]{:S(2)}) collective-permute-start(f32[128,128]{1,0:T(8,128)S(1)} %partial_codes.1.mine_ref), channel_id=1, source_target_pairs={{0,1},{1,0},{2,3},{3,2},{4,5},{5,4},{6,7},{7,6},{8,9},{9,8},{10,11... | collective-permute-start | bytes 196616 | tf_op jit(solution)/shard_map/ppermute | solution.py:312
  5.1 4.9 %collective-permute-start.1 = (s32[72,128]{1,0:T(8,128)S(1)}, s32[72,128]{1,0:T(8,128)S(1)}, u32[]{:S(2)}, u32[]{:S(2)}) collective-permute-start(s32[72,128]{1,0:T(8,128)S(1)} %get-tuple-element.10.message_ref), channel_id=1, source_target_pairs={{0,4},{1,8},{2,6},{3,10},{4,0},{5,12},{6,2},{7,14},{9,1},{8,13},{1... | collective-permute-start | bytes 110600 | tf_op jit(solution)/shard_map/ppermute | solution.py:327
  8.1 6.3 %collective-permute-start.3 = (s32[72,128]{1,0:T(8,128)S(1)}, s32[72,128]{1,0:T(8,128)S(1)}, u32[]{:S(2)}, u32[]{:S(2)}) collective-permute-start(s32[72,128]{1,0:T(8,128)S(1)} %get-tuple-element.10.message_ref), channel_id=1, source_target_pairs={{0,2},{1,14},{2,0},{3,12},{4,6},{5,10},{6,4},{7,8},{9,7},{8,11},{1... | collective-permute-start | bytes 110600 | tf_op jit(solution)/shard_map/ppermute | solution.py:327
  10.0 4.5 %collective-permute-start.4 = (s32[72,128]{1,0:T(8,128)S(1)}, s32[72,128]{1,0:T(8,128)S(1)}, u32[]{:S(2)}, u32[]{:S(2)}) collective-permute-start(s32[72,128]{1,0:T(8,128)S(1)} %collective-permute-done.1.refs_0_), channel_id=1, source_target_pairs={{0,2},{1,5},{2,0},{3,7},{4,6},{5,1},{6,4},{7,3},{8,12},{9,11},{10,... | collective-permute-start | bytes 110600 | tf_op jit(solution)/shard_map/ppermute | solution.py:327
  12.3 4.0 %collective-permute-start.2 = (s32[72,128]{1,0:T(8,128)S(1)}, s32[72,128]{1,0:T(8,128)S(1)}, u32[]{:S(2)}, u32[]{:S(2)}) collective-permute-start(s32[72,128]{1,0:T(8,128)S(1)} %collective-permute-done.1.refs_0_), channel_id=1, source_target_pairs={{0,16},{1,3},{2,18},{3,1},{4,20},{5,7},{6,22},{7,5},{8,10},{9,25},... | collective-permute-start | bytes 110600 | tf_op jit(solution)/shard_map/ppermute | solution.py:327

commit v14 on v13

--- a/solution.py
+++ b/solution.py
@@ -21,8 +21,16 @@
 
 
 def pieces_of(depth):
-    size = next(size for size in (2048, 1792, 1024, 512, 256, 128, depth) if depth % size == 0)
+    size = next(size for size in (1792, 1024, 512, 256, 128, depth) if depth % size == 0)
     return [(at, size) for at in range(0, depth, size)]
+
+
+def weights_of(depth):
+    pieces = pieces_of(depth)
+    return [
+        (at, sum(size for _, size in pieces[n : n + 2])) if n % 2 == 0 else None
+        for n, (at, _) in enumerate(pieces)
+    ]
 
 
 def sum_of(parts):
@@ -44,17 +52,17 @@
 def codes_kernel(x_hbm, y_hbm, wx_hbm, wy_hbm, out_ref, x, y, wx, wy, sems):
     at_core = lax.axis_index("tensor")
     rank = wx.shape[0]
-    jobs = []
+    jobs, sent = [], 0
     for src, w_src, dst, w_dst, row in ((y_hbm, wy_hbm, y, wy, 0), (x_hbm, wx_hbm, x, wx, rank)):
         depth = dst.shape[1]
-        for at, size in pieces_of(depth):
-            there = pl.multiple_of(at_core * depth + at, 128)
-            here = pl.ds(at, size)
-            sem = 2 * len(jobs)
-            copies = (
-                pltpu.make_async_copy(w_src.at[:, pl.ds(there, size)], w_dst.at[:, here], sems.at[sem]),
-                pltpu.make_async_copy(src.at[:, here], dst.at[:, here], sems.at[sem + 1]),
-            )
+        for (at, size), ahead in zip(pieces_of(depth), weights_of(depth)):
+            copies = []
+            if ahead:
+                there = pl.multiple_of(at_core * depth + ahead[0], 128)
+                copies.append((w_src.at[:, pl.ds(there, ahead[1])], w_dst.at[:, pl.ds(*ahead)]))
+            copies.append((src.at[:, pl.ds(at, size)], dst.at[:, pl.ds(at, size)]))
+            copies = [pltpu.make_async_copy(*ends, sems.at[sent + n]) for n, ends in enumerate(copies)]
+            sent += len(copies)
             for copy in copies:
                 copy.start()
             jobs.append((copies, dst, w_dst, row, at, size))
@@ -243,66 +251,71 @@
     return lax.rem(lax.bitwise_xor(shard, jnp.where(own_half, near, far)), half)
 
 
-def gram_kernel(message_ref, grads_ref, ins_ref, scores_ref, *refs):
-    blocks, (sum_ref, out_ref, scores_out_ref, sems) = refs[:-4], refs[-4:]
-    scores_copy = pltpu.make_async_copy(scores_ref, scores_out_ref, sems.at[0])
-    scores_copy.start()
-    half = len(blocks) + 1
+def blocks_at(shard, half, own_half, numbers, refs):
+    parts = []
+    for ref, n in zip(refs, numbers):
+        far, near = origins(2 * half)[n]
+        place = lax.rem(lax.bitwise_xor(shard, jnp.where(own_half, near, far)), half)
+        parts.append((ref[...], place))
+    return parts
+
+
+def position(half):
     shard, core = lax.axis_index("dp"), lax.axis_index("tensor")
-    own_half = lax.div(shard, half) == core
-    found = origins(2 * half)
-    parts = [
-        (block[...], place_of(shard, half, own_half, origin)) for block, origin in zip(blocks, found)
-    ]
+    return shard, lax.div(shard, half) == core
+
+
+def early_kernel(half, numbers, message_ref, grads_ref, ins_ref, *refs):
+    blocks, sum_ref = refs[:-1], refs[-1]
+    shard, own_half = position(half)
+    parts = blocks_at(shard, half, own_half, numbers, blocks)
     parts.append((message_ref[...], jnp.where(own_half, lax.rem(shard, half), -half)))
     sum_ref[...] = gram_sum(half, message_ref, grads_ref, ins_ref, parts)
 
-    @pl.when(own_half)
+
+def finish_kernel(half, numbers, on_own, message_ref, grads_ref, ins_ref, scores_ref, sum_ref, *refs):
+    blocks, (out_ref, scores_out_ref, total, sems) = refs[: len(numbers)], refs[-4:]
+    shard, own_half = position(half)
+
+    @pl.when(own_half if on_own else jnp.logical_not(own_half))
     def _():
-        copy = pltpu.make_async_copy(sum_ref, out_ref, sems.at[1])
+        scores_copy = pltpu.make_async_copy(scores_ref, scores_out_ref, sems.at[0])
+        scores_copy.start()
+        parts = blocks_at(shard, half, own_half, numbers, blocks)
+        total[...] = sum_ref[...] + gram_sum(half, message_ref, grads_ref, ins_ref, parts)
+        copy = pltpu.make_async_copy(total, out_ref, sems.at[1])
         copy.start()
         copy.wait()
-
-    scores_copy.wait()
-
-
-def last_kernel(half, message_ref, grads_ref, ins_ref, block_ref, sum_ref, _, out_ref, total, sem):
-    shard, core = lax.axis_index("dp"), lax.axis_index("tensor")
-    own_half = lax.div(shard, half) == core
-
-    @pl.when(jnp.logical_not(own_half))
-    def _():
-        place = place_of(shard, half, own_half, origins(2 * half)[-1])
-        parts = [(block_ref[...], place)]
-        total[...] = sum_ref[...] + gram_sum(half, message_ref, grads_ref, ins_ref, parts)
-        copy = pltpu.make_async_copy(total, out_ref, sem)
-        copy.start()
-        copy.wait()
+        scores_copy.wait()
 
 
 def gram_of(message, grads, ins, scores, blocks):
     half = len(blocks)
     rows = jax.ShapeDtypeStruct((DOCS_DEV, half * DOCS_DEV), jnp.float32)
-    so_far, gram, scores = pl.pallas_call(
-        gram_kernel,
-        out_shape=(rows, rows, jax.ShapeDtypeStruct(scores.shape, scores.dtype)),
-        in_specs=[VMEM] * (3 + half),
-        out_specs=(VMEM, HBM, HBM),
-        scratch_shapes=[pltpu.SemaphoreType.DMA((2,))],
+    operands = (message, grads, ins)
+    early, late = range(half - 3), [*range(half - 3, half)]
+    so_far = pl.pallas_call(
+        functools.partial(early_kernel, half, early),
+        out_shape=rows,
+        in_specs=[VMEM] * (3 + len(early)),
+        out_specs=VMEM,
         compiler_params=SMALL,
-        name="gram_rows",
-    )(message, grads, ins, scores, *blocks[:-1])
-    gram = pl.pallas_call(
-        functools.partial(last_kernel, half),
-        out_shape=rows,
-        in_specs=[VMEM] * 5 + [HBM],
-        out_specs=HBM,
-        scratch_shapes=[pltpu.VMEM(rows.shape, rows.dtype), pltpu.SemaphoreType.DMA],
-        input_output_aliases={5: 0},
-        compiler_params=SMALL,
-        name="gram_last",
-    )(message, grads, ins, blocks[-1], so_far, gram)
-    return gram, scores
+        name="gram_early",
+    )(*operands, *(blocks[n] for n in early))
+    results = ()
+    for on_own, numbers in ((True, late[:-1]), (False, late)):
+        first = 5 + len(numbers)
+        results = pl.pallas_call(
+            functools.partial(finish_kernel, half, numbers, on_own),
+            out_shape=(rows, jax.ShapeDtypeStruct(scores.shape, scores.dtype)),
+            in_specs=[VMEM] * first + [HBM] * len(results),
+            out_specs=(HBM, HBM),
+            scratch_shapes=[pltpu.VMEM(rows.shape, rows.dtype), pltpu.SemaphoreType.DMA((2,))],
+            input_output_aliases={first + n: n for n in range(len(results))},
+            compiler_params=SMALL,
+            name="gram_own" if on_own else "gram_other",
+        )(*operands, scores, so_far, *(blocks[n] for n in numbers), *results)
+    return results
 
 
 def local(inputs, out_grads, proj_in, proj_out, doc_ids, queries):

time: 16.4 us -> 16.5 us (level)
  Pallas kernels: 4.58 us -> 5.07 us
  waiting for transfers between devices: 2.18 us -> 1.76 us
    pallas_call x2 -> x3, Pallas kernels: 1.12 us -> 1.55 us  [the longest x2 1.1 us: gram_of(): pl.pallas_call(functools.partial(finish_kernel, half, numbers, on_own), o...]
    ppermute x4, waiting for transfers between devices: 1.28 us -> 0.86 us  [local(): lax.ppermute(blocks[what] if what >= 0 else message, ('groups', 'dp', 'te...]
  transfers between devices with their start and end apart: 5 -> 5, of which waited for: 4 -> 3; matrix products, arithmetic and copies ran while one was open for 0% -> 0% of each run, Pallas kernels for 10% -> 12%
where the time goes in v14:
time: 16.5 us; the launch traced here: 16.4 us
  starting transfers between devices  8.84 us (54%)
  Pallas kernels  5.07 us (31%)
  waiting for transfers between devices  1.76 us (11%)
  between operations  0.69 us (4%)
    ppermute x4, starting transfers between devices, local(): lax.ppermute(blocks[what] if what >= 0 else message, ('groups', 'dp', 'te...  8.31 us
    pallas_call x1, Pallas kernels, partial_codes(): pl.pallas_call(codes_kernel, out_shape=jax.ShapeDtypeStruct((2 * rank, to...  2.92 us
    pallas_call x2, Pallas kernels, gram_of(): pl.pallas_call(functools.partial(finish_kernel, half, numbers, on_own), o...  1.1 us
    ppermute x1, waiting for transfers between devices, local(): other = lax.ppermute(mine, 'tensor', [(0, 1), (1, 0)])  0.9 us
    ppermute x4, waiting for transfers between devices, local(): lax.ppermute(blocks[what] if what >= 0 else message, ('groups', 'dp', 'te...  0.86 us
    ppermute x1, starting transfers between devices, local(): other = lax.ppermute(mine, 'tensor', [(0, 1), (1, 0)])  0.52 us
    pallas_call x1, Pallas kernels, score_docs(): pl.pallas_call(scores_kernel, out_shape=(jax.ShapeDtypeStruct((DOCS_DEV,...  0.46 us
    pallas_call x1, Pallas kernels, gram_of(): pl.pallas_call(functools.partial(early_kernel, half, early), out_shape=ro...  0.45 us
  transfers between devices with their start and end apart: 5, of which 3 were waited for; matrix products, arithmetic and copies ran while one was open for 0% of the time, Pallas kernels for 12%

profile of v14, /device:TPU:0, one launch (start us, length us, event | category | flops | bytes accessed | tf_op | source)
XLA Modules:
  0.0 16.4 jit_solution(8531987497488767355)
XLA Ops:
  0.6 0.0 copy-start.1
  0.6 0.0 copy-start
  0.7 2.9 %partial_codes.1.mine_ref = f32[128,128]{1,0:T(8,128)S(1)} custom-call(bf16[128,7168]{1,0:T(8,128)(2,1)} %x_hbm.1, bf16[128,2048]{1,0:T(8,128)(2,1)} %y_hbm.1, bf16[64,14336]{1,0:T(8,128)(2,1)} %bitcast.2, bf16[64,4096]{1,0:T(8,128)(2,1)} %bitcast.3), custom_call_target="tpu_custom_call" | custom-call | tf_op jit(solution)/shard_map/partial_codes/pallas_call | solution.py:84
  3.6 0.5 %collective-permute-start = (f32[128,128]{1,0:T(8,128)S(1)}, f32[128,128]{1,0:T(8,128)S(1)}, u32[]{:S(2)}, u32[]{:S(2)}) collective-permute-start(f32[128,128]{1,0:T(8,128)S(1)} %partial_codes.1.mine_ref), channel_id=1, source_target_pairs={{0,1},{1,0},{2,3},{3,2},{4,5},{5,4},{6,7},{7,6},{8,9},{9,8},{10,11... | collective-permute-start | bytes 196616 | tf_op jit(solution)/shard_map/ppermute | solution.py:325
  4.1 0.9 %collective-permute-done.other_ref = f32[128,128]{1,0:T(8,128)S(1)} collective-permute-done((f32[128,128]{1,0:T(8,128)S(1)}, f32[128,128]{1,0:T(8,128)S(1)}, u32[]{:S(2)}, u32[]{:S(2)}) %collective-permute-start) | collective-permute-done | bytes 65568 | tf_op jit(solution)/shard_map/ppermute | solution.py:325
  5.0 0.0 copy-done.1
  5.0 0.1 pack_codes.1
  5.1 3.0 %collective-permute-start.1 = (s32[72,128]{1,0:T(8,128)S(1)}, s32[72,128]{1,0:T(8,128)S(1)}, u32[]{:S(2)}, u32[]{:S(2)}) collective-permute-start(s32[72,128]{1,0:T(8,128)S(1)} %get-tuple-element.9.message_ref), channel_id=1, source_target_pairs={{0,4},{1,8},{2,6},{3,10},{4,0},{5,12},{6,2},{7,14},{9,1},{8,13},{1... | collective-permute-start | bytes 110600 | tf_op jit(solution)/shard_map/ppermute | solution.py:340
  8.1 1.5 %collective-permute-start.2 = (s32[72,128]{1,0:T(8,128)S(1)}, s32[72,128]{1,0:T(8,128)S(1)}, u32[]{:S(2)}, u32[]{:S(2)}) collective-permute-start(s32[72,128]{1,0:T(8,128)S(1)} %get-tuple-element.9.message_ref), channel_id=1, source_target_pairs={{0,2},{1,14},{2,0},{3,12},{4,6},{5,10},{6,4},{7,8},{9,7},{8,11},{1... | collective-permute-start | bytes 110600 | tf_op jit(solution)/shard_map/ppermute | solution.py:340
  9.6 0.4 %collective-permute-done.1.refs_0_ = s32[72,128]{1,0:T(8,128)S(1)} collective-permute-done((s32[72,128]{1,0:T(8,128)S(1)}, s32[72,128]{1,0:T(8,128)S(1)}, u32[]{:S(2)}, u32[]{:S(2)}) %collective-permute-start.1) | collective-permute-done | bytes 36896 | tf_op jit(solution)/shard_map/ppermute | solution.py:340
  10.1 2.3 %collective-permute-start.3 = (s32[72,128]{1,0:T(8,128)S(1)}, s32[72,128]{1,0:T(8,128)S(1)}, u32[]{:S(2)}, u32[]{:S(2)}) collective-permute-start(s32[72,128]{1,0:T(8,128)S(1)} %collective-permute-done.1.refs_0_), channel_id=1, source_target_pairs={{0,2},{1,5},{2,0},{3,7},{4,6},{5,1},{6,4},{7,3},{8,12},{9,11},{10,... | collective-permute-start | bytes 110600 | tf_op jit(solution)/shard_map/ppermute | solution.py:340
  12.4 1.5 %collective-permute-start.4 = (s32[72,128]{1,0:T(8,128)S(1)}, s32[72,128]{1,0:T(8,128)S(1)}, u32[]{:S(2)}, u32[]{:S(2)}) collective-permute-start(s32[72,128]{1,0:T(8,128)S(1)} %collective-permute-done.1.refs_0_), channel_id=1, source_target_pairs={{0,16},{1,3},{2,18},{3,1},{4,20},{5,7},{6,22},{7,5},{8,10},{9,25},... | collective-permute-start | bytes 110600 | tf_op jit(solution)/shard_map/ppermute | solution.py:340
  13.9 0.0 copy-done
  13.9 0.5 %score_docs.1 = (f32[8,16]{1,0:T(8,128)S(1)}, bf16[128,256]{1,0:T(8,128)(2,1)S(1)}, bf16[128,256]{1,0:T(8,128)(2,1)S(1)}) custom-call(f32[128,128]{1,0:T(8,128)S(1)} %get-tuple-element.10.own_ref, s32[72,128]{1,0:T(8,128)S(1)} %get-tuple-element.9.message_ref, f32[16,4096]{1,0:T(8,128)S(1)} %copy-done), custom_call_target="tpu_custom_call" | custom-call | flops 67108864 | bytes 524288 | tf_op jit(solution)/shard_map/score_docs/pallas_call | solution.py:187
  14.4 0.5 %gram_early.1.sum_ref = f32[8,32]{1,0:T(8,128)S(1)} custom-call(s32[72,128]{1,0:T(8,128)S(1)} %get-tuple-element.9.message_ref, bf16[128,256]{1,0:T(8,128)(2,1)S(1)} %get-tuple-element.11.grads_ref, bf16[128,256]{1,0:T(8,128)(2,1)S(1)} %get-tuple-element.12.ins_ref, s32[72,128]{1,0:T(8,128)S(1)} %collective-permute-done.1.refs_0_), custom_call_target="tpu_custom_call" | custom-call | tf_op jit(solution)/shard_map/gram_early/pallas_call | solution.py:297
  14.8 0.0 collective-permute-done.2.refs_0_
  14.8 0.0 collective-permute-done.3.refs_1_
  14.8 1.1 %gram_own.1 = (f32[8,32]{1,0:T(8,128)}, f32[8,16]{1,0:T(8,128)}) custom-call(s32[72,128]{1,0:T(8,128)S(1)} %get-tuple-element.9.message_ref, bf16[128,256]{1,0:T(8,128)(2,1)S(1)} %get-tuple-element.11.grads_ref, bf16[128,256]{1,0:T(8,128)(2,1)S(1)} %get-tuple-element.12.ins_ref, f32[8,16]{1,0:T(8,128)S(1)} %get-tuple-element.13.scores_ref, ...), custom_call_target="tpu_custom_call" | custom-call | tf_op jit(solution)/shard_map/gram_own/pallas_call | solution.py:308
  15.9 0.4 %collective-permute-done.4.refs_2_ = s32[72,128]{1,0:T(8,128)S(1)} collective-permute-done((s32[72,128]{1,0:T(8,128)S(1)}, s32[72,128]{1,0:T(8,128)S(1)}, u32[]{:S(2)}, u32[]{:S(2)}) %collective-permute-start.4) | collective-permute-done | bytes 36896 | tf_op jit(solution)/shard_map/ppermute | solution.py:340
  (1 shorter events, 0.0 us)
Async XLA Ops:
  0.6 4.4 %copy-start.1 = (s32[1,128]{1,0:T(1,128)S(1)}, s32[1,128]{1,0:T(1,128)}, u32[]{:S(2)}) copy-start(s32[1,128]{1,0:T(1,128)} %ids_ref.1) | copy-start | bytes 1540
  0.6 13.3 %copy-start = (f32[16,4096]{1,0:T(8,128)S(1)}, f32[16,4096]{1,0:T(8,128)}, u32[]{:S(2)}) copy-start(f32[16,4096]{1,0:T(8,128)} %queries.1) | copy-start | bytes 786436
  3.6 1.4 %collective-permute-start = (f32[128,128]{1,0:T(8,128)S(1)}, f32[128,128]{1,0:T(8,128)S(1)}, u32[]{:S(2)}, u32[]{:S(2)}) collective-permute-start(f32[128,128]{1,0:T(8,128)S(1)} %partial_codes.1.mine_ref), channel_id=1, source_target_pairs={{0,1},{1,0},{2,3},{3,2},{4,5},{5,4},{6,7},{7,6},{8,9},{9,8},{10,11... | collective-permute-start | bytes 196616 | tf_op jit(solution)/shard_map/ppermute | solution.py:325
  5.1 4.9 %collective-permute-start.1 = (s32[72,128]{1,0:T(8,128)S(1)}, s32[72,128]{1,0:T(8,128)S(1)}, u32[]{:S(2)}, u32[]{:S(2)}) collective-permute-start(s32[72,128]{1,0:T(8,128)S(1)} %get-tuple-element.9.message_ref), channel_id=1, source_target_pairs={{0,4},{1,8},{2,6},{3,10},{4,0},{5,12},{6,2},{7,14},{9,1},{8,13},{1... | collective-permute-start | bytes 110600 | tf_op jit(solution)/shard_map/ppermute | solution.py:340
  8.1 6.7 %collective-permute-start.2 = (s32[72,128]{1,0:T(8,128)S(1)}, s32[72,128]{1,0:T(8,128)S(1)}, u32[]{:S(2)}, u32[]{:S(2)}) collective-permute-start(s32[72,128]{1,0:T(8,128)S(1)} %get-tuple-element.9.message_ref), channel_id=1, source_target_pairs={{0,2},{1,14},{2,0},{3,12},{4,6},{5,10},{6,4},{7,8},{9,7},{8,11},{1... | collective-permute-start | bytes 110600 | tf_op jit(solution)/shard_map/ppermute | solution.py:340
  10.1 4.8 %collective-permute-start.3 = (s32[72,128]{1,0:T(8,128)S(1)}, s32[72,128]{1,0:T(8,128)S(1)}, u32[]{:S(2)}, u32[]{:S(2)}) collective-permute-start(s32[72,128]{1,0:T(8,128)S(1)} %collective-permute-done.1.refs_0_), channel_id=1, source_target_pairs={{0,2},{1,5},{2,0},{3,7},{4,6},{5,1},{6,4},{7,3},{8,12},{9,11},{10,... | collective-permute-start | bytes 110600 | tf_op jit(solution)/shard_map/ppermute | solution.py:340
  12.4 4.0 %collective-permute-start.4 = (s32[72,128]{1,0:T(8,128)S(1)}, s32[72,128]{1,0:T(8,128)S(1)}, u32[]{:S(2)}, u32[]{:S(2)}) collective-permute-start(s32[72,128]{1,0:T(8,128)S(1)} %collective-permute-done.1.refs_0_), channel_id=1, source_target_pairs={{0,16},{1,3},{2,18},{3,1},{4,20},{5,7},{6,22},{7,5},{8,10},{9,25},... | collective-permute-start | bytes 110600 | tf_op jit(solution)/shard_map/ppermute | solution.py:340

commit v15 on v14

--- a/solution.py
+++ b/solution.py
@@ -21,16 +21,8 @@
 
 
 def pieces_of(depth):
-    size = next(size for size in (1792, 1024, 512, 256, 128, depth) if depth % size == 0)
+    size = next(size for size in (2048, 1792, 1024, 512, 256, 128, depth) if depth % size == 0)
     return [(at, size) for at in range(0, depth, size)]
-
-
-def weights_of(depth):
-    pieces = pieces_of(depth)
-    return [
-        (at, sum(size for _, size in pieces[n : n + 2])) if n % 2 == 0 else None
-        for n, (at, _) in enumerate(pieces)
-    ]
 
 
 def sum_of(parts):
@@ -52,17 +44,17 @@
 def codes_kernel(x_hbm, y_hbm, wx_hbm, wy_hbm, out_ref, x, y, wx, wy, sems):
     at_core = lax.axis_index("tensor")
     rank = wx.shape[0]
-    jobs, sent = [], 0
+    jobs = []
     for src, w_src, dst, w_dst, row in ((y_hbm, wy_hbm, y, wy, 0), (x_hbm, wx_hbm, x, wx, rank)):
         depth = dst.shape[1]
-        for (at, size), ahead in zip(pieces_of(depth), weights_of(depth)):
-            copies = []
-            if ahead:
-                there = pl.multiple_of(at_core * depth + ahead[0], 128)
-                copies.append((w_src.at[:, pl.ds(there, ahead[1])], w_dst.at[:, pl.ds(*ahead)]))
-            copies.append((src.at[:, pl.ds(at, size)], dst.at[:, pl.ds(at, size)]))
-            copies = [pltpu.make_async_copy(*ends, sems.at[sent + n]) for n, ends in enumerate(copies)]
-            sent += len(copies)
+        for at, size in pieces_of(depth):
+            there = pl.multiple_of(at_core * depth + at, 128)
+            here = pl.ds(at, size)
+            sem = 2 * len(jobs)
+            copies = (
+                pltpu.make_async_copy(w_src.at[:, pl.ds(there, size)], w_dst.at[:, here], sems.at[sem]),
+                pltpu.make_async_copy(src.at[:, here], dst.at[:, here], sems.at[sem + 1]),
+            )
             for copy in copies:
                 copy.start()
             jobs.append((copies, dst, w_dst, row, at, size))
@@ -202,16 +194,21 @@
 def plan(shards):
     half = shards // 2
     if half == 4:
-        return [(-1, 4, 2, (1,)), (-1, 7, 1, (1,)), (0, 2, 1, ()), (0, 1, 0, ())]
-    direct = [(-1, half + n, n + 1, ()) for n in range(0, half, 2)]
-    return direct + [(n, 1, 1, ()) for n in reversed(range(half // 2))]
+        return [
+            (-1, (4, 4), (2, 1), (1,)),
+            (-1, (7, 7), (1, 2), (1,)),
+            (0, (2, 1), (1, 2), ()),
+            (0, (1, 2), (2, 1), ()),
+        ]
+    direct = [(-1, (half + n,) * 2, (n + 1,) * 2, ()) for n in range(0, half, 2)]
+    return direct + [(n, (1, 1), (1, 1), ()) for n in reversed(range(half // 2))]
 
 
 def origins(shards):
     found = []
     for what, other, own, _ in plan(shards):
-        before = found[what] if what >= 0 else (0, 0)
-        found.append((before[0] ^ other, before[1] ^ own if own else 0))
+        before = found[what] if what >= 0 else ((0, 0), (0, 0))
+        found.append([[a ^ b for a, b in zip(*pair)] for pair in zip(before, (other, own))])
     return found
 
 
@@ -254,7 +251,7 @@
 def blocks_at(shard, half, own_half, numbers, refs):
     parts = []
     for ref, n in zip(refs, numbers):
-        far, near = origins(2 * half)[n]
+        far, near = (jnp.where(shard < half, *bits) for bits in origins(2 * half)[n])
         place = lax.rem(lax.bitwise_xor(shard, jnp.where(own_half, near, far)), half)
         parts.append((ref[...], place))
     return parts
@@ -325,19 +322,16 @@
     other = lax.ppermute(mine, "tensor", [(0, 1), (1, 0)])
     own, message = pack(mine, other, doc_ids)
     blocks = []
-    groups = lax.axis_size("groups")
     for what, far, near, crossed in plan(shards):
         moves = []
-        for group in range(groups):
-            for s in range(shards):
-                side = s // half
-                for core in range(2):
-                    to = s ^ (near if core == side else far)
-                    to_group = (group + 1) % groups if to == s else group
-                    to_core = core if to // half == side else 1 - core
-                    by = 1 - core if side in crossed else core
-                    moves.append((2 * (shards * group + s) + by, 2 * (shards * to_group + to) + to_core))
-        blocks.append(lax.ppermute(blocks[what] if what >= 0 else message, ("groups", "dp", "tensor"), moves))
+        for s in range(shards):
+            side = s // half
+            for core in range(2):
+                to = s ^ (near if core == side else far)[side]
+                to_core = core if to // half == side else 1 - core
+                by = 1 - core if side in crossed else core
+                moves.append((2 * s + by, 2 * to + to_core))
+        blocks.append(lax.ppermute(blocks[what] if what >= 0 else message, ("dp", "tensor"), moves))
     scores, grads, ins = score_docs(own, message, queries)
     return gram_of(message, grads, ins, scores, blocks)
 

time: 16.5 us -> 16.5 us (level)
  waiting for transfers between devices: 1.76 us -> 2.11 us
  starting transfers between devices: 8.84 us -> 8.5 us
    ppermute x4, waiting for transfers between devices: 0.86 us -> 1.21 us  [local(): lax.ppermute(blocks[what] if what >= 0 else message, ('dp', 'tensor'), mo...]
    ppermute x4, starting transfers between devices: 8.31 us -> 7.98 us  [local(): lax.ppermute(blocks[what] if what >= 0 else message, ('dp', 'tensor'), mo...]
  transfers between devices with their start and end apart: 5 -> 5, of which waited for: 3 -> 4; matrix products, arithmetic and copies ran while one was open for 0% -> 0% of each run, Pallas kernels for 12% -> 12%
where the time goes in v15:
time: 16.5 us; the launch traced here: 16.3 us
  starting transfers between devices  8.5 us (52%)
  Pallas kernels  5.01 us (30%)
  waiting for transfers between devices  2.11 us (13%)
  between operations  0.69 us (4%)
    ppermute x4, starting transfers between devices, local(): lax.ppermute(blocks[what] if what >= 0 else message, ('dp', 'tensor'), mo...  7.98 us
    pallas_call x1, Pallas kernels, partial_codes(): pl.pallas_call(codes_kernel, out_shape=jax.ShapeDtypeStruct((2 * rank, to...  2.87 us
    ppermute x4, waiting for transfers between devices, local(): lax.ppermute(blocks[what] if what >= 0 else message, ('dp', 'tensor'), mo...  1.21 us
    pallas_call x2, Pallas kernels, gram_of(): pl.pallas_call(functools.partial(finish_kernel, half, numbers, on_own), o...  1.09 us
    ppermute x1, waiting for transfers between devices, local(): other = lax.ppermute(mine, 'tensor', [(0, 1), (1, 0)])  0.9 us
    ppermute x1, starting transfers between devices, local(): other = lax.ppermute(mine, 'tensor', [(0, 1), (1, 0)])  0.52 us
    pallas_call x1, Pallas kernels, score_docs(): pl.pallas_call(scores_kernel, out_shape=(jax.ShapeDtypeStruct((DOCS_DEV,...  0.46 us
    pallas_call x1, Pallas kernels, gram_of(): pl.pallas_call(functools.partial(early_kernel, half, early), out_shape=ro...  0.45 us
  transfers between devices with their start and end apart: 5, of which 4 were waited for; matrix products, arithmetic and copies ran while one was open for 0% of the time, Pallas kernels for 12%

profile of v15, /device:TPU:0, one launch (start us, length us, event | category | flops | bytes accessed | tf_op | source)
XLA Modules:
  0.0 16.3 jit_solution(4681972704647631466)
XLA Ops:
  0.6 0.0 copy-start.1
  0.6 0.0 copy-start
  0.7 2.9 %partial_codes.1.mine_ref = f32[128,128]{1,0:T(8,128)S(1)} custom-call(bf16[128,7168]{1,0:T(8,128)(2,1)} %x_hbm.1, bf16[128,2048]{1,0:T(8,128)(2,1)} %y_hbm.1, bf16[64,14336]{1,0:T(8,128)(2,1)} %bitcast.2, bf16[64,4096]{1,0:T(8,128)(2,1)} %bitcast.3), custom_call_target="tpu_custom_call" | custom-call | tf_op jit(solution)/shard_map/partial_codes/pallas_call | solution.py:76
  3.5 0.5 %collective-permute-start = (f32[128,128]{1,0:T(8,128)S(1)}, f32[128,128]{1,0:T(8,128)S(1)}, u32[]{:S(2)}, u32[]{:S(2)}) collective-permute-start(f32[128,128]{1,0:T(8,128)S(1)} %partial_codes.1.mine_ref), channel_id=1, source_target_pairs={{0,1},{1,0},{2,3},{3,2},{4,5},{5,4},{6,7},{7,6},{8,9},{9,8},{10,11... | collective-permute-start | bytes 196616 | tf_op jit(solution)/shard_map/ppermute | solution.py:322
  4.0 0.9 %collective-permute-done.other_ref = f32[128,128]{1,0:T(8,128)S(1)} collective-permute-done((f32[128,128]{1,0:T(8,128)S(1)}, f32[128,128]{1,0:T(8,128)S(1)}, u32[]{:S(2)}, u32[]{:S(2)}) %collective-permute-start) | collective-permute-done | bytes 65568 | tf_op jit(solution)/shard_map/ppermute | solution.py:322
  4.9 0.0 copy-done.1
  4.9 0.1 pack_codes.1
  5.1 3.0 %collective-permute-start.1 = (s32[72,128]{1,0:T(8,128)S(1)}, s32[72,128]{1,0:T(8,128)S(1)}, u32[]{:S(2)}, u32[]{:S(2)}) collective-permute-start(s32[72,128]{1,0:T(8,128)S(1)} %get-tuple-element.9.message_ref), channel_id=1, source_target_pairs={{0,4},{1,8},{2,6},{3,10},{4,0},{5,12},{6,2},{7,14},{9,1},{8,11},{1... | collective-permute-start | bytes 110600 | tf_op jit(solution)/shard_map/ppermute | solution.py:334
  8.1 1.5 %collective-permute-start.2 = (s32[72,128]{1,0:T(8,128)S(1)}, s32[72,128]{1,0:T(8,128)S(1)}, u32[]{:S(2)}, u32[]{:S(2)}) collective-permute-start(s32[72,128]{1,0:T(8,128)S(1)} %get-tuple-element.9.message_ref), channel_id=1, source_target_pairs={{0,2},{1,14},{2,0},{3,12},{4,6},{5,10},{6,4},{7,8},{9,7},{8,13},{1... | collective-permute-start | bytes 110600 | tf_op jit(solution)/shard_map/ppermute | solution.py:334
  9.6 0.4 %collective-permute-done.1.refs_0_ = s32[72,128]{1,0:T(8,128)S(1)} collective-permute-done((s32[72,128]{1,0:T(8,128)S(1)}, s32[72,128]{1,0:T(8,128)S(1)}, u32[]{:S(2)}, u32[]{:S(2)}) %collective-permute-start.1) | collective-permute-done | bytes 36896 | tf_op jit(solution)/shard_map/ppermute | solution.py:334
  10.0 2.3 %collective-permute-start.3 = (s32[72,128]{1,0:T(8,128)S(1)}, s32[72,128]{1,0:T(8,128)S(1)}, u32[]{:S(2)}, u32[]{:S(2)}) collective-permute-start(s32[72,128]{1,0:T(8,128)S(1)} %collective-permute-done.1.refs_0_), channel_id=1, source_target_pairs={{0,2},{1,5},{2,0},{3,7},{4,6},{5,1},{6,4},{7,3},{8,10},{9,13},{10,... | collective-permute-start | bytes 110600 | tf_op jit(solution)/shard_map/ppermute | solution.py:334
  12.3 1.2 %collective-permute-start.4 = (s32[72,128]{1,0:T(8,128)S(1)}, s32[72,128]{1,0:T(8,128)S(1)}, u32[]{:S(2)}, u32[]{:S(2)}) collective-permute-start(s32[72,128]{1,0:T(8,128)S(1)} %collective-permute-done.1.refs_0_), channel_id=1, source_target_pairs={{0,4},{1,3},{2,6},{3,1},{4,0},{5,7},{6,2},{7,5},{8,12},{9,11},{10,... | collective-permute-start | bytes 110600 | tf_op jit(solution)/shard_map/ppermute | solution.py:334
  13.5 0.0 copy-done
  13.5 0.5 %score_docs.1 = (f32[8,16]{1,0:T(8,128)S(1)}, bf16[128,256]{1,0:T(8,128)(2,1)S(1)}, bf16[128,256]{1,0:T(8,128)(2,1)S(1)}) custom-call(f32[128,128]{1,0:T(8,128)S(1)} %get-tuple-element.10.own_ref, s32[72,128]{1,0:T(8,128)S(1)} %get-tuple-element.9.message_ref, f32[16,4096]{1,0:T(8,128)S(1)} %copy-done), custom_call_target="tpu_custom_call" | custom-call | flops 67108864 | bytes 524288 | tf_op jit(solution)/shard_map/score_docs/pallas_call | solution.py:179
  14.0 0.5 %gram_early.1.sum_ref = f32[8,32]{1,0:T(8,128)S(1)} custom-call(s32[72,128]{1,0:T(8,128)S(1)} %get-tuple-element.9.message_ref, bf16[128,256]{1,0:T(8,128)(2,1)S(1)} %get-tuple-element.11.grads_ref, bf16[128,256]{1,0:T(8,128)(2,1)S(1)} %get-tuple-element.12.ins_ref, s32[72,128]{1,0:T(8,128)S(1)} %collective-permute-done.1.refs_0_), custom_call_target="tpu_custom_call" | custom-call | tf_op jit(solution)/shard_map/gram_early/pallas_call | solution.py:294
  14.4 0.0 collective-permute-done.2.refs_0_
  14.4 0.1 collective-permute-done.3.refs_1_
  14.5 1.1 %gram_own.1 = (f32[8,32]{1,0:T(8,128)}, f32[8,16]{1,0:T(8,128)}) custom-call(s32[72,128]{1,0:T(8,128)S(1)} %get-tuple-element.9.message_ref, bf16[128,256]{1,0:T(8,128)(2,1)S(1)} %get-tuple-element.11.grads_ref, bf16[128,256]{1,0:T(8,128)(2,1)S(1)} %get-tuple-element.12.ins_ref, f32[8,16]{1,0:T(8,128)S(1)} %get-tuple-element.13.scores_ref, ...), custom_call_target="tpu_custom_call" | custom-call | tf_op jit(solution)/shard_map/gram_own/pallas_call | solution.py:305
  15.6 0.7 %collective-permute-done.4.refs_2_ = s32[72,128]{1,0:T(8,128)S(1)} collective-permute-done((s32[72,128]{1,0:T(8,128)S(1)}, s32[72,128]{1,0:T(8,128)S(1)}, u32[]{:S(2)}, u32[]{:S(2)}) %collective-permute-start.4) | collective-permute-done | bytes 36896 | tf_op jit(solution)/shard_map/ppermute | solution.py:334
  (1 shorter events, 0.0 us)
Async XLA Ops:
  0.6 4.3 %copy-start.1 = (s32[1,128]{1,0:T(1,128)S(1)}, s32[1,128]{1,0:T(1,128)}, u32[]{:S(2)}) copy-start(s32[1,128]{1,0:T(1,128)} %ids_ref.1) | copy-start | bytes 1540
  0.6 12.9 %copy-start = (f32[16,4096]{1,0:T(8,128)S(1)}, f32[16,4096]{1,0:T(8,128)}, u32[]{:S(2)}) copy-start(f32[16,4096]{1,0:T(8,128)} %queries.1) | copy-start | bytes 786436
  3.5 1.4 %collective-permute-start = (f32[128,128]{1,0:T(8,128)S(1)}, f32[128,128]{1,0:T(8,128)S(1)}, u32[]{:S(2)}, u32[]{:S(2)}) collective-permute-start(f32[128,128]{1,0:T(8,128)S(1)} %partial_codes.1.mine_ref), channel_id=1, source_target_pairs={{0,1},{1,0},{2,3},{3,2},{4,5},{5,4},{6,7},{7,6},{8,9},{9,8},{10,11... | collective-permute-start | bytes 196616 | tf_op jit(solution)/shard_map/ppermute | solution.py:322
  5.1 4.9 %collective-permute-start.1 = (s32[72,128]{1,0:T(8,128)S(1)}, s32[72,128]{1,0:T(8,128)S(1)}, u32[]{:S(2)}, u32[]{:S(2)}) collective-permute-start(s32[72,128]{1,0:T(8,128)S(1)} %get-tuple-element.9.message_ref), channel_id=1, source_target_pairs={{0,4},{1,8},{2,6},{3,10},{4,0},{5,12},{6,2},{7,14},{9,1},{8,11},{1... | collective-permute-start | bytes 110600 | tf_op jit(solution)/shard_map/ppermute | solution.py:334
  8.1 6.4 %collective-permute-start.2 = (s32[72,128]{1,0:T(8,128)S(1)}, s32[72,128]{1,0:T(8,128)S(1)}, u32[]{:S(2)}, u32[]{:S(2)}) collective-permute-start(s32[72,128]{1,0:T(8,128)S(1)} %get-tuple-element.9.message_ref), channel_id=1, source_target_pairs={{0,2},{1,14},{2,0},{3,12},{4,6},{5,10},{6,4},{7,8},{9,7},{8,13},{1... | collective-permute-start | bytes 110600 | tf_op jit(solution)/shard_map/ppermute | solution.py:334
  10.0 4.5 %collective-permute-start.3 = (s32[72,128]{1,0:T(8,128)S(1)}, s32[72,128]{1,0:T(8,128)S(1)}, u32[]{:S(2)}, u32[]{:S(2)}) collective-permute-start(s32[72,128]{1,0:T(8,128)S(1)} %collective-permute-done.1.refs_0_), channel_id=1, source_target_pairs={{0,2},{1,5},{2,0},{3,7},{4,6},{5,1},{6,4},{7,3},{8,10},{9,13},{10,... | collective-permute-start | bytes 110600 | tf_op jit(solution)/shard_map/ppermute | solution.py:334
  12.3 4.0 %collective-permute-start.4 = (s32[72,128]{1,0:T(8,128)S(1)}, s32[72,128]{1,0:T(8,128)S(1)}, u32[]{:S(2)}, u32[]{:S(2)}) collective-permute-start(s32[72,128]{1,0:T(8,128)S(1)} %collective-permute-done.1.refs_0_), channel_id=1, source_target_pairs={{0,4},{1,3},{2,6},{3,1},{4,0},{5,7},{6,2},{7,5},{8,12},{9,11},{10,... | collective-permute-start | bytes 110600 | tf_op jit(solution)/shard_map/ppermute | solution.py:334

commit v16 on v15

--- a/solution.py
+++ b/solution.py
@@ -195,9 +195,9 @@
     half = shards // 2
     if half == 4:
         return [
-            (-1, (4, 4), (2, 1), (1,)),
-            (-1, (7, 7), (1, 2), (1,)),
-            (0, (2, 1), (1, 2), ()),
+            (-1, (4, 4), (1, 1), (1,)),
+            (-1, (7, 7), (2, 2), (1,)),
+            (0, (2, 1), (2, 2), ()),
             (0, (1, 2), (2, 1), ()),
         ]
     direct = [(-1, (half + n,) * 2, (n + 1,) * 2, ()) for n in range(0, half, 2)]
@@ -270,27 +270,45 @@
     sum_ref[...] = gram_sum(half, message_ref, grads_ref, ins_ref, parts)
 
 
-def finish_kernel(half, numbers, on_own, message_ref, grads_ref, ins_ref, scores_ref, sum_ref, *refs):
-    blocks, (out_ref, scores_out_ref, total, sems) = refs[: len(numbers)], refs[-4:]
+def write_out(total_ref, scores_ref, out_ref, scores_out_ref, sems):
+    copies = (
+        pltpu.make_async_copy(scores_ref, scores_out_ref, sems.at[0]),
+        pltpu.make_async_copy(total_ref, out_ref, sems.at[1]),
+    )
+    for copy in copies:
+        copy.start()
+    for copy in copies:
+        copy.wait()
+
+
+def middle_kernel(half, numbers, message_ref, grads_ref, ins_ref, scores_ref, sum_ref, *refs):
+    blocks, (out_ref, scores_out_ref, total_ref, sems) = refs[:-4], refs[-4:]
     shard, own_half = position(half)
-
-    @pl.when(own_half if on_own else jnp.logical_not(own_half))
+    parts = blocks_at(shard, half, own_half, numbers, blocks)
+    total_ref[...] = sum_ref[...] + gram_sum(half, message_ref, grads_ref, ins_ref, parts)
+
+    @pl.when(own_half)
     def _():
-        scores_copy = pltpu.make_async_copy(scores_ref, scores_out_ref, sems.at[0])
-        scores_copy.start()
-        parts = blocks_at(shard, half, own_half, numbers, blocks)
-        total[...] = sum_ref[...] + gram_sum(half, message_ref, grads_ref, ins_ref, parts)
-        copy = pltpu.make_async_copy(total, out_ref, sems.at[1])
-        copy.start()
-        copy.wait()
-        scores_copy.wait()
+        write_out(total_ref, scores_ref, out_ref, scores_out_ref, sems)
+
+
+def last_kernel(half, message_ref, grads_ref, ins_ref, scores_ref, sum_ref, block_ref, *refs):
+    out_ref, scores_out_ref, total_ref, sems = refs[-4:]
+    shard, own_half = position(half)
+
+    @pl.when(jnp.logical_not(own_half))
+    def _():
+        parts = blocks_at(shard, half, own_half, [half - 1], [block_ref])
+        total_ref[...] = sum_ref[...] + gram_sum(half, message_ref, grads_ref, ins_ref, parts)
+        write_out(total_ref, scores_ref, out_ref, scores_out_ref, sems)
 
 
 def gram_of(message, grads, ins, scores, blocks):
     half = len(blocks)
     rows = jax.ShapeDtypeStruct((DOCS_DEV, half * DOCS_DEV), jnp.float32)
+    results = (rows, jax.ShapeDtypeStruct(scores.shape, scores.dtype))
     operands = (message, grads, ins)
-    early, late = range(half - 3), [*range(half - 3, half)]
+    early, middle = range(half - 3), range(half - 3, half - 1)
     so_far = pl.pallas_call(
         functools.partial(early_kernel, half, early),
         out_shape=rows,
@@ -299,20 +317,25 @@
         compiler_params=SMALL,
         name="gram_early",
     )(*operands, *(blocks[n] for n in early))
-    results = ()
-    for on_own, numbers in ((True, late[:-1]), (False, late)):
-        first = 5 + len(numbers)
-        results = pl.pallas_call(
-            functools.partial(finish_kernel, half, numbers, on_own),
-            out_shape=(rows, jax.ShapeDtypeStruct(scores.shape, scores.dtype)),
-            in_specs=[VMEM] * first + [HBM] * len(results),
-            out_specs=(HBM, HBM),
-            scratch_shapes=[pltpu.VMEM(rows.shape, rows.dtype), pltpu.SemaphoreType.DMA((2,))],
-            input_output_aliases={first + n: n for n in range(len(results))},
-            compiler_params=SMALL,
-            name="gram_own" if on_own else "gram_other",
-        )(*operands, scores, so_far, *(blocks[n] for n in numbers), *results)
-    return results
+    *results_own, so_far = pl.pallas_call(
+        functools.partial(middle_kernel, half, middle),
+        out_shape=(*results, rows),
+        in_specs=[VMEM] * (5 + len(middle)),
+        out_specs=(HBM, HBM, VMEM),
+        scratch_shapes=[pltpu.SemaphoreType.DMA((2,))],
+        compiler_params=SMALL,
+        name="gram_middle",
+    )(*operands, scores, so_far, *(blocks[n] for n in middle))
+    return pl.pallas_call(
+        functools.partial(last_kernel, half),
+        out_shape=results,
+        in_specs=[VMEM] * 6 + [HBM] * 2,
+        out_specs=(HBM, HBM),
+        scratch_shapes=[pltpu.VMEM(rows.shape, rows.dtype), pltpu.SemaphoreType.DMA((2,))],
+        input_output_aliases={6: 0, 7: 1},
+        compiler_params=SMALL,
+        name="gram_last",
+    )(*operands, scores, so_far, blocks[-1], *results_own)
 
 
 def local(inputs, out_grads, proj_in, proj_out, doc_ids, queries):

time: 16.5 us -> 16.3 us (0.988)
  starting transfers between devices: 8.5 us -> 7.12 us
  waiting for transfers between devices: 2.11 us -> 3.18 us
    ppermute x4, starting transfers between devices: 7.98 us -> 6.6 us  [local(): lax.ppermute(blocks[what] if what >= 0 else message, ('dp', 'tensor'), mo...]
    ppermute x4, waiting for transfers between devices: 1.21 us -> 2.27 us  [local(): lax.ppermute(blocks[what] if what >= 0 else message, ('dp', 'tensor'), mo...]
where the time goes in v16:
time: 16.3 us; the launch traced here: 16 us
  starting transfers between devices  7.12 us (44%)
  Pallas kernels  5.01 us (31%)
  waiting for transfers between devices  3.18 us (20%)
  between operations  0.69 us (4%)
    ppermute x4, starting transfers between devices, local(): lax.ppermute(blocks[what] if what >= 0 else message, ('dp', 'tensor'), mo...  6.6 us
    pallas_call x1, Pallas kernels, partial_codes(): pl.pallas_call(codes_kernel, out_shape=jax.ShapeDtypeStruct((2 * rank, to...  2.87 us
    ppermute x4, waiting for transfers between devices, local(): lax.ppermute(blocks[what] if what >= 0 else message, ('dp', 'tensor'), mo...  2.27 us
    pallas_call x1, Pallas kernels, gram_of(): pl.pallas_call(functools.partial(middle_kernel, half, middle), out_shape=...  1.07 us
    ppermute x1, waiting for transfers between devices, local(): other = lax.ppermute(mine, 'tensor', [(0, 1), (1, 0)])  0.9 us
    ppermute x1, starting transfers between devices, local(): other = lax.ppermute(mine, 'tensor', [(0, 1), (1, 0)])  0.52 us
    pallas_call x1, Pallas kernels, score_docs(): pl.pallas_call(scores_kernel, out_shape=(jax.ShapeDtypeStruct((DOCS_DEV,...  0.47 us
    pallas_call x1, Pallas kernels, gram_of(): pl.pallas_call(functools.partial(early_kernel, half, early), out_shape=ro...  0.45 us
  transfers between devices with their start and end apart: 5, of which 4 were waited for; matrix products, arithmetic and copies ran while one was open for 0% of the time, Pallas kernels for 12%

profile of v16, /device:TPU:0, one launch (start us, length us, event | category | flops | bytes accessed | tf_op | source)
XLA Modules:
  0.0 16.0 jit_solution(2362984904535358725)
XLA Ops:
  0.6 0.0 copy-start.1
  0.6 0.0 copy-start
  0.7 2.9 %partial_codes.1.mine_ref = f32[128,128]{1,0:T(8,128)S(1)} custom-call(bf16[128,7168]{1,0:T(8,128)(2,1)} %x_hbm.1, bf16[128,2048]{1,0:T(8,128)(2,1)} %y_hbm.1, bf16[64,14336]{1,0:T(8,128)(2,1)} %bitcast.2, bf16[64,4096]{1,0:T(8,128)(2,1)} %bitcast.3), custom_call_target="tpu_custom_call" | custom-call | tf_op jit(solution)/shard_map/partial_codes/pallas_call | solution.py:76
  3.5 0.5 %collective-permute-start = (f32[128,128]{1,0:T(8,128)S(1)}, f32[128,128]{1,0:T(8,128)S(1)}, u32[]{:S(2)}, u32[]{:S(2)}) collective-permute-start(f32[128,128]{1,0:T(8,128)S(1)} %partial_codes.1.mine_ref), channel_id=1, source_target_pairs={{0,1},{1,0},{2,3},{3,2},{4,5},{5,4},{6,7},{7,6},{8,9},{9,8},{10,11... | collective-permute-start | bytes 196616 | tf_op jit(solution)/shard_map/ppermute | solution.py:345
  4.0 0.9 %collective-permute-done.other_ref = f32[128,128]{1,0:T(8,128)S(1)} collective-permute-done((f32[128,128]{1,0:T(8,128)S(1)}, f32[128,128]{1,0:T(8,128)S(1)}, u32[]{:S(2)}, u32[]{:S(2)}) %collective-permute-start) | collective-permute-done | bytes 65568 | tf_op jit(solution)/shard_map/ppermute | solution.py:345
  4.9 0.0 copy-done.1
  4.9 0.1 pack_codes.1
  5.1 2.9 %collective-permute-start.1 = (s32[72,128]{1,0:T(8,128)S(1)}, s32[72,128]{1,0:T(8,128)S(1)}, u32[]{:S(2)}, u32[]{:S(2)}) collective-permute-start(s32[72,128]{1,0:T(8,128)S(1)} %get-tuple-element.10.message_ref), channel_id=1, source_target_pairs={{0,2},{1,8},{2,0},{3,10},{4,6},{5,12},{6,4},{7,14},{9,1},{8,11},{1... | collective-permute-start | bytes 110600 | tf_op jit(solution)/shard_map/ppermute | solution.py:357
  8.0 1.6 %collective-permute-start.2 = (s32[72,128]{1,0:T(8,128)S(1)}, s32[72,128]{1,0:T(8,128)S(1)}, u32[]{:S(2)}, u32[]{:S(2)}) collective-permute-start(s32[72,128]{1,0:T(8,128)S(1)} %get-tuple-element.10.message_ref), channel_id=1, source_target_pairs={{0,4},{1,14},{2,6},{3,12},{4,0},{5,10},{6,2},{7,8},{9,7},{8,13},{1... | collective-permute-start | bytes 110600 | tf_op jit(solution)/shard_map/ppermute | solution.py:357
  9.6 0.4 %collective-permute-done.1.refs_0_ = s32[72,128]{1,0:T(8,128)S(1)} collective-permute-done((s32[72,128]{1,0:T(8,128)S(1)}, s32[72,128]{1,0:T(8,128)S(1)}, u32[]{:S(2)}, u32[]{:S(2)}) %collective-permute-start.1) | collective-permute-done | bytes 36896 | tf_op jit(solution)/shard_map/ppermute | solution.py:357
  9.9 2.1 %collective-permute-start.3 = (s32[72,128]{1,0:T(8,128)S(1)}, s32[72,128]{1,0:T(8,128)S(1)}, u32[]{:S(2)}, u32[]{:S(2)}) collective-permute-start(s32[72,128]{1,0:T(8,128)S(1)} %collective-permute-done.1.refs_0_), channel_id=1, source_target_pairs={{0,4},{1,5},{2,6},{3,7},{4,0},{5,1},{6,2},{7,3},{8,10},{9,13},{10,... | collective-permute-start | bytes 110600 | tf_op jit(solution)/shard_map/ppermute | solution.py:357
  12.0 0.0 collective-permute-start.4
  12.1 0.0 copy-done
  12.1 0.5 %score_docs.1 = (f32[8,16]{1,0:T(8,128)S(1)}, bf16[128,256]{1,0:T(8,128)(2,1)S(1)}, bf16[128,256]{1,0:T(8,128)(2,1)S(1)}) custom-call(f32[128,128]{1,0:T(8,128)S(1)} %get-tuple-element.11.own_ref, s32[72,128]{1,0:T(8,128)S(1)} %get-tuple-element.10.message_ref, f32[16,4096]{1,0:T(8,128)S(1)} %copy-done), custom_call_target="tpu_custom_call" | custom-call | flops 67108864 | bytes 524288 | tf_op jit(solution)/shard_map/score_docs/pallas_call | solution.py:179
  12.5 0.5 %gram_early.1.sum_ref = f32[8,32]{1,0:T(8,128)S(1)} custom-call(s32[72,128]{1,0:T(8,128)S(1)} %get-tuple-element.10.message_ref, bf16[128,256]{1,0:T(8,128)(2,1)S(1)} %get-tuple-element.12.grads_ref, bf16[128,256]{1,0:T(8,128)(2,1)S(1)} %get-tuple-element.13.ins_ref, s32[72,128]{1,0:T(8,128)S(1)} %collective-permute-done.1.refs_0_), custom_call_target="tpu_custom_call" | custom-call | tf_op jit(solution)/shard_map/gram_early/pallas_call | solution.py:312
  13.0 0.0 collective-permute-done.2.refs_0_
  13.0 1.0 %collective-permute-done.3.refs_1_ = s32[72,128]{1,0:T(8,128)S(1)} collective-permute-done((s32[72,128]{1,0:T(8,128)S(1)}, s32[72,128]{1,0:T(8,128)S(1)}, u32[]{:S(2)}, u32[]{:S(2)}) %collective-permute-start.3) | collective-permute-done | bytes 36896 | tf_op jit(solution)/shard_map/ppermute | solution.py:357
  14.0 1.1 %gram_middle.1 = (f32[8,32]{1,0:T(8,128)}, f32[8,16]{1,0:T(8,128)}, f32[8,32]{1,0:T(8,128)S(1)}) custom-call(s32[72,128]{1,0:T(8,128)S(1)} %get-tuple-element.10.message_ref, bf16[128,256]{1,0:T(8,128)(2,1)S(1)} %get-tuple-element.12.grads_ref, bf16[128,256]{1,0:T(8,128)(2,1)S(1)} %get-tuple-element.13.ins_ref, f32[8,16]{1,0:T(8,128)S(1)} %get-tuple-element.14.scores_ref, ...), custom_call_target="tpu_custom_call" | custom-call | tf_op jit(solution)/shard_map/gram_middle/pallas_call | solution.py:320
  15.0 0.9 %collective-permute-done.4.block_ref = s32[72,128]{1,0:T(8,128)S(1)} collective-permute-done((s32[72,128]{1,0:T(8,128)S(1)}, s32[72,128]{1,0:T(8,128)S(1)}, u32[]{:S(2)}, u32[]{:S(2)}) %collective-permute-start.4) | collective-permute-done | bytes 36896 | tf_op jit(solution)/shard_map/ppermute | solution.py:357
  (1 shorter events, 0.0 us)
Async XLA Ops:
  0.6 4.3 %copy-start.1 = (s32[1,128]{1,0:T(1,128)S(1)}, s32[1,128]{1,0:T(1,128)}, u32[]{:S(2)}) copy-start(s32[1,128]{1,0:T(1,128)} %ids_ref.1) | copy-start | bytes 1540
  0.6 11.4 %copy-start = (f32[16,4096]{1,0:T(8,128)S(1)}, f32[16,4096]{1,0:T(8,128)}, u32[]{:S(2)}) copy-start(f32[16,4096]{1,0:T(8,128)} %queries.1) | copy-start | bytes 786436
  3.5 1.4 %collective-permute-start = (f32[128,128]{1,0:T(8,128)S(1)}, f32[128,128]{1,0:T(8,128)S(1)}, u32[]{:S(2)}, u32[]{:S(2)}) collective-permute-start(f32[128,128]{1,0:T(8,128)S(1)} %partial_codes.1.mine_ref), channel_id=1, source_target_pairs={{0,1},{1,0},{2,3},{3,2},{4,5},{5,4},{6,7},{7,6},{8,9},{9,8},{10,11... | collective-permute-start | bytes 196616 | tf_op jit(solution)/shard_map/ppermute | solution.py:345
  5.1 4.8 %collective-permute-start.1 = (s32[72,128]{1,0:T(8,128)S(1)}, s32[72,128]{1,0:T(8,128)S(1)}, u32[]{:S(2)}, u32[]{:S(2)}) collective-permute-start(s32[72,128]{1,0:T(8,128)S(1)} %get-tuple-element.10.message_ref), channel_id=1, source_target_pairs={{0,2},{1,8},{2,0},{3,10},{4,6},{5,12},{6,4},{7,14},{9,1},{8,11},{1... | collective-permute-start | bytes 110600 | tf_op jit(solution)/shard_map/ppermute | solution.py:357
  8.0 5.0 %collective-permute-start.2 = (s32[72,128]{1,0:T(8,128)S(1)}, s32[72,128]{1,0:T(8,128)S(1)}, u32[]{:S(2)}, u32[]{:S(2)}) collective-permute-start(s32[72,128]{1,0:T(8,128)S(1)} %get-tuple-element.10.message_ref), channel_id=1, source_target_pairs={{0,4},{1,14},{2,6},{3,12},{4,0},{5,10},{6,2},{7,8},{9,7},{8,13},{1... | collective-permute-start | bytes 110600 | tf_op jit(solution)/shard_map/ppermute | solution.py:357
  9.9 4.0 %collective-permute-start.3 = (s32[72,128]{1,0:T(8,128)S(1)}, s32[72,128]{1,0:T(8,128)S(1)}, u32[]{:S(2)}, u32[]{:S(2)}) collective-permute-start(s32[72,128]{1,0:T(8,128)S(1)} %collective-permute-done.1.refs_0_), channel_id=1, source_target_pairs={{0,4},{1,5},{2,6},{3,7},{4,0},{5,1},{6,2},{7,3},{8,10},{9,13},{10,... | collective-permute-start | bytes 110600 | tf_op jit(solution)/shard_map/ppermute | solution.py:357
  12.0 4.0 %collective-permute-start.4 = (s32[72,128]{1,0:T(8,128)S(1)}, s32[72,128]{1,0:T(8,128)S(1)}, u32[]{:S(2)}, u32[]{:S(2)}) collective-permute-start(s32[72,128]{1,0:T(8,128)S(1)} %collective-permute-done.1.refs_0_), channel_id=1, source_target_pairs={{0,4},{1,3},{2,6},{3,1},{4,0},{5,7},{6,2},{7,5},{8,12},{9,11},{10,... | collective-permute-start | bytes 110600 | tf_op jit(solution)/shard_map/ppermute | solution.py:357

commit v17 on v15

--- a/solution.py
+++ b/solution.py
@@ -21,8 +21,9 @@
 
 
 def pieces_of(depth):
-    size = next(size for size in (2048, 1792, 1024, 512, 256, 128, depth) if depth % size == 0)
-    return [(at, size) for at in range(0, depth, size)]
+    count = -(-depth // 2432)
+    size = -(-depth // (count * 128)) * 128
+    return [(at, min(size, depth - at)) for at in range(0, depth, size)]
 
 
 def sum_of(parts):
@@ -195,9 +196,9 @@
     half = shards // 2
     if half == 4:
         return [
-            (-1, (4, 4), (2, 1), (1,)),
-            (-1, (7, 7), (1, 2), (1,)),
-            (0, (2, 1), (1, 2), ()),
+            (-1, (4, 4), (1, 1), (1,)),
+            (-1, (7, 7), (2, 2), (1,)),
+            (0, (2, 1), (2, 2), ()),
             (0, (1, 2), (2, 1), ()),
         ]
     direct = [(-1, (half + n,) * 2, (n + 1,) * 2, ()) for n in range(0, half, 2)]

time: 16.5 us -> 16.3 us (0.988)
  starting transfers between devices: 8.5 us -> 7.13 us
  waiting for transfers between devices: 2.11 us -> 3.17 us
    ppermute x4, starting transfers between devices: 7.98 us -> 6.61 us  [local(): lax.ppermute(blocks[what] if what >= 0 else message, ('dp', 'tensor'), mo...]
    ppermute x4, waiting for transfers between devices: 1.21 us -> 2.27 us  [local(): lax.ppermute(blocks[what] if what >= 0 else message, ('dp', 'tensor'), mo...]
where the time goes in v17:
time: 16.3 us; the launch traced here: 16 us
  starting transfers between devices  7.13 us (44%)
  Pallas kernels  4.96 us (30%)
  waiting for transfers between devices  3.17 us (19%)
  between operations  0.69 us (4%)
    ppermute x4, starting transfers between devices, local(): lax.ppermute(blocks[what] if what >= 0 else message, ('dp', 'tensor'), mo...  6.61 us
    pallas_call x1, Pallas kernels, partial_codes(): pl.pallas_call(codes_kernel, out_shape=jax.ShapeDtypeStruct((2 * rank, to...  2.81 us
    ppermute x4, waiting for transfers between devices, local(): lax.ppermute(blocks[what] if what >= 0 else message, ('dp', 'tensor'), mo...  2.27 us
    pallas_call x2, Pallas kernels, gram_of(): pl.pallas_call(functools.partial(finish_kernel, half, numbers, on_own), o...  1.09 us
    ppermute x1, waiting for transfers between devices, local(): other = lax.ppermute(mine, 'tensor', [(0, 1), (1, 0)])  0.9 us
    ppermute x1, starting transfers between devices, local(): other = lax.ppermute(mine, 'tensor', [(0, 1), (1, 0)])  0.52 us
    pallas_call x1, Pallas kernels, score_docs(): pl.pallas_call(scores_kernel, out_shape=(jax.ShapeDtypeStruct((DOCS_DEV,...  0.47 us
    pallas_call x1, Pallas kernels, gram_of(): pl.pallas_call(functools.partial(early_kernel, half, early), out_shape=ro...  0.45 us
  transfers between devices with their start and end apart: 5, of which 4 were waited for; matrix products, arithmetic and copies ran while one was open for 0% of the time, Pallas kernels for 12%

profile of v17, /device:TPU:0, one launch (start us, length us, event | category | flops | bytes accessed | tf_op | source)
XLA Modules:
  0.0 16.0 jit_solution(5017046302361791864)
XLA Ops:
  0.6 0.0 copy-start.1
  0.6 0.0 copy-start
  0.7 2.8 %partial_codes.1.mine_ref = f32[128,128]{1,0:T(8,128)S(1)} custom-call(bf16[128,7168]{1,0:T(8,128)(2,1)} %x_hbm.1, bf16[128,2048]{1,0:T(8,128)(2,1)} %y_hbm.1, bf16[64,14336]{1,0:T(8,128)(2,1)} %bitcast.2, bf16[64,4096]{1,0:T(8,128)(2,1)} %bitcast.3), custom_call_target="tpu_custom_call" | custom-call | tf_op jit(solution)/shard_map/partial_codes/pallas_call | solution.py:77
  3.5 0.5 %collective-permute-start = (f32[128,128]{1,0:T(8,128)S(1)}, f32[128,128]{1,0:T(8,128)S(1)}, u32[]{:S(2)}, u32[]{:S(2)}) collective-permute-start(f32[128,128]{1,0:T(8,128)S(1)} %partial_codes.1.mine_ref), channel_id=1, source_target_pairs={{0,1},{1,0},{2,3},{3,2},{4,5},{5,4},{6,7},{7,6},{8,9},{9,8},{10,11... | collective-permute-start | bytes 196616 | tf_op jit(solution)/shard_map/ppermute | solution.py:323
  4.0 0.9 %collective-permute-done.other_ref = f32[128,128]{1,0:T(8,128)S(1)} collective-permute-done((f32[128,128]{1,0:T(8,128)S(1)}, f32[128,128]{1,0:T(8,128)S(1)}, u32[]{:S(2)}, u32[]{:S(2)}) %collective-permute-start) | collective-permute-done | bytes 65568 | tf_op jit(solution)/shard_map/ppermute | solution.py:323
  4.9 0.0 copy-done.1
  4.9 0.1 pack_codes.1
  5.0 2.9 %collective-permute-start.1 = (s32[72,128]{1,0:T(8,128)S(1)}, s32[72,128]{1,0:T(8,128)S(1)}, u32[]{:S(2)}, u32[]{:S(2)}) collective-permute-start(s32[72,128]{1,0:T(8,128)S(1)} %get-tuple-element.9.message_ref), channel_id=1, source_target_pairs={{0,2},{1,8},{2,0},{3,10},{4,6},{5,12},{6,4},{7,14},{9,1},{8,11},{1... | collective-permute-start | bytes 110600 | tf_op jit(solution)/shard_map/ppermute | solution.py:335
  7.9 1.6 %collective-permute-start.2 = (s32[72,128]{1,0:T(8,128)S(1)}, s32[72,128]{1,0:T(8,128)S(1)}, u32[]{:S(2)}, u32[]{:S(2)}) collective-permute-start(s32[72,128]{1,0:T(8,128)S(1)} %get-tuple-element.9.message_ref), channel_id=1, source_target_pairs={{0,4},{1,14},{2,6},{3,12},{4,0},{5,10},{6,2},{7,8},{9,7},{8,13},{1... | collective-permute-start | bytes 110600 | tf_op jit(solution)/shard_map/ppermute | solution.py:335
  9.5 0.4 %collective-permute-done.1.refs_0_ = s32[72,128]{1,0:T(8,128)S(1)} collective-permute-done((s32[72,128]{1,0:T(8,128)S(1)}, s32[72,128]{1,0:T(8,128)S(1)}, u32[]{:S(2)}, u32[]{:S(2)}) %collective-permute-start.1) | collective-permute-done | bytes 36896 | tf_op jit(solution)/shard_map/ppermute | solution.py:335
  9.9 2.1 %collective-permute-start.3 = (s32[72,128]{1,0:T(8,128)S(1)}, s32[72,128]{1,0:T(8,128)S(1)}, u32[]{:S(2)}, u32[]{:S(2)}) collective-permute-start(s32[72,128]{1,0:T(8,128)S(1)} %collective-permute-done.1.refs_0_), channel_id=1, source_target_pairs={{0,4},{1,5},{2,6},{3,7},{4,0},{5,1},{6,2},{7,3},{8,10},{9,13},{10,... | collective-permute-start | bytes 110600 | tf_op jit(solution)/shard_map/ppermute | solution.py:335
  12.0 0.0 collective-permute-start.4
  12.0 0.0 copy-done
  12.0 0.5 %score_docs.1 = (f32[8,16]{1,0:T(8,128)S(1)}, bf16[128,256]{1,0:T(8,128)(2,1)S(1)}, bf16[128,256]{1,0:T(8,128)(2,1)S(1)}) custom-call(f32[128,128]{1,0:T(8,128)S(1)} %get-tuple-element.10.own_ref, s32[72,128]{1,0:T(8,128)S(1)} %get-tuple-element.9.message_ref, f32[16,4096]{1,0:T(8,128)S(1)} %copy-done), custom_call_target="tpu_custom_call" | custom-call | flops 67108864 | bytes 524288 | tf_op jit(solution)/shard_map/score_docs/pallas_call | solution.py:180
  12.5 0.5 %gram_early.1.sum_ref = f32[8,32]{1,0:T(8,128)S(1)} custom-call(s32[72,128]{1,0:T(8,128)S(1)} %get-tuple-element.9.message_ref, bf16[128,256]{1,0:T(8,128)(2,1)S(1)} %get-tuple-element.11.grads_ref, bf16[128,256]{1,0:T(8,128)(2,1)S(1)} %get-tuple-element.12.ins_ref, s32[72,128]{1,0:T(8,128)S(1)} %collective-permute-done.1.refs_0_), custom_call_target="tpu_custom_call" | custom-call | tf_op jit(solution)/shard_map/gram_early/pallas_call | solution.py:295
  12.9 0.0 collective-permute-done.2.refs_0_
  12.9 1.0 %collective-permute-done.3.refs_1_ = s32[72,128]{1,0:T(8,128)S(1)} collective-permute-done((s32[72,128]{1,0:T(8,128)S(1)}, s32[72,128]{1,0:T(8,128)S(1)}, u32[]{:S(2)}, u32[]{:S(2)}) %collective-permute-start.3) | collective-permute-done | bytes 36896 | tf_op jit(solution)/shard_map/ppermute | solution.py:335
  13.9 1.1 %gram_own.1 = (f32[8,32]{1,0:T(8,128)}, f32[8,16]{1,0:T(8,128)}) custom-call(s32[72,128]{1,0:T(8,128)S(1)} %get-tuple-element.9.message_ref, bf16[128,256]{1,0:T(8,128)(2,1)S(1)} %get-tuple-element.11.grads_ref, bf16[128,256]{1,0:T(8,128)(2,1)S(1)} %get-tuple-element.12.ins_ref, f32[8,16]{1,0:T(8,128)S(1)} %get-tuple-element.13.scores_ref, ...), custom_call_target="tpu_custom_call" | custom-call | tf_op jit(solution)/shard_map/gram_own/pallas_call | solution.py:306
  15.0 0.9 %collective-permute-done.4.refs_2_ = s32[72,128]{1,0:T(8,128)S(1)} collective-permute-done((s32[72,128]{1,0:T(8,128)S(1)}, s32[72,128]{1,0:T(8,128)S(1)}, u32[]{:S(2)}, u32[]{:S(2)}) %collective-permute-start.4) | collective-permute-done | bytes 36896 | tf_op jit(solution)/shard_map/ppermute | solution.py:335
  (1 shorter events, 0.0 us)
Async XLA Ops:
  0.6 4.3 %copy-start.1 = (s32[1,128]{1,0:T(1,128)S(1)}, s32[1,128]{1,0:T(1,128)}, u32[]{:S(2)}) copy-start(s32[1,128]{1,0:T(1,128)} %ids_ref.1) | copy-start | bytes 1540
  0.6 11.4 %copy-start = (f32[16,4096]{1,0:T(8,128)S(1)}, f32[16,4096]{1,0:T(8,128)}, u32[]{:S(2)}) copy-start(f32[16,4096]{1,0:T(8,128)} %queries.1) | copy-start | bytes 786436
  3.5 1.4 %collective-permute-start = (f32[128,128]{1,0:T(8,128)S(1)}, f32[128,128]{1,0:T(8,128)S(1)}, u32[]{:S(2)}, u32[]{:S(2)}) collective-permute-start(f32[128,128]{1,0:T(8,128)S(1)} %partial_codes.1.mine_ref), channel_id=1, source_target_pairs={{0,1},{1,0},{2,3},{3,2},{4,5},{5,4},{6,7},{7,6},{8,9},{9,8},{10,11... | collective-permute-start | bytes 196616 | tf_op jit(solution)/shard_map/ppermute | solution.py:323
  5.0 4.8 %collective-permute-start.1 = (s32[72,128]{1,0:T(8,128)S(1)}, s32[72,128]{1,0:T(8,128)S(1)}, u32[]{:S(2)}, u32[]{:S(2)}) collective-permute-start(s32[72,128]{1,0:T(8,128)S(1)} %get-tuple-element.9.message_ref), channel_id=1, source_target_pairs={{0,2},{1,8},{2,0},{3,10},{4,6},{5,12},{6,4},{7,14},{9,1},{8,11},{1... | collective-permute-start | bytes 110600 | tf_op jit(solution)/shard_map/ppermute | solution.py:335
  7.9 5.0 %collective-permute-start.2 = (s32[72,128]{1,0:T(8,128)S(1)}, s32[72,128]{1,0:T(8,128)S(1)}, u32[]{:S(2)}, u32[]{:S(2)}) collective-permute-start(s32[72,128]{1,0:T(8,128)S(1)} %get-tuple-element.9.message_ref), channel_id=1, source_target_pairs={{0,4},{1,14},{2,6},{3,12},{4,0},{5,10},{6,2},{7,8},{9,7},{8,13},{1... | collective-permute-start | bytes 110600 | tf_op jit(solution)/shard_map/ppermute | solution.py:335
  9.9 4.0 %collective-permute-start.3 = (s32[72,128]{1,0:T(8,128)S(1)}, s32[72,128]{1,0:T(8,128)S(1)}, u32[]{:S(2)}, u32[]{:S(2)}) collective-permute-start(s32[72,128]{1,0:T(8,128)S(1)} %collective-permute-done.1.refs_0_), channel_id=1, source_target_pairs={{0,4},{1,5},{2,6},{3,7},{4,0},{5,1},{6,2},{7,3},{8,10},{9,13},{10,... | collective-permute-start | bytes 110600 | tf_op jit(solution)/shard_map/ppermute | solution.py:335
  12.0 4.0 %collective-permute-start.4 = (s32[72,128]{1,0:T(8,128)S(1)}, s32[72,128]{1,0:T(8,128)S(1)}, u32[]{:S(2)}, u32[]{:S(2)}) collective-permute-start(s32[72,128]{1,0:T(8,128)S(1)} %collective-permute-done.1.refs_0_), channel_id=1, source_target_pairs={{0,4},{1,3},{2,6},{3,1},{4,0},{5,7},{6,2},{7,5},{8,12},{9,11},{10,... | collective-permute-start | bytes 110600 | tf_op jit(solution)/shard_map/ppermute | solution.py:335

commit v18 on v16

--- a/solution.py
+++ b/solution.py
@@ -21,8 +21,9 @@
 
 
 def pieces_of(depth):
-    size = next(size for size in (2048, 1792, 1024, 512, 256, 128, depth) if depth % size == 0)
-    return [(at, size) for at in range(0, depth, size)]
+    count = -(-depth // 2432)
+    size = -(-depth // (count * 128)) * 128
+    return [(at, min(size, depth - at)) for at in range(0, depth, size)]
 
 
 def sum_of(parts):
@@ -134,7 +135,7 @@
     )(mine, other, doc_ids)
 
 
-def scores_kernel(own_ref, message_ref, queries, scores_ref, grads_ref, ins_ref):
+def scores_kernel(own_ref, message_ref, queries, scores_ref, grads_ref, ins_ref, feats_ref):
     rows, tokens = own_ref.shape
     rank = rows // 2
     grads = own_ref[:rank, :]
@@ -152,6 +153,7 @@
         jnp.concatenate([i_high, i_low, i_high], axis=1),
         NT,
     )
+    feats_ref[...] = jnp.concatenate(halves(feats), axis=1)
     left = lax.broadcasted_iota(jnp.int32, (DOCS_DEV, 2 * rank), 1) < rank
     pairs = [
         jnp.where(
@@ -182,9 +184,10 @@
             jax.ShapeDtypeStruct((DOCS_DEV, queries.shape[0]), jnp.float32),
             operand,
             operand,
+            jax.ShapeDtypeStruct((rank * DOCS_DEV, 4 * rank), jnp.bfloat16),
         ),
         in_specs=[VMEM] * 3,
-        out_specs=(VMEM, VMEM, VMEM),
+        out_specs=(VMEM,) * 4,
         compiler_params=SMALL,
         cost_estimate=pl.CostEstimate(flops=1 << 26, bytes_accessed=1 << 19, transcendentals=0),
         name="score_docs",
@@ -292,18 +295,30 @@
         write_out(total_ref, scores_ref, out_ref, scores_out_ref, sems)
 
 
-def last_kernel(half, message_ref, grads_ref, ins_ref, scores_ref, sum_ref, block_ref, *refs):
+def last_kernel(half, feats_ref, scores_ref, sum_ref, block_ref, *refs):
     out_ref, scores_out_ref, total_ref, sems = refs[-4:]
     shard, own_half = position(half)
+    rank = feats_ref.shape[1] // 4
 
     @pl.when(jnp.logical_not(own_half))
     def _():
-        parts = blocks_at(shard, half, own_half, [half - 1], [block_ref])
-        total_ref[...] = sum_ref[...] + gram_sum(half, message_ref, grads_ref, ins_ref, parts)
+        ((block, place),) = blocks_at(shard, half, own_half, [half - 1], [block_ref])
+        codes = block[:rank, :]
+        grads = lax.shift_right_arithmetic(codes, 16).astype(jnp.float32)
+        ins = lax.shift_right_arithmetic(lax.shift_left(codes, 16), 16).astype(jnp.float32)
+        high, low = halves(ins)
+        shares = dot(feats_ref[...], jnp.concatenate([high, low, high, low], axis=0), NN)
+        terms = [shares[i * DOCS_DEV : (i + 1) * DOCS_DEV, :] * grads[i : i + 1, :] for i in range(rank)]
+        grades = block[rank + 1 : rank + 2, :] + block[rank + 2 : rank + 3, :]
+        scales = jnp.exp2(grades.astype(jnp.float32) * (1.0 / STEPS)) * (1.0 / (TOP * TOP * rank * rank))
+        high, low = halves(sum_of(terms) * scales)
+        theirs = members(block[rank : rank + 1, :] + place * DOCS_DEV, half * DOCS_DEV).astype(jnp.bfloat16)
+        part = dot(jnp.concatenate([high, low], axis=0), theirs, NT)
+        total_ref[...] = sum_ref[...] + (part[:DOCS_DEV, :] + part[DOCS_DEV:, :])
         write_out(total_ref, scores_ref, out_ref, scores_out_ref, sems)
 
 
-def gram_of(message, grads, ins, scores, blocks):
+def gram_of(message, grads, ins, feats, scores, blocks):
     half = len(blocks)
     rows = jax.ShapeDtypeStruct((DOCS_DEV, half * DOCS_DEV), jnp.float32)
     results = (rows, jax.ShapeDtypeStruct(scores.shape, scores.dtype))
@@ -329,13 +344,13 @@
     return pl.pallas_call(
         functools.partial(last_kernel, half),
         out_shape=results,
-        in_specs=[VMEM] * 6 + [HBM] * 2,
+        in_specs=[VMEM] * 4 + [HBM] * 2,
         out_specs=(HBM, HBM),
         scratch_shapes=[pltpu.VMEM(rows.shape, rows.dtype), pltpu.SemaphoreType.DMA((2,))],
-        input_output_aliases={6: 0, 7: 1},
+        input_output_aliases={4: 0, 5: 1},
         compiler_params=SMALL,
         name="gram_last",
-    )(*operands, scores, so_far, blocks[-1], *results_own)
+    )(feats, scores, so_far, blocks[-1], *results_own)
 
 
 def local(inputs, out_grads, proj_in, proj_out, doc_ids, queries):
@@ -355,8 +370,8 @@
                 by = 1 - core if side in crossed else core
                 moves.append((2 * s + by, 2 * to + to_core))
         blocks.append(lax.ppermute(blocks[what] if what >= 0 else message, ("dp", "tensor"), moves))
-    scores, grads, ins = score_docs(own, message, queries)
-    return gram_of(message, grads, ins, scores, blocks)
+    scores, grads, ins, feats = score_docs(own, message, queries)
+    return gram_of(message, grads, ins, feats, scores, blocks)
 
 
 def solution(mesh):

time: 16.3 us -> 16.2 us (level)
  transfers between devices with their start and end apart: 5 -> 5, of which waited for: 4 -> 4; matrix products, arithmetic and copies ran while one was open for 0% -> 0% of each run, Pallas kernels for 12% -> 13%
where the time goes in v18:
time: 16.2 us; the launch traced here: 16 us
  starting transfers between devices  7.13 us (44%)
  Pallas kernels  4.99 us (31%)
  waiting for transfers between devices  3.14 us (19%)
  between operations  0.69 us (4%)
    ppermute x4, starting transfers between devices, local(): lax.ppermute(blocks[what] if what >= 0 else message, ('dp', 'tensor'), mo...  6.61 us
    pallas_call x1, Pallas kernels, partial_codes(): pl.pallas_call(codes_kernel, out_shape=jax.ShapeDtypeStruct((2 * rank, to...  2.81 us
    ppermute x4, waiting for transfers between devices, local(): lax.ppermute(blocks[what] if what >= 0 else message, ('dp', 'tensor'), mo...  2.24 us
    pallas_call x1, Pallas kernels, gram_of(): pl.pallas_call(functools.partial(middle_kernel, half, middle), out_shape=...  1.07 us
    ppermute x1, waiting for transfers between devices, local(): other = lax.ppermute(mine, 'tensor', [(0, 1), (1, 0)])  0.9 us
    ppermute x1, starting transfers between devices, local(): other = lax.ppermute(mine, 'tensor', [(0, 1), (1, 0)])  0.52 us
    pallas_call x1, Pallas kernels, score_docs(): pl.pallas_call(scores_kernel, out_shape=(jax.ShapeDtypeStruct((DOCS_DEV,...  0.5 us
    pallas_call x1, Pallas kernels, gram_of(): pl.pallas_call(functools.partial(early_kernel, half, early), out_shape=ro...  0.45 us
  transfers between devices with their start and end apart: 5, of which 4 were waited for; matrix products, arithmetic and copies ran while one was open for 0% of the time, Pallas kernels for 13%

profile of v18, /device:TPU:0, one launch (start us, length us, event | category | flops | bytes accessed | tf_op | source)
XLA Modules:
  0.0 16.0 jit_solution(10253595386638629941)
XLA Ops:
  0.6 0.0 copy-start.1
  0.6 0.0 copy-start
  0.7 2.8 %partial_codes.1.mine_ref = f32[128,128]{1,0:T(8,128)S(1)} custom-call(bf16[128,7168]{1,0:T(8,128)(2,1)} %x_hbm.1, bf16[128,2048]{1,0:T(8,128)(2,1)} %y_hbm.1, bf16[64,14336]{1,0:T(8,128)(2,1)} %bitcast.2, bf16[64,4096]{1,0:T(8,128)(2,1)} %bitcast.3), custom_call_target="tpu_custom_call" | custom-call | tf_op jit(solution)/shard_map/partial_codes/pallas_call | solution.py:77
  3.5 0.5 %collective-permute-start = (f32[128,128]{1,0:T(8,128)S(1)}, f32[128,128]{1,0:T(8,128)S(1)}, u32[]{:S(2)}, u32[]{:S(2)}) collective-permute-start(f32[128,128]{1,0:T(8,128)S(1)} %partial_codes.1.mine_ref), channel_id=1, source_target_pairs={{0,1},{1,0},{2,3},{3,2},{4,5},{5,4},{6,7},{7,6},{8,9},{9,8},{10,11... | collective-permute-start | bytes 196616 | tf_op jit(solution)/shard_map/ppermute | solution.py:360
  4.0 0.9 %collective-permute-done.other_ref = f32[128,128]{1,0:T(8,128)S(1)} collective-permute-done((f32[128,128]{1,0:T(8,128)S(1)}, f32[128,128]{1,0:T(8,128)S(1)}, u32[]{:S(2)}, u32[]{:S(2)}) %collective-permute-start) | collective-permute-done | bytes 65568 | tf_op jit(solution)/shard_map/ppermute | solution.py:360
  4.9 0.0 copy-done.1
  4.9 0.1 pack_codes.1
  5.0 2.9 %collective-permute-start.1 = (s32[72,128]{1,0:T(8,128)S(1)}, s32[72,128]{1,0:T(8,128)S(1)}, u32[]{:S(2)}, u32[]{:S(2)}) collective-permute-start(s32[72,128]{1,0:T(8,128)S(1)} %get-tuple-element.12.message_ref), channel_id=1, source_target_pairs={{0,2},{1,8},{2,0},{3,10},{4,6},{5,12},{6,4},{7,14},{9,1},{8,11},{1... | collective-permute-start | bytes 110600 | tf_op jit(solution)/shard_map/ppermute | solution.py:372
  7.9 1.6 %collective-permute-start.2 = (s32[72,128]{1,0:T(8,128)S(1)}, s32[72,128]{1,0:T(8,128)S(1)}, u32[]{:S(2)}, u32[]{:S(2)}) collective-permute-start(s32[72,128]{1,0:T(8,128)S(1)} %get-tuple-element.12.message_ref), channel_id=1, source_target_pairs={{0,4},{1,14},{2,6},{3,12},{4,0},{5,10},{6,2},{7,8},{9,7},{8,13},{1... | collective-permute-start | bytes 110600 | tf_op jit(solution)/shard_map/ppermute | solution.py:372
  9.5 0.4 %collective-permute-done.1.refs_0_ = s32[72,128]{1,0:T(8,128)S(1)} collective-permute-done((s32[72,128]{1,0:T(8,128)S(1)}, s32[72,128]{1,0:T(8,128)S(1)}, u32[]{:S(2)}, u32[]{:S(2)}) %collective-permute-start.1) | collective-permute-done | bytes 36896 | tf_op jit(solution)/shard_map/ppermute | solution.py:372
  9.9 2.1 %collective-permute-start.3 = (s32[72,128]{1,0:T(8,128)S(1)}, s32[72,128]{1,0:T(8,128)S(1)}, u32[]{:S(2)}, u32[]{:S(2)}) collective-permute-start(s32[72,128]{1,0:T(8,128)S(1)} %collective-permute-done.1.refs_0_), channel_id=1, source_target_pairs={{0,4},{1,5},{2,6},{3,7},{4,0},{5,1},{6,2},{7,3},{8,10},{9,13},{10,... | collective-permute-start | bytes 110600 | tf_op jit(solution)/shard_map/ppermute | solution.py:372
  12.0 0.0 collective-permute-start.4
  12.0 0.0 copy-done
  12.0 0.5 %score_docs.1 = (f32[8,16]{1,0:T(8,128)S(1)}, bf16[128,256]{1,0:T(8,128)(2,1)S(1)}, bf16[128,256]{1,0:T(8,128)(2,1)S(1)}, bf16[512,256]{1,0:T(8,128)(2,1)S(1)}) custom-call(f32[128,128]{1,0:T(8,128)S(1)} %get-tuple-element.11.own_ref, s32[72,128]{1,0:T(8,128)S(1)} %get-tuple-element.12.message_ref, f32[16,4096]{1,0:T(8,128)S(1)} %copy-done), custom_call_target="tpu_custom_call" | custom-call | flops 67108864 | bytes 524288 | tf_op jit(solution)/shard_map/score_docs/pallas_call | solution.py:181
  12.5 0.5 %gram_early.1.sum_ref = f32[8,32]{1,0:T(8,128)S(1)} custom-call(s32[72,128]{1,0:T(8,128)S(1)} %get-tuple-element.12.message_ref, bf16[128,256]{1,0:T(8,128)(2,1)S(1)} %get-tuple-element.15.grads_ref, bf16[128,256]{1,0:T(8,128)(2,1)S(1)} %get-tuple-element.16.ins_ref, s32[72,128]{1,0:T(8,128)S(1)} %collective-permute-done.1.refs_0_), custom_call_target="tpu_custom_call" | custom-call | tf_op jit(solution)/shard_map/gram_early/pallas_call | solution.py:327
  13.0 0.0 collective-permute-done.2.refs_0_
  13.0 0.9 %collective-permute-done.3.refs_1_ = s32[72,128]{1,0:T(8,128)S(1)} collective-permute-done((s32[72,128]{1,0:T(8,128)S(1)}, s32[72,128]{1,0:T(8,128)S(1)}, u32[]{:S(2)}, u32[]{:S(2)}) %collective-permute-start.3) | collective-permute-done | bytes 36896 | tf_op jit(solution)/shard_map/ppermute | solution.py:372
  13.9 1.1 %gram_middle.1 = (f32[8,32]{1,0:T(8,128)}, f32[8,16]{1,0:T(8,128)}, f32[8,32]{1,0:T(8,128)S(1)}) custom-call(s32[72,128]{1,0:T(8,128)S(1)} %get-tuple-element.12.message_ref, bf16[128,256]{1,0:T(8,128)(2,1)S(1)} %get-tuple-element.15.grads_ref, bf16[128,256]{1,0:T(8,128)(2,1)S(1)} %get-tuple-element.16.ins_ref, f32[8,16]{1,0:T(8,128)S(1)} %get-tuple-element.14.scores_ref, ...), custom_call_target="tpu_custom_call" | custom-call | tf_op jit(solution)/shard_map/gram_middle/pallas_call | solution.py:335
  15.0 0.9 %collective-permute-done.4.block_ref = s32[72,128]{1,0:T(8,128)S(1)} collective-permute-done((s32[72,128]{1,0:T(8,128)S(1)}, s32[72,128]{1,0:T(8,128)S(1)}, u32[]{:S(2)}, u32[]{:S(2)}) %collective-permute-start.4) | collective-permute-done | bytes 36896 | tf_op jit(solution)/shard_map/ppermute | solution.py:372
  (1 shorter events, 0.0 us)
Async XLA Ops:
  0.6 4.3 %copy-start.1 = (s32[1,128]{1,0:T(1,128)S(1)}, s32[1,128]{1,0:T(1,128)}, u32[]{:S(2)}) copy-start(s32[1,128]{1,0:T(1,128)} %ids_ref.1) | copy-start | bytes 1540
  0.6 11.4 %copy-start = (f32[16,4096]{1,0:T(8,128)S(1)}, f32[16,4096]{1,0:T(8,128)}, u32[]{:S(2)}) copy-start(f32[16,4096]{1,0:T(8,128)} %queries.1) | copy-start | bytes 786436
  3.5 1.4 %collective-permute-start = (f32[128,128]{1,0:T(8,128)S(1)}, f32[128,128]{1,0:T(8,128)S(1)}, u32[]{:S(2)}, u32[]{:S(2)}) collective-permute-start(f32[128,128]{1,0:T(8,128)S(1)} %partial_codes.1.mine_ref), channel_id=1, source_target_pairs={{0,1},{1,0},{2,3},{3,2},{4,5},{5,4},{6,7},{7,6},{8,9},{9,8},{10,11... | collective-permute-start | bytes 196616 | tf_op jit(solution)/shard_map/ppermute | solution.py:360
  5.0 4.8 %collective-permute-start.1 = (s32[72,128]{1,0:T(8,128)S(1)}, s32[72,128]{1,0:T(8,128)S(1)}, u32[]{:S(2)}, u32[]{:S(2)}) collective-permute-start(s32[72,128]{1,0:T(8,128)S(1)} %get-tuple-element.12.message_ref), channel_id=1, source_target_pairs={{0,2},{1,8},{2,0},{3,10},{4,6},{5,12},{6,4},{7,14},{9,1},{8,11},{1... | collective-permute-start | bytes 110600 | tf_op jit(solution)/shard_map/ppermute | solution.py:372
  7.9 5.0 %collective-permute-start.2 = (s32[72,128]{1,0:T(8,128)S(1)}, s32[72,128]{1,0:T(8,128)S(1)}, u32[]{:S(2)}, u32[]{:S(2)}) collective-permute-start(s32[72,128]{1,0:T(8,128)S(1)} %get-tuple-element.12.message_ref), channel_id=1, source_target_pairs={{0,4},{1,14},{2,6},{3,12},{4,0},{5,10},{6,2},{7,8},{9,7},{8,13},{1... | collective-permute-start | bytes 110600 | tf_op jit(solution)/shard_map/ppermute | solution.py:372
  9.9 4.0 %collective-permute-start.3 = (s32[72,128]{1,0:T(8,128)S(1)}, s32[72,128]{1,0:T(8,128)S(1)}, u32[]{:S(2)}, u32[]{:S(2)}) collective-permute-start(s32[72,128]{1,0:T(8,128)S(1)} %collective-permute-done.1.refs_0_), channel_id=1, source_target_pairs={{0,4},{1,5},{2,6},{3,7},{4,0},{5,1},{6,2},{7,3},{8,10},{9,13},{10,... | collective-permute-start | bytes 110600 | tf_op jit(solution)/shard_map/ppermute | solution.py:372
  12.0 4.0 %collective-permute-start.4 = (s32[72,128]{1,0:T(8,128)S(1)}, s32[72,128]{1,0:T(8,128)S(1)}, u32[]{:S(2)}, u32[]{:S(2)}) collective-permute-start(s32[72,128]{1,0:T(8,128)S(1)} %collective-permute-done.1.refs_0_), channel_id=1, source_target_pairs={{0,4},{1,3},{2,6},{3,1},{4,0},{5,7},{6,2},{7,5},{8,12},{9,11},{10,... | collective-permute-start | bytes 110600 | tf_op jit(solution)/shard_map/ppermute | solution.py:372

commit v19 on v18

--- a/solution.py
+++ b/solution.py
@@ -21,14 +21,15 @@
 
 
 def pieces_of(depth):
-    count = -(-depth // 2432)
+    count = -(-depth // 3584)
     size = -(-depth // (count * 128)) * 128
     return [(at, min(size, depth - at)) for at in range(0, depth, size)]
 
 
 def sum_of(parts):
     while len(parts) > 1:
-        parts = [sum(parts[n : n + 2]) for n in range(0, len(parts), 2)]
+        ends = parts[-1:] if len(parts) % 2 else []
+        parts = [a + b for a, b in zip(parts[::2], parts[1::2])] + ends
     return parts[0]
 
 
@@ -273,26 +274,30 @@
     sum_ref[...] = gram_sum(half, message_ref, grads_ref, ins_ref, parts)
 
 
-def write_out(total_ref, scores_ref, out_ref, scores_out_ref, sems):
-    copies = (
-        pltpu.make_async_copy(scores_ref, scores_out_ref, sems.at[0]),
-        pltpu.make_async_copy(total_ref, out_ref, sems.at[1]),
-    )
-    for copy in copies:
-        copy.start()
-    for copy in copies:
-        copy.wait()
+def sent(src_ref, dst_ref, sem):
+    copy = pltpu.make_async_copy(src_ref, dst_ref, sem)
+    copy.start()
+    return copy
 
 
 def middle_kernel(half, numbers, message_ref, grads_ref, ins_ref, scores_ref, sum_ref, *refs):
     blocks, (out_ref, scores_out_ref, total_ref, sems) = refs[:-4], refs[-4:]
     shard, own_half = position(half)
-    parts = blocks_at(shard, half, own_half, numbers, blocks)
-    total_ref[...] = sum_ref[...] + gram_sum(half, message_ref, grads_ref, ins_ref, parts)
+
+    def total():
+        parts = blocks_at(shard, half, own_half, numbers, blocks)
+        total_ref[...] = sum_ref[...] + gram_sum(half, message_ref, grads_ref, ins_ref, parts)
 
     @pl.when(own_half)
     def _():
-        write_out(total_ref, scores_ref, out_ref, scores_out_ref, sems)
+        scores_copy = sent(scores_ref, scores_out_ref, sems.at[0])
+        total()
+        sent(total_ref, out_ref, sems.at[1]).wait()
+        scores_copy.wait()
+
+    @pl.when(jnp.logical_not(own_half))
+    def _():
+        total()
 
 
 def last_kernel(half, feats_ref, scores_ref, sum_ref, block_ref, *refs):
@@ -302,6 +307,7 @@
 
     @pl.when(jnp.logical_not(own_half))
     def _():
+        scores_copy = sent(scores_ref, scores_out_ref, sems.at[0])
         ((block, place),) = blocks_at(shard, half, own_half, [half - 1], [block_ref])
         codes = block[:rank, :]
         grads = lax.shift_right_arithmetic(codes, 16).astype(jnp.float32)
@@ -315,7 +321,8 @@
         theirs = members(block[rank : rank + 1, :] + place * DOCS_DEV, half * DOCS_DEV).astype(jnp.bfloat16)
         part = dot(jnp.concatenate([high, low], axis=0), theirs, NT)
         total_ref[...] = sum_ref[...] + (part[:DOCS_DEV, :] + part[DOCS_DEV:, :])
-        write_out(total_ref, scores_ref, out_ref, scores_out_ref, sems)
+        sent(total_ref, out_ref, sems.at[1]).wait()
+        scores_copy.wait()
 
 
 def gram_of(message, grads, ins, feats, scores, blocks):

time: 16.2 us -> 16.3 us (level)
  transfers between devices with their start and end apart: 5 -> 5, of which waited for: 4 -> 4; matrix products, arithmetic and copies ran while one was open for 0% -> 0% of each run, Pallas kernels for 13% -> 12%
where the time goes in v19:
time: 16.3 us; the launch traced here: 16.1 us
  starting transfers between devices  7.13 us (44%)
  Pallas kernels  5.08 us (31%)
  waiting for transfers between devices  3.16 us (19%)
  between operations  0.69 us (4%)
    ppermute x4, starting transfers between devices, local(): lax.ppermute(blocks[what] if what >= 0 else message, ('dp', 'tensor'), mo...  6.61 us
    pallas_call x1, Pallas kernels, partial_codes(): pl.pallas_call(codes_kernel, out_shape=jax.ShapeDtypeStruct((2 * rank, to...  2.92 us
    ppermute x4, waiting for transfers between devices, local(): lax.ppermute(blocks[what] if what >= 0 else message, ('dp', 'tensor'), mo...  2.26 us
    pallas_call x1, Pallas kernels, gram_of(): pl.pallas_call(functools.partial(middle_kernel, half, middle), out_shape=...  1.07 us
    ppermute x1, waiting for transfers between devices, local(): other = lax.ppermute(mine, 'tensor', [(0, 1), (1, 0)])  0.9 us
    ppermute x1, starting transfers between devices, local(): other = lax.ppermute(mine, 'tensor', [(0, 1), (1, 0)])  0.52 us
    pallas_call x1, Pallas kernels, score_docs(): pl.pallas_call(scores_kernel, out_shape=(jax.ShapeDtypeStruct((DOCS_DEV,...  0.49 us
    pallas_call x1, Pallas kernels, gram_of(): pl.pallas_call(functools.partial(early_kernel, half, early), out_shape=ro...  0.45 us
  transfers between devices with their start and end apart: 5, of which 4 were waited for; matrix products, arithmetic and copies ran while one was open for 0% of the time, Pallas kernels for 12%

profile of v19, /device:TPU:0, one launch (start us, length us, event | category | flops | bytes accessed | tf_op | source)
XLA Modules:
  0.0 16.1 jit_solution(6248033852200636690)
XLA Ops:
  0.6 0.0 copy-start.1
  0.6 0.0 copy-start
  0.7 2.9 %partial_codes.1.mine_ref = f32[128,128]{1,0:T(8,128)S(1)} custom-call(bf16[128,7168]{1,0:T(8,128)(2,1)} %x_hbm.1, bf16[128,2048]{1,0:T(8,128)(2,1)} %y_hbm.1, bf16[64,14336]{1,0:T(8,128)(2,1)} %bitcast.2, bf16[64,4096]{1,0:T(8,128)(2,1)} %bitcast.3), custom_call_target="tpu_custom_call" | custom-call | tf_op jit(solution)/shard_map/partial_codes/pallas_call | solution.py:78
  3.6 0.5 %collective-permute-start = (f32[128,128]{1,0:T(8,128)S(1)}, f32[128,128]{1,0:T(8,128)S(1)}, u32[]{:S(2)}, u32[]{:S(2)}) collective-permute-start(f32[128,128]{1,0:T(8,128)S(1)} %partial_codes.1.mine_ref), channel_id=1, source_target_pairs={{0,1},{1,0},{2,3},{3,2},{4,5},{5,4},{6,7},{7,6},{8,9},{9,8},{10,11... | collective-permute-start | bytes 196616 | tf_op jit(solution)/shard_map/ppermute | solution.py:367
  4.1 0.9 %collective-permute-done.other_ref = f32[128,128]{1,0:T(8,128)S(1)} collective-permute-done((f32[128,128]{1,0:T(8,128)S(1)}, f32[128,128]{1,0:T(8,128)S(1)}, u32[]{:S(2)}, u32[]{:S(2)}) %collective-permute-start) | collective-permute-done | bytes 65568 | tf_op jit(solution)/shard_map/ppermute | solution.py:367
  5.0 0.0 copy-done.1
  5.0 0.1 pack_codes.1
  5.1 2.9 %collective-permute-start.1 = (s32[72,128]{1,0:T(8,128)S(1)}, s32[72,128]{1,0:T(8,128)S(1)}, u32[]{:S(2)}, u32[]{:S(2)}) collective-permute-start(s32[72,128]{1,0:T(8,128)S(1)} %get-tuple-element.12.message_ref), channel_id=1, source_target_pairs={{0,2},{1,8},{2,0},{3,10},{4,6},{5,12},{6,4},{7,14},{9,1},{8,11},{1... | collective-permute-start | bytes 110600 | tf_op jit(solution)/shard_map/ppermute | solution.py:379
  8.0 1.6 %collective-permute-start.2 = (s32[72,128]{1,0:T(8,128)S(1)}, s32[72,128]{1,0:T(8,128)S(1)}, u32[]{:S(2)}, u32[]{:S(2)}) collective-permute-start(s32[72,128]{1,0:T(8,128)S(1)} %get-tuple-element.12.message_ref), channel_id=1, source_target_pairs={{0,4},{1,14},{2,6},{3,12},{4,0},{5,10},{6,2},{7,8},{9,7},{8,13},{1... | collective-permute-start | bytes 110600 | tf_op jit(solution)/shard_map/ppermute | solution.py:379
  9.6 0.4 %collective-permute-done.1.refs_0_ = s32[72,128]{1,0:T(8,128)S(1)} collective-permute-done((s32[72,128]{1,0:T(8,128)S(1)}, s32[72,128]{1,0:T(8,128)S(1)}, u32[]{:S(2)}, u32[]{:S(2)}) %collective-permute-start.1) | collective-permute-done | bytes 36896 | tf_op jit(solution)/shard_map/ppermute | solution.py:379
  10.0 2.1 %collective-permute-start.3 = (s32[72,128]{1,0:T(8,128)S(1)}, s32[72,128]{1,0:T(8,128)S(1)}, u32[]{:S(2)}, u32[]{:S(2)}) collective-permute-start(s32[72,128]{1,0:T(8,128)S(1)} %collective-permute-done.1.refs_0_), channel_id=1, source_target_pairs={{0,4},{1,5},{2,6},{3,7},{4,0},{5,1},{6,2},{7,3},{8,10},{9,13},{10,... | collective-permute-start | bytes 110600 | tf_op jit(solution)/shard_map/ppermute | solution.py:379
  12.1 0.0 collective-permute-start.4
  12.1 0.0 copy-done
  12.1 0.5 %score_docs.1 = (f32[8,16]{1,0:T(8,128)S(1)}, bf16[128,256]{1,0:T(8,128)(2,1)S(1)}, bf16[128,256]{1,0:T(8,128)(2,1)S(1)}, bf16[512,256]{1,0:T(8,128)(2,1)S(1)}) custom-call(f32[128,128]{1,0:T(8,128)S(1)} %get-tuple-element.11.own_ref, s32[72,128]{1,0:T(8,128)S(1)} %get-tuple-element.12.message_ref, f32[16,4096]{1,0:T(8,128)S(1)} %copy-done), custom_call_target="tpu_custom_call" | custom-call | flops 67108864 | bytes 524288 | tf_op jit(solution)/shard_map/score_docs/pallas_call | solution.py:182
  12.6 0.5 %gram_early.1.sum_ref = f32[8,32]{1,0:T(8,128)S(1)} custom-call(s32[72,128]{1,0:T(8,128)S(1)} %get-tuple-element.12.message_ref, bf16[128,256]{1,0:T(8,128)(2,1)S(1)} %get-tuple-element.15.grads_ref, bf16[128,256]{1,0:T(8,128)(2,1)S(1)} %get-tuple-element.16.ins_ref, s32[72,128]{1,0:T(8,128)S(1)} %collective-permute-done.1.refs_0_), custom_call_target="tpu_custom_call" | custom-call | tf_op jit(solution)/shard_map/gram_early/pallas_call | solution.py:334
  13.1 0.0 collective-permute-done.2.refs_0_
  13.1 0.9 %collective-permute-done.3.refs_1_ = s32[72,128]{1,0:T(8,128)S(1)} collective-permute-done((s32[72,128]{1,0:T(8,128)S(1)}, s32[72,128]{1,0:T(8,128)S(1)}, u32[]{:S(2)}, u32[]{:S(2)}) %collective-permute-start.3) | collective-permute-done | bytes 36896 | tf_op jit(solution)/shard_map/ppermute | solution.py:379
  14.0 1.1 %gram_middle.1 = (f32[8,32]{1,0:T(8,128)}, f32[8,16]{1,0:T(8,128)}, f32[8,32]{1,0:T(8,128)S(1)}) custom-call(s32[72,128]{1,0:T(8,128)S(1)} %get-tuple-element.12.message_ref, bf16[128,256]{1,0:T(8,128)(2,1)S(1)} %get-tuple-element.15.grads_ref, bf16[128,256]{1,0:T(8,128)(2,1)S(1)} %get-tuple-element.16.ins_ref, f32[8,16]{1,0:T(8,128)S(1)} %get-tuple-element.14.scores_ref, ...), custom_call_target="tpu_custom_call" | custom-call | tf_op jit(solution)/shard_map/gram_middle/pallas_call | solution.py:342
  15.1 0.9 %collective-permute-done.4.block_ref = s32[72,128]{1,0:T(8,128)S(1)} collective-permute-done((s32[72,128]{1,0:T(8,128)S(1)}, s32[72,128]{1,0:T(8,128)S(1)}, u32[]{:S(2)}, u32[]{:S(2)}) %collective-permute-start.4) | collective-permute-done | bytes 36896 | tf_op jit(solution)/shard_map/ppermute | solution.py:379
  (1 shorter events, 0.0 us)
Async XLA Ops:
  0.6 4.4 %copy-start.1 = (s32[1,128]{1,0:T(1,128)S(1)}, s32[1,128]{1,0:T(1,128)}, u32[]{:S(2)}) copy-start(s32[1,128]{1,0:T(1,128)} %ids_ref.1) | copy-start | bytes 1540
  0.6 11.5 %copy-start = (f32[16,4096]{1,0:T(8,128)S(1)}, f32[16,4096]{1,0:T(8,128)}, u32[]{:S(2)}) copy-start(f32[16,4096]{1,0:T(8,128)} %queries.1) | copy-start | bytes 786436
  3.6 1.4 %collective-permute-start = (f32[128,128]{1,0:T(8,128)S(1)}, f32[128,128]{1,0:T(8,128)S(1)}, u32[]{:S(2)}, u32[]{:S(2)}) collective-permute-start(f32[128,128]{1,0:T(8,128)S(1)} %partial_codes.1.mine_ref), channel_id=1, source_target_pairs={{0,1},{1,0},{2,3},{3,2},{4,5},{5,4},{6,7},{7,6},{8,9},{9,8},{10,11... | collective-permute-start | bytes 196616 | tf_op jit(solution)/shard_map/ppermute | solution.py:367
  5.1 4.8 %collective-permute-start.1 = (s32[72,128]{1,0:T(8,128)S(1)}, s32[72,128]{1,0:T(8,128)S(1)}, u32[]{:S(2)}, u32[]{:S(2)}) collective-permute-start(s32[72,128]{1,0:T(8,128)S(1)} %get-tuple-element.12.message_ref), channel_id=1, source_target_pairs={{0,2},{1,8},{2,0},{3,10},{4,6},{5,12},{6,4},{7,14},{9,1},{8,11},{1... | collective-permute-start | bytes 110600 | tf_op jit(solution)/shard_map/ppermute | solution.py:379
  8.0 5.0 %collective-permute-start.2 = (s32[72,128]{1,0:T(8,128)S(1)}, s32[72,128]{1,0:T(8,128)S(1)}, u32[]{:S(2)}, u32[]{:S(2)}) collective-permute-start(s32[72,128]{1,0:T(8,128)S(1)} %get-tuple-element.12.message_ref), channel_id=1, source_target_pairs={{0,4},{1,14},{2,6},{3,12},{4,0},{5,10},{6,2},{7,8},{9,7},{8,13},{1... | collective-permute-start | bytes 110600 | tf_op jit(solution)/shard_map/ppermute | solution.py:379
  10.0 4.0 %collective-permute-start.3 = (s32[72,128]{1,0:T(8,128)S(1)}, s32[72,128]{1,0:T(8,128)S(1)}, u32[]{:S(2)}, u32[]{:S(2)}) collective-permute-start(s32[72,128]{1,0:T(8,128)S(1)} %collective-permute-done.1.refs_0_), channel_id=1, source_target_pairs={{0,4},{1,5},{2,6},{3,7},{4,0},{5,1},{6,2},{7,3},{8,10},{9,13},{10,... | collective-permute-start | bytes 110600 | tf_op jit(solution)/shard_map/ppermute | solution.py:379
  12.1 4.0 %collective-permute-start.4 = (s32[72,128]{1,0:T(8,128)S(1)}, s32[72,128]{1,0:T(8,128)S(1)}, u32[]{:S(2)}, u32[]{:S(2)}) collective-permute-start(s32[72,128]{1,0:T(8,128)S(1)} %collective-permute-done.1.refs_0_), channel_id=1, source_target_pairs={{0,4},{1,3},{2,6},{3,1},{4,0},{5,7},{6,2},{7,5},{8,12},{9,11},{10,... | collective-permute-start | bytes 110600 | tf_op jit(solution)/shard_map/ppermute | solution.py:379

commit v20 on v18

--- a/solution.py
+++ b/solution.py
@@ -198,10 +198,10 @@
     half = shards // 2
     if half == 4:
         return [
-            (-1, (4, 4), (1, 1), (1,)),
-            (-1, (7, 7), (2, 2), (1,)),
-            (0, (2, 1), (2, 2), ()),
-            (0, (1, 2), (2, 1), ()),
+            (-1, (4, 4), (1, 2), (1,)),
+            (-1, (7, 7), (2, 1), (1,)),
+            (0, (2, 2), (2, 1), ()),
+            (0, (1, 1), (2, 2), ()),
         ]
     direct = [(-1, (half + n,) * 2, (n + 1,) * 2, ()) for n in range(0, half, 2)]
     return direct + [(n, (1, 1), (1, 1), ()) for n in reversed(range(half // 2))]

time: 16.2 us -> 16.2 us (level)
  no operation moved by 1% of the time
where the time goes in v20:
time: 16.2 us; the launch traced here: 16 us
  starting transfers between devices  7.13 us (44%)
  Pallas kernels  4.99 us (31%)
  waiting for transfers between devices  3.14 us (19%)
  between operations  0.69 us (4%)
    ppermute x4, starting transfers between devices, local(): lax.ppermute(blocks[what] if what >= 0 else message, ('dp', 'tensor'), mo...  6.61 us
    pallas_call x1, Pallas kernels, partial_codes(): pl.pallas_call(codes_kernel, out_shape=jax.ShapeDtypeStruct((2 * rank, to...  2.81 us
    ppermute x4, waiting for transfers between devices, local(): lax.ppermute(blocks[what] if what >= 0 else message, ('dp', 'tensor'), mo...  2.24 us
    pallas_call x1, Pallas kernels, gram_of(): pl.pallas_call(functools.partial(middle_kernel, half, middle), out_shape=...  1.07 us
    ppermute x1, waiting for transfers between devices, local(): other = lax.ppermute(mine, 'tensor', [(0, 1), (1, 0)])  0.9 us
    ppermute x1, starting transfers between devices, local(): other = lax.ppermute(mine, 'tensor', [(0, 1), (1, 0)])  0.52 us
    pallas_call x1, Pallas kernels, score_docs(): pl.pallas_call(scores_kernel, out_shape=(jax.ShapeDtypeStruct((DOCS_DEV,...  0.5 us
    pallas_call x1, Pallas kernels, gram_of(): pl.pallas_call(functools.partial(early_kernel, half, early), out_shape=ro...  0.45 us
  transfers between devices with their start and end apart: 5, of which 4 were waited for; matrix products, arithmetic and copies ran while one was open for 0% of the time, Pallas kernels for 13%

profile of v20, /device:TPU:0, one launch (start us, length us, event | category | flops | bytes accessed | tf_op | source)
XLA Modules:
  0.0 16.0 jit_solution(9801991069011601567)
XLA Ops:
  0.6 0.0 copy-start.1
  0.6 0.0 copy-start
  0.7 2.8 %partial_codes.1.mine_ref = f32[128,128]{1,0:T(8,128)S(1)} custom-call(bf16[128,7168]{1,0:T(8,128)(2,1)} %x_hbm.1, bf16[128,2048]{1,0:T(8,128)(2,1)} %y_hbm.1, bf16[64,14336]{1,0:T(8,128)(2,1)} %bitcast.2, bf16[64,4096]{1,0:T(8,128)(2,1)} %bitcast.3), custom_call_target="tpu_custom_call" | custom-call | tf_op jit(solution)/shard_map/partial_codes/pallas_call | solution.py:77
  3.5 0.5 %collective-permute-start = (f32[128,128]{1,0:T(8,128)S(1)}, f32[128,128]{1,0:T(8,128)S(1)}, u32[]{:S(2)}, u32[]{:S(2)}) collective-permute-start(f32[128,128]{1,0:T(8,128)S(1)} %partial_codes.1.mine_ref), channel_id=1, source_target_pairs={{0,1},{1,0},{2,3},{3,2},{4,5},{5,4},{6,7},{7,6},{8,9},{9,8},{10,11... | collective-permute-start | bytes 196616 | tf_op jit(solution)/shard_map/ppermute | solution.py:360
  4.0 0.9 %collective-permute-done.other_ref = f32[128,128]{1,0:T(8,128)S(1)} collective-permute-done((f32[128,128]{1,0:T(8,128)S(1)}, f32[128,128]{1,0:T(8,128)S(1)}, u32[]{:S(2)}, u32[]{:S(2)}) %collective-permute-start) | collective-permute-done | bytes 65568 | tf_op jit(solution)/shard_map/ppermute | solution.py:360
  4.9 0.0 copy-done.1
  4.9 0.1 pack_codes.1
  5.0 2.9 %collective-permute-start.1 = (s32[72,128]{1,0:T(8,128)S(1)}, s32[72,128]{1,0:T(8,128)S(1)}, u32[]{:S(2)}, u32[]{:S(2)}) collective-permute-start(s32[72,128]{1,0:T(8,128)S(1)} %get-tuple-element.12.message_ref), channel_id=1, source_target_pairs={{0,2},{1,8},{2,0},{3,10},{4,6},{5,12},{6,4},{7,14},{9,1},{8,13},{1... | collective-permute-start | bytes 110600 | tf_op jit(solution)/shard_map/ppermute | solution.py:372
  7.9 1.6 %collective-permute-start.2 = (s32[72,128]{1,0:T(8,128)S(1)}, s32[72,128]{1,0:T(8,128)S(1)}, u32[]{:S(2)}, u32[]{:S(2)}) collective-permute-start(s32[72,128]{1,0:T(8,128)S(1)} %get-tuple-element.12.message_ref), channel_id=1, source_target_pairs={{0,4},{1,14},{2,6},{3,12},{4,0},{5,10},{6,2},{7,8},{9,7},{8,11},{1... | collective-permute-start | bytes 110600 | tf_op jit(solution)/shard_map/ppermute | solution.py:372
  9.5 0.4 %collective-permute-done.1.refs_0_ = s32[72,128]{1,0:T(8,128)S(1)} collective-permute-done((s32[72,128]{1,0:T(8,128)S(1)}, s32[72,128]{1,0:T(8,128)S(1)}, u32[]{:S(2)}, u32[]{:S(2)}) %collective-permute-start.1) | collective-permute-done | bytes 36896 | tf_op jit(solution)/shard_map/ppermute | solution.py:372
  9.9 2.1 %collective-permute-start.3 = (s32[72,128]{1,0:T(8,128)S(1)}, s32[72,128]{1,0:T(8,128)S(1)}, u32[]{:S(2)}, u32[]{:S(2)}) collective-permute-start(s32[72,128]{1,0:T(8,128)S(1)} %collective-permute-done.1.refs_0_), channel_id=1, source_target_pairs={{0,4},{1,5},{2,6},{3,7},{4,0},{5,1},{6,2},{7,3},{8,12},{9,11},{10,... | collective-permute-start | bytes 110600 | tf_op jit(solution)/shard_map/ppermute | solution.py:372
  12.0 0.0 collective-permute-start.4
  12.0 0.0 copy-done
  12.0 0.5 %score_docs.1 = (f32[8,16]{1,0:T(8,128)S(1)}, bf16[128,256]{1,0:T(8,128)(2,1)S(1)}, bf16[128,256]{1,0:T(8,128)(2,1)S(1)}, bf16[512,256]{1,0:T(8,128)(2,1)S(1)}) custom-call(f32[128,128]{1,0:T(8,128)S(1)} %get-tuple-element.11.own_ref, s32[72,128]{1,0:T(8,128)S(1)} %get-tuple-element.12.message_ref, f32[16,4096]{1,0:T(8,128)S(1)} %copy-done), custom_call_target="tpu_custom_call" | custom-call | flops 67108864 | bytes 524288 | tf_op jit(solution)/shard_map/score_docs/pallas_call | solution.py:181
  12.5 0.5 %gram_early.1.sum_ref = f32[8,32]{1,0:T(8,128)S(1)} custom-call(s32[72,128]{1,0:T(8,128)S(1)} %get-tuple-element.12.message_ref, bf16[128,256]{1,0:T(8,128)(2,1)S(1)} %get-tuple-element.15.grads_ref, bf16[128,256]{1,0:T(8,128)(2,1)S(1)} %get-tuple-element.16.ins_ref, s32[72,128]{1,0:T(8,128)S(1)} %collective-permute-done.1.refs_0_), custom_call_target="tpu_custom_call" | custom-call | tf_op jit(solution)/shard_map/gram_early/pallas_call | solution.py:327
  13.0 0.0 collective-permute-done.2.refs_0_
  13.0 1.0 %collective-permute-done.3.refs_1_ = s32[72,128]{1,0:T(8,128)S(1)} collective-permute-done((s32[72,128]{1,0:T(8,128)S(1)}, s32[72,128]{1,0:T(8,128)S(1)}, u32[]{:S(2)}, u32[]{:S(2)}) %collective-permute-start.3) | collective-permute-done | bytes 36896 | tf_op jit(solution)/shard_map/ppermute | solution.py:372
  14.0 1.1 %gram_middle.1 = (f32[8,32]{1,0:T(8,128)}, f32[8,16]{1,0:T(8,128)}, f32[8,32]{1,0:T(8,128)S(1)}) custom-call(s32[72,128]{1,0:T(8,128)S(1)} %get-tuple-element.12.message_ref, bf16[128,256]{1,0:T(8,128)(2,1)S(1)} %get-tuple-element.15.grads_ref, bf16[128,256]{1,0:T(8,128)(2,1)S(1)} %get-tuple-element.16.ins_ref, f32[8,16]{1,0:T(8,128)S(1)} %get-tuple-element.14.scores_ref, ...), custom_call_target="tpu_custom_call" | custom-call | tf_op jit(solution)/shard_map/gram_middle/pallas_call | solution.py:335
  15.1 0.9 %collective-permute-done.4.block_ref = s32[72,128]{1,0:T(8,128)S(1)} collective-permute-done((s32[72,128]{1,0:T(8,128)S(1)}, s32[72,128]{1,0:T(8,128)S(1)}, u32[]{:S(2)}, u32[]{:S(2)}) %collective-permute-start.4) | collective-permute-done | bytes 36896 | tf_op jit(solution)/shard_map/ppermute | solution.py:372
  (1 shorter events, 0.0 us)
Async XLA Ops:
  0.6 4.3 %copy-start.1 = (s32[1,128]{1,0:T(1,128)S(1)}, s32[1,128]{1,0:T(1,128)}, u32[]{:S(2)}) copy-start(s32[1,128]{1,0:T(1,128)} %ids_ref.1) | copy-start | bytes 1540
  0.6 11.4 %copy-start = (f32[16,4096]{1,0:T(8,128)S(1)}, f32[16,4096]{1,0:T(8,128)}, u32[]{:S(2)}) copy-start(f32[16,4096]{1,0:T(8,128)} %queries.1) | copy-start | bytes 786436
  3.5 1.4 %collective-permute-start = (f32[128,128]{1,0:T(8,128)S(1)}, f32[128,128]{1,0:T(8,128)S(1)}, u32[]{:S(2)}, u32[]{:S(2)}) collective-permute-start(f32[128,128]{1,0:T(8,128)S(1)} %partial_codes.1.mine_ref), channel_id=1, source_target_pairs={{0,1},{1,0},{2,3},{3,2},{4,5},{5,4},{6,7},{7,6},{8,9},{9,8},{10,11... | collective-permute-start | bytes 196616 | tf_op jit(solution)/shard_map/ppermute | solution.py:360
  5.0 4.8 %collective-permute-start.1 = (s32[72,128]{1,0:T(8,128)S(1)}, s32[72,128]{1,0:T(8,128)S(1)}, u32[]{:S(2)}, u32[]{:S(2)}) collective-permute-start(s32[72,128]{1,0:T(8,128)S(1)} %get-tuple-element.12.message_ref), channel_id=1, source_target_pairs={{0,2},{1,8},{2,0},{3,10},{4,6},{5,12},{6,4},{7,14},{9,1},{8,13},{1... | collective-permute-start | bytes 110600 | tf_op jit(solution)/shard_map/ppermute | solution.py:372
  7.9 5.0 %collective-permute-start.2 = (s32[72,128]{1,0:T(8,128)S(1)}, s32[72,128]{1,0:T(8,128)S(1)}, u32[]{:S(2)}, u32[]{:S(2)}) collective-permute-start(s32[72,128]{1,0:T(8,128)S(1)} %get-tuple-element.12.message_ref), channel_id=1, source_target_pairs={{0,4},{1,14},{2,6},{3,12},{4,0},{5,10},{6,2},{7,8},{9,7},{8,11},{1... | collective-permute-start | bytes 110600 | tf_op jit(solution)/shard_map/ppermute | solution.py:372
  9.9 4.1 %collective-permute-start.3 = (s32[72,128]{1,0:T(8,128)S(1)}, s32[72,128]{1,0:T(8,128)S(1)}, u32[]{:S(2)}, u32[]{:S(2)}) collective-permute-start(s32[72,128]{1,0:T(8,128)S(1)} %collective-permute-done.1.refs_0_), channel_id=1, source_target_pairs={{0,4},{1,5},{2,6},{3,7},{4,0},{5,1},{6,2},{7,3},{8,12},{9,11},{10,... | collective-permute-start | bytes 110600 | tf_op jit(solution)/shard_map/ppermute | solution.py:372
  12.0 4.0 %collective-permute-start.4 = (s32[72,128]{1,0:T(8,128)S(1)}, s32[72,128]{1,0:T(8,128)S(1)}, u32[]{:S(2)}, u32[]{:S(2)}) collective-permute-start(s32[72,128]{1,0:T(8,128)S(1)} %collective-permute-done.1.refs_0_), channel_id=1, source_target_pairs={{0,4},{1,3},{2,6},{3,1},{4,0},{5,7},{6,2},{7,5},{8,10},{9,13},{10,... | collective-permute-start | bytes 110600 | tf_op jit(solution)/shard_map/ppermute | solution.py:372

commit v21 on v18

--- a/solution.py
+++ b/solution.py
@@ -46,7 +46,7 @@
     at_core = lax.axis_index("tensor")
     rank = wx.shape[0]
     jobs = []
-    for src, w_src, dst, w_dst, row in ((y_hbm, wy_hbm, y, wy, 0), (x_hbm, wx_hbm, x, wx, rank)):
+    for src, w_src, dst, w_dst, row in ((x_hbm, wx_hbm, x, wx, rank), (y_hbm, wy_hbm, y, wy, 0)):
         depth = dst.shape[1]
         for at, size in pieces_of(depth):
             there = pl.multiple_of(at_core * depth + at, 128)

time: 16.2 us -> 16.2 us (level)
  no operation moved by 1% of the time
where the time goes in v21:
time: 16.2 us; the launch traced here: 16 us
  starting transfers between devices  7.13 us (44%)
  Pallas kernels  5.06 us (31%)
  waiting for transfers between devices  3.16 us (20%)
  between operations  0.69 us (4%)
    ppermute x4, starting transfers between devices, local(): lax.ppermute(blocks[what] if what >= 0 else message, ('dp', 'tensor'), mo...  6.61 us
    pallas_call x1, Pallas kernels, partial_codes(): pl.pallas_call(codes_kernel, out_shape=jax.ShapeDtypeStruct((2 * rank, to...  2.9 us
    ppermute x4, waiting for transfers between devices, local(): lax.ppermute(blocks[what] if what >= 0 else message, ('dp', 'tensor'), mo...  2.26 us
    pallas_call x1, Pallas kernels, gram_of(): pl.pallas_call(functools.partial(middle_kernel, half, middle), out_shape=...  1.07 us
    ppermute x1, waiting for transfers between devices, local(): other = lax.ppermute(mine, 'tensor', [(0, 1), (1, 0)])  0.9 us
    ppermute x1, starting transfers between devices, local(): other = lax.ppermute(mine, 'tensor', [(0, 1), (1, 0)])  0.52 us
    pallas_call x1, Pallas kernels, score_docs(): pl.pallas_call(scores_kernel, out_shape=(jax.ShapeDtypeStruct((DOCS_DEV,...  0.49 us
    pallas_call x1, Pallas kernels, gram_of(): pl.pallas_call(functools.partial(early_kernel, half, early), out_shape=ro...  0.45 us
  transfers between devices with their start and end apart: 5, of which 4 were waited for; matrix products, arithmetic and copies ran while one was open for 0% of the time, Pallas kernels for 13%

profile of v21, /device:TPU:0, one launch (start us, length us, event | category | flops | bytes accessed | tf_op | source)
XLA Modules:
  0.0 16.0 jit_solution(3854676210091532562)
XLA Ops:
  0.6 0.0 copy-start.1
  0.6 0.0 copy-start
  0.7 2.9 %partial_codes.1.mine_ref = f32[128,128]{1,0:T(8,128)S(1)} custom-call(bf16[128,7168]{1,0:T(8,128)(2,1)} %x_hbm.1, bf16[128,2048]{1,0:T(8,128)(2,1)} %y_hbm.1, bf16[64,14336]{1,0:T(8,128)(2,1)} %bitcast.2, bf16[64,4096]{1,0:T(8,128)(2,1)} %bitcast.3), custom_call_target="tpu_custom_call" | custom-call | tf_op jit(solution)/shard_map/partial_codes/pallas_call | solution.py:77
  3.6 0.5 %collective-permute-start = (f32[128,128]{1,0:T(8,128)S(1)}, f32[128,128]{1,0:T(8,128)S(1)}, u32[]{:S(2)}, u32[]{:S(2)}) collective-permute-start(f32[128,128]{1,0:T(8,128)S(1)} %partial_codes.1.mine_ref), channel_id=1, source_target_pairs={{0,1},{1,0},{2,3},{3,2},{4,5},{5,4},{6,7},{7,6},{8,9},{9,8},{10,11... | collective-permute-start | bytes 196616 | tf_op jit(solution)/shard_map/ppermute | solution.py:360
  4.1 0.9 %collective-permute-done.other_ref = f32[128,128]{1,0:T(8,128)S(1)} collective-permute-done((f32[128,128]{1,0:T(8,128)S(1)}, f32[128,128]{1,0:T(8,128)S(1)}, u32[]{:S(2)}, u32[]{:S(2)}) %collective-permute-start) | collective-permute-done | bytes 65568 | tf_op jit(solution)/shard_map/ppermute | solution.py:360
  5.0 0.0 copy-done.1
  5.0 0.1 pack_codes.1
  5.1 2.9 %collective-permute-start.1 = (s32[72,128]{1,0:T(8,128)S(1)}, s32[72,128]{1,0:T(8,128)S(1)}, u32[]{:S(2)}, u32[]{:S(2)}) collective-permute-start(s32[72,128]{1,0:T(8,128)S(1)} %get-tuple-element.12.message_ref), channel_id=1, source_target_pairs={{0,2},{1,8},{2,0},{3,10},{4,6},{5,12},{6,4},{7,14},{9,1},{8,11},{1... | collective-permute-start | bytes 110600 | tf_op jit(solution)/shard_map/ppermute | solution.py:372
  8.0 1.6 %collective-permute-start.2 = (s32[72,128]{1,0:T(8,128)S(1)}, s32[72,128]{1,0:T(8,128)S(1)}, u32[]{:S(2)}, u32[]{:S(2)}) collective-permute-start(s32[72,128]{1,0:T(8,128)S(1)} %get-tuple-element.12.message_ref), channel_id=1, source_target_pairs={{0,4},{1,14},{2,6},{3,12},{4,0},{5,10},{6,2},{7,8},{9,7},{8,13},{1... | collective-permute-start | bytes 110600 | tf_op jit(solution)/shard_map/ppermute | solution.py:372
  9.6 0.4 %collective-permute-done.1.refs_0_ = s32[72,128]{1,0:T(8,128)S(1)} collective-permute-done((s32[72,128]{1,0:T(8,128)S(1)}, s32[72,128]{1,0:T(8,128)S(1)}, u32[]{:S(2)}, u32[]{:S(2)}) %collective-permute-start.1) | collective-permute-done | bytes 36896 | tf_op jit(solution)/shard_map/ppermute | solution.py:372
  9.9 2.1 %collective-permute-start.3 = (s32[72,128]{1,0:T(8,128)S(1)}, s32[72,128]{1,0:T(8,128)S(1)}, u32[]{:S(2)}, u32[]{:S(2)}) collective-permute-start(s32[72,128]{1,0:T(8,128)S(1)} %collective-permute-done.1.refs_0_), channel_id=1, source_target_pairs={{0,4},{1,5},{2,6},{3,7},{4,0},{5,1},{6,2},{7,3},{8,10},{9,13},{10,... | collective-permute-start | bytes 110600 | tf_op jit(solution)/shard_map/ppermute | solution.py:372
  12.1 0.0 collective-permute-start.4
  12.1 0.0 copy-done
  12.1 0.5 %score_docs.1 = (f32[8,16]{1,0:T(8,128)S(1)}, bf16[128,256]{1,0:T(8,128)(2,1)S(1)}, bf16[128,256]{1,0:T(8,128)(2,1)S(1)}, bf16[512,256]{1,0:T(8,128)(2,1)S(1)}) custom-call(f32[128,128]{1,0:T(8,128)S(1)} %get-tuple-element.11.own_ref, s32[72,128]{1,0:T(8,128)S(1)} %get-tuple-element.12.message_ref, f32[16,4096]{1,0:T(8,128)S(1)} %copy-done), custom_call_target="tpu_custom_call" | custom-call | flops 67108864 | bytes 524288 | tf_op jit(solution)/shard_map/score_docs/pallas_call | solution.py:181
  12.6 0.5 %gram_early.1.sum_ref = f32[8,32]{1,0:T(8,128)S(1)} custom-call(s32[72,128]{1,0:T(8,128)S(1)} %get-tuple-element.12.message_ref, bf16[128,256]{1,0:T(8,128)(2,1)S(1)} %get-tuple-element.15.grads_ref, bf16[128,256]{1,0:T(8,128)(2,1)S(1)} %get-tuple-element.16.ins_ref, s32[72,128]{1,0:T(8,128)S(1)} %collective-permute-done.1.refs_0_), custom_call_target="tpu_custom_call" | custom-call | tf_op jit(solution)/shard_map/gram_early/pallas_call | solution.py:327
  13.0 0.0 collective-permute-done.2.refs_0_
  13.0 0.9 %collective-permute-done.3.refs_1_ = s32[72,128]{1,0:T(8,128)S(1)} collective-permute-done((s32[72,128]{1,0:T(8,128)S(1)}, s32[72,128]{1,0:T(8,128)S(1)}, u32[]{:S(2)}, u32[]{:S(2)}) %collective-permute-start.3) | collective-permute-done | bytes 36896 | tf_op jit(solution)/shard_map/ppermute | solution.py:372
  14.0 1.1 %gram_middle.1 = (f32[8,32]{1,0:T(8,128)}, f32[8,16]{1,0:T(8,128)}, f32[8,32]{1,0:T(8,128)S(1)}) custom-call(s32[72,128]{1,0:T(8,128)S(1)} %get-tuple-element.12.message_ref, bf16[128,256]{1,0:T(8,128)(2,1)S(1)} %get-tuple-element.15.grads_ref, bf16[128,256]{1,0:T(8,128)(2,1)S(1)} %get-tuple-element.16.ins_ref, f32[8,16]{1,0:T(8,128)S(1)} %get-tuple-element.14.scores_ref, ...), custom_call_target="tpu_custom_call" | custom-call | tf_op jit(solution)/shard_map/gram_middle/pallas_call | solution.py:335
  15.1 0.9 %collective-permute-done.4.block_ref = s32[72,128]{1,0:T(8,128)S(1)} collective-permute-done((s32[72,128]{1,0:T(8,128)S(1)}, s32[72,128]{1,0:T(8,128)S(1)}, u32[]{:S(2)}, u32[]{:S(2)}) %collective-permute-start.4) | collective-permute-done | bytes 36896 | tf_op jit(solution)/shard_map/ppermute | solution.py:372
  (1 shorter events, 0.0 us)
Async XLA Ops:
  0.6 4.3 %copy-start.1 = (s32[1,128]{1,0:T(1,128)S(1)}, s32[1,128]{1,0:T(1,128)}, u32[]{:S(2)}) copy-start(s32[1,128]{1,0:T(1,128)} %ids_ref.1) | copy-start | bytes 1540
  0.6 11.5 %copy-start = (f32[16,4096]{1,0:T(8,128)S(1)}, f32[16,4096]{1,0:T(8,128)}, u32[]{:S(2)}) copy-start(f32[16,4096]{1,0:T(8,128)} %queries.1) | copy-start | bytes 786436
  3.6 1.4 %collective-permute-start = (f32[128,128]{1,0:T(8,128)S(1)}, f32[128,128]{1,0:T(8,128)S(1)}, u32[]{:S(2)}, u32[]{:S(2)}) collective-permute-start(f32[128,128]{1,0:T(8,128)S(1)} %partial_codes.1.mine_ref), channel_id=1, source_target_pairs={{0,1},{1,0},{2,3},{3,2},{4,5},{5,4},{6,7},{7,6},{8,9},{9,8},{10,11... | collective-permute-start | bytes 196616 | tf_op jit(solution)/shard_map/ppermute | solution.py:360
  5.1 4.8 %collective-permute-start.1 = (s32[72,128]{1,0:T(8,128)S(1)}, s32[72,128]{1,0:T(8,128)S(1)}, u32[]{:S(2)}, u32[]{:S(2)}) collective-permute-start(s32[72,128]{1,0:T(8,128)S(1)} %get-tuple-element.12.message_ref), channel_id=1, source_target_pairs={{0,2},{1,8},{2,0},{3,10},{4,6},{5,12},{6,4},{7,14},{9,1},{8,11},{1... | collective-permute-start | bytes 110600 | tf_op jit(solution)/shard_map/ppermute | solution.py:372
  8.0 5.0 %collective-permute-start.2 = (s32[72,128]{1,0:T(8,128)S(1)}, s32[72,128]{1,0:T(8,128)S(1)}, u32[]{:S(2)}, u32[]{:S(2)}) collective-permute-start(s32[72,128]{1,0:T(8,128)S(1)} %get-tuple-element.12.message_ref), channel_id=1, source_target_pairs={{0,4},{1,14},{2,6},{3,12},{4,0},{5,10},{6,2},{7,8},{9,7},{8,13},{1... | collective-permute-start | bytes 110600 | tf_op jit(solution)/shard_map/ppermute | solution.py:372
  9.9 4.0 %collective-permute-start.3 = (s32[72,128]{1,0:T(8,128)S(1)}, s32[72,128]{1,0:T(8,128)S(1)}, u32[]{:S(2)}, u32[]{:S(2)}) collective-permute-start(s32[72,128]{1,0:T(8,128)S(1)} %collective-permute-done.1.refs_0_), channel_id=1, source_target_pairs={{0,4},{1,5},{2,6},{3,7},{4,0},{5,1},{6,2},{7,3},{8,10},{9,13},{10,... | collective-permute-start | bytes 110600 | tf_op jit(solution)/shard_map/ppermute | solution.py:372
  12.1 4.0 %collective-permute-start.4 = (s32[72,128]{1,0:T(8,128)S(1)}, s32[72,128]{1,0:T(8,128)S(1)}, u32[]{:S(2)}, u32[]{:S(2)}) collective-permute-start(s32[72,128]{1,0:T(8,128)S(1)} %collective-permute-done.1.refs_0_), channel_id=1, source_target_pairs={{0,4},{1,3},{2,6},{3,1},{4,0},{5,7},{6,2},{7,5},{8,12},{9,11},{10,... | collective-permute-start | bytes 110600 | tf_op jit(solution)/shard_map/ppermute | solution.py:372

commit v22 on v18

--- a/solution.py
+++ b/solution.py
@@ -307,8 +307,19 @@
         grads = lax.shift_right_arithmetic(codes, 16).astype(jnp.float32)
         ins = lax.shift_right_arithmetic(lax.shift_left(codes, 16), 16).astype(jnp.float32)
         high, low = halves(ins)
-        shares = dot(feats_ref[...], jnp.concatenate([high, low, high, low], axis=0), NN)
-        terms = [shares[i * DOCS_DEV : (i + 1) * DOCS_DEV, :] * grads[i : i + 1, :] for i in range(rank)]
+        right = jnp.concatenate([high, low, high, low], axis=0)
+        count = rank // 4
+        terms = []
+        for first in range(0, rank, count):
+            shares = dot(feats_ref[first * DOCS_DEV : (first + count) * DOCS_DEV, :], right, NN)
+            terms.append(
+                sum_of(
+                    [
+                        shares[n * DOCS_DEV : (n + 1) * DOCS_DEV, :] * grads[first + n : first + n + 1, :]
+                        for n in range(count)
+                    ]
+                )
+            )
         grades = block[rank + 1 : rank + 2, :] + block[rank + 2 : rank + 3, :]
         scales = jnp.exp2(grades.astype(jnp.float32) * (1.0 / STEPS)) * (1.0 / (TOP * TOP * rank * rank))
         high, low = halves(sum_of(terms) * scales)

time: 16.2 us -> 16.1 us (level)
  no operation moved by 1% of the time
where the time goes in v22:
time: 16.1 us; the launch traced here: 16 us
  starting transfers between devices  7.13 us (44%)
  Pallas kernels  4.99 us (31%)
  waiting for transfers between devices  3.14 us (20%)
  between operations  0.69 us (4%)
    ppermute x4, starting transfers between devices, local(): lax.ppermute(blocks[what] if what >= 0 else message, ('dp', 'tensor'), mo...  6.61 us
    pallas_call x1, Pallas kernels, partial_codes(): pl.pallas_call(codes_kernel, out_shape=jax.ShapeDtypeStruct((2 * rank, to...  2.81 us
    ppermute x4, waiting for transfers between devices, local(): lax.ppermute(blocks[what] if what >= 0 else message, ('dp', 'tensor'), mo...  2.24 us
    pallas_call x1, Pallas kernels, gram_of(): pl.pallas_call(functools.partial(middle_kernel, half, middle), out_shape=...  1.07 us
    ppermute x1, waiting for transfers between devices, local(): other = lax.ppermute(mine, 'tensor', [(0, 1), (1, 0)])  0.9 us
    ppermute x1, starting transfers between devices, local(): other = lax.ppermute(mine, 'tensor', [(0, 1), (1, 0)])  0.52 us
    pallas_call x1, Pallas kernels, score_docs(): pl.pallas_call(scores_kernel, out_shape=(jax.ShapeDtypeStruct((DOCS_DEV,...  0.5 us
    pallas_call x1, Pallas kernels, gram_of(): pl.pallas_call(functools.partial(early_kernel, half, early), out_shape=ro...  0.45 us
  transfers between devices with their start and end apart: 5, of which 4 were waited for; matrix products, arithmetic and copies ran while one was open for 0% of the time, Pallas kernels for 13%

profile of v22, /device:TPU:0, one launch (start us, length us, event | category | flops | bytes accessed | tf_op | source)
XLA Modules:
  0.0 16.0 jit_solution(14560025075504881041)
XLA Ops:
  0.6 0.0 copy-start.1
  0.6 0.0 copy-start
  0.7 2.8 %partial_codes.1.mine_ref = f32[128,128]{1,0:T(8,128)S(1)} custom-call(bf16[128,7168]{1,0:T(8,128)(2,1)} %x_hbm.1, bf16[128,2048]{1,0:T(8,128)(2,1)} %y_hbm.1, bf16[64,14336]{1,0:T(8,128)(2,1)} %bitcast.2, bf16[64,4096]{1,0:T(8,128)(2,1)} %bitcast.3), custom_call_target="tpu_custom_call" | custom-call | tf_op jit(solution)/shard_map/partial_codes/pallas_call | solution.py:77
  3.5 0.5 %collective-permute-start = (f32[128,128]{1,0:T(8,128)S(1)}, f32[128,128]{1,0:T(8,128)S(1)}, u32[]{:S(2)}, u32[]{:S(2)}) collective-permute-start(f32[128,128]{1,0:T(8,128)S(1)} %partial_codes.1.mine_ref), channel_id=1, source_target_pairs={{0,1},{1,0},{2,3},{3,2},{4,5},{5,4},{6,7},{7,6},{8,9},{9,8},{10,11... | collective-permute-start | bytes 196616 | tf_op jit(solution)/shard_map/ppermute | solution.py:371
  4.0 0.9 %collective-permute-done.other_ref = f32[128,128]{1,0:T(8,128)S(1)} collective-permute-done((f32[128,128]{1,0:T(8,128)S(1)}, f32[128,128]{1,0:T(8,128)S(1)}, u32[]{:S(2)}, u32[]{:S(2)}) %collective-permute-start) | collective-permute-done | bytes 65568 | tf_op jit(solution)/shard_map/ppermute | solution.py:371
  4.9 0.0 copy-done.1
  4.9 0.1 pack_codes.1
  5.0 2.9 %collective-permute-start.1 = (s32[72,128]{1,0:T(8,128)S(1)}, s32[72,128]{1,0:T(8,128)S(1)}, u32[]{:S(2)}, u32[]{:S(2)}) collective-permute-start(s32[72,128]{1,0:T(8,128)S(1)} %get-tuple-element.12.message_ref), channel_id=1, source_target_pairs={{0,2},{1,8},{2,0},{3,10},{4,6},{5,12},{6,4},{7,14},{9,1},{8,11},{1... | collective-permute-start | bytes 110600 | tf_op jit(solution)/shard_map/ppermute | solution.py:383
  7.9 1.6 %collective-permute-start.2 = (s32[72,128]{1,0:T(8,128)S(1)}, s32[72,128]{1,0:T(8,128)S(1)}, u32[]{:S(2)}, u32[]{:S(2)}) collective-permute-start(s32[72,128]{1,0:T(8,128)S(1)} %get-tuple-element.12.message_ref), channel_id=1, source_target_pairs={{0,4},{1,14},{2,6},{3,12},{4,0},{5,10},{6,2},{7,8},{9,7},{8,13},{1... | collective-permute-start | bytes 110600 | tf_op jit(solution)/shard_map/ppermute | solution.py:383
  9.5 0.4 %collective-permute-done.1.refs_0_ = s32[72,128]{1,0:T(8,128)S(1)} collective-permute-done((s32[72,128]{1,0:T(8,128)S(1)}, s32[72,128]{1,0:T(8,128)S(1)}, u32[]{:S(2)}, u32[]{:S(2)}) %collective-permute-start.1) | collective-permute-done | bytes 36896 | tf_op jit(solution)/shard_map/ppermute | solution.py:383
  9.9 2.1 %collective-permute-start.3 = (s32[72,128]{1,0:T(8,128)S(1)}, s32[72,128]{1,0:T(8,128)S(1)}, u32[]{:S(2)}, u32[]{:S(2)}) collective-permute-start(s32[72,128]{1,0:T(8,128)S(1)} %collective-permute-done.1.refs_0_), channel_id=1, source_target_pairs={{0,4},{1,5},{2,6},{3,7},{4,0},{5,1},{6,2},{7,3},{8,10},{9,13},{10,... | collective-permute-start | bytes 110600 | tf_op jit(solution)/shard_map/ppermute | solution.py:383
  12.0 0.0 collective-permute-start.4
  12.0 0.0 copy-done
  12.0 0.5 %score_docs.1 = (f32[8,16]{1,0:T(8,128)S(1)}, bf16[128,256]{1,0:T(8,128)(2,1)S(1)}, bf16[128,256]{1,0:T(8,128)(2,1)S(1)}, bf16[512,256]{1,0:T(8,128)(2,1)S(1)}) custom-call(f32[128,128]{1,0:T(8,128)S(1)} %get-tuple-element.11.own_ref, s32[72,128]{1,0:T(8,128)S(1)} %get-tuple-element.12.message_ref, f32[16,4096]{1,0:T(8,128)S(1)} %copy-done), custom_call_target="tpu_custom_call" | custom-call | flops 67108864 | bytes 524288 | tf_op jit(solution)/shard_map/score_docs/pallas_call | solution.py:181
  12.5 0.5 %gram_early.1.sum_ref = f32[8,32]{1,0:T(8,128)S(1)} custom-call(s32[72,128]{1,0:T(8,128)S(1)} %get-tuple-element.12.message_ref, bf16[128,256]{1,0:T(8,128)(2,1)S(1)} %get-tuple-element.15.grads_ref, bf16[128,256]{1,0:T(8,128)(2,1)S(1)} %get-tuple-element.16.ins_ref, s32[72,128]{1,0:T(8,128)S(1)} %collective-permute-done.1.refs_0_), custom_call_target="tpu_custom_call" | custom-call | tf_op jit(solution)/shard_map/gram_early/pallas_call | solution.py:338
  13.0 0.0 collective-permute-done.2.refs_0_
  13.0 0.9 %collective-permute-done.3.refs_1_ = s32[72,128]{1,0:T(8,128)S(1)} collective-permute-done((s32[72,128]{1,0:T(8,128)S(1)}, s32[72,128]{1,0:T(8,128)S(1)}, u32[]{:S(2)}, u32[]{:S(2)}) %collective-permute-start.3) | collective-permute-done | bytes 36896 | tf_op jit(solution)/shard_map/ppermute | solution.py:383
  13.9 1.1 %gram_middle.1 = (f32[8,32]{1,0:T(8,128)}, f32[8,16]{1,0:T(8,128)}, f32[8,32]{1,0:T(8,128)S(1)}) custom-call(s32[72,128]{1,0:T(8,128)S(1)} %get-tuple-element.12.message_ref, bf16[128,256]{1,0:T(8,128)(2,1)S(1)} %get-tuple-element.15.grads_ref, bf16[128,256]{1,0:T(8,128)(2,1)S(1)} %get-tuple-element.16.ins_ref, f32[8,16]{1,0:T(8,128)S(1)} %get-tuple-element.14.scores_ref, ...), custom_call_target="tpu_custom_call" | custom-call | tf_op jit(solution)/shard_map/gram_middle/pallas_call | solution.py:346
  15.0 0.9 %collective-permute-done.4.block_ref = s32[72,128]{1,0:T(8,128)S(1)} collective-permute-done((s32[72,128]{1,0:T(8,128)S(1)}, s32[72,128]{1,0:T(8,128)S(1)}, u32[]{:S(2)}, u32[]{:S(2)}) %collective-permute-start.4) | collective-permute-done | bytes 36896 | tf_op jit(solution)/shard_map/ppermute | solution.py:383
  (1 shorter events, 0.0 us)
Async XLA Ops:
  0.6 4.3 %copy-start.1 = (s32[1,128]{1,0:T(1,128)S(1)}, s32[1,128]{1,0:T(1,128)}, u32[]{:S(2)}) copy-start(s32[1,128]{1,0:T(1,128)} %ids_ref.1) | copy-start | bytes 1540
  0.6 11.4 %copy-start = (f32[16,4096]{1,0:T(8,128)S(1)}, f32[16,4096]{1,0:T(8,128)}, u32[]{:S(2)}) copy-start(f32[16,4096]{1,0:T(8,128)} %queries.1) | copy-start | bytes 786436
  3.5 1.4 %collective-permute-start = (f32[128,128]{1,0:T(8,128)S(1)}, f32[128,128]{1,0:T(8,128)S(1)}, u32[]{:S(2)}, u32[]{:S(2)}) collective-permute-start(f32[128,128]{1,0:T(8,128)S(1)} %partial_codes.1.mine_ref), channel_id=1, source_target_pairs={{0,1},{1,0},{2,3},{3,2},{4,5},{5,4},{6,7},{7,6},{8,9},{9,8},{10,11... | collective-permute-start | bytes 196616 | tf_op jit(solution)/shard_map/ppermute | solution.py:371
  5.0 4.8 %collective-permute-start.1 = (s32[72,128]{1,0:T(8,128)S(1)}, s32[72,128]{1,0:T(8,128)S(1)}, u32[]{:S(2)}, u32[]{:S(2)}) collective-permute-start(s32[72,128]{1,0:T(8,128)S(1)} %get-tuple-element.12.message_ref), channel_id=1, source_target_pairs={{0,2},{1,8},{2,0},{3,10},{4,6},{5,12},{6,4},{7,14},{9,1},{8,11},{1... | collective-permute-start | bytes 110600 | tf_op jit(solution)/shard_map/ppermute | solution.py:383
  7.9 5.0 %collective-permute-start.2 = (s32[72,128]{1,0:T(8,128)S(1)}, s32[72,128]{1,0:T(8,128)S(1)}, u32[]{:S(2)}, u32[]{:S(2)}) collective-permute-start(s32[72,128]{1,0:T(8,128)S(1)} %get-tuple-element.12.message_ref), channel_id=1, source_target_pairs={{0,4},{1,14},{2,6},{3,12},{4,0},{5,10},{6,2},{7,8},{9,7},{8,13},{1... | collective-permute-start | bytes 110600 | tf_op jit(solution)/shard_map/ppermute | solution.py:383
  9.9 4.0 %collective-permute-start.3 = (s32[72,128]{1,0:T(8,128)S(1)}, s32[72,128]{1,0:T(8,128)S(1)}, u32[]{:S(2)}, u32[]{:S(2)}) collective-permute-start(s32[72,128]{1,0:T(8,128)S(1)} %collective-permute-done.1.refs_0_), channel_id=1, source_target_pairs={{0,4},{1,5},{2,6},{3,7},{4,0},{5,1},{6,2},{7,3},{8,10},{9,13},{10,... | collective-permute-start | bytes 110600 | tf_op jit(solution)/shard_map/ppermute | solution.py:383
  12.0 4.0 %collective-permute-start.4 = (s32[72,128]{1,0:T(8,128)S(1)}, s32[72,128]{1,0:T(8,128)S(1)}, u32[]{:S(2)}, u32[]{:S(2)}) collective-permute-start(s32[72,128]{1,0:T(8,128)S(1)} %collective-permute-done.1.refs_0_), channel_id=1, source_target_pairs={{0,4},{1,3},{2,6},{3,1},{4,0},{5,7},{6,2},{7,5},{8,12},{9,11},{10,... | collective-permute-start | bytes 110600 | tf_op jit(solution)/shard_map/ppermute | solution.py:383

commit v23 on v18

--- a/solution.py
+++ b/solution.py
@@ -56,8 +56,8 @@
                 pltpu.make_async_copy(w_src.at[:, pl.ds(there, size)], w_dst.at[:, here], sems.at[sem]),
                 pltpu.make_async_copy(src.at[:, here], dst.at[:, here], sems.at[sem + 1]),
             )
-            for copy in copies:
-                copy.start()
+            for priority, copy in zip((1, 0), copies):
+                copy.start(priority=priority)
             jobs.append((copies, dst, w_dst, row, at, size))
     totals = {}
     for copies, dst, w_dst, row, at, size in jobs:

time: 16.2 us -> 16.6 us (1.025)
  Pallas kernels: 4.99 us -> 5.44 us
    pallas_call x1, Pallas kernels: 2.81 us -> 3.26 us  [partial_codes(): pl.pallas_call(codes_kernel, out_shape=jax.ShapeDtypeStruct((2 * rank, to...]
  transfers between devices with their start and end apart: 5 -> 5, of which waited for: 4 -> 4; matrix products, arithmetic and copies ran while one was open for 0% -> 0% of each run, Pallas kernels for 13% -> 12%
where the time goes in v23:
time: 16.6 us; the launch traced here: 16.4 us
  starting transfers between devices  7.13 us (43%)
  Pallas kernels  5.44 us (33%)
  waiting for transfers between devices  3.14 us (19%)
  between operations  0.69 us (4%)
    ppermute x4, starting transfers between devices, local(): lax.ppermute(blocks[what] if what >= 0 else message, ('dp', 'tensor'), mo...  6.6 us
    pallas_call x1, Pallas kernels, partial_codes(): pl.pallas_call(codes_kernel, out_shape=jax.ShapeDtypeStruct((2 * rank, to...  3.26 us
    ppermute x4, waiting for transfers between devices, local(): lax.ppermute(blocks[what] if what >= 0 else message, ('dp', 'tensor'), mo...  2.24 us
    pallas_call x1, Pallas kernels, gram_of(): pl.pallas_call(functools.partial(middle_kernel, half, middle), out_shape=...  1.07 us
    ppermute x1, waiting for transfers between devices, local(): other = lax.ppermute(mine, 'tensor', [(0, 1), (1, 0)])  0.9 us
    ppermute x1, starting transfers between devices, local(): other = lax.ppermute(mine, 'tensor', [(0, 1), (1, 0)])  0.52 us
    pallas_call x1, Pallas kernels, score_docs(): pl.pallas_call(scores_kernel, out_shape=(jax.ShapeDtypeStruct((DOCS_DEV,...  0.5 us
    pallas_call x1, Pallas kernels, gram_of(): pl.pallas_call(functools.partial(early_kernel, half, early), out_shape=ro...  0.45 us
  transfers between devices with their start and end apart: 5, of which 4 were waited for; matrix products, arithmetic and copies ran while one was open for 0% of the time, Pallas kernels for 12%

profile of v23, /device:TPU:0, one launch (start us, length us, event | category | flops | bytes accessed | tf_op | source)
XLA Modules:
  0.0 16.4 jit_solution(15949906158864236533)
XLA Ops:
  0.6 0.0 copy-start.1
  0.6 0.0 copy-start
  0.7 3.3 %partial_codes.1.mine_ref = f32[128,128]{1,0:T(8,128)S(1)} custom-call(bf16[128,7168]{1,0:T(8,128)(2,1)} %x_hbm.1, bf16[128,2048]{1,0:T(8,128)(2,1)} %y_hbm.1, bf16[64,14336]{1,0:T(8,128)(2,1)} %bitcast.2, bf16[64,4096]{1,0:T(8,128)(2,1)} %bitcast.3), custom_call_target="tpu_custom_call" | custom-call | tf_op jit(solution)/shard_map/partial_codes/pallas_call | solution.py:77
  3.9 0.5 %collective-permute-start = (f32[128,128]{1,0:T(8,128)S(1)}, f32[128,128]{1,0:T(8,128)S(1)}, u32[]{:S(2)}, u32[]{:S(2)}) collective-permute-start(f32[128,128]{1,0:T(8,128)S(1)} %partial_codes.1.mine_ref), channel_id=1, source_target_pairs={{0,1},{1,0},{2,3},{3,2},{4,5},{5,4},{6,7},{7,6},{8,9},{9,8},{10,11... | collective-permute-start | bytes 196616 | tf_op jit(solution)/shard_map/ppermute | solution.py:360
  4.4 0.9 %collective-permute-done.other_ref = f32[128,128]{1,0:T(8,128)S(1)} collective-permute-done((f32[128,128]{1,0:T(8,128)S(1)}, f32[128,128]{1,0:T(8,128)S(1)}, u32[]{:S(2)}, u32[]{:S(2)}) %collective-permute-start) | collective-permute-done | bytes 65568 | tf_op jit(solution)/shard_map/ppermute | solution.py:360
  5.3 0.0 copy-done.1
  5.3 0.1 pack_codes.1
  5.5 2.9 %collective-permute-start.1 = (s32[72,128]{1,0:T(8,128)S(1)}, s32[72,128]{1,0:T(8,128)S(1)}, u32[]{:S(2)}, u32[]{:S(2)}) collective-permute-start(s32[72,128]{1,0:T(8,128)S(1)} %get-tuple-element.12.message_ref), channel_id=1, source_target_pairs={{0,2},{1,8},{2,0},{3,10},{4,6},{5,12},{6,4},{7,14},{9,1},{8,11},{1... | collective-permute-start | bytes 110600 | tf_op jit(solution)/shard_map/ppermute | solution.py:372
  8.4 1.6 %collective-permute-start.2 = (s32[72,128]{1,0:T(8,128)S(1)}, s32[72,128]{1,0:T(8,128)S(1)}, u32[]{:S(2)}, u32[]{:S(2)}) collective-permute-start(s32[72,128]{1,0:T(8,128)S(1)} %get-tuple-element.12.message_ref), channel_id=1, source_target_pairs={{0,4},{1,14},{2,6},{3,12},{4,0},{5,10},{6,2},{7,8},{9,7},{8,13},{1... | collective-permute-start | bytes 110600 | tf_op jit(solution)/shard_map/ppermute | solution.py:372
  10.0 0.4 %collective-permute-done.1.refs_0_ = s32[72,128]{1,0:T(8,128)S(1)} collective-permute-done((s32[72,128]{1,0:T(8,128)S(1)}, s32[72,128]{1,0:T(8,128)S(1)}, u32[]{:S(2)}, u32[]{:S(2)}) %collective-permute-start.1) | collective-permute-done | bytes 36896 | tf_op jit(solution)/shard_map/ppermute | solution.py:372
  10.3 2.1 %collective-permute-start.3 = (s32[72,128]{1,0:T(8,128)S(1)}, s32[72,128]{1,0:T(8,128)S(1)}, u32[]{:S(2)}, u32[]{:S(2)}) collective-permute-start(s32[72,128]{1,0:T(8,128)S(1)} %collective-permute-done.1.refs_0_), channel_id=1, source_target_pairs={{0,4},{1,5},{2,6},{3,7},{4,0},{5,1},{6,2},{7,3},{8,10},{9,13},{10,... | collective-permute-start | bytes 110600 | tf_op jit(solution)/shard_map/ppermute | solution.py:372
  12.4 0.0 collective-permute-start.4
  12.5 0.0 copy-done
  12.5 0.5 %score_docs.1 = (f32[8,16]{1,0:T(8,128)S(1)}, bf16[128,256]{1,0:T(8,128)(2,1)S(1)}, bf16[128,256]{1,0:T(8,128)(2,1)S(1)}, bf16[512,256]{1,0:T(8,128)(2,1)S(1)}) custom-call(f32[128,128]{1,0:T(8,128)S(1)} %get-tuple-element.11.own_ref, s32[72,128]{1,0:T(8,128)S(1)} %get-tuple-element.12.message_ref, f32[16,4096]{1,0:T(8,128)S(1)} %copy-done), custom_call_target="tpu_custom_call" | custom-call | flops 67108864 | bytes 524288 | tf_op jit(solution)/shard_map/score_docs/pallas_call | solution.py:181
  13.0 0.5 %gram_early.1.sum_ref = f32[8,32]{1,0:T(8,128)S(1)} custom-call(s32[72,128]{1,0:T(8,128)S(1)} %get-tuple-element.12.message_ref, bf16[128,256]{1,0:T(8,128)(2,1)S(1)} %get-tuple-element.15.grads_ref, bf16[128,256]{1,0:T(8,128)(2,1)S(1)} %get-tuple-element.16.ins_ref, s32[72,128]{1,0:T(8,128)S(1)} %collective-permute-done.1.refs_0_), custom_call_target="tpu_custom_call" | custom-call | tf_op jit(solution)/shard_map/gram_early/pallas_call | solution.py:327
  13.4 0.0 collective-permute-done.2.refs_0_
  13.4 0.9 %collective-permute-done.3.refs_1_ = s32[72,128]{1,0:T(8,128)S(1)} collective-permute-done((s32[72,128]{1,0:T(8,128)S(1)}, s32[72,128]{1,0:T(8,128)S(1)}, u32[]{:S(2)}, u32[]{:S(2)}) %collective-permute-start.3) | collective-permute-done | bytes 36896 | tf_op jit(solution)/shard_map/ppermute | solution.py:372
  14.4 1.1 %gram_middle.1 = (f32[8,32]{1,0:T(8,128)}, f32[8,16]{1,0:T(8,128)}, f32[8,32]{1,0:T(8,128)S(1)}) custom-call(s32[72,128]{1,0:T(8,128)S(1)} %get-tuple-element.12.message_ref, bf16[128,256]{1,0:T(8,128)(2,1)S(1)} %get-tuple-element.15.grads_ref, bf16[128,256]{1,0:T(8,128)(2,1)S(1)} %get-tuple-element.16.ins_ref, f32[8,16]{1,0:T(8,128)S(1)} %get-tuple-element.14.scores_ref, ...), custom_call_target="tpu_custom_call" | custom-call | tf_op jit(solution)/shard_map/gram_middle/pallas_call | solution.py:335
  15.4 0.9 %collective-permute-done.4.block_ref = s32[72,128]{1,0:T(8,128)S(1)} collective-permute-done((s32[72,128]{1,0:T(8,128)S(1)}, s32[72,128]{1,0:T(8,128)S(1)}, u32[]{:S(2)}, u32[]{:S(2)}) %collective-permute-start.4) | collective-permute-done | bytes 36896 | tf_op jit(solution)/shard_map/ppermute | solution.py:372
  (1 shorter events, 0.0 us)
Async XLA Ops:
  0.6 4.7 %copy-start.1 = (s32[1,128]{1,0:T(1,128)S(1)}, s32[1,128]{1,0:T(1,128)}, u32[]{:S(2)}) copy-start(s32[1,128]{1,0:T(1,128)} %ids_ref.1) | copy-start | bytes 1540
  0.6 11.8 %copy-start = (f32[16,4096]{1,0:T(8,128)S(1)}, f32[16,4096]{1,0:T(8,128)}, u32[]{:S(2)}) copy-start(f32[16,4096]{1,0:T(8,128)} %queries.1) | copy-start | bytes 786436
  3.9 1.4 %collective-permute-start = (f32[128,128]{1,0:T(8,128)S(1)}, f32[128,128]{1,0:T(8,128)S(1)}, u32[]{:S(2)}, u32[]{:S(2)}) collective-permute-start(f32[128,128]{1,0:T(8,128)S(1)} %partial_codes.1.mine_ref), channel_id=1, source_target_pairs={{0,1},{1,0},{2,3},{3,2},{4,5},{5,4},{6,7},{7,6},{8,9},{9,8},{10,11... | collective-permute-start | bytes 196616 | tf_op jit(solution)/shard_map/ppermute | solution.py:360
  5.5 4.8 %collective-permute-start.1 = (s32[72,128]{1,0:T(8,128)S(1)}, s32[72,128]{1,0:T(8,128)S(1)}, u32[]{:S(2)}, u32[]{:S(2)}) collective-permute-start(s32[72,128]{1,0:T(8,128)S(1)} %get-tuple-element.12.message_ref), channel_id=1, source_target_pairs={{0,2},{1,8},{2,0},{3,10},{4,6},{5,12},{6,4},{7,14},{9,1},{8,11},{1... | collective-permute-start | bytes 110600 | tf_op jit(solution)/shard_map/ppermute | solution.py:372
  8.4 5.0 %collective-permute-start.2 = (s32[72,128]{1,0:T(8,128)S(1)}, s32[72,128]{1,0:T(8,128)S(1)}, u32[]{:S(2)}, u32[]{:S(2)}) collective-permute-start(s32[72,128]{1,0:T(8,128)S(1)} %get-tuple-element.12.message_ref), channel_id=1, source_target_pairs={{0,4},{1,14},{2,6},{3,12},{4,0},{5,10},{6,2},{7,8},{9,7},{8,13},{1... | collective-permute-start | bytes 110600 | tf_op jit(solution)/shard_map/ppermute | solution.py:372
  10.3 4.0 %collective-permute-start.3 = (s32[72,128]{1,0:T(8,128)S(1)}, s32[72,128]{1,0:T(8,128)S(1)}, u32[]{:S(2)}, u32[]{:S(2)}) collective-permute-start(s32[72,128]{1,0:T(8,128)S(1)} %collective-permute-done.1.refs_0_), channel_id=1, source_target_pairs={{0,4},{1,5},{2,6},{3,7},{4,0},{5,1},{6,2},{7,3},{8,10},{9,13},{10,... | collective-permute-start | bytes 110600 | tf_op jit(solution)/shard_map/ppermute | solution.py:372
  12.4 4.0 %collective-permute-start.4 = (s32[72,128]{1,0:T(8,128)S(1)}, s32[72,128]{1,0:T(8,128)S(1)}, u32[]{:S(2)}, u32[]{:S(2)}) collective-permute-start(s32[72,128]{1,0:T(8,128)S(1)} %collective-permute-done.1.refs_0_), channel_id=1, source_target_pairs={{0,4},{1,3},{2,6},{3,1},{4,0},{5,7},{6,2},{7,5},{8,12},{9,11},{10,... | collective-permute-start | bytes 110600 | tf_op jit(solution)/shard_map/ppermute | solution.py:372

commit v24 on v18

--- a/solution.py
+++ b/solution.py
@@ -22,8 +22,15 @@
 
 def pieces_of(depth):
     count = -(-depth // 2432)
-    size = -(-depth // (count * 128)) * 128
-    return [(at, min(size, depth - at)) for at in range(0, depth, size)]
+    pieces, at = [], 0
+    for n in range(count):
+        share = 1.0 + 0.19 * ((count - 1) / 2 - n)
+        size = max(round(depth * share / (count * 128)), 1) * 128
+        size = depth - at if n == count - 1 else min(size, depth - at)
+        if size > 0:
+            pieces.append((at, size))
+        at += size
+    return pieces
 
 
 def sum_of(parts):

time: 16.2 us -> 16.2 us (level)
  no operation moved by 1% of the time
where the time goes in v24:
time: 16.2 us; the launch traced here: 16 us
  starting transfers between devices  7.13 us (44%)
  Pallas kernels  5.03 us (31%)
  waiting for transfers between devices  3.16 us (20%)
  between operations  0.69 us (4%)
    ppermute x4, starting transfers between devices, local(): lax.ppermute(blocks[what] if what >= 0 else message, ('dp', 'tensor'), mo...  6.62 us
    pallas_call x1, Pallas kernels, partial_codes(): pl.pallas_call(codes_kernel, out_shape=jax.ShapeDtypeStruct((2 * rank, to...  2.87 us
    ppermute x4, waiting for transfers between devices, local(): lax.ppermute(blocks[what] if what >= 0 else message, ('dp', 'tensor'), mo...  2.25 us
    pallas_call x1, Pallas kernels, gram_of(): pl.pallas_call(functools.partial(middle_kernel, half, middle), out_shape=...  1.07 us
    ppermute x1, waiting for transfers between devices, local(): other = lax.ppermute(mine, 'tensor', [(0, 1), (1, 0)])  0.9 us
    ppermute x1, starting transfers between devices, local(): other = lax.ppermute(mine, 'tensor', [(0, 1), (1, 0)])  0.51 us
    pallas_call x1, Pallas kernels, score_docs(): pl.pallas_call(scores_kernel, out_shape=(jax.ShapeDtypeStruct((DOCS_DEV,...  0.49 us
    pallas_call x1, Pallas kernels, gram_of(): pl.pallas_call(functools.partial(early_kernel, half, early), out_shape=ro...  0.45 us
  transfers between devices with their start and end apart: 5, of which 4 were waited for; matrix products, arithmetic and copies ran while one was open for 0% of the time, Pallas kernels for 13%

profile of v24, /device:TPU:0, one launch (start us, length us, event | category | flops | bytes accessed | tf_op | source)
XLA Modules:
  0.0 16.0 jit_solution(2221053160028994566)
XLA Ops:
  0.6 0.0 copy-start.1
  0.6 0.0 copy-start
  0.7 2.9 %partial_codes.1.mine_ref = f32[128,128]{1,0:T(8,128)S(1)} custom-call(bf16[128,7168]{1,0:T(8,128)(2,1)} %x_hbm.1, bf16[128,2048]{1,0:T(8,128)(2,1)} %y_hbm.1, bf16[64,14336]{1,0:T(8,128)(2,1)} %bitcast.2, bf16[64,4096]{1,0:T(8,128)(2,1)} %bitcast.3), custom_call_target="tpu_custom_call" | custom-call | tf_op jit(solution)/shard_map/partial_codes/pallas_call | solution.py:84
  3.5 0.5 %collective-permute-start = (f32[128,128]{1,0:T(8,128)S(1)}, f32[128,128]{1,0:T(8,128)S(1)}, u32[]{:S(2)}, u32[]{:S(2)}) collective-permute-start(f32[128,128]{1,0:T(8,128)S(1)} %partial_codes.1.mine_ref), channel_id=1, source_target_pairs={{0,1},{1,0},{2,3},{3,2},{4,5},{5,4},{6,7},{7,6},{8,9},{9,8},{10,11... | collective-permute-start | bytes 196616 | tf_op jit(solution)/shard_map/ppermute | solution.py:367
  4.0 0.9 %collective-permute-done.other_ref = f32[128,128]{1,0:T(8,128)S(1)} collective-permute-done((f32[128,128]{1,0:T(8,128)S(1)}, f32[128,128]{1,0:T(8,128)S(1)}, u32[]{:S(2)}, u32[]{:S(2)}) %collective-permute-start) | collective-permute-done | bytes 65568 | tf_op jit(solution)/shard_map/ppermute | solution.py:367
  4.9 0.0 copy-done.1
  4.9 0.1 pack_codes.1
  5.1 2.9 %collective-permute-start.1 = (s32[72,128]{1,0:T(8,128)S(1)}, s32[72,128]{1,0:T(8,128)S(1)}, u32[]{:S(2)}, u32[]{:S(2)}) collective-permute-start(s32[72,128]{1,0:T(8,128)S(1)} %get-tuple-element.12.message_ref), channel_id=1, source_target_pairs={{0,2},{1,8},{2,0},{3,10},{4,6},{5,12},{6,4},{7,14},{9,1},{8,11},{1... | collective-permute-start | bytes 110600 | tf_op jit(solution)/shard_map/ppermute | solution.py:379
  8.0 1.6 %collective-permute-start.2 = (s32[72,128]{1,0:T(8,128)S(1)}, s32[72,128]{1,0:T(8,128)S(1)}, u32[]{:S(2)}, u32[]{:S(2)}) collective-permute-start(s32[72,128]{1,0:T(8,128)S(1)} %get-tuple-element.12.message_ref), channel_id=1, source_target_pairs={{0,4},{1,14},{2,6},{3,12},{4,0},{5,10},{6,2},{7,8},{9,7},{8,13},{1... | collective-permute-start | bytes 110600 | tf_op jit(solution)/shard_map/ppermute | solution.py:379
  9.6 0.4 %collective-permute-done.1.refs_0_ = s32[72,128]{1,0:T(8,128)S(1)} collective-permute-done((s32[72,128]{1,0:T(8,128)S(1)}, s32[72,128]{1,0:T(8,128)S(1)}, u32[]{:S(2)}, u32[]{:S(2)}) %collective-permute-start.1) | collective-permute-done | bytes 36896 | tf_op jit(solution)/shard_map/ppermute | solution.py:379
  9.9 2.1 %collective-permute-start.3 = (s32[72,128]{1,0:T(8,128)S(1)}, s32[72,128]{1,0:T(8,128)S(1)}, u32[]{:S(2)}, u32[]{:S(2)}) collective-permute-start(s32[72,128]{1,0:T(8,128)S(1)} %collective-permute-done.1.refs_0_), channel_id=1, source_target_pairs={{0,4},{1,5},{2,6},{3,7},{4,0},{5,1},{6,2},{7,3},{8,10},{9,13},{10,... | collective-permute-start | bytes 110600 | tf_op jit(solution)/shard_map/ppermute | solution.py:379
  12.0 0.0 collective-permute-start.4
  12.1 0.0 copy-done
  12.1 0.5 %score_docs.1 = (f32[8,16]{1,0:T(8,128)S(1)}, bf16[128,256]{1,0:T(8,128)(2,1)S(1)}, bf16[128,256]{1,0:T(8,128)(2,1)S(1)}, bf16[512,256]{1,0:T(8,128)(2,1)S(1)}) custom-call(f32[128,128]{1,0:T(8,128)S(1)} %get-tuple-element.11.own_ref, s32[72,128]{1,0:T(8,128)S(1)} %get-tuple-element.12.message_ref, f32[16,4096]{1,0:T(8,128)S(1)} %copy-done), custom_call_target="tpu_custom_call" | custom-call | flops 67108864 | bytes 524288 | tf_op jit(solution)/shard_map/score_docs/pallas_call | solution.py:188
  12.6 0.5 %gram_early.1.sum_ref = f32[8,32]{1,0:T(8,128)S(1)} custom-call(s32[72,128]{1,0:T(8,128)S(1)} %get-tuple-element.12.message_ref, bf16[128,256]{1,0:T(8,128)(2,1)S(1)} %get-tuple-element.15.grads_ref, bf16[128,256]{1,0:T(8,128)(2,1)S(1)} %get-tuple-element.16.ins_ref, s32[72,128]{1,0:T(8,128)S(1)} %collective-permute-done.1.refs_0_), custom_call_target="tpu_custom_call" | custom-call | tf_op jit(solution)/shard_map/gram_early/pallas_call | solution.py:334
  13.0 0.0 collective-permute-done.2.refs_0_
  13.0 0.9 %collective-permute-done.3.refs_1_ = s32[72,128]{1,0:T(8,128)S(1)} collective-permute-done((s32[72,128]{1,0:T(8,128)S(1)}, s32[72,128]{1,0:T(8,128)S(1)}, u32[]{:S(2)}, u32[]{:S(2)}) %collective-permute-start.3) | collective-permute-done | bytes 36896 | tf_op jit(solution)/shard_map/ppermute | solution.py:379
  14.0 1.1 %gram_middle.1 = (f32[8,32]{1,0:T(8,128)}, f32[8,16]{1,0:T(8,128)}, f32[8,32]{1,0:T(8,128)S(1)}) custom-call(s32[72,128]{1,0:T(8,128)S(1)} %get-tuple-element.12.message_ref, bf16[128,256]{1,0:T(8,128)(2,1)S(1)} %get-tuple-element.15.grads_ref, bf16[128,256]{1,0:T(8,128)(2,1)S(1)} %get-tuple-element.16.ins_ref, f32[8,16]{1,0:T(8,128)S(1)} %get-tuple-element.14.scores_ref, ...), custom_call_target="tpu_custom_call" | custom-call | tf_op jit(solution)/shard_map/gram_middle/pallas_call | solution.py:342
  15.0 0.9 %collective-permute-done.4.block_ref = s32[72,128]{1,0:T(8,128)S(1)} collective-permute-done((s32[72,128]{1,0:T(8,128)S(1)}, s32[72,128]{1,0:T(8,128)S(1)}, u32[]{:S(2)}, u32[]{:S(2)}) %collective-permute-start.4) | collective-permute-done | bytes 36896 | tf_op jit(solution)/shard_map/ppermute | solution.py:379
  (1 shorter events, 0.0 us)
Async XLA Ops:
  0.6 4.3 %copy-start.1 = (s32[1,128]{1,0:T(1,128)S(1)}, s32[1,128]{1,0:T(1,128)}, u32[]{:S(2)}) copy-start(s32[1,128]{1,0:T(1,128)} %ids_ref.1) | copy-start | bytes 1540
  0.6 11.4 %copy-start = (f32[16,4096]{1,0:T(8,128)S(1)}, f32[16,4096]{1,0:T(8,128)}, u32[]{:S(2)}) copy-start(f32[16,4096]{1,0:T(8,128)} %queries.1) | copy-start | bytes 786436
  3.5 1.4 %collective-permute-start = (f32[128,128]{1,0:T(8,128)S(1)}, f32[128,128]{1,0:T(8,128)S(1)}, u32[]{:S(2)}, u32[]{:S(2)}) collective-permute-start(f32[128,128]{1,0:T(8,128)S(1)} %partial_codes.1.mine_ref), channel_id=1, source_target_pairs={{0,1},{1,0},{2,3},{3,2},{4,5},{5,4},{6,7},{7,6},{8,9},{9,8},{10,11... | collective-permute-start | bytes 196616 | tf_op jit(solution)/shard_map/ppermute | solution.py:367
  5.1 4.8 %collective-permute-start.1 = (s32[72,128]{1,0:T(8,128)S(1)}, s32[72,128]{1,0:T(8,128)S(1)}, u32[]{:S(2)}, u32[]{:S(2)}) collective-permute-start(s32[72,128]{1,0:T(8,128)S(1)} %get-tuple-element.12.message_ref), channel_id=1, source_target_pairs={{0,2},{1,8},{2,0},{3,10},{4,6},{5,12},{6,4},{7,14},{9,1},{8,11},{1... | collective-permute-start | bytes 110600 | tf_op jit(solution)/shard_map/ppermute | solution.py:379
  8.0 5.0 %collective-permute-start.2 = (s32[72,128]{1,0:T(8,128)S(1)}, s32[72,128]{1,0:T(8,128)S(1)}, u32[]{:S(2)}, u32[]{:S(2)}) collective-permute-start(s32[72,128]{1,0:T(8,128)S(1)} %get-tuple-element.12.message_ref), channel_id=1, source_target_pairs={{0,4},{1,14},{2,6},{3,12},{4,0},{5,10},{6,2},{7,8},{9,7},{8,13},{1... | collective-permute-start | bytes 110600 | tf_op jit(solution)/shard_map/ppermute | solution.py:379
  9.9 4.0 %collective-permute-start.3 = (s32[72,128]{1,0:T(8,128)S(1)}, s32[72,128]{1,0:T(8,128)S(1)}, u32[]{:S(2)}, u32[]{:S(2)}) collective-permute-start(s32[72,128]{1,0:T(8,128)S(1)} %collective-permute-done.1.refs_0_), channel_id=1, source_target_pairs={{0,4},{1,5},{2,6},{3,7},{4,0},{5,1},{6,2},{7,3},{8,10},{9,13},{10,... | collective-permute-start | bytes 110600 | tf_op jit(solution)/shard_map/ppermute | solution.py:379
  12.0 4.0 %collective-permute-start.4 = (s32[72,128]{1,0:T(8,128)S(1)}, s32[72,128]{1,0:T(8,128)S(1)}, u32[]{:S(2)}, u32[]{:S(2)}) collective-permute-start(s32[72,128]{1,0:T(8,128)S(1)} %collective-permute-done.1.refs_0_), channel_id=1, source_target_pairs={{0,4},{1,3},{2,6},{3,1},{4,0},{5,7},{6,2},{7,5},{8,12},{9,11},{10,... | collective-permute-start | bytes 110600 | tf_op jit(solution)/shard_map/ppermute | solution.py:379

commit v25 on v18

--- a/solution.py
+++ b/solution.py
@@ -199,7 +199,7 @@
     if half == 4:
         return [
             (-1, (4, 4), (1, 1), (1,)),
-            (-1, (7, 7), (2, 2), (1,)),
+            (-1, (7, 7), (2, 2), ()),
             (0, (2, 1), (2, 2), ()),
             (0, (1, 2), (2, 1), ()),
         ]

time: 16.2 us -> 16.5 us (1.019)
  the two profiles are of different devices: /device:TPU:0 before, /device:TPU:1 now
where the time goes in v25:
time: 16.5 us; the launch traced here: 16.4 us
  starting transfers between devices  7.54 us (46%)
  Pallas kernels  5.36 us (32%)
  waiting for transfers between devices  2.78 us (17%)
  between operations  0.69 us (4%)
    ppermute x4, starting transfers between devices, local(): lax.ppermute(blocks[what] if what >= 0 else message, ('dp', 'tensor'), mo...  7.42 us
    pallas_call x1, Pallas kernels, partial_codes(): pl.pallas_call(codes_kernel, out_shape=jax.ShapeDtypeStruct((2 * rank, to...  2.81 us
    ppermute x4, waiting for transfers between devices, local(): lax.ppermute(blocks[what] if what >= 0 else message, ('dp', 'tensor'), mo...  1.58 us
    ppermute x1, waiting for transfers between devices, local(): other = lax.ppermute(mine, 'tensor', [(0, 1), (1, 0)])  1.2 us
    pallas_call x1, Pallas kernels, gram_of(): pl.pallas_call(functools.partial(last_kernel, half), out_shape=results, i...  0.99 us
    pallas_call x1, Pallas kernels, score_docs(): pl.pallas_call(scores_kernel, out_shape=(jax.ShapeDtypeStruct((DOCS_DEV,...  0.49 us
    pallas_call x1, Pallas kernels, gram_of(): pl.pallas_call(functools.partial(middle_kernel, half, middle), out_shape=...  0.48 us
    pallas_call x1, Pallas kernels, gram_of(): pl.pallas_call(functools.partial(early_kernel, half, early), out_shape=ro...  0.45 us
  transfers between devices with their start and end apart: 5, of which 2 were waited for; matrix products, arithmetic and copies ran while one was open for 0% of the time, Pallas kernels for 9%

profile of v25, /device:TPU:1, one launch (start us, length us, event | category | flops | bytes accessed | tf_op | source)
XLA Modules:
  0.0 16.4 jit_solution(546667030357036750)
XLA Ops:
  0.6 0.0 copy-start.1
  0.6 0.0 copy-start
  0.7 2.8 %partial_codes.1.mine_ref = f32[128,128]{1,0:T(8,128)S(1)} custom-call(bf16[128,7168]{1,0:T(8,128)(2,1)} %x_hbm.1, bf16[128,2048]{1,0:T(8,128)(2,1)} %y_hbm.1, bf16[64,14336]{1,0:T(8,128)(2,1)} %bitcast.2, bf16[64,4096]{1,0:T(8,128)(2,1)} %bitcast.3), custom_call_target="tpu_custom_call" | custom-call | tf_op jit(solution)/shard_map/partial_codes/pallas_call | solution.py:77
  3.5 0.1 collective-permute-start
  3.6 1.2 %collective-permute-done.other_ref = f32[128,128]{1,0:T(8,128)S(1)} collective-permute-done((f32[128,128]{1,0:T(8,128)S(1)}, f32[128,128]{1,0:T(8,128)S(1)}, u32[]{:S(2)}, u32[]{:S(2)}) %collective-permute-start) | collective-permute-done | bytes 65568 | tf_op jit(solution)/shard_map/ppermute | solution.py:360
  4.8 0.0 copy-done.1
  4.8 0.1 pack_codes.1
  4.9 3.8 %collective-permute-start.1 = (s32[72,128]{1,0:T(8,128)S(1)}, s32[72,128]{1,0:T(8,128)S(1)}, u32[]{:S(2)}, u32[]{:S(2)}) collective-permute-start(s32[72,128]{1,0:T(8,128)S(1)} %get-tuple-element.12.message_ref), channel_id=1, source_target_pairs={{0,2},{1,8},{2,0},{3,10},{4,6},{5,12},{6,4},{7,14},{9,1},{8,11},{1... | collective-permute-start | bytes 110600 | tf_op jit(solution)/shard_map/ppermute | solution.py:372
  8.7 2.2 %collective-permute-start.2 = (s32[72,128]{1,0:T(8,128)S(1)}, s32[72,128]{1,0:T(8,128)S(1)}, u32[]{:S(2)}, u32[]{:S(2)}) collective-permute-start(s32[72,128]{1,0:T(8,128)S(1)} %get-tuple-element.12.message_ref), channel_id=1, source_target_pairs={{0,4},{1,14},{2,6},{3,12},{4,0},{5,10},{6,2},{7,8},{8,7},{9,13},{1... | collective-permute-start | bytes 110600 | tf_op jit(solution)/shard_map/ppermute | solution.py:372
  10.9 0.0 collective-permute-done.1.refs_0_
  10.9 0.2 %collective-permute-start.3 = (s32[72,128]{1,0:T(8,128)S(1)}, s32[72,128]{1,0:T(8,128)S(1)}, u32[]{:S(2)}, u32[]{:S(2)}) collective-permute-start(s32[72,128]{1,0:T(8,128)S(1)} %collective-permute-done.1.refs_0_), channel_id=1, source_target_pairs={{0,4},{1,5},{2,6},{3,7},{4,0},{5,1},{6,2},{7,3},{8,10},{9,13},{10,... | collective-permute-start | bytes 110600 | tf_op jit(solution)/shard_map/ppermute | solution.py:372
  11.2 1.2 %collective-permute-start.4 = (s32[72,128]{1,0:T(8,128)S(1)}, s32[72,128]{1,0:T(8,128)S(1)}, u32[]{:S(2)}, u32[]{:S(2)}) collective-permute-start(s32[72,128]{1,0:T(8,128)S(1)} %collective-permute-done.1.refs_0_), channel_id=1, source_target_pairs={{0,4},{1,3},{2,6},{3,1},{4,0},{5,7},{6,2},{7,5},{8,12},{9,11},{10,... | collective-permute-start | bytes 110600 | tf_op jit(solution)/shard_map/ppermute | solution.py:372
  12.4 0.0 copy-done
  12.4 0.5 %score_docs.1 = (f32[8,16]{1,0:T(8,128)S(1)}, bf16[128,256]{1,0:T(8,128)(2,1)S(1)}, bf16[128,256]{1,0:T(8,128)(2,1)S(1)}, bf16[512,256]{1,0:T(8,128)(2,1)S(1)}) custom-call(f32[128,128]{1,0:T(8,128)S(1)} %get-tuple-element.11.own_ref, s32[72,128]{1,0:T(8,128)S(1)} %get-tuple-element.12.message_ref, f32[16,4096]{1,0:T(8,128)S(1)} %copy-done), custom_call_target="tpu_custom_call" | custom-call | flops 67108864 | bytes 524288 | tf_op jit(solution)/shard_map/score_docs/pallas_call | solution.py:181
  12.9 0.5 %gram_early.1.sum_ref = f32[8,32]{1,0:T(8,128)S(1)} custom-call(s32[72,128]{1,0:T(8,128)S(1)} %get-tuple-element.12.message_ref, bf16[128,256]{1,0:T(8,128)(2,1)S(1)} %get-tuple-element.15.grads_ref, bf16[128,256]{1,0:T(8,128)(2,1)S(1)} %get-tuple-element.16.ins_ref, s32[72,128]{1,0:T(8,128)S(1)} %collective-permute-done.1.refs_0_), custom_call_target="tpu_custom_call" | custom-call | tf_op jit(solution)/shard_map/gram_early/pallas_call | solution.py:327
  13.3 1.6 %collective-permute-done.2.refs_0_ = s32[72,128]{1,0:T(8,128)S(1)} collective-permute-done((s32[72,128]{1,0:T(8,128)S(1)}, s32[72,128]{1,0:T(8,128)S(1)}, u32[]{:S(2)}, u32[]{:S(2)}) %collective-permute-start.2) | collective-permute-done | bytes 36896 | tf_op jit(solution)/shard_map/ppermute | solution.py:372
  14.9 0.0 collective-permute-done.3.refs_1_
  14.9 0.5 %gram_middle.1 = (f32[8,32]{1,0:T(8,128)}, f32[8,16]{1,0:T(8,128)}, f32[8,32]{1,0:T(8,128)S(1)}) custom-call(s32[72,128]{1,0:T(8,128)S(1)} %get-tuple-element.12.message_ref, bf16[128,256]{1,0:T(8,128)(2,1)S(1)} %get-tuple-element.15.grads_ref, bf16[128,256]{1,0:T(8,128)(2,1)S(1)} %get-tuple-element.16.ins_ref, f32[8,16]{1,0:T(8,128)S(1)} %get-tuple-element.14.scores_ref, ...), custom_call_target="tpu_custom_call" | custom-call | tf_op jit(solution)/shard_map/gram_middle/pallas_call | solution.py:335
  15.4 0.0 collective-permute-done.4.block_ref
  15.4 1.0 %gram_last.1 = (f32[8,32]{1,0:T(8,128)}, f32[8,16]{1,0:T(8,128)}) custom-call(bf16[512,256]{1,0:T(8,128)(2,1)S(1)} %get-tuple-element.13.feats_ref, f32[8,16]{1,0:T(8,128)S(1)} %get-tuple-element.14.scores_ref, f32[8,32]{1,0:T(8,128)S(1)} %get-tuple-element.17.sum_ref, ...), custom_call_target="tpu_custom_call", output_to_operand_aliasing={{0}: (4, {}), {1}: (5, {})} | custom-call | tf_op jit(solution)/shard_map/gram_last/pallas_call | solution.py:344
Async XLA Ops:
  0.6 4.2 %copy-start.1 = (s32[1,128]{1,0:T(1,128)S(1)}, s32[1,128]{1,0:T(1,128)}, u32[]{:S(2)}) copy-start(s32[1,128]{1,0:T(1,128)} %ids_ref.1) | copy-start | bytes 1540
  0.6 11.7 %copy-start = (f32[16,4096]{1,0:T(8,128)S(1)}, f32[16,4096]{1,0:T(8,128)}, u32[]{:S(2)}) copy-start(f32[16,4096]{1,0:T(8,128)} %queries.1) | copy-start | bytes 786436
  3.5 1.3 %collective-permute-start = (f32[128,128]{1,0:T(8,128)S(1)}, f32[128,128]{1,0:T(8,128)S(1)}, u32[]{:S(2)}, u32[]{:S(2)}) collective-permute-start(f32[128,128]{1,0:T(8,128)S(1)} %partial_codes.1.mine_ref), channel_id=1, source_target_pairs={{0,1},{1,0},{2,3},{3,2},{4,5},{5,4},{6,7},{7,6},{8,9},{9,8},{10,11... | collective-permute-start | bytes 196616 | tf_op jit(solution)/shard_map/ppermute | solution.py:360
  4.9 6.0 %collective-permute-start.1 = (s32[72,128]{1,0:T(8,128)S(1)}, s32[72,128]{1,0:T(8,128)S(1)}, u32[]{:S(2)}, u32[]{:S(2)}) collective-permute-start(s32[72,128]{1,0:T(8,128)S(1)} %get-tuple-element.12.message_ref), channel_id=1, source_target_pairs={{0,2},{1,8},{2,0},{3,10},{4,6},{5,12},{6,4},{7,14},{9,1},{8,11},{1... | collective-permute-start | bytes 110600 | tf_op jit(solution)/shard_map/ppermute | solution.py:372
  8.7 6.2 %collective-permute-start.2 = (s32[72,128]{1,0:T(8,128)S(1)}, s32[72,128]{1,0:T(8,128)S(1)}, u32[]{:S(2)}, u32[]{:S(2)}) collective-permute-start(s32[72,128]{1,0:T(8,128)S(1)} %get-tuple-element.12.message_ref), channel_id=1, source_target_pairs={{0,4},{1,14},{2,6},{3,12},{4,0},{5,10},{6,2},{7,8},{8,7},{9,13},{1... | collective-permute-start | bytes 110600 | tf_op jit(solution)/shard_map/ppermute | solution.py:372
  10.9 4.0 %collective-permute-start.3 = (s32[72,128]{1,0:T(8,128)S(1)}, s32[72,128]{1,0:T(8,128)S(1)}, u32[]{:S(2)}, u32[]{:S(2)}) collective-permute-start(s32[72,128]{1,0:T(8,128)S(1)} %collective-permute-done.1.refs_0_), channel_id=1, source_target_pairs={{0,4},{1,5},{2,6},{3,7},{4,0},{5,1},{6,2},{7,3},{8,10},{9,13},{10,... | collective-permute-start | bytes 110600 | tf_op jit(solution)/shard_map/ppermute | solution.py:372
  11.2 4.2 %collective-permute-start.4 = (s32[72,128]{1,0:T(8,128)S(1)}, s32[72,128]{1,0:T(8,128)S(1)}, u32[]{:S(2)}, u32[]{:S(2)}) collective-permute-start(s32[72,128]{1,0:T(8,128)S(1)} %collective-permute-done.1.refs_0_), channel_id=1, source_target_pairs={{0,4},{1,3},{2,6},{3,1},{4,0},{5,7},{6,2},{7,5},{8,12},{9,11},{10,... | collective-permute-start | bytes 110600 | tf_op jit(solution)/shard_map/ppermute | solution.py:372
